TPU v7x, 32 devices: a whole 2x2x4 slice. The times are simulated.
32 devices in a mesh: groups: 2 (over y), dp: 4 (over z), tensor: 2 (over x), seq: 2 (over core).
Axes of the slice: x: 2, y: 2, z: 4, core: 2. Of those that a mesh axis runs over, the one named last changes fastest.
Arguments:
- acts: bfloat16 [64, 256, 4096], P(('groups', 'dp'), 'seq', 'tensor'), parts along dimension 0, may hold values from -6 to 6
- grads: bfloat16 [64, 256, 14336], P(('groups', 'dp'), 'seq', 'tensor'), parts along dimension 0, may hold values from -0.375 to 0.375
- in_ids: int32 [64], P('tensor'), may hold values from 0 to 31
- in_signs: int32 [64], P('tensor'), may hold values from 0 to 1
- out_ids: int32 [224], P('tensor'), may hold values from 0 to 31
- out_signs: int32 [224], P('tensor'), may hold values from 0 to 1
- in_table: bfloat16 [32, 4096], replicated, may hold values from -0.09375 to 0.09375
- out_table: bfloat16 [32, 4096], replicated, may hold values from -0.046875 to 0.046875
Outputs:
- projected: float32 [64, 4096], P(('groups', 'dp'), ('tensor', 'seq')), parts along dimension 0
- fisher: float32 [8192, 4096], P(('groups', 'tensor', 'seq'), 'dp'), parts along dimension 0
There are 2 independent parts, one for each index of `groups`. A program takes and returns all parts, laid end to end along the dimension named above; an argument that names none is the same for every part. Nothing has to cross between parts.
Inputs may be any that keep to these rules, and one draw needn't show every extreme that they name: `in_signs`: signs are bits: the block's sign is 2 s - 1. `out_signs`: signs are bits: the block's sign is 2 s - 1.
All inputs are finite; a program needn't handle non-finite values.
Results may differ from a plain program's by a relative error of at most 0.0003.
Values sent between devices are 32-bit elements; how exact they have to be, the bound alone decides.
No kernel may reach another device: no remote copies, remote signals or barrier semaphores. Data moves between devices by JAX's collectives and lax.ppermute only.
A program may use at most 64 MiB of HBM per device.

v0:
```python
import jax
import jax.numpy as jnp
from jax import lax
from jax.sharding import PartitionSpec as P

PROJ = 64


def local_matrix(ids, signs, table):
    choose = (ids[:, None] == jnp.arange(table.shape[0], dtype=jnp.int32)[None, :]).astype(
        jnp.float32
    )
    choose = (choose * (2 * signs - 1).astype(jnp.float32)[:, None]).astype(jnp.bfloat16)
    blocks = jnp.dot(choose, table, preferred_element_type=jnp.float32)
    return blocks.reshape(-1, PROJ).astype(jnp.bfloat16)


def local(acts, grads, in_ids, in_signs, out_ids, out_signs, in_table, out_table):
    count, tokens, width_in = acts.shape
    in_proj = local_matrix(in_ids, in_signs, in_table)
    out_proj = local_matrix(out_ids, out_signs, out_table)
    act_part = jnp.dot(acts.reshape(-1, width_in), in_proj, preferred_element_type=jnp.float32)
    grad_part = jnp.dot(
        grads.reshape(-1, grads.shape[2]), out_proj, preferred_element_type=jnp.float32
    )
    joined = jnp.concatenate([act_part, grad_part], axis=1).reshape(count, tokens, 2 * PROJ)
    summed = lax.psum(joined, "tensor")
    act_low = summed[:, :, :PROJ]
    grad_low = summed[:, :, PROJ:]
    partial_kron = jnp.einsum("etp,etq->epq", grad_low, act_low, precision=lax.Precision.HIGHEST)
    kron = lax.psum(partial_kron.reshape(-1, PROJ * PROJ), "seq")
    shards = lax.axis_size("tensor") * lax.axis_size("seq")
    row_width = kron.shape[1] // shards
    place = lax.axis_index("tensor") * lax.axis_size("seq") + lax.axis_index("seq")
    mine = lax.dynamic_slice_in_dim(kron, place * row_width, row_width, 1)
    groups_dp = lax.axis_size("dp")
    col_width = kron.shape[1] // groups_dp
    every = lax.all_gather(kron, "dp", axis=0, tiled=True)
    left = lax.dynamic_slice_in_dim(every, place * row_width, row_width, 1)
    right = lax.dynamic_slice_in_dim(every, lax.axis_index("dp") * col_width, col_width, 1)
    fisher = (
        lax.dot_general(left, right, (((0,), (0,)), ((), ())), precision=lax.Precision.HIGHEST)
        / left.shape[0]
    )
    return (mine, fisher)


def solution(mesh):
    in_specs = (
        P(("groups", "dp"), "seq", "tensor"),
        P(("groups", "dp"), "seq", "tensor"),
        P("tensor"),
        P("tensor"),
        P("tensor"),
        P("tensor"),
        P(),
        P(),
    )
    out_specs = (P(("groups", "dp"), ("tensor", "seq")), P(("groups", "tensor", "seq"), "dp"))
    return jax.shard_map(local, mesh=mesh, in_specs=in_specs, out_specs=out_specs, check_vma=False)
```

profile of v0, /device:TPU:0, one launch (start us, length us, event | category | flops | bytes accessed | tf_op | source)
XLA Modules:
  0.0 109.8 jit_solution(18204182587707396200)
XLA Ops:
  7.2 0.0 copy-start
  7.2 0.0 all-reduce.3.cloned.1.call-start
  7.2 0.7 add_convert_fusion.1
  7.9 0.7 add_convert_fusion
  8.6 1.2 %convolution_convert_fusion.1 = bf16[32,4096]{1,0:T(8,128)(2,1)S(1)} fusion(bf16[32,4096]{1,0:T(8,128)(2,1)} %param.14, bf16[32]{0:T(256)(128)(2,1)S(1)} %add_convert_fusion.1, s32[32]{0:T(128)} %param.10), kind=kOutput, calls=%fused_computation.1 | convolution fusion | flops 8521728 | bytes 524480 | tf_op jit(solution)/shard_map/dot_general | solution.py:14
  9.8 0.5 convert_element_type.29
  10.4 0.0 copy-done
  10.4 1.1 %convolution_convert_fusion = bf16[112,4096]{1,0:T(8,128)(2,1)S(1)} fusion(bf16[32,4096]{1,0:T(8,128)(2,1)S(1)} %copy-done, bf16[112]{0:T(256)(128)(2,1)S(1)} %add_convert_fusion, s32[112]{0:T(128)} %param.12), kind=kOutput, calls=%fused_computation | convolution fusion | flops 29826048 | bytes 1180320 | tf_op jit(solution)/shard_map/dot_general | solution.py:14
  11.5 2.0 %convert_element_type.33 = bf16[7168,64]{1,0:T(8,128)(2,1)S(1)} reshape(bf16[112,4096]{1,0:T(8,128)(2,1)S(1)} %convolution_convert_fusion) | data formatting | bytes 1835008 | tf_op jit(solution)/shard_map/convert_element_type | solution.py:15
  13.5 3.6 %convolution_bitcast_fusion.1 = f32[1024,64]{0,1:T(8,128)S(1)} fusion(bf16[2048,64]{1,0:T(8,128)(2,1)S(1)} %convert_element_type.29, bf16[1024,2048]{1,0:T(8,128)(2,1)} %bitcast.18), kind=kOutput, calls=%fused_computation.4 | convolution fusion | flops 268435456 | bytes 4718592 | tf_op jit(solution)/shard_map/dot_general | solution.py:22
  17.1 9.8 %convolution_bitcast_fusion = f32[1024,64]{0,1:T(8,128)S(1)} fusion(bf16[7168,64]{1,0:T(8,128)(2,1)S(1)} %convert_element_type.33, bf16[1024,7168]{1,0:T(8,128)(2,1)} %bitcast.17), kind=kOutput, calls=%fused_computation.3 | convolution fusion | flops 939524096 | bytes 15859712 | tf_op jit(solution)/shard_map/dot_general | solution.py:23
  26.9 0.8 copy_bitcast_fusion
  27.7 0.0 all-reduce.3.cloned.1.call-update
  27.7 0.0 all-reduce.5.cloned.1.call-start
  27.8 31.4 %all-reduce.3.cloned.1.call-done = f32[8,128,128]{1,2,0:T(8,128)} async-done(((f32[8,128,128]{1,2,0:T(8,128)}), f32[8,128,128]{1,2,0:T(8,128)}) %all-reduce.3.cloned.1.call-update) | async-done | bytes 524304 | tf_op jit(solution)/shard_map/psum | solution.py:27
  59.2 1.6 %fusion = f32[8,64,64]{2,1,0:T(8,128)S(1)} fusion(f32[8,128,128]{1,2,0:T(8,128)} %all-reduce.3.cloned.1.call-done), kind=kOutput, calls=%fused_computation.7 | convolution fusion | flops 50331648 | bytes 655360 | tf_op jit(solution)/shard_map/etp,etq->epq/dot_general | solution.py:30
  60.7 0.8 reshape.27
  61.5 0.0 all-reduce.5.cloned.1.call-update
  61.6 18.6 %all-reduce.5.cloned.1.call-done = f32[8,4096]{1,0:T(8,128)} async-done(((f32[8,4096]{1,0:T(8,128)}), f32[8,4096]{1,0:T(8,128)}) %all-reduce.5.cloned.1.call-update) | async-done | bytes 131088 | tf_op jit(solution)/shard_map/psum | solution.py:31
  80.1 16.5 %all_gather.3 = f32[32,4096]{1,0:T(8,128)S(1)} all-gather(f32[8,4096]{1,0:T(8,128)} %all-reduce.5.cloned.1.call-done), channel_id=1, replica_groups=mesh['groups'=2,'dp'=4,'tensor'=2,'seq'=2] {'dp'}, dimensions={0}, use_global_device_ids=true | all-gather | bytes 655360 | tf_op jit(solution)/shard_map/all_gather | solution.py:38
  96.6 5.0 %convolution_multiply_fusion = f32[1024,1024]{1,0:T(8,128)} fusion(f32[32,4096]{1,0:T(8,128)S(1)} %all_gather.3, s32[]{:T(128)S(6)} %select_n.8, s32[]{:T(128)S(6)} %select_n.7), kind=kOutput, calls=%fused_computation.2 | convolution fusion | flops 403701760 | bytes 4456456 | tf_op jit(solution)/shard_map/dot_general | solution.py:42
  101.6 1.4 %constant_dynamic-slice_fusion = f32[8,1024]{1,0:T(8,128)} fusion(f32[8,4096]{1,0:T(8,128)} %all-reduce.5.cloned.1.call-done, s32[]{:T(128)S(6)} %select_n.7), kind=kLoop, calls=%fused_computation.23 | loop fusion | bytes 65540 | tf_op jit(solution)/shard_map/dynamic_slice | solution.py:35
Async XLA Ops:
  7.2 3.2 %copy-start = (bf16[32,4096]{1,0:T(8,128)(2,1)S(1)}, bf16[32,4096]{1,0:T(8,128)(2,1)}, u32[]{:S(2)}) copy-start(bf16[32,4096]{1,0:T(8,128)(2,1)} %param.15) | copy-start | bytes 786436
  7.2 52.0 %all-reduce.3.cloned.1.call-start = ((), (), s32[]{:S(2)}) async-start(), calls=%async_computation | async-start | bytes 1048576 | tf_op jit(solution)/shard_map/psum | solution.py:27
  27.7 52.4 %all-reduce.5.cloned.1.call-start = ((), (), s32[]{:S(2)}) async-start(), calls=%async_computation.1 | async-start | bytes 262144 | tf_op jit(solution)/shard_map/psum | solution.py:31
Sparse Core Ops, SparseCore 0:
  27.8 31.2 all-reduce.2
  62.2 17.9 all-reduce.4
where the time goes:
time: 110 us
  waiting for transfers between devices  50 us (45%)
  matrix products  22.3 us (20%)
  blocking collectives  16.5 us (15%)
  between operations  14.1 us (13%)
  local copies, waits for them, and re-layouts  4.71 us (4%)
  other arithmetic  2.19 us (2%)
    psum x1, waiting for transfers between devices, local(): summed = lax.psum(joined, 'tensor')  31.4 us
    psum x1, waiting for transfers between devices, local(): kron = lax.psum(partial_kron.reshape(-1, PROJ * PROJ), 'seq')  18.6 us
    all_gather x1, blocking collectives, local(): every = lax.all_gather(kron, 'dp', axis=0, tiled=True)  16.5 us
    dot_general x1, matrix products, local(): jnp.dot(grads.reshape(-1, grads.shape[2]), out_proj, preferred_element_ty...  9.76 us
    dot_general x1, matrix products, local(): lax.dot_general(left, right, (((0,), (0,)), ((), ())), precision=lax.Prec...  5.01 us
    dot_general x1, matrix products, local(): jnp.dot(acts.reshape(-1, width_in), in_proj, preferred_element_type=jnp.f...  3.59 us
    convert_element_type x2, local copies, waits for them, and re-layouts, local_matrix(): return blocks.reshape(-1, PROJ).astype(jnp.bfloat16)  2.55 us
    dot_general x2, matrix products, local_matrix(): blocks = jnp.dot(choose, table, preferred_element_type=jnp.float32)  2.33 us
  transfers between devices with their start and end apart: 2, of which 2 were waited for; matrix products, arithmetic and copies ran while one was open for 0% of the time, Pallas kernels for 0%

commit v1 on v0

v1 whole, which is shorter than its diff:
```python
import functools

import jax
import jax.numpy as jnp
from jax import lax
from jax.experimental import pallas as pl
from jax.experimental.pallas import tpu as pltpu
from jax.sharding import PartitionSpec as P

PROJ = 64
BLOCK = 64
LANES = 128
VMEM_BYTES = 48 * 1024 * 1024
PLANE = ("tensor", "seq")


def chunk_of(width):
    chunk = 1024
    while width % chunk:
        chunk -= LANES
    return chunk


def split3(x):
    high = x.astype(jnp.bfloat16)
    rest = x - high.astype(jnp.float32)
    mid = rest.astype(jnp.bfloat16)
    low = (rest - mid.astype(jnp.float32)).astype(jnp.bfloat16)
    return high, mid, low


def build_matrix(ids, signs, table, spread, matrix):
    entries = table.shape[0]
    left = lax.broadcasted_iota(jnp.int32, (entries, LANES), 1) < PROJ
    for row in range(BLOCK):
        pair = row // 2 * LANES
        both = table[:, pair : pair + LANES].astype(jnp.float32)
        keep = left if row % 2 == 0 else jnp.logical_not(left)
        spread[pl.ds(row, entries, stride=BLOCK), :] = jnp.where(keep, both, 0.0)
    blocks = ids.shape[0]
    unroll = 4 if blocks % 4 == 0 else 1

    def some(step, carry):
        for part in range(unroll):
            j = step * unroll + part
            start = pl.multiple_of(ids[j] * BLOCK, BLOCK)
            sign = (2 * signs[j] - 1).astype(jnp.float32)
            into = pl.multiple_of(j * BLOCK, BLOCK)
            matrix[pl.ds(into, BLOCK), :] = (spread[pl.ds(start, BLOCK), :] * sign).astype(jnp.bfloat16)
        return carry

    lax.fori_loop(0, blocks // unroll, some, 0)


def project_kernel(transpose, ids, signs, table, rows_ref, out, spread, matrix, held, total, sems):
    chunks, _, chunk = held.shape
    copies = [
        pltpu.make_async_copy(rows_ref.at[:, pl.ds(c * chunk, chunk)], held.at[c], sems.at[c])
        for c in range(chunks)
    ]
    for copy in copies:
        copy.start()
    build_matrix(ids, signs, table, spread, matrix)
    for c, copy in enumerate(copies):
        copy.wait()
        part = jnp.dot(
            held[c], matrix[pl.ds(c * chunk, chunk), :], preferred_element_type=jnp.float32
        )
        if c == 0:
            total[...] = part
        else:
            total[...] += part
    pairs, tokens, _ = out.shape
    left = lax.broadcasted_iota(jnp.int32, (tokens, LANES), 1) < PROJ
    for pair in range(pairs):
        first = total[pl.ds(2 * pair * tokens, tokens), :]
        second = total[pl.ds((2 * pair + 1) * tokens, tokens), :]
        first = first + pltpu.roll(first, PROJ, 1)
        second = second + pltpu.roll(second, PROJ, 1)
        packed = jnp.where(left, first, second)
        out[pair] = packed.T if transpose else packed


def project(values, ids, signs, table, transpose, name):
    count, tokens, width = values.shape
    chunk = chunk_of(width)
    chunks = width // chunk
    rows = count * tokens
    smem = pl.BlockSpec(memory_space=pltpu.SMEM)
    vmem = pl.BlockSpec(memory_space=pltpu.VMEM)
    shape = (count // 2, LANES, tokens) if transpose else (count // 2, tokens, LANES)
    return pl.pallas_call(
        functools.partial(project_kernel, transpose),
        out_shape=jax.ShapeDtypeStruct(shape, jnp.float32),
        in_specs=[smem, smem, vmem, pl.BlockSpec(memory_space=pl.ANY)],
        out_specs=vmem,
        scratch_shapes=[
            pltpu.VMEM((table.shape[0] * BLOCK, LANES), jnp.float32),
            pltpu.VMEM((width, LANES), jnp.bfloat16),
            pltpu.VMEM((chunks, rows, chunk), jnp.bfloat16),
            pltpu.VMEM((rows, LANES), jnp.float32),
            pltpu.SemaphoreType.DMA((chunks,)),
        ],
        compiler_params=pltpu.CompilerParams(vmem_limit_bytes=VMEM_BYTES),
        cost_estimate=pl.CostEstimate(
            flops=2 * rows * width * LANES, bytes_accessed=2 * rows * width, transcendentals=0
        ),
        name=name,
    )(ids, signs, table, values.reshape(rows, width))


def kron_kernel(shards, acts, grads, *refs):
    summands, outs, products = refs[: len(refs) - shards - 1], refs[-shards - 1 : -1], refs[-1]
    pairs, tokens, _ = acts.shape
    for pair in range(pairs):
        act = acts[pair]
        for other in summands:
            act = act + other[pair]
        a1, a2, a3 = split3(act)
        g1, g2, g3 = split3(grads[pair])
        left = jnp.concatenate([g1, g1, g2, g1, g3, g2], axis=1)
        right = jnp.concatenate([a1, a2, a1, a3, a1, a2], axis=0)
        products[pl.ds(pair * LANES, LANES), :] = jnp.dot(left, right, preferred_element_type=jnp.float32)
    count = 2 * pairs
    lower = lax.broadcasted_iota(jnp.int32, (count, LANES), 1) < PROJ
    even = lax.broadcasted_iota(jnp.int32, (count, LANES), 0) % 2 == 0
    here = even == lower
    width = outs[0].shape[1]
    if shards == 1:
        place = 0
    else:
        place = lax.axis_index("tensor") * lax.axis_size("seq") + lax.axis_index("seq")
    for step, out in enumerate(outs):
        piece = lax.rem(place + step, shards) if shards > 1 else 0
        for tile in range(width // LANES):
            row = piece * (width // PROJ) + 2 * tile
            both = []
            for p in (row, row + 1):
                v = products[pl.ds(p, count, stride=PROJ), :]
                both.append(jnp.where(here, v, pltpu.roll(v, PROJ, 1)))
            out[:, pl.ds(tile * LANES, LANES)] = jnp.where(lower, both[0], both[1])


def kron_pieces(act_parts, grads, shards):
    pairs, _, tokens = grads.shape
    vmem = pl.BlockSpec(memory_space=pltpu.VMEM)
    piece = jax.ShapeDtypeStruct((2 * pairs, PROJ * PROJ // shards), jnp.float32)
    return pl.pallas_call(
        functools.partial(kron_kernel, shards),
        out_shape=[piece] * shards,
        in_specs=[vmem] * (1 + len(act_parts)),
        out_specs=[vmem] * shards,
        scratch_shapes=[pltpu.VMEM((pairs * LANES, LANES), jnp.float32)],
        compiler_params=pltpu.CompilerParams(vmem_limit_bytes=VMEM_BYTES),
        name="kron",
    )(act_parts[0], grads, *act_parts[1:])


def fisher_kernel(scale, order, *refs):
    pieces = order.shape[0] // 2
    lefts, rights = refs[:pieces], refs[pieces : 2 * pieces]
    out, left, right, left_parts, right_parts = refs[2 * pieces :]
    rows = lefts[0].shape[0]

    @pl.when(pl.program_id(0) == 0)
    def _():
        for k in range(pieces):
            left[pl.ds(pl.multiple_of(order[k] * rows, 8), rows), :] = lefts[k][...]
            right[pl.ds(pl.multiple_of(order[pieces + k] * rows, 8), rows), :] = rights[k][...]
        l1, l2, l3 = split3(left[...])
        r1, r2, r3 = split3(right[...] * scale)
        left_parts[...] = jnp.concatenate([l1, l1, l2, l1, l3, l2], axis=0)
        right_parts[...] = jnp.concatenate([r1, r2, r1, r3, r1, r2], axis=0)

    height = out.shape[0]
    start = pl.multiple_of(pl.program_id(0) * height, LANES)
    out[...] = lax.dot_general(
        left_parts[:, pl.ds(start, height)],
        right_parts[...],
        (((0,), (0,)), ((), ())),
        preferred_element_type=jnp.float32,
    )


def fisher_block(lefts, rights, order):
    pieces = len(lefts)
    rows, height = lefts[0].shape
    width = rights[0].shape[1]
    total = rows * pieces
    block = height // 4
    whole = pl.BlockSpec((rows, height), lambda i: (0, 0))
    whole_right = pl.BlockSpec((rows, width), lambda i: (0, 0))
    return pl.pallas_call(
        functools.partial(fisher_kernel, 1.0 / total),
        grid=(height // block,),
        out_shape=jax.ShapeDtypeStruct((height, width), jnp.float32),
        in_specs=[pl.BlockSpec(memory_space=pltpu.SMEM)] + [whole] * pieces + [whole_right] * pieces,
        out_specs=pl.BlockSpec((block, width), lambda i: (i, 0)),
        scratch_shapes=[
            pltpu.VMEM((total, height), jnp.float32),
            pltpu.VMEM((total, width), jnp.float32),
            pltpu.VMEM((6 * total, height), jnp.bfloat16),
            pltpu.VMEM((6 * total, width), jnp.bfloat16),
        ],
        compiler_params=pltpu.CompilerParams(vmem_limit_bytes=VMEM_BYTES),
        name="fisher",
    )(order, *lefts, *rights)


def local(acts, grads, in_ids, in_signs, out_ids, out_signs, in_table, out_table):
    tensor, seq, dp = (lax.axis_size(name) for name in ("tensor", "seq", "dp"))
    shards = tensor * seq
    place = lax.axis_index("tensor") * seq + lax.axis_index("seq")
    mine_dp = lax.axis_index("dp")

    act = project(acts, in_ids, in_signs, in_table, False, "project_acts")
    if tensor == 2:
        act_parts = [act, lax.ppermute(act, "tensor", [(0, 1), (1, 0)])]
    else:
        act_parts = [lax.psum(act, "tensor")]
    grad = project(grads, out_ids, out_signs, out_table, True, "project_grads")

    if shards != dp or shards > 4:
        kron = lax.psum(kron_pieces(act_parts, grad, 1)[0], PLANE)
        width = kron.shape[1] // shards
        mine = lax.dynamic_slice_in_dim(kron, place * width, width, 1)
        every = lax.all_gather(kron, "dp", axis=0, tiled=True)
        left = lax.dynamic_slice_in_dim(every, place * width, width, 1)
        columns = kron.shape[1] // dp
        right = lax.dynamic_slice_in_dim(every, mine_dp * columns, columns, 1)
        fisher = lax.dot_general(
            left, right, (((0,), (0,)), ((), ())), precision=lax.Precision.HIGHEST
        ) / left.shape[0]
        return mine, fisher

    pieces = kron_pieces(act_parts, grad, shards)
    mine = pieces[0]
    for k in range(1, shards):
        mine = mine + lax.ppermute(pieces[k], PLANE, [(p, (p + k) % shards) for p in range(shards)])

    lefts, rights = [mine], []
    for k in range(1, dp):
        lefts.append(lax.ppermute(mine, "dp", [(d, (d + k) % dp) for d in range(dp)]))
    for k in range(dp):
        pairs = [
            (d * shards + p, p * shards + (d + k) % shards) for d in range(dp) for p in range(shards)
        ]
        rights.append(lax.ppermute(mine, ("dp",) + PLANE, pairs))
    steps = jnp.arange(dp, dtype=jnp.int32)
    order = jnp.concatenate([(mine_dp - steps) % dp, (place - steps) % dp]).astype(jnp.int32)
    return mine, fisher_block(lefts, rights, order)


def solution(mesh):
    in_specs = (
        P(("groups", "dp"), "seq", "tensor"),
        P(("groups", "dp"), "seq", "tensor"),
        P("tensor"),
        P("tensor"),
        P("tensor"),
        P("tensor"),
        P(),
        P(),
    )
    out_specs = (P(("groups", "dp"), ("tensor", "seq")), P(("groups", "tensor", "seq"), "dp"))
    return jax.shard_map(local, mesh=mesh, in_specs=in_specs, out_specs=out_specs, check_vma=False)
```

time: 110 us -> 48.1 us (0.44)
  waiting for transfers between devices: 50 us -> 7.1 us
  matrix products: 22.3 us -> 0 us
  Pallas kernels: 0 us -> 18.8 us
  starting transfers between devices: 0.08 us -> 16.7 us
  blocking collectives: 16.5 us -> 0 us
  between operations: 14.1 us -> 0.73 us
  other arithmetic: 2.19 us -> 0.1 us
    psum x2 -> x0, waiting for transfers between devices: 50 us -> none  [the longest x1 31.4 us: local(): summed = lax.psum(joined, 'tensor')]
    dot_general x6 -> x0, matrix products: 22.3 us -> none  [the longest x1 9.76 us: local(): jnp.dot(grads.reshape(-1, grads.shape[2]), out_proj, preferred_element_ty...]
    pallas_call x0 -> x4, Pallas kernels: none -> 18.8 us  [the longest x2 14.6 us: project(): pl.pallas_call(functools.partial(project_kernel, transpose), out_shape=ja...]
    ppermute x0 -> x11, starting transfers between devices: none -> 16.7 us  [the longest x3 6.92 us: local(): lax.ppermute(mine, 'dp', [(d, (d + k) % dp) for d in range(dp)])]
    all_gather x1 -> x0, blocking collectives: 16.5 us -> none  [local(): every = lax.all_gather(kron, 'dp', axis=0, tiled=True)]
    ppermute x0 -> x11, waiting for transfers between devices: none -> 7.1 us  [the longest x3 4.82 us: local(): lax.ppermute(mine, 'dp', [(d, (d + k) % dp) for d in range(dp)])]
    unnamed x2 -> x16, local copies, waits for them, and re-layouts: 0.01 us -> 4.47 us
    convert_element_type x2 -> x0, local copies, waits for them, and re-layouts: 2.55 us -> none  [local_matrix(): return blocks.reshape(-1, PROJ).astype(jnp.bfloat16)]
  transfers between devices with their start and end apart: 2 -> 11, of which waited for: 2 -> 5; matrix products, arithmetic and copies ran while one was open for 0% -> 0% of each run, Pallas kernels for 0% -> 21%
where the time goes in v1:
time: 48.1 us; the launch traced here: 47.9 us
  Pallas kernels  18.8 us (39%)
  starting transfers between devices  16.7 us (35%)
  waiting for transfers between devices  7.1 us (15%)
  local copies, waits for them, and re-layouts  4.47 us (9%)
  between operations  0.73 us (2%)
    pallas_call x2, Pallas kernels, project(): pl.pallas_call(functools.partial(project_kernel, transpose), out_shape=ja...  14.6 us
    ppermute x3, starting transfers between devices, local(): lax.ppermute(mine, 'dp', [(d, (d + k) % dp) for d in range(dp)])  6.92 us
    ppermute x4, starting transfers between devices, local(): rights.append(lax.ppermute(mine, ('dp',) + PLANE, pairs))  4.94 us
    ppermute x3, waiting for transfers between devices, local(): lax.ppermute(mine, 'dp', [(d, (d + k) % dp) for d in range(dp)])  4.82 us
    unnamed x16, local copies, waits for them, and re-layouts  4.47 us
    pallas_call x1, Pallas kernels, fisher_block(): pl.pallas_call(functools.partial(fisher_kernel, 1.0 / total), grid=(heigh...  3.63 us
    ppermute x1, starting transfers between devices, local(): act_parts = [act, lax.ppermute(act, 'tensor', [(0, 1), (1, 0)])]  3.01 us
    ppermute x3, waiting for transfers between devices, local(): lax.ppermute(pieces[k], PLANE, [(p, (p + k) % shards) for p in range(shar...  2.26 us
  transfers between devices with their start and end apart: 11, of which 5 were waited for; matrix products, arithmetic and copies ran while one was open for 0% of the time, Pallas kernels for 21%

profile of v1, /device:TPU:0, one launch (start us, length us, event | category | flops | bytes accessed | tf_op | source)
XLA Modules:
  0.0 47.9 jit_solution(12280604664301121511)
XLA Ops:
  0.6 0.0 copy-start.7
  0.6 0.0 copy-start.6
  0.7 0.0 copy-start
  0.7 2.2 %copy-done = bf16[8,128,2048]{2,1,0:T(8,128)(2,1)S(1)} copy-done((bf16[8,128,2048]{2,1,0:T(8,128)(2,1)S(1)}, bf16[8,128,2048]{2,1,0:T(8,128)(2,1)}, u32[]{:S(2)}) %copy-start) | copy-done | bytes 4194328
  2.9 0.0 copy-start.2
  2.9 0.9 %copy-done.2 = bf16[32,4096]{1,0:T(8,128)(2,1)S(1)} copy-done((bf16[32,4096]{1,0:T(8,128)(2,1)S(1)}, bf16[32,4096]{1,0:T(8,128)(2,1)}, u32[]{:S(2)}) %copy-start.2) | copy-done | bytes 262168
  3.8 0.0 copy-start.4
  3.8 0.7 %copy-done.4 = s32[32]{0:T(128)S(1)} copy-done((s32[32]{0:T(128)S(1)}, s32[32]{0:T(128)}, u32[]{:S(2)}) %copy-start.4) | copy-done | bytes 152
  4.5 0.0 copy-start.5
  4.5 0.7 %copy-done.5 = s32[32]{0:T(128)S(1)} copy-done((s32[32]{0:T(128)S(1)}, s32[32]{0:T(128)}, u32[]{:S(2)}) %copy-start.5) | copy-done | bytes 152
  5.1 0.0 copy-start.1
  5.1 4.6 %project_acts.1.acts = f32[4,128,128]{2,1,0:T(8,128)S(1)} custom-call(s32[32]{0:T(128)S(1)} %copy-done.4, s32[32]{0:T(128)S(1)} %copy-done.5, bf16[32,4096]{1,0:T(8,128)(2,1)S(1)} %copy-done.2, bf16[1024,2048]{1,0:T(8,128)(2,1)S(1)} %bitcast.2), custom_call_target="tpu_custom_call" | custom-call | flops 536870912 | bytes 4194304 | tf_op jit(solution)/shard_map/project_acts/pallas_call | solution.py:92
  9.8 3.0 %collective-permute-start = (f32[4,128,128]{2,1,0:T(8,128)S(1)}, f32[4,128,128]{2,1,0:T(8,128)S(1)}, u32[]{:S(2)}, u32[]{:S(2)}) collective-permute-start(f32[4,128,128]{2,1,0:T(8,128)S(1)} %project_acts.1.acts), channel_id=1, source_target_pairs={{0,2},{2,0},{1,3},{3,1},{4,6},{6,4},{5,7},{7,5},{8,10},{10,8},{9,1... | collective-permute-start | bytes 786440 | tf_op jit(solution)/shard_map/ppermute | solution.py:218
  12.8 0.0 copy-done.7
  12.8 0.0 copy-done.6
  12.8 0.0 copy-done.1
  12.8 9.9 %project_grads.1.grads = f32[4,128,128]{2,1,0:T(8,128)S(1)} custom-call(s32[112]{0:T(128)S(1)} %copy-done.6, s32[112]{0:T(128)S(1)} %copy-done.7, bf16[32,4096]{1,0:T(8,128)(2,1)S(1)} %copy-done.1, bf16[1024,7168]{1,0:T(8,128)(2,1)} %bitcast.3), custom_call_target="tpu_custom_call" | custom-call | flops 1879048192 | bytes 14680064 | tf_op jit(solution)/shard_map/project_grads/pallas_call | solution.py:92
  22.7 0.0 collective-permute-done.refs_0_
  22.7 0.6 %kron.1 = (f32[8,1024]{1,0:T(8,128)S(1)}, f32[8,1024]{1,0:T(8,128)S(1)}, f32[8,1024]{1,0:T(8,128)S(1)}, f32[8,1024]{1,0:T(8,128)S(1)}) custom-call(f32[4,128,128]{2,1,0:T(8,128)S(1)} %project_acts.1.acts, f32[4,128,128]{2,1,0:T(8,128)S(1)} %project_grads.1.grads, f32[4,128,128]{2,1,0:T(8,128)S(1)} %collective-permute-done.refs_0_), custom_call_target="tpu_custom_call" | custom-call | tf_op jit(solution)/shard_map/kron/pallas_call | solution.py:148
  23.3 0.1 collective-permute-start.1
  23.4 0.1 collective-permute-start.2
  23.5 1.7 %collective-permute-start.3 = (f32[8,1024]{1,0:T(8,128)S(1)}, f32[8,1024]{1,0:T(8,128)S(1)}, u32[]{:S(2)}, u32[]{:S(2)}) collective-permute-start(f32[8,1024]{1,0:T(8,128)S(1)} %get-tuple-element.9), channel_id=1, source_target_pairs={{0,3},{1,0},{2,1},{3,2},{4,7},{5,4},{6,5},{7,6},{8,11},{9,8},{10,9... | collective-permute-start | bytes 98312 | tf_op jit(solution)/shard_map/ppermute | solution.py:239
  25.1 1.6 %collective-permute-done.1 = f32[8,1024]{1,0:T(8,128)S(1)} collective-permute-done((f32[8,1024]{1,0:T(8,128)S(1)}, f32[8,1024]{1,0:T(8,128)S(1)}, u32[]{:S(2)}, u32[]{:S(2)}) %collective-permute-start.1) | collective-permute-done | bytes 32800 | tf_op jit(solution)/shard_map/ppermute | solution.py:239
  26.7 0.7 %collective-permute-done.2 = f32[8,1024]{1,0:T(8,128)S(1)} collective-permute-done((f32[8,1024]{1,0:T(8,128)S(1)}, f32[8,1024]{1,0:T(8,128)S(1)}, u32[]{:S(2)}, u32[]{:S(2)}) %collective-permute-start.2) | collective-permute-done | bytes 32800 | tf_op jit(solution)/shard_map/ppermute | solution.py:239
  27.4 0.0 collective-permute-done.3
  27.4 0.0 copy-start.3
  27.4 1.1 %collective-permute-start.10 = (f32[8,1024]{1,0:T(8,128)S(1)}, f32[8,1024]{1,0:T(8,128)S(1)}, u32[]{:S(2)}, u32[]{:S(2)}) collective-permute-start(f32[8,1024]{1,0:T(8,128)S(1)} %add_add_fusion.refs_0_), channel_id=1, source_target_pairs={{0,3},{1,7},{2,11},{3,15},{4,0},{5,4},{6,8},{7,12},{8,1},{9,5},{10... | collective-permute-start | bytes 98312 | tf_op jit(solution)/shard_map/ppermute | solution.py:248
  28.6 2.8 %collective-permute-start.9 = (f32[8,1024]{1,0:T(8,128)S(1)}, f32[8,1024]{1,0:T(8,128)S(1)}, u32[]{:S(2)}, u32[]{:S(2)}) collective-permute-start(f32[8,1024]{1,0:T(8,128)S(1)} %add_add_fusion.refs_0_), channel_id=1, source_target_pairs={{0,2},{1,6},{2,10},{3,14},{4,3},{5,7},{6,11},{7,15},{8,0},{9,4},{1... | collective-permute-start | bytes 98312 | tf_op jit(solution)/shard_map/ppermute | solution.py:248
  31.4 0.4 collective-permute-start.8
  31.7 0.7 %collective-permute-start.7 = (f32[8,1024]{1,0:T(8,128)S(1)}, f32[8,1024]{1,0:T(8,128)S(1)}, u32[]{:S(2)}, u32[]{:S(2)}) collective-permute-start(f32[8,1024]{1,0:T(8,128)S(1)} %add_add_fusion.refs_0_), channel_id=1, source_target_pairs={{0,0},{1,4},{2,8},{3,12},{4,1},{5,5},{6,9},{7,13},{8,2},{9,6},{10,... | collective-permute-start | bytes 98312 | tf_op jit(solution)/shard_map/ppermute | solution.py:248
  32.4 6.1 %collective-permute-start.6 = (f32[8,1024]{1,0:T(8,128)S(1)}, f32[8,1024]{1,0:T(8,128)S(1)}, u32[]{:S(2)}, u32[]{:S(2)}) collective-permute-start(f32[8,1024]{1,0:T(8,128)S(1)} %add_add_fusion.refs_0_), channel_id=1, source_target_pairs={{0,12},{4,0},{8,4},{12,8},{1,13},{5,1},{9,5},{13,9},{2,14},{6,2},{... | collective-permute-start | bytes 98312 | tf_op jit(solution)/shard_map/ppermute | solution.py:243
  38.4 0.0 collective-permute-done.10.refs_7_
  38.5 0.0 collective-permute-start.5
  38.5 0.0 collective-permute-done.9.refs_6_
  38.5 0.9 %collective-permute-start.4 = (f32[8,1024]{1,0:T(8,128)S(1)}, f32[8,1024]{1,0:T(8,128)S(1)}, u32[]{:S(2)}, u32[]{:S(2)}) collective-permute-start(f32[8,1024]{1,0:T(8,128)S(1)} %add_add_fusion.refs_0_), channel_id=1, source_target_pairs={{0,4},{4,8},{8,12},{12,0},{1,5},{5,9},{9,13},{13,1},{2,6},{6,10},{... | collective-permute-start | bytes 98312 | tf_op jit(solution)/shard_map/ppermute | solution.py:243
  39.3 0.1 pad_add_fusion.order
  39.4 0.0 collective-permute-done.8.refs_5_
  39.4 0.0 collective-permute-done.7.refs_4_
  39.4 0.6 %collective-permute-done.6.refs_3_ = f32[8,1024]{1,0:T(8,128)S(1)} collective-permute-done((f32[8,1024]{1,0:T(8,128)S(1)}, f32[8,1024]{1,0:T(8,128)S(1)}, u32[]{:S(2)}, u32[]{:S(2)}) %collective-permute-start.6) | collective-permute-done | bytes 32800 | tf_op jit(solution)/shard_map/ppermute | solution.py:243
  40.0 3.2 %collective-permute-done.5.refs_2_ = f32[8,1024]{1,0:T(8,128)S(1)} collective-permute-done((f32[8,1024]{1,0:T(8,128)S(1)}, f32[8,1024]{1,0:T(8,128)S(1)}, u32[]{:S(2)}, u32[]{:S(2)}) %collective-permute-start.5) | collective-permute-done | bytes 32800 | tf_op jit(solution)/shard_map/ppermute | solution.py:243
  43.3 1.0 %collective-permute-done.4.refs_1_ = f32[8,1024]{1,0:T(8,128)S(1)} collective-permute-done((f32[8,1024]{1,0:T(8,128)S(1)}, f32[8,1024]{1,0:T(8,128)S(1)}, u32[]{:S(2)}, u32[]{:S(2)}) %collective-permute-start.4) | collective-permute-done | bytes 32800 | tf_op jit(solution)/shard_map/ppermute | solution.py:243
  44.2 3.6 %fisher.1 = f32[1024,1024]{1,0:T(8,128)} custom-call(s32[8]{0:T(128)S(1)} %pad_add_fusion.order, f32[8,1024]{1,0:T(8,128)S(1)} %add_add_fusion.refs_0_, f32[8,1024]{1,0:T(8,128)S(1)} %collective-permute-done.4.refs_1_, f32[8,1024]{1,0:T(8,128)S(1)} %collective-permute-done.5.refs_2_, f32[8,1024]{1,0:T(8,128)S(1)} %collective-permute-done.6.refs_3_, ...), custom_call_target="tpu_custom_call" | custom-call | tf_op jit(solution)/shard_map/fisher/pallas_call | solution.py:193
  47.9 0.0 copy-done.3
  (2 shorter events, 0.0 us)
Async XLA Ops:
  0.6 12.1 %copy-start.7 = (s32[112]{0:T(128)S(1)}, s32[112]{0:T(128)}, u32[]{:S(2)}) copy-start(s32[112]{0:T(128)} %signs.3) | copy-start | bytes 1348
  0.6 12.1 %copy-start.6 = (s32[112]{0:T(128)S(1)}, s32[112]{0:T(128)}, u32[]{:S(2)}) copy-start(s32[112]{0:T(128)} %ids.3) | copy-start | bytes 1348
  0.7 2.2 %copy-start = (bf16[8,128,2048]{2,1,0:T(8,128)(2,1)S(1)}, bf16[8,128,2048]{2,1,0:T(8,128)(2,1)}, u32[]{:S(2)}) copy-start(bf16[8,128,2048]{2,1,0:T(8,128)(2,1)} %param.8) | copy-start | bytes 12582916
  2.9 0.9 %copy-start.2 = (bf16[32,4096]{1,0:T(8,128)(2,1)S(1)}, bf16[32,4096]{1,0:T(8,128)(2,1)}, u32[]{:S(2)}) copy-start(bf16[32,4096]{1,0:T(8,128)(2,1)} %table.2) | copy-start | bytes 786436
  3.8 0.7 %copy-start.4 = (s32[32]{0:T(128)S(1)}, s32[32]{0:T(128)}, u32[]{:S(2)}) copy-start(s32[32]{0:T(128)} %ids.2) | copy-start | bytes 388
  4.5 0.7 %copy-start.5 = (s32[32]{0:T(128)S(1)}, s32[32]{0:T(128)}, u32[]{:S(2)}) copy-start(s32[32]{0:T(128)} %signs.2) | copy-start | bytes 388
  5.1 7.7 %copy-start.1 = (bf16[32,4096]{1,0:T(8,128)(2,1)S(1)}, bf16[32,4096]{1,0:T(8,128)(2,1)}, u32[]{:S(2)}) copy-start(bf16[32,4096]{1,0:T(8,128)(2,1)} %table.3) | copy-start | bytes 786436
  9.8 12.9 %collective-permute-start = (f32[4,128,128]{2,1,0:T(8,128)S(1)}, f32[4,128,128]{2,1,0:T(8,128)S(1)}, u32[]{:S(2)}, u32[]{:S(2)}) collective-permute-start(f32[4,128,128]{2,1,0:T(8,128)S(1)} %project_acts.1.acts), channel_id=1, source_target_pairs={{0,2},{2,0},{1,3},{3,1},{4,6},{6,4},{5,7},{7,5},{8,10},{10,8},{9,1... | collective-permute-start | bytes 786440 | tf_op jit(solution)/shard_map/ppermute | solution.py:218
  23.3 3.4 %collective-permute-start.1 = (f32[8,1024]{1,0:T(8,128)S(1)}, f32[8,1024]{1,0:T(8,128)S(1)}, u32[]{:S(2)}, u32[]{:S(2)}) collective-permute-start(f32[8,1024]{1,0:T(8,128)S(1)} %get-tuple-element.7), channel_id=1, source_target_pairs={{0,1},{1,2},{2,3},{3,0},{4,5},{5,6},{6,7},{7,4},{8,9},{9,10},{10,1... | collective-permute-start | bytes 98312 | tf_op jit(solution)/shard_map/ppermute | solution.py:239
  23.4 4.0 %collective-permute-start.2 = (f32[8,1024]{1,0:T(8,128)S(1)}, f32[8,1024]{1,0:T(8,128)S(1)}, u32[]{:S(2)}, u32[]{:S(2)}) collective-permute-start(f32[8,1024]{1,0:T(8,128)S(1)} %get-tuple-element.8), channel_id=1, source_target_pairs={{0,2},{1,3},{2,0},{3,1},{4,6},{5,7},{6,4},{7,5},{8,10},{9,11},{10,... | collective-permute-start | bytes 98312 | tf_op jit(solution)/shard_map/ppermute | solution.py:239
  23.5 3.9 %collective-permute-start.3 = (f32[8,1024]{1,0:T(8,128)S(1)}, f32[8,1024]{1,0:T(8,128)S(1)}, u32[]{:S(2)}, u32[]{:S(2)}) collective-permute-start(f32[8,1024]{1,0:T(8,128)S(1)} %get-tuple-element.9), channel_id=1, source_target_pairs={{0,3},{1,0},{2,1},{3,2},{4,7},{5,4},{6,5},{7,6},{8,11},{9,8},{10,9... | collective-permute-start | bytes 98312 | tf_op jit(solution)/shard_map/ppermute | solution.py:239
  27.4 20.4 %copy-start.3 = (f32[8,1024]{1,0:T(8,128)}, f32[8,1024]{1,0:T(8,128)S(1)}, u32[]{:S(2)}) copy-start(f32[8,1024]{1,0:T(8,128)S(1)} %add_add_fusion.refs_0_) | copy-start | bytes 98308
  27.4 11.0 %collective-permute-start.10 = (f32[8,1024]{1,0:T(8,128)S(1)}, f32[8,1024]{1,0:T(8,128)S(1)}, u32[]{:S(2)}, u32[]{:S(2)}) collective-permute-start(f32[8,1024]{1,0:T(8,128)S(1)} %add_add_fusion.refs_0_), channel_id=1, source_target_pairs={{0,3},{1,7},{2,11},{3,15},{4,0},{5,4},{6,8},{7,12},{8,1},{9,5},{10... | collective-permute-start | bytes 98312 | tf_op jit(solution)/shard_map/ppermute | solution.py:248
  28.6 9.9 %collective-permute-start.9 = (f32[8,1024]{1,0:T(8,128)S(1)}, f32[8,1024]{1,0:T(8,128)S(1)}, u32[]{:S(2)}, u32[]{:S(2)}) collective-permute-start(f32[8,1024]{1,0:T(8,128)S(1)} %add_add_fusion.refs_0_), channel_id=1, source_target_pairs={{0,2},{1,6},{2,10},{3,14},{4,3},{5,7},{6,11},{7,15},{8,0},{9,4},{1... | collective-permute-start | bytes 98312 | tf_op jit(solution)/shard_map/ppermute | solution.py:248
  31.4 8.0 %collective-permute-start.8 = (f32[8,1024]{1,0:T(8,128)S(1)}, f32[8,1024]{1,0:T(8,128)S(1)}, u32[]{:S(2)}, u32[]{:S(2)}) collective-permute-start(f32[8,1024]{1,0:T(8,128)S(1)} %add_add_fusion.refs_0_), channel_id=1, source_target_pairs={{0,1},{1,5},{2,9},{3,13},{4,2},{5,6},{6,10},{7,14},{8,3},{9,7},{10... | collective-permute-start | bytes 98312 | tf_op jit(solution)/shard_map/ppermute | solution.py:248
  31.7 7.7 %collective-permute-start.7 = (f32[8,1024]{1,0:T(8,128)S(1)}, f32[8,1024]{1,0:T(8,128)S(1)}, u32[]{:S(2)}, u32[]{:S(2)}) collective-permute-start(f32[8,1024]{1,0:T(8,128)S(1)} %add_add_fusion.refs_0_), channel_id=1, source_target_pairs={{0,0},{1,4},{2,8},{3,12},{4,1},{5,5},{6,9},{7,13},{8,2},{9,6},{10,... | collective-permute-start | bytes 98312 | tf_op jit(solution)/shard_map/ppermute | solution.py:248
  32.4 7.7 %collective-permute-start.6 = (f32[8,1024]{1,0:T(8,128)S(1)}, f32[8,1024]{1,0:T(8,128)S(1)}, u32[]{:S(2)}, u32[]{:S(2)}) collective-permute-start(f32[8,1024]{1,0:T(8,128)S(1)} %add_add_fusion.refs_0_), channel_id=1, source_target_pairs={{0,12},{4,0},{8,4},{12,8},{1,13},{5,1},{9,5},{13,9},{2,14},{6,2},{... | collective-permute-start | bytes 98312 | tf_op jit(solution)/shard_map/ppermute | solution.py:243
  38.5 4.8 %collective-permute-start.5 = (f32[8,1024]{1,0:T(8,128)S(1)}, f32[8,1024]{1,0:T(8,128)S(1)}, u32[]{:S(2)}, u32[]{:S(2)}) collective-permute-start(f32[8,1024]{1,0:T(8,128)S(1)} %add_add_fusion.refs_0_), channel_id=1, source_target_pairs={{0,8},{4,12},{8,0},{12,4},{1,9},{5,13},{9,1},{13,5},{2,10},{6,14},... | collective-permute-start | bytes 98312 | tf_op jit(solution)/shard_map/ppermute | solution.py:243
  38.5 5.8 %collective-permute-start.4 = (f32[8,1024]{1,0:T(8,128)S(1)}, f32[8,1024]{1,0:T(8,128)S(1)}, u32[]{:S(2)}, u32[]{:S(2)}) collective-permute-start(f32[8,1024]{1,0:T(8,128)S(1)} %add_add_fusion.refs_0_), channel_id=1, source_target_pairs={{0,4},{4,8},{8,12},{12,0},{1,5},{5,9},{9,13},{13,1},{2,6},{6,10},{... | collective-permute-start | bytes 98312 | tf_op jit(solution)/shard_map/ppermute | solution.py:243

commit v2 on v1

v2 whole, which is shorter than its diff:
```python
import functools

import jax
import jax.numpy as jnp
from jax import lax
from jax.experimental import pallas as pl
from jax.experimental.pallas import tpu as pltpu
from jax.sharding import PartitionSpec as P

PROJ = 64
BLOCK = 64
LANES = 128
VMEM_BYTES = 48 * 1024 * 1024
ALL_VMEM = 48 * 1024 * 1024
PLANE = ("tensor", "seq")


def chunk_of(width, most):
    chunk = most
    while width % chunk:
        chunk -= LANES
    return chunk


def split3(x):
    high = x.astype(jnp.bfloat16)
    rest = x - high.astype(jnp.float32)
    mid = rest.astype(jnp.bfloat16)
    low = (rest - mid.astype(jnp.float32)).astype(jnp.bfloat16)
    return high, mid, low


def spread_table(table, spread, signed):
    entries = table.shape[0]
    left = lax.broadcasted_iota(jnp.int32, (entries, LANES), 1) < PROJ
    for row in range(BLOCK):
        pair = row // 2 * LANES
        both = table[:, pair : pair + LANES].astype(jnp.float32)
        keep = left if row % 2 == 0 else jnp.logical_not(left)
        spread[pl.ds(row, entries, stride=BLOCK), :] = jnp.where(keep, both, 0.0)
    plain = spread[...].astype(jnp.bfloat16)
    signed[pl.ds(entries * BLOCK, entries * BLOCK), :] = plain
    signed[pl.ds(0, entries * BLOCK), :] = -plain


def lay_blocks(ids, signs, entries, signed, matrix, first, last):
    for j in range(first, last):
        start = pl.multiple_of((signs[j] * entries + ids[j]) * BLOCK, BLOCK)
        matrix[pl.ds(j * BLOCK, BLOCK), :] = signed[pl.ds(start, BLOCK), :]


def project_kernel(transpose, fetch, ids, signs, table, rows_ref, out, spread, signed, matrix, held, total, sems, *own):
    chunks, _, chunk = held.shape
    copies = [
        pltpu.make_async_copy(rows_ref.at[:, pl.ds(c * chunk, chunk)], held.at[c], sems.at[c])
        for c in range(chunks)
    ]
    if fetch:
        small = [
            pltpu.make_async_copy(source, kept, sems.at[chunks + k])
            for k, (source, kept) in enumerate(zip((table, ids, signs), own))
        ]
        for copy in small:
            copy.start()
        table, ids, signs = own
    for copy in copies:
        copy.start()
    if fetch:
        small[0].wait()
    spread_table(table, spread, signed)
    if fetch:
        small[1].wait()
        small[2].wait()
    blocks = chunk // BLOCK
    lay = functools.partial(lay_blocks, ids, signs, table.shape[0], signed, matrix)
    lay(0, blocks)
    for c, copy in enumerate(copies):
        copy.wait()
        if c + 1 < chunks:
            lay((c + 1) * blocks, (c + 2) * blocks)
        part = jnp.dot(
            held[c], matrix[pl.ds(c * chunk, chunk), :], preferred_element_type=jnp.float32
        )
        if c == 0:
            total[...] = part
        else:
            total[...] += part
    pairs, tokens, _ = out.shape
    left = lax.broadcasted_iota(jnp.int32, (tokens, LANES), 1) < PROJ
    for pair in range(pairs):
        first = total[pl.ds(2 * pair * tokens, tokens), :]
        second = total[pl.ds((2 * pair + 1) * tokens, tokens), :]
        first = first + pltpu.roll(first, PROJ, 1)
        second = second + pltpu.roll(second, PROJ, 1)
        packed = jnp.where(left, first, second)
        out[pair] = packed.T if transpose else packed


def project(values, ids, signs, table, transpose, fetch, most, name):
    count, tokens, width = values.shape
    chunk = chunk_of(width, most)
    chunks = width // chunk
    rows = count * tokens
    entries = table.shape[0]
    smem = pl.BlockSpec(memory_space=pltpu.SMEM)
    vmem = pl.BlockSpec(memory_space=pltpu.VMEM)
    hbm = pl.BlockSpec(memory_space=pltpu.HBM)
    shape = (count // 2, LANES, tokens) if transpose else (count // 2, tokens, LANES)
    own = [
        pltpu.VMEM(table.shape, table.dtype),
        pltpu.SMEM(ids.shape, ids.dtype),
        pltpu.SMEM(signs.shape, signs.dtype),
    ]
    operands = [ids, signs, table, values.reshape(rows, width)]
    if fetch:
        operands = [pltpu.with_memory_space_constraint(each, pltpu.HBM) for each in operands]
    return pl.pallas_call(
        functools.partial(project_kernel, transpose, fetch),
        out_shape=jax.ShapeDtypeStruct(shape, jnp.float32),
        in_specs=[hbm] * 4 if fetch else [smem, smem, vmem, hbm],
        out_specs=vmem,
        scratch_shapes=[
            pltpu.VMEM((entries * BLOCK, LANES), jnp.float32),
            pltpu.VMEM((2 * entries * BLOCK, LANES), jnp.bfloat16),
            pltpu.VMEM((width, LANES), jnp.bfloat16),
            pltpu.VMEM((chunks, rows, chunk), jnp.bfloat16),
            pltpu.VMEM((rows, LANES), jnp.float32),
            pltpu.SemaphoreType.DMA((chunks + 3,)),
        ]
        + (own if fetch else []),
        compiler_params=pltpu.CompilerParams(vmem_limit_bytes=ALL_VMEM if fetch else VMEM_BYTES),
        cost_estimate=pl.CostEstimate(
            flops=2 * rows * width * LANES, bytes_accessed=2 * rows * width, transcendentals=0
        ),
        name=name,
    )(*operands)


def kron_kernel(acts, grads, *refs):
    summands, out, products = refs[:-2], refs[-2], refs[-1]
    pairs, tokens, _ = acts.shape
    for pair in range(pairs):
        act = acts[pair]
        for other in summands:
            act = act + other[pair]
        a1, a2, a3 = split3(act)
        g1, g2, g3 = split3(grads[pair])
        left = jnp.concatenate([g1, g1, g2, g1, g3, g2], axis=1)
        right = jnp.concatenate([a1, a2, a1, a3, a1, a2], axis=0)
        products[pl.ds(pair * LANES, LANES), :] = jnp.dot(left, right, preferred_element_type=jnp.float32)
    count = 2 * pairs
    lower = lax.broadcasted_iota(jnp.int32, (count, LANES), 1) < PROJ
    even = lax.broadcasted_iota(jnp.int32, (count, LANES), 0) % 2 == 0
    here = even == lower
    for tile in range(out.shape[1] // LANES):
        both = []
        for p in (2 * tile, 2 * tile + 1):
            v = products[pl.ds(p, count, stride=PROJ), :]
            both.append(jnp.where(here, v, pltpu.roll(v, PROJ, 1)))
        out[:, pl.ds(tile * LANES, LANES)] = jnp.where(lower, both[0], both[1])


def kron_of(act_parts, grads):
    pairs = grads.shape[0]
    vmem = pl.BlockSpec(memory_space=pltpu.VMEM)
    return pl.pallas_call(
        kron_kernel,
        out_shape=jax.ShapeDtypeStruct((2 * pairs, PROJ * PROJ), jnp.float32),
        in_specs=[vmem] * (1 + len(act_parts)),
        out_specs=vmem,
        scratch_shapes=[pltpu.VMEM((pairs * LANES, LANES), jnp.float32)],
        compiler_params=pltpu.CompilerParams(vmem_limit_bytes=VMEM_BYTES),
        name="kron",
    )(act_parts[0], grads, *act_parts[1:])


def place_in_plane():
    return lax.axis_index("tensor") * lax.axis_size("seq") + lax.axis_index("seq")


def pieces_kernel(here, there, mine, *parcels):
    count, width = mine.shape
    dp = len(parcels)
    start = pl.multiple_of(place_in_plane() * width, LANES)
    row = here[:, pl.ds(start, width)] + there[:, pl.ds(start, width)]
    mine[...] = row
    for k, parcel in enumerate(parcels):
        parcel[pl.ds(0, count), :] = row
        other = lax.rem(lax.axis_index("dp") + k, dp)
        start = pl.multiple_of(other * width, LANES)
        parcel[pl.ds(count, count), :] = here[:, pl.ds(start, width)] + there[:, pl.ds(start, width)]


def pieces_of(here, there, dp):
    count, width = here.shape
    vmem = pl.BlockSpec(memory_space=pltpu.VMEM)
    shapes = [(count, width // dp)] + [(2 * count, width // dp)] * dp
    return pl.pallas_call(
        pieces_kernel,
        out_shape=[jax.ShapeDtypeStruct(shape, jnp.float32) for shape in shapes],
        in_specs=[vmem] * 2,
        out_specs=[vmem] * len(shapes),
        compiler_params=pltpu.CompilerParams(vmem_limit_bytes=VMEM_BYTES),
        name="pieces",
    )(here, there)


def fisher_kernel(scale, *refs):
    parcels, (out, left_parts, right_parts) = refs[:-3], refs[-3:]
    rows = parcels[0].shape[0] // 2

    @pl.when(pl.program_id(0) == 0)
    def _():
        left = jnp.concatenate([parcel[pl.ds(0, rows), :] for parcel in parcels], axis=0)
        right = jnp.concatenate([parcel[pl.ds(rows, rows), :] for parcel in parcels], axis=0)
        l1, l2, l3 = split3(left)
        r1, r2, r3 = split3(right * scale)
        left_parts[...] = jnp.concatenate([l1, l1, l2, l1, l3, l2], axis=0)
        right_parts[...] = jnp.concatenate([r1, r2, r1, r3, r1, r2], axis=0)

    height = out.shape[0]
    start = pl.multiple_of(pl.program_id(0) * height, LANES)
    out[...] = lax.dot_general(
        left_parts[:, pl.ds(start, height)],
        right_parts[...],
        (((0,), (0,)), ((), ())),
        preferred_element_type=jnp.float32,
    )


def fisher_block(parcels):
    rows, width = parcels[0].shape
    total = rows // 2 * len(parcels)
    block = LANES
    whole = pl.BlockSpec((rows, width), lambda i: (0, 0))
    return pl.pallas_call(
        functools.partial(fisher_kernel, 1.0 / total),
        grid=(width // block,),
        out_shape=jax.ShapeDtypeStruct((width, width), jnp.float32),
        in_specs=[whole] * len(parcels),
        out_specs=pl.BlockSpec((block, width), lambda i: (i, 0)),
        scratch_shapes=[pltpu.VMEM((6 * total, width), jnp.bfloat16)] * 2,
        compiler_params=pltpu.CompilerParams(vmem_limit_bytes=VMEM_BYTES),
        name="fisher",
    )(*parcels)


def local(acts, grads, in_ids, in_signs, out_ids, out_signs, in_table, out_table):
    tensor, seq, dp = (lax.axis_size(name) for name in ("tensor", "seq", "dp"))
    shards = tensor * seq

    act = project(acts, in_ids, in_signs, in_table, False, True, 512, "project_acts")
    if tensor == 2:
        act_parts = [act, lax.ppermute(act, "tensor", [(0, 1), (1, 0)])]
    else:
        act_parts = [lax.psum(act, "tensor")]
    grad = project(grads, out_ids, out_signs, out_table, True, False, 1024, "project_grads")
    kron = kron_of(act_parts, grad)

    if tensor != 2 or seq != 2 or shards != dp:
        kron = lax.psum(kron, PLANE)
        width = kron.shape[1] // shards
        place = place_in_plane()
        mine = lax.dynamic_slice_in_dim(kron, place * width, width, 1)
        every = lax.all_gather(kron, "dp", axis=0, tiled=True)
        left = lax.dynamic_slice_in_dim(every, place * width, width, 1)
        columns = kron.shape[1] // dp
        right = lax.dynamic_slice_in_dim(every, lax.axis_index("dp") * columns, columns, 1)
        fisher = lax.dot_general(
            left, right, (((0,), (0,)), ((), ())), precision=lax.Precision.HIGHEST
        ) / left.shape[0]
        return mine, fisher

    swap = [(0, 1), (1, 0)]
    kron = kron + lax.ppermute(kron, "seq", swap)
    mine, *parcels = pieces_of(kron, lax.ppermute(kron, "tensor", swap), dp)
    for k in range(1, dp):
        parcels[k] = lax.ppermute(parcels[k], "dp", [(d, (d + k) % dp) for d in range(dp)])
    return mine, fisher_block(parcels)


def solution(mesh):
    in_specs = (
        P(("groups", "dp"), "seq", "tensor"),
        P(("groups", "dp"), "seq", "tensor"),
        P("tensor"),
        P("tensor"),
        P("tensor"),
        P("tensor"),
        P(),
        P(),
    )
    out_specs = (P(("groups", "dp"), ("tensor", "seq")), P(("groups", "tensor", "seq"), "dp"))
    return jax.shard_map(local, mesh=mesh, in_specs=in_specs, out_specs=out_specs, check_vma=False)
```

time: 48.1 us -> 40.2 us (0.84)
  starting transfers between devices: 16.7 us -> 8.7 us
  local copies, waits for them, and re-layouts: 4.47 us -> 0.01 us
  waiting for transfers between devices: 7.1 us -> 10.2 us
  Pallas kernels: 18.8 us -> 20.5 us
    ppermute x10 -> x5, starting transfers between devices: 13.7 us -> 5.69 us  [the longest x3 5.52 us: local(): lax.ppermute(parcels[k], 'dp', [(d, (d + k) % dp) for d in range(dp)])]
    unnamed x16 -> x6, local copies, waits for them, and re-layouts: 4.47 us -> 0.01 us
    ppermute x10 -> x5, waiting for transfers between devices: 7.1 us -> 10.2 us  [the longest x1 5.51 us: local(): mine, *parcels = pieces_of(kron, lax.ppermute(kron, 'tensor', swap), dp)]
    pallas_call x4 -> x5, Pallas kernels: 18.8 us -> 20.5 us  [the longest x2 14.7 us: project(): pl.pallas_call(functools.partial(project_kernel, transpose, fetch), out_s...]
  transfers between devices with their start and end apart: 11 -> 6, of which waited for: 5 -> 4; matrix products, arithmetic and copies ran while one was open for 0% -> 0% of each run, Pallas kernels for 21% -> 25%
where the time goes in v2:
time: 40.2 us; the launch traced here: 40.1 us
  Pallas kernels  20.5 us (51%)
  waiting for transfers between devices  10.2 us (25%)
  starting transfers between devices  8.7 us (22%)
  between operations  0.7 us (2%)
    pallas_call x2, Pallas kernels, project(): pl.pallas_call(functools.partial(project_kernel, transpose, fetch), out_s...  14.7 us
    ppermute x3, starting transfers between devices, local(): lax.ppermute(parcels[k], 'dp', [(d, (d + k) % dp) for d in range(dp)])  5.52 us
    ppermute x1, waiting for transfers between devices, local(): mine, *parcels = pieces_of(kron, lax.ppermute(kron, 'tensor', swap), dp)  5.51 us
    pallas_call x1, Pallas kernels, fisher_block(): pl.pallas_call(functools.partial(fisher_kernel, 1.0 / total), grid=(width...  4.55 us
    ppermute x3, waiting for transfers between devices, local(): lax.ppermute(parcels[k], 'dp', [(d, (d + k) % dp) for d in range(dp)])  3.31 us
    ppermute x1, starting transfers between devices, local(): act_parts = [act, lax.ppermute(act, 'tensor', [(0, 1), (1, 0)])]  3 us
    ppermute x1, waiting for transfers between devices, local(): kron = kron + lax.ppermute(kron, 'seq', swap)  1.33 us
  transfers between devices with their start and end apart: 6, of which 4 were waited for; matrix products, arithmetic and copies ran while one was open for 0% of the time, Pallas kernels for 25%

profile of v2, /device:TPU:0, one launch (start us, length us, event | category | flops | bytes accessed | tf_op | source)
XLA Modules:
  0.0 40.1 jit_solution(14754950220795714183)
XLA Ops:
  0.6 0.0 copy-start
  0.6 0.0 copy-start.2
  0.7 0.0 copy-start.1
  0.7 4.8 %project_acts.1.acts = f32[4,128,128]{2,1,0:T(8,128)S(1)} custom-call(s32[32]{0:T(128)} %ids.2, s32[32]{0:T(128)} %signs.2, bf16[32,4096]{1,0:T(8,128)(2,1)} %table.2, bf16[1024,2048]{1,0:T(8,128)(2,1)} %bitcast.3), custom_call_target="tpu_custom_call" | custom-call | flops 536870912 | bytes 4194304 | tf_op jit(solution)/shard_map/project_acts/pallas_call | solution.py:117
  5.5 3.0 %collective-permute-start = (f32[4,128,128]{2,1,0:T(8,128)S(1)}, f32[4,128,128]{2,1,0:T(8,128)S(1)}, u32[]{:S(2)}, u32[]{:S(2)}) collective-permute-start(f32[4,128,128]{2,1,0:T(8,128)S(1)} %project_acts.1.acts), channel_id=1, source_target_pairs={{0,2},{2,0},{1,3},{3,1},{4,6},{6,4},{5,7},{7,5},{8,10},{10,8},{9,1... | collective-permute-start | bytes 786440 | tf_op jit(solution)/shard_map/ppermute | solution.py:254
  8.5 0.0 copy-done
  8.5 0.0 copy-done.2
  8.5 0.0 copy-done.1
  8.5 9.9 %project_grads.1.grads = f32[4,128,128]{2,1,0:T(8,128)S(1)} custom-call(s32[112]{0:T(128)S(1)} %copy-done.1, s32[112]{0:T(128)S(1)} %copy-done.2, bf16[32,4096]{1,0:T(8,128)(2,1)S(1)} %copy-done, bf16[1024,7168]{1,0:T(8,128)(2,1)} %bitcast.2), custom_call_target="tpu_custom_call" | custom-call | flops 1879048192 | bytes 14680064 | tf_op jit(solution)/shard_map/project_grads/pallas_call | solution.py:117
  18.4 0.0 collective-permute-done.refs_0_
  18.4 0.6 %kron.1 = f32[8,4096]{1,0:T(8,128)S(1)} custom-call(f32[4,128,128]{2,1,0:T(8,128)S(1)} %project_acts.1.acts, f32[4,128,128]{2,1,0:T(8,128)S(1)} %project_grads.1.grads, f32[4,128,128]{2,1,0:T(8,128)S(1)} %collective-permute-done.refs_0_), custom_call_target="tpu_custom_call" | custom-call | tf_op jit(solution)/shard_map/kron/pallas_call | solution.py:166
  19.0 0.1 collective-permute-start.1
  19.1 1.3 %collective-permute-done.1 = f32[8,4096]{1,0:T(8,128)S(1)} collective-permute-done((f32[8,4096]{1,0:T(8,128)S(1)}, f32[8,4096]{1,0:T(8,128)S(1)}, u32[]{:S(2)}, u32[]{:S(2)}) %collective-permute-start.1) | collective-permute-done | bytes 131104 | tf_op jit(solution)/shard_map/ppermute | solution.py:275
  20.4 0.1 collective-permute-start.2
  20.6 5.5 %collective-permute-done.2.there = f32[8,4096]{1,0:T(8,128)S(1)} collective-permute-done((f32[8,4096]{1,0:T(8,128)S(1)}, f32[8,4096]{1,0:T(8,128)S(1)}, u32[]{:S(2)}, u32[]{:S(2)}) %collective-permute-start.2) | collective-permute-done | bytes 131104 | tf_op jit(solution)/shard_map/ppermute | solution.py:276
  26.1 0.6 %pieces.1 = (f32[8,1024]{1,0:T(8,128)}, f32[16,1024]{1,0:T(8,128)S(1)}, f32[16,1024]{1,0:T(8,128)S(1)}, f32[16,1024]{1,0:T(8,128)S(1)}, f32[16,1024]{1,0:T(8,128)S(1)}) custom-call(f32[8,4096]{1,0:T(8,128)S(1)} %add.3.here, f32[8,4096]{1,0:T(8,128)S(1)} %collective-permute-done.2.there), custom_call_target="tpu_custom_call" | custom-call | tf_op jit(solution)/shard_map/pieces/pallas_call | solution.py:198
  26.7 1.6 %collective-permute-start.3 = (f32[16,1024]{1,0:T(8,128)S(1)}, f32[16,1024]{1,0:T(8,128)S(1)}, u32[]{:S(2)}, u32[]{:S(2)}) collective-permute-start(f32[16,1024]{1,0:T(8,128)S(1)} %get-tuple-element.9), channel_id=1, source_target_pairs={{0,4},{4,8},{8,12},{12,0},{1,5},{5,9},{9,13},{13,1},{2,6},{6,10},{... | collective-permute-start | bytes 196616 | tf_op jit(solution)/shard_map/ppermute | solution.py:278
  28.3 2.6 %collective-permute-start.4 = (f32[16,1024]{1,0:T(8,128)S(1)}, f32[16,1024]{1,0:T(8,128)S(1)}, u32[]{:S(2)}, u32[]{:S(2)}) collective-permute-start(f32[16,1024]{1,0:T(8,128)S(1)} %get-tuple-element.10), channel_id=1, source_target_pairs={{0,8},{4,12},{8,0},{12,4},{1,9},{5,13},{9,1},{13,5},{2,10},{6,14},... | collective-permute-start | bytes 196616 | tf_op jit(solution)/shard_map/ppermute | solution.py:278
  30.9 1.4 %collective-permute-start.5 = (f32[16,1024]{1,0:T(8,128)S(1)}, f32[16,1024]{1,0:T(8,128)S(1)}, u32[]{:S(2)}, u32[]{:S(2)}) collective-permute-start(f32[16,1024]{1,0:T(8,128)S(1)} %get-tuple-element.11), channel_id=1, source_target_pairs={{0,12},{4,0},{8,4},{12,8},{1,13},{5,1},{9,5},{13,9},{2,14},{6,2},{... | collective-permute-start | bytes 196616 | tf_op jit(solution)/shard_map/ppermute | solution.py:278
  32.2 1.3 %collective-permute-done.3.refs_1_ = f32[16,1024]{1,0:T(8,128)S(1)} collective-permute-done((f32[16,1024]{1,0:T(8,128)S(1)}, f32[16,1024]{1,0:T(8,128)S(1)}, u32[]{:S(2)}, u32[]{:S(2)}) %collective-permute-start.3) | collective-permute-done | bytes 65568 | tf_op jit(solution)/shard_map/ppermute | solution.py:278
  33.5 2.0 %collective-permute-done.4.refs_2_ = f32[16,1024]{1,0:T(8,128)S(1)} collective-permute-done((f32[16,1024]{1,0:T(8,128)S(1)}, f32[16,1024]{1,0:T(8,128)S(1)}, u32[]{:S(2)}, u32[]{:S(2)}) %collective-permute-start.4) | collective-permute-done | bytes 65568 | tf_op jit(solution)/shard_map/ppermute | solution.py:278
  35.5 0.0 collective-permute-done.5.refs_3_
  35.5 4.5 %fisher.1 = f32[1024,1024]{1,0:T(8,128)} custom-call(f32[16,1024]{1,0:T(8,128)S(1)} %get-tuple-element.8.refs_0_, f32[16,1024]{1,0:T(8,128)S(1)} %collective-permute-done.3.refs_1_, f32[16,1024]{1,0:T(8,128)S(1)} %collective-permute-done.4.refs_2_, f32[16,1024]{1,0:T(8,128)S(1)} %collective-permute-done.5.refs_3_), custom_call_target="tpu_custom_call" | custom-call | tf_op jit(solution)/shard_map/fisher/pallas_call | solution.py:236
  (1 shorter events, 0.0 us)
Async XLA Ops:
  0.6 7.9 %copy-start = (bf16[32,4096]{1,0:T(8,128)(2,1)S(1)}, bf16[32,4096]{1,0:T(8,128)(2,1)}, u32[]{:S(2)}) copy-start(bf16[32,4096]{1,0:T(8,128)(2,1)} %table.3) | copy-start | bytes 786436
  0.6 7.9 %copy-start.2 = (s32[112]{0:T(128)S(1)}, s32[112]{0:T(128)}, u32[]{:S(2)}) copy-start(s32[112]{0:T(128)} %signs.3) | copy-start | bytes 1348
  0.7 7.8 %copy-start.1 = (s32[112]{0:T(128)S(1)}, s32[112]{0:T(128)}, u32[]{:S(2)}) copy-start(s32[112]{0:T(128)} %ids.3) | copy-start | bytes 1348
  5.5 12.9 %collective-permute-start = (f32[4,128,128]{2,1,0:T(8,128)S(1)}, f32[4,128,128]{2,1,0:T(8,128)S(1)}, u32[]{:S(2)}, u32[]{:S(2)}) collective-permute-start(f32[4,128,128]{2,1,0:T(8,128)S(1)} %project_acts.1.acts), channel_id=1, source_target_pairs={{0,2},{2,0},{1,3},{3,1},{4,6},{6,4},{5,7},{7,5},{8,10},{10,8},{9,1... | collective-permute-start | bytes 786440 | tf_op jit(solution)/shard_map/ppermute | solution.py:254
  19.0 1.4 %collective-permute-start.1 = (f32[8,4096]{1,0:T(8,128)S(1)}, f32[8,4096]{1,0:T(8,128)S(1)}, u32[]{:S(2)}, u32[]{:S(2)}) collective-permute-start(f32[8,4096]{1,0:T(8,128)S(1)} %kron.1), channel_id=1, source_target_pairs={{0,1},{1,0},{2,3},{3,2},{4,5},{5,4},{6,7},{7,6},{8,9},{9,8},{10,11... | collective-permute-start | bytes 393224 | tf_op jit(solution)/shard_map/ppermute | solution.py:275
  20.4 5.6 %collective-permute-start.2 = (f32[8,4096]{1,0:T(8,128)S(1)}, f32[8,4096]{1,0:T(8,128)S(1)}, u32[]{:S(2)}, u32[]{:S(2)}) collective-permute-start(f32[8,4096]{1,0:T(8,128)S(1)} %add.3.here), channel_id=1, source_target_pairs={{0,2},{2,0},{1,3},{3,1},{4,6},{6,4},{5,7},{7,5},{8,10},{10,8},{9,1... | collective-permute-start | bytes 393224 | tf_op jit(solution)/shard_map/ppermute | solution.py:276
  26.7 6.8 %collective-permute-start.3 = (f32[16,1024]{1,0:T(8,128)S(1)}, f32[16,1024]{1,0:T(8,128)S(1)}, u32[]{:S(2)}, u32[]{:S(2)}) collective-permute-start(f32[16,1024]{1,0:T(8,128)S(1)} %get-tuple-element.9), channel_id=1, source_target_pairs={{0,4},{4,8},{8,12},{12,0},{1,5},{5,9},{9,13},{13,1},{2,6},{6,10},{... | collective-permute-start | bytes 196616 | tf_op jit(solution)/shard_map/ppermute | solution.py:278
  28.3 7.2 %collective-permute-start.4 = (f32[16,1024]{1,0:T(8,128)S(1)}, f32[16,1024]{1,0:T(8,128)S(1)}, u32[]{:S(2)}, u32[]{:S(2)}) collective-permute-start(f32[16,1024]{1,0:T(8,128)S(1)} %get-tuple-element.10), channel_id=1, source_target_pairs={{0,8},{4,12},{8,0},{12,4},{1,9},{5,13},{9,1},{13,5},{2,10},{6,14},... | collective-permute-start | bytes 196616 | tf_op jit(solution)/shard_map/ppermute | solution.py:278
  30.9 4.7 %collective-permute-start.5 = (f32[16,1024]{1,0:T(8,128)S(1)}, f32[16,1024]{1,0:T(8,128)S(1)}, u32[]{:S(2)}, u32[]{:S(2)}) collective-permute-start(f32[16,1024]{1,0:T(8,128)S(1)} %get-tuple-element.11), channel_id=1, source_target_pairs={{0,12},{4,0},{8,4},{12,8},{1,13},{5,1},{9,5},{13,9},{2,14},{6,2},{... | collective-permute-start | bytes 196616 | tf_op jit(solution)/shard_map/ppermute | solution.py:278

commit v3 on v2

--- a/solution.py
+++ b/solution.py
@@ -49,7 +49,7 @@
         matrix[pl.ds(j * BLOCK, BLOCK), :] = signed[pl.ds(start, BLOCK), :]
 
 
-def project_kernel(transpose, fetch, ids, signs, table, rows_ref, out, spread, signed, matrix, held, total, sems, *own):
+def project_kernel(fetch, ids, signs, table, rows_ref, out, spread, signed, matrix, held, total, sems, *own):
     chunks, _, chunk = held.shape
     copies = [
         pltpu.make_async_copy(rows_ref.at[:, pl.ds(c * chunk, chunk)], held.at[c], sems.at[c])
@@ -78,25 +78,24 @@
         copy.wait()
         if c + 1 < chunks:
             lay((c + 1) * blocks, (c + 2) * blocks)
-        part = jnp.dot(
-            held[c], matrix[pl.ds(c * chunk, chunk), :], preferred_element_type=jnp.float32
+        part = lax.dot_general(
+            matrix[pl.ds(c * chunk, chunk), :],
+            held[c],
+            (((0,), (1,)), ((), ())),
+            preferred_element_type=jnp.float32,
         )
         if c == 0:
             total[...] = part
         else:
             total[...] += part
-    pairs, tokens, _ = out.shape
-    left = lax.broadcasted_iota(jnp.int32, (tokens, LANES), 1) < PROJ
+    pairs, _, tokens = out.shape
     for pair in range(pairs):
-        first = total[pl.ds(2 * pair * tokens, tokens), :]
-        second = total[pl.ds((2 * pair + 1) * tokens, tokens), :]
-        first = first + pltpu.roll(first, PROJ, 1)
-        second = second + pltpu.roll(second, PROJ, 1)
-        packed = jnp.where(left, first, second)
-        out[pair] = packed.T if transpose else packed
-
-
-def project(values, ids, signs, table, transpose, fetch, most, name):
+        for half in range(2):
+            lanes = pl.ds((2 * pair + half) * tokens, tokens)
+            out[pair, pl.ds(half * PROJ, PROJ), :] = total[pl.ds(0, PROJ), lanes] + total[pl.ds(PROJ, PROJ), lanes]
+
+
+def project(values, ids, signs, table, fetch, most, name):
     count, tokens, width = values.shape
     chunk = chunk_of(width, most)
     chunks = width // chunk
@@ -105,7 +104,7 @@
     smem = pl.BlockSpec(memory_space=pltpu.SMEM)
     vmem = pl.BlockSpec(memory_space=pltpu.VMEM)
     hbm = pl.BlockSpec(memory_space=pltpu.HBM)
-    shape = (count // 2, LANES, tokens) if transpose else (count // 2, tokens, LANES)
+    shape = (count // 2, LANES, tokens)
     own = [
         pltpu.VMEM(table.shape, table.dtype),
         pltpu.SMEM(ids.shape, ids.dtype),
@@ -115,7 +114,7 @@
     if fetch:
         operands = [pltpu.with_memory_space_constraint(each, pltpu.HBM) for each in operands]
     return pl.pallas_call(
-        functools.partial(project_kernel, transpose, fetch),
+        functools.partial(project_kernel, fetch),
         out_shape=jax.ShapeDtypeStruct(shape, jnp.float32),
         in_specs=[hbm] * 4 if fetch else [smem, smem, vmem, hbm],
         out_specs=vmem,
@@ -124,7 +123,7 @@
             pltpu.VMEM((2 * entries * BLOCK, LANES), jnp.bfloat16),
             pltpu.VMEM((width, LANES), jnp.bfloat16),
             pltpu.VMEM((chunks, rows, chunk), jnp.bfloat16),
-            pltpu.VMEM((rows, LANES), jnp.float32),
+            pltpu.VMEM((LANES, rows), jnp.float32),
             pltpu.SemaphoreType.DMA((chunks + 3,)),
         ]
         + (own if fetch else []),
@@ -138,7 +137,7 @@
 
 def kron_kernel(acts, grads, *refs):
     summands, out, products = refs[:-2], refs[-2], refs[-1]
-    pairs, tokens, _ = acts.shape
+    pairs = acts.shape[0]
     for pair in range(pairs):
         act = acts[pair]
         for other in summands:
@@ -146,8 +145,10 @@
         a1, a2, a3 = split3(act)
         g1, g2, g3 = split3(grads[pair])
         left = jnp.concatenate([g1, g1, g2, g1, g3, g2], axis=1)
-        right = jnp.concatenate([a1, a2, a1, a3, a1, a2], axis=0)
-        products[pl.ds(pair * LANES, LANES), :] = jnp.dot(left, right, preferred_element_type=jnp.float32)
+        right = jnp.concatenate([a1, a2, a1, a3, a1, a2], axis=1)
+        products[pl.ds(pair * LANES, LANES), :] = lax.dot_general(
+            left, right, (((1,), (1,)), ((), ())), preferred_element_type=jnp.float32
+        )
     count = 2 * pairs
     lower = lax.broadcasted_iota(jnp.int32, (count, LANES), 1) < PROJ
     even = lax.broadcasted_iota(jnp.int32, (count, LANES), 0) % 2 == 0
@@ -206,40 +207,40 @@
 
 
 def fisher_kernel(scale, *refs):
-    parcels, (out, left_parts, right_parts) = refs[:-3], refs[-3:]
+    parcels, (out, made, sems) = refs[:-3], refs[-3:]
     rows = parcels[0].shape[0] // 2
-
-    @pl.when(pl.program_id(0) == 0)
-    def _():
-        left = jnp.concatenate([parcel[pl.ds(0, rows), :] for parcel in parcels], axis=0)
-        right = jnp.concatenate([parcel[pl.ds(rows, rows), :] for parcel in parcels], axis=0)
-        l1, l2, l3 = split3(left)
-        r1, r2, r3 = split3(right * scale)
-        left_parts[...] = jnp.concatenate([l1, l1, l2, l1, l3, l2], axis=0)
-        right_parts[...] = jnp.concatenate([r1, r2, r1, r3, r1, r2], axis=0)
-
-    height = out.shape[0]
-    start = pl.multiple_of(pl.program_id(0) * height, LANES)
-    out[...] = lax.dot_general(
-        left_parts[:, pl.ds(start, height)],
-        right_parts[...],
-        (((0,), (0,)), ((), ())),
-        preferred_element_type=jnp.float32,
-    )
+    left = jnp.concatenate([parcel[pl.ds(0, rows), :] for parcel in parcels], axis=0)
+    right = jnp.concatenate([parcel[pl.ds(rows, rows), :] for parcel in parcels], axis=0)
+    l1, l2, l3 = split3(left)
+    r1, r2, r3 = split3(right * scale)
+    left_parts = jnp.concatenate([l1, l1, l2, l1, l3, l2, l2, l3], axis=0).T
+    right_parts = jnp.concatenate([r1, r2, r1, r3, r1, r2, r3, r2], axis=0)
+    blocks, _, width = made.shape
+    copies = []
+    for block in range(blocks):
+        columns = slice(block * width, (block + 1) * width)
+        made[block] = jnp.dot(left_parts, right_parts[:, columns], preferred_element_type=jnp.float32)
+        copies.append(
+            pltpu.make_async_copy(made.at[block], out.at[:, pl.ds(block * width, width)], sems.at[block])
+        )
+        copies[-1].start()
+    for copy in copies:
+        copy.wait()
 
 
 def fisher_block(parcels):
     rows, width = parcels[0].shape
     total = rows // 2 * len(parcels)
-    block = LANES
-    whole = pl.BlockSpec((rows, width), lambda i: (0, 0))
+    blocks = 4
     return pl.pallas_call(
         functools.partial(fisher_kernel, 1.0 / total),
-        grid=(width // block,),
         out_shape=jax.ShapeDtypeStruct((width, width), jnp.float32),
-        in_specs=[whole] * len(parcels),
-        out_specs=pl.BlockSpec((block, width), lambda i: (i, 0)),
-        scratch_shapes=[pltpu.VMEM((6 * total, width), jnp.bfloat16)] * 2,
+        in_specs=[pl.BlockSpec(memory_space=pltpu.VMEM)] * len(parcels),
+        out_specs=pl.BlockSpec(memory_space=pltpu.HBM),
+        scratch_shapes=[
+            pltpu.VMEM((blocks, width, width // blocks), jnp.float32),
+            pltpu.SemaphoreType.DMA((blocks,)),
+        ],
         compiler_params=pltpu.CompilerParams(vmem_limit_bytes=VMEM_BYTES),
         name="fisher",
     )(*parcels)
@@ -249,12 +250,12 @@
     tensor, seq, dp = (lax.axis_size(name) for name in ("tensor", "seq", "dp"))
     shards = tensor * seq
 
-    act = project(acts, in_ids, in_signs, in_table, False, True, 512, "project_acts")
+    act = project(acts, in_ids, in_signs, in_table, True, 512, "project_acts")
     if tensor == 2:
         act_parts = [act, lax.ppermute(act, "tensor", [(0, 1), (1, 0)])]
     else:
         act_parts = [lax.psum(act, "tensor")]
-    grad = project(grads, out_ids, out_signs, out_table, True, False, 1024, "project_grads")
+    grad = project(grads, out_ids, out_signs, out_table, False, 1024, "project_grads")
     kron = kron_of(act_parts, grad)
 
     if tensor != 2 or seq != 2 or shards != dp:

time: 40.2 us -> 34.5 us (0.86)
  Pallas kernels: 20.5 us -> 14.8 us
  waiting for transfers between devices: 10.2 us -> 9.47 us
  starting transfers between devices: 8.7 us -> 9.38 us
    pallas_call x3, Pallas kernels: 19.3 us -> 13.6 us  [the longest x2 11.1 us: project(): pl.pallas_call(functools.partial(project_kernel, fetch), out_shape=jax.Sh...]
    ppermute x1, waiting for transfers between devices: 5.51 us -> 4.83 us  [local(): mine, *parcels = pieces_of(kron, lax.ppermute(kron, 'tensor', swap), dp)]
    ppermute x1, starting transfers between devices: 0.11 us -> 0.79 us  [local(): mine, *parcels = pieces_of(kron, lax.ppermute(kron, 'tensor', swap), dp)]
  transfers between devices with their start and end apart: 6 -> 6, of which waited for: 4 -> 4; matrix products, arithmetic and copies ran while one was open for 0% -> 0% of each run, Pallas kernels for 25% -> 21%
where the time goes in v3:
time: 34.5 us; the launch traced here: 34.4 us
  Pallas kernels  14.8 us (43%)
  waiting for transfers between devices  9.47 us (27%)
  starting transfers between devices  9.38 us (27%)
  between operations  0.71 us (2%)
    pallas_call x2, Pallas kernels, project(): pl.pallas_call(functools.partial(project_kernel, fetch), out_shape=jax.Sh...  11.1 us
    ppermute x3, starting transfers between devices, local(): lax.ppermute(parcels[k], 'dp', [(d, (d + k) % dp) for d in range(dp)])  5.52 us
    ppermute x1, waiting for transfers between devices, local(): mine, *parcels = pieces_of(kron, lax.ppermute(kron, 'tensor', swap), dp)  4.83 us
    ppermute x3, waiting for transfers between devices, local(): lax.ppermute(parcels[k], 'dp', [(d, (d + k) % dp) for d in range(dp)])  3.31 us
    ppermute x1, starting transfers between devices, local(): act_parts = [act, lax.ppermute(act, 'tensor', [(0, 1), (1, 0)])]  2.99 us
    pallas_call x1, Pallas kernels, fisher_block(): pl.pallas_call(functools.partial(fisher_kernel, 1.0 / total), out_shape=j...  2.51 us
    ppermute x1, waiting for transfers between devices, local(): kron = kron + lax.ppermute(kron, 'seq', swap)  1.33 us
    ppermute x1, starting transfers between devices, local(): mine, *parcels = pieces_of(kron, lax.ppermute(kron, 'tensor', swap), dp)  0.79 us
  transfers between devices with their start and end apart: 6, of which 4 were waited for; matrix products, arithmetic and copies ran while one was open for 0% of the time, Pallas kernels for 21%

profile of v3, /device:TPU:0, one launch (start us, length us, event | category | flops | bytes accessed | tf_op | source)
XLA Modules:
  0.0 34.4 jit_solution(12036874103289582711)
XLA Ops:
  0.6 0.0 copy-start
  0.6 0.0 copy-start.2
  0.7 0.0 copy-start.1
  0.7 3.8 %project_acts.1.acts = f32[4,128,128]{2,1,0:T(8,128)S(1)} custom-call(s32[32]{0:T(128)} %ids.2, s32[32]{0:T(128)} %signs.2, bf16[32,4096]{1,0:T(8,128)(2,1)} %table.2, bf16[1024,2048]{1,0:T(8,128)(2,1)} %bitcast.3), custom_call_target="tpu_custom_call" | custom-call | flops 536870912 | bytes 4194304 | tf_op jit(solution)/shard_map/project_acts/pallas_call | solution.py:116
  4.5 3.0 %collective-permute-start = (f32[4,128,128]{2,1,0:T(8,128)S(1)}, f32[4,128,128]{2,1,0:T(8,128)S(1)}, u32[]{:S(2)}, u32[]{:S(2)}) collective-permute-start(f32[4,128,128]{2,1,0:T(8,128)S(1)} %project_acts.1.acts), channel_id=1, source_target_pairs={{0,2},{2,0},{1,3},{3,1},{4,6},{6,4},{5,7},{7,5},{8,10},{10,8},{9,1... | collective-permute-start | bytes 786440 | tf_op jit(solution)/shard_map/ppermute | solution.py:255
  7.5 0.0 copy-done
  7.5 0.0 copy-done.2
  7.5 0.0 copy-done.1
  7.5 7.3 %project_grads.1.grads = f32[4,128,128]{2,1,0:T(8,128)S(1)} custom-call(s32[112]{0:T(128)S(1)} %copy-done.1, s32[112]{0:T(128)S(1)} %copy-done.2, bf16[32,4096]{1,0:T(8,128)(2,1)S(1)} %copy-done, bf16[1024,7168]{1,0:T(8,128)(2,1)} %bitcast.2), custom_call_target="tpu_custom_call" | custom-call | flops 1879048192 | bytes 14680064 | tf_op jit(solution)/shard_map/project_grads/pallas_call | solution.py:116
  14.8 0.0 collective-permute-done.refs_0_
  14.8 0.6 %kron.1 = f32[8,4096]{1,0:T(8,128)S(1)} custom-call(f32[4,128,128]{2,1,0:T(8,128)S(1)} %project_acts.1.acts, f32[4,128,128]{2,1,0:T(8,128)S(1)} %project_grads.1.grads, f32[4,128,128]{2,1,0:T(8,128)S(1)} %collective-permute-done.refs_0_), custom_call_target="tpu_custom_call" | custom-call | tf_op jit(solution)/shard_map/kron/pallas_call | solution.py:167
  15.4 0.1 collective-permute-start.1
  15.5 1.3 %collective-permute-done.1 = f32[8,4096]{1,0:T(8,128)S(1)} collective-permute-done((f32[8,4096]{1,0:T(8,128)S(1)}, f32[8,4096]{1,0:T(8,128)S(1)}, u32[]{:S(2)}, u32[]{:S(2)}) %collective-permute-start.1) | collective-permute-done | bytes 131104 | tf_op jit(solution)/shard_map/ppermute | solution.py:276
  16.8 0.8 %collective-permute-start.2 = (f32[8,4096]{1,0:T(8,128)S(1)}, f32[8,4096]{1,0:T(8,128)S(1)}, u32[]{:S(2)}, u32[]{:S(2)}) collective-permute-start(f32[8,4096]{1,0:T(8,128)S(1)} %add.3.here), channel_id=1, source_target_pairs={{0,2},{2,0},{1,3},{3,1},{4,6},{6,4},{5,7},{7,5},{8,10},{10,8},{9,1... | collective-permute-start | bytes 393224 | tf_op jit(solution)/shard_map/ppermute | solution.py:277
  17.6 4.8 %collective-permute-done.2.there = f32[8,4096]{1,0:T(8,128)S(1)} collective-permute-done((f32[8,4096]{1,0:T(8,128)S(1)}, f32[8,4096]{1,0:T(8,128)S(1)}, u32[]{:S(2)}, u32[]{:S(2)}) %collective-permute-start.2) | collective-permute-done | bytes 131104 | tf_op jit(solution)/shard_map/ppermute | solution.py:277
  22.4 0.6 %pieces.1 = (f32[8,1024]{1,0:T(8,128)}, f32[16,1024]{1,0:T(8,128)S(1)}, f32[16,1024]{1,0:T(8,128)S(1)}, f32[16,1024]{1,0:T(8,128)S(1)}, f32[16,1024]{1,0:T(8,128)S(1)}) custom-call(f32[8,4096]{1,0:T(8,128)S(1)} %add.3.here, f32[8,4096]{1,0:T(8,128)S(1)} %collective-permute-done.2.there), custom_call_target="tpu_custom_call" | custom-call | tf_op jit(solution)/shard_map/pieces/pallas_call | solution.py:199
  23.0 1.6 %collective-permute-start.3 = (f32[16,1024]{1,0:T(8,128)S(1)}, f32[16,1024]{1,0:T(8,128)S(1)}, u32[]{:S(2)}, u32[]{:S(2)}) collective-permute-start(f32[16,1024]{1,0:T(8,128)S(1)} %get-tuple-element.9), channel_id=1, source_target_pairs={{0,4},{4,8},{8,12},{12,0},{1,5},{5,9},{9,13},{13,1},{2,6},{6,10},{... | collective-permute-start | bytes 196616 | tf_op jit(solution)/shard_map/ppermute | solution.py:279
  24.6 2.6 %collective-permute-start.4 = (f32[16,1024]{1,0:T(8,128)S(1)}, f32[16,1024]{1,0:T(8,128)S(1)}, u32[]{:S(2)}, u32[]{:S(2)}) collective-permute-start(f32[16,1024]{1,0:T(8,128)S(1)} %get-tuple-element.10), channel_id=1, source_target_pairs={{0,8},{4,12},{8,0},{12,4},{1,9},{5,13},{9,1},{13,5},{2,10},{6,14},... | collective-permute-start | bytes 196616 | tf_op jit(solution)/shard_map/ppermute | solution.py:279
  27.2 1.3 %collective-permute-start.5 = (f32[16,1024]{1,0:T(8,128)S(1)}, f32[16,1024]{1,0:T(8,128)S(1)}, u32[]{:S(2)}, u32[]{:S(2)}) collective-permute-start(f32[16,1024]{1,0:T(8,128)S(1)} %get-tuple-element.11), channel_id=1, source_target_pairs={{0,12},{4,0},{8,4},{12,8},{1,13},{5,1},{9,5},{13,9},{2,14},{6,2},{... | collective-permute-start | bytes 196616 | tf_op jit(solution)/shard_map/ppermute | solution.py:279
  28.6 1.3 %collective-permute-done.3.refs_1_ = f32[16,1024]{1,0:T(8,128)S(1)} collective-permute-done((f32[16,1024]{1,0:T(8,128)S(1)}, f32[16,1024]{1,0:T(8,128)S(1)}, u32[]{:S(2)}, u32[]{:S(2)}) %collective-permute-start.3) | collective-permute-done | bytes 65568 | tf_op jit(solution)/shard_map/ppermute | solution.py:279
  29.9 2.0 %collective-permute-done.4.refs_2_ = f32[16,1024]{1,0:T(8,128)S(1)} collective-permute-done((f32[16,1024]{1,0:T(8,128)S(1)}, f32[16,1024]{1,0:T(8,128)S(1)}, u32[]{:S(2)}, u32[]{:S(2)}) %collective-permute-start.4) | collective-permute-done | bytes 65568 | tf_op jit(solution)/shard_map/ppermute | solution.py:279
  31.8 0.0 collective-permute-done.5.refs_3_
  31.9 2.5 %fisher.1 = f32[1024,1024]{1,0:T(8,128)} custom-call(f32[16,1024]{1,0:T(8,128)S(1)} %get-tuple-element.8.refs_0_, f32[16,1024]{1,0:T(8,128)S(1)} %collective-permute-done.3.refs_1_, f32[16,1024]{1,0:T(8,128)S(1)} %collective-permute-done.4.refs_2_, f32[16,1024]{1,0:T(8,128)S(1)} %collective-permute-done.5.refs_3_), custom_call_target="tpu_custom_call" | custom-call | tf_op jit(solution)/shard_map/fisher/pallas_call | solution.py:235
  (1 shorter events, 0.0 us)
Async XLA Ops:
  0.6 6.8 %copy-start = (bf16[32,4096]{1,0:T(8,128)(2,1)S(1)}, bf16[32,4096]{1,0:T(8,128)(2,1)}, u32[]{:S(2)}) copy-start(bf16[32,4096]{1,0:T(8,128)(2,1)} %table.3) | copy-start | bytes 786436
  0.6 6.8 %copy-start.2 = (s32[112]{0:T(128)S(1)}, s32[112]{0:T(128)}, u32[]{:S(2)}) copy-start(s32[112]{0:T(128)} %signs.3) | copy-start | bytes 1348
  0.7 6.8 %copy-start.1 = (s32[112]{0:T(128)S(1)}, s32[112]{0:T(128)}, u32[]{:S(2)}) copy-start(s32[112]{0:T(128)} %ids.3) | copy-start | bytes 1348
  4.5 10.3 %collective-permute-start = (f32[4,128,128]{2,1,0:T(8,128)S(1)}, f32[4,128,128]{2,1,0:T(8,128)S(1)}, u32[]{:S(2)}, u32[]{:S(2)}) collective-permute-start(f32[4,128,128]{2,1,0:T(8,128)S(1)} %project_acts.1.acts), channel_id=1, source_target_pairs={{0,2},{2,0},{1,3},{3,1},{4,6},{6,4},{5,7},{7,5},{8,10},{10,8},{9,1... | collective-permute-start | bytes 786440 | tf_op jit(solution)/shard_map/ppermute | solution.py:255
  15.4 1.4 %collective-permute-start.1 = (f32[8,4096]{1,0:T(8,128)S(1)}, f32[8,4096]{1,0:T(8,128)S(1)}, u32[]{:S(2)}, u32[]{:S(2)}) collective-permute-start(f32[8,4096]{1,0:T(8,128)S(1)} %kron.1), channel_id=1, source_target_pairs={{0,1},{1,0},{2,3},{3,2},{4,5},{5,4},{6,7},{7,6},{8,9},{9,8},{10,11... | collective-permute-start | bytes 393224 | tf_op jit(solution)/shard_map/ppermute | solution.py:276
  16.8 5.6 %collective-permute-start.2 = (f32[8,4096]{1,0:T(8,128)S(1)}, f32[8,4096]{1,0:T(8,128)S(1)}, u32[]{:S(2)}, u32[]{:S(2)}) collective-permute-start(f32[8,4096]{1,0:T(8,128)S(1)} %add.3.here), channel_id=1, source_target_pairs={{0,2},{2,0},{1,3},{3,1},{4,6},{6,4},{5,7},{7,5},{8,10},{10,8},{9,1... | collective-permute-start | bytes 393224 | tf_op jit(solution)/shard_map/ppermute | solution.py:277
  23.0 6.8 %collective-permute-start.3 = (f32[16,1024]{1,0:T(8,128)S(1)}, f32[16,1024]{1,0:T(8,128)S(1)}, u32[]{:S(2)}, u32[]{:S(2)}) collective-permute-start(f32[16,1024]{1,0:T(8,128)S(1)} %get-tuple-element.9), channel_id=1, source_target_pairs={{0,4},{4,8},{8,12},{12,0},{1,5},{5,9},{9,13},{13,1},{2,6},{6,10},{... | collective-permute-start | bytes 196616 | tf_op jit(solution)/shard_map/ppermute | solution.py:279
  24.6 7.2 %collective-permute-start.4 = (f32[16,1024]{1,0:T(8,128)S(1)}, f32[16,1024]{1,0:T(8,128)S(1)}, u32[]{:S(2)}, u32[]{:S(2)}) collective-permute-start(f32[16,1024]{1,0:T(8,128)S(1)} %get-tuple-element.10), channel_id=1, source_target_pairs={{0,8},{4,12},{8,0},{12,4},{1,9},{5,13},{9,1},{13,5},{2,10},{6,14},... | collective-permute-start | bytes 196616 | tf_op jit(solution)/shard_map/ppermute | solution.py:279
  27.2 4.7 %collective-permute-start.5 = (f32[16,1024]{1,0:T(8,128)S(1)}, f32[16,1024]{1,0:T(8,128)S(1)}, u32[]{:S(2)}, u32[]{:S(2)}) collective-permute-start(f32[16,1024]{1,0:T(8,128)S(1)} %get-tuple-element.11), channel_id=1, source_target_pairs={{0,12},{4,0},{8,4},{12,8},{1,13},{5,1},{9,5},{13,9},{2,14},{6,2},{... | collective-permute-start | bytes 196616 | tf_op jit(solution)/shard_map/ppermute | solution.py:279

commit v4 on v3

v4 whole, which is shorter than its diff:
```python
import functools

import jax
import jax.numpy as jnp
from jax import lax
from jax.experimental import pallas as pl
from jax.experimental.pallas import tpu as pltpu
from jax.sharding import PartitionSpec as P

PROJ = 64
BLOCK = 64
LANES = 128
VMEM_BYTES = 48 * 1024 * 1024
PLANE = ("tensor", "seq")


HALVES = 2


def chunks_of(width, most):
    if width >= 4 * most:
        inner = width - most
        ends = [most // 2] * 2
    else:
        inner, ends = width, []
    chunk = most
    while inner % chunk:
        chunk -= LANES
    return ends[:1] + [chunk] * (inner // chunk) + ends[1:]


def split3(x):
    high = x.astype(jnp.bfloat16)
    rest = x - high.astype(jnp.float32)
    mid = rest.astype(jnp.bfloat16)
    low = (rest - mid.astype(jnp.float32)).astype(jnp.bfloat16)
    return high, mid, low


def spread_table(table, spread, signed):
    entries = table.shape[0]
    stride = spread.shape[0] // entries
    for row in range(0, BLOCK, 2):
        both = table[:, row * PROJ : row * PROJ + LANES].astype(jnp.float32)
        spread[pl.ds(row, entries, stride=stride), :] = both
        spread[pl.ds(row + 1, entries, stride=stride), :] = pltpu.roll(both, PROJ, 1)
    for entry in range(entries):
        block = spread[pl.ds(entry * stride, BLOCK), :].astype(jnp.bfloat16)
        signed[pl.ds((entries + entry) * BLOCK, BLOCK), :] = block
        signed[pl.ds(entry * BLOCK, BLOCK), :] = -block


def lay_blocks(ids, signs, entries, signed, matrix, first, last):
    for j in range(first, last):
        start = pl.multiple_of((signs[j] * entries + ids[j]) * BLOCK, BLOCK)
        matrix[pl.ds(j * BLOCK, BLOCK), :] = signed[pl.ds(start, BLOCK), :]


def project_kernel(widths, fetch, ids, signs, table, rows_ref, *refs):
    outs, (spread, signed, matrix, held, total, sems, *own) = refs[:HALVES], refs[HALVES:]
    copies, starts, start = [], [], 0
    for c, width in enumerate(widths):
        columns = pl.ds(start, width)
        copies.append(pltpu.make_async_copy(rows_ref.at[:, columns], held.at[:, columns], sems.at[c]))
        starts.append(start)
        start += width
    if fetch:
        small = [
            pltpu.make_async_copy(source, kept, sems.at[len(widths) + k])
            for k, (source, kept) in enumerate(zip((table, ids, signs), own))
        ]
        for copy in small:
            copy.start()
        table, ids, signs = own
    for copy in copies:
        copy.start()
    if fetch:
        small[0].wait()
    spread_table(table, spread, signed)
    if fetch:
        small[1].wait()
        small[2].wait()
    lay = functools.partial(lay_blocks, ids, signs, table.shape[0], signed, matrix)
    lay(0, widths[0] // BLOCK)
    for c, copy in enumerate(copies):
        columns = pl.ds(starts[c], widths[c])
        copy.wait()
        if c + 1 < len(widths):
            lay(starts[c + 1] // BLOCK, (starts[c + 1] + widths[c + 1]) // BLOCK)
        part = lax.dot_general(
            matrix[columns, :PROJ],
            held[:, columns],
            (((0,), (1,)), ((), ())),
            preferred_element_type=jnp.float32,
        )
        if c == 0:
            total[...] = part
        else:
            total[...] += part
    pairs, _, tokens = outs[0].shape
    for h, out in enumerate(outs):
        for pair in range(pairs):
            for side in range(2):
                example = 2 * (h * pairs + pair) + side
                out[pair, pl.ds(side * PROJ, PROJ), :] = total[:, pl.ds(example * tokens, tokens)]


def project(values, ids, signs, table, fetch, most, name):
    count, tokens, width = values.shape
    widths = chunks_of(width, most)
    rows = count * tokens
    entries = table.shape[0]
    smem = pl.BlockSpec(memory_space=pltpu.SMEM)
    vmem = pl.BlockSpec(memory_space=pltpu.VMEM)
    hbm = pl.BlockSpec(memory_space=pltpu.HBM)
    own = [
        pltpu.VMEM(table.shape, table.dtype),
        pltpu.SMEM(ids.shape, ids.dtype),
        pltpu.SMEM(signs.shape, signs.dtype),
    ]
    operands = [ids, signs, table, values.reshape(rows, width)]
    if fetch:
        operands = [pltpu.with_memory_space_constraint(each, pltpu.HBM) for each in operands]
    return pl.pallas_call(
        functools.partial(project_kernel, widths, fetch),
        out_shape=[jax.ShapeDtypeStruct((count // 2 // HALVES, LANES, tokens), jnp.float32)] * HALVES,
        in_specs=[hbm] * 4 if fetch else [smem, smem, vmem, hbm],
        out_specs=[vmem] * HALVES,
        scratch_shapes=[
            pltpu.VMEM((entries * (BLOCK + 8), LANES), jnp.float32),
            pltpu.VMEM((2 * entries * BLOCK, LANES), jnp.bfloat16),
            pltpu.VMEM((width, LANES), jnp.bfloat16),
            pltpu.VMEM((rows, width), jnp.bfloat16),
            pltpu.VMEM((PROJ, rows), jnp.float32),
            pltpu.SemaphoreType.DMA((len(widths) + 3,)),
        ]
        + (own if fetch else []),
        compiler_params=pltpu.CompilerParams(vmem_limit_bytes=VMEM_BYTES),
        cost_estimate=pl.CostEstimate(
            flops=2 * rows * width * LANES, bytes_accessed=2 * rows * width, transcendentals=0
        ),
        name=name,
    )(*operands)


def kron_kernel(acts, grads, *refs):
    summands, out, products = refs[:-2], refs[-2], refs[-1]
    pairs = acts.shape[0]
    for pair in range(pairs):
        act = acts[pair]
        for other in summands:
            act = act + other[pair]
        a1, a2, a3 = split3(act)
        g1, g2, g3 = split3(grads[pair])
        left = jnp.concatenate([g1, g1, g2, g1, g3, g2], axis=1)
        right = jnp.concatenate([a1, a2, a1, a3, a1, a2], axis=1)
        products[pl.ds(pair * LANES, LANES), :] = lax.dot_general(
            left, right, (((1,), (1,)), ((), ())), preferred_element_type=jnp.float32
        )
    count = 2 * pairs
    lower = lax.broadcasted_iota(jnp.int32, (count, LANES), 1) < PROJ
    even = lax.broadcasted_iota(jnp.int32, (count, LANES), 0) % 2 == 0
    here = even == lower
    for tile in range(out.shape[1] // LANES):
        both = []
        for p in (2 * tile, 2 * tile + 1):
            v = products[pl.ds(p, count, stride=PROJ), :]
            both.append(jnp.where(here, v, pltpu.roll(v, PROJ, 1)))
        out[:, pl.ds(tile * LANES, LANES)] = jnp.where(lower, both[0], both[1])


def kron_of(act_parts, grads):
    pairs = grads.shape[0]
    vmem = pl.BlockSpec(memory_space=pltpu.VMEM)
    return pl.pallas_call(
        kron_kernel,
        out_shape=jax.ShapeDtypeStruct((2 * pairs, PROJ * PROJ), jnp.float32),
        in_specs=[vmem] * (1 + len(act_parts)),
        out_specs=vmem,
        scratch_shapes=[pltpu.VMEM((pairs * LANES, LANES), jnp.float32)],
        compiler_params=pltpu.CompilerParams(vmem_limit_bytes=VMEM_BYTES),
        name="kron",
    )(act_parts[0], grads, *act_parts[1:])


def place_in_plane():
    return lax.axis_index("tensor") * lax.axis_size("seq") + lax.axis_index("seq")


def pieces_kernel(here, there, *parcels):
    count = here.shape[0]
    dp = len(parcels)
    width = parcels[0].shape[1]
    start = pl.multiple_of(place_in_plane() * width, LANES)
    row = here[:, pl.ds(start, width)] + there[:, pl.ds(start, width)]
    for k, parcel in enumerate(parcels):
        parcel[pl.ds(0, count), :] = row
        other = lax.rem(lax.axis_index("dp") + k, dp)
        start = pl.multiple_of(other * width, LANES)
        parcel[pl.ds(count, count), :] = here[:, pl.ds(start, width)] + there[:, pl.ds(start, width)]


def pieces_of(here, there, dp):
    count, width = here.shape
    vmem = pl.BlockSpec(memory_space=pltpu.VMEM)
    return pl.pallas_call(
        pieces_kernel,
        out_shape=[jax.ShapeDtypeStruct((2 * count, width // dp), jnp.float32)] * dp,
        in_specs=[vmem] * 2,
        out_specs=[vmem] * dp,
        compiler_params=pltpu.CompilerParams(vmem_limit_bytes=VMEM_BYTES),
        name="pieces",
    )(here, there)


def fisher_kernel(scale, *refs):
    parcels, (mine, out, made, kept, left, right, sems) = refs[:-7], refs[-7:]
    rows = parcels[0].shape[0] // 2
    for k, parcel in enumerate(parcels):
        left[pl.ds(k * rows, rows), :] = parcel[pl.ds(0, rows), :]
        right[pl.ds(k * rows, rows), :] = parcel[pl.ds(rows, rows), :]
    blocks, _, width = made.shape
    kept[...] = left[pl.ds(0, kept.shape[0]), :]
    copies = [pltpu.make_async_copy(kept, mine, sems.at[blocks])]
    copies[0].start()
    l1, l2, l3 = split3(left[...])
    r1, r2, r3 = split3(right[...] * scale)
    left_parts = jnp.concatenate([l1, l1, l2, l1, l3, l2, l2, l3], axis=0).T
    right_parts = jnp.concatenate([r1, r2, r1, r3, r1, r2, r3, r2], axis=0)
    for block in range(blocks):
        columns = slice(block * width, (block + 1) * width)
        made[block] = jnp.dot(left_parts, right_parts[:, columns], preferred_element_type=jnp.float32)
        copies.append(
            pltpu.make_async_copy(made.at[block], out.at[:, pl.ds(block * width, width)], sems.at[block])
        )
        copies[-1].start()
    for copy in copies:
        copy.wait()


def fisher_block(parcels):
    rows, width = parcels[0].shape
    rows //= 2
    total = rows * len(parcels)
    blocks = 4
    hbm = pl.BlockSpec(memory_space=pltpu.HBM)
    return pl.pallas_call(
        functools.partial(fisher_kernel, 1.0 / total),
        out_shape=[
            jax.ShapeDtypeStruct((rows * HALVES, width), jnp.float32),
            jax.ShapeDtypeStruct((width, width), jnp.float32),
        ],
        in_specs=[pl.BlockSpec(memory_space=pltpu.VMEM)] * len(parcels),
        out_specs=[hbm] * 2,
        scratch_shapes=[
            pltpu.VMEM((blocks, width, width // blocks), jnp.float32),
            pltpu.VMEM((rows * HALVES, width), jnp.float32),
            pltpu.VMEM((total, width), jnp.float32),
            pltpu.VMEM((total, width), jnp.float32),
            pltpu.SemaphoreType.DMA((blocks + 1,)),
        ],
        compiler_params=pltpu.CompilerParams(vmem_limit_bytes=VMEM_BYTES),
        name="fisher",
    )(*parcels)


def local(acts, grads, in_ids, in_signs, out_ids, out_signs, in_table, out_table):
    tensor, seq, dp = (lax.axis_size(name) for name in ("tensor", "seq", "dp"))
    shards = tensor * seq
    swap = [(0, 1), (1, 0)]

    act_halves = project(acts, in_ids, in_signs, in_table, True, 512, "project_acts")
    if tensor == 2:
        act_halves = [[act, lax.ppermute(act, "tensor", swap)] for act in act_halves]
    else:
        act_halves = [[lax.psum(act, "tensor")] for act in act_halves]
    grad_halves = project(grads, out_ids, out_signs, out_table, False, 1024, "project_grads")
    krons = [kron_of(parts, grad) for parts, grad in zip(act_halves, grad_halves)]

    if tensor != 2 or seq != 2 or shards != dp:
        kron = lax.psum(jnp.concatenate(krons, axis=0), PLANE)
        width = kron.shape[1] // shards
        place = place_in_plane()
        mine = lax.dynamic_slice_in_dim(kron, place * width, width, 1)
        every = lax.all_gather(kron, "dp", axis=0, tiled=True)
        left = lax.dynamic_slice_in_dim(every, place * width, width, 1)
        columns = kron.shape[1] // dp
        right = lax.dynamic_slice_in_dim(every, lax.axis_index("dp") * columns, columns, 1)
        fisher = lax.dot_general(
            left, right, (((0,), (0,)), ((), ())), precision=lax.Precision.HIGHEST
        ) / left.shape[0]
        return mine, fisher

    krons = [kron + lax.ppermute(kron, "seq", swap) for kron in krons]
    there = [lax.ppermute(kron, "tensor", swap) for kron in krons]
    halves = [pieces_of(kron, other, dp) for kron, other in zip(krons, there)]
    parcels = [parcel[0] for parcel in halves]
    for k in range(1, dp):
        for parcel in halves:
            parcels.append(lax.ppermute(parcel[k], "dp", [(d, (d + k) % dp) for d in range(dp)]))
    mine, fisher = fisher_block(parcels)
    return mine, fisher


def solution(mesh):
    in_specs = (
        P(("groups", "dp"), "seq", "tensor"),
        P(("groups", "dp"), "seq", "tensor"),
        P("tensor"),
        P("tensor"),
        P("tensor"),
        P("tensor"),
        P(),
        P(),
    )
    out_specs = (P(("groups", "dp"), ("tensor", "seq")), P(("groups", "tensor", "seq"), "dp"))
    return jax.shard_map(local, mesh=mesh, in_specs=in_specs, out_specs=out_specs, check_vma=False)
```

time: 34.5 us -> 35.2 us (1.020)
  starting transfers between devices: 9.38 us -> 16.4 us
  waiting for transfers between devices: 9.47 us -> 4.59 us
  Pallas kernels: 14.8 us -> 13.3 us
    ppermute x6 -> x12, starting transfers between devices: 9.38 us -> 16.4 us  [the longest x6 10 us: local(): lax.ppermute(parcel[k], 'dp', [(d, (d + k) % dp) for d in range(dp)])]
    ppermute x6 -> x12, waiting for transfers between devices: 9.47 us -> 4.59 us  [the longest x6 2.49 us: local(): lax.ppermute(parcel[k], 'dp', [(d, (d + k) % dp) for d in range(dp)])]
    pallas_call x4 -> x5, Pallas kernels: 14.3 us -> 12.5 us  [the longest x2 9.93 us: project(): pl.pallas_call(functools.partial(project_kernel, widths, fetch), out_shap...]
    pallas_call x1 -> x2, Pallas kernels: 0.56 us -> 0.81 us  [kron_of(): pl.pallas_call(kron_kernel, out_shape=jax.ShapeDtypeStruct((2 * pairs, PR...]
  transfers between devices with their start and end apart: 6 -> 12, of which waited for: 4 -> 4; matrix products, arithmetic and copies ran while one was open for 0% -> 0% of each run, Pallas kernels for 21% -> 22%
where the time goes in v4:
time: 35.2 us; the launch traced here: 35.1 us
  starting transfers between devices  16.4 us (47%)
  Pallas kernels  13.3 us (38%)
  waiting for transfers between devices  4.59 us (13%)
  between operations  0.74 us (2%)
    ppermute x6, starting transfers between devices, local(): lax.ppermute(parcel[k], 'dp', [(d, (d + k) % dp) for d in range(dp)])  10 us
    pallas_call x2, Pallas kernels, project(): pl.pallas_call(functools.partial(project_kernel, widths, fetch), out_shap...  9.93 us
    ppermute x2, starting transfers between devices, local(): lax.ppermute(act, 'tensor', swap)  3.08 us
    ppermute x2, starting transfers between devices, local(): there = [lax.ppermute(kron, 'tensor', swap) for kron in krons]  2.62 us
    pallas_call x1, Pallas kernels, fisher_block(): pl.pallas_call(functools.partial(fisher_kernel, 1.0 / total), out_shape=[...  2.55 us
    ppermute x6, waiting for transfers between devices, local(): lax.ppermute(parcel[k], 'dp', [(d, (d + k) % dp) for d in range(dp)])  2.49 us
    ppermute x2, waiting for transfers between devices, local(): there = [lax.ppermute(kron, 'tensor', swap) for kron in krons]  1.83 us
    pallas_call x2, Pallas kernels, kron_of(): pl.pallas_call(kron_kernel, out_shape=jax.ShapeDtypeStruct((2 * pairs, PR...  0.81 us
  transfers between devices with their start and end apart: 12, of which 4 were waited for; matrix products, arithmetic and copies ran while one was open for 0% of the time, Pallas kernels for 22%

profile of v4, /device:TPU:0, one launch (start us, length us, event | category | flops | bytes accessed | tf_op | source)
XLA Modules:
  0.0 35.1 jit_solution(14400769491727227478)
XLA Ops:
  0.6 0.0 copy-start
  0.6 0.0 copy-start.2
  0.7 0.0 copy-start.1
  0.7 2.9 %project_acts.1 = (f32[2,128,128]{2,1,0:T(8,128)S(1)}, f32[2,128,128]{2,1,0:T(8,128)S(1)}) custom-call(s32[32]{0:T(128)} %ids.2, s32[32]{0:T(128)} %signs.2, bf16[32,4096]{1,0:T(8,128)(2,1)} %table.2, bf16[1024,2048]{1,0:T(8,128)(2,1)} %bitcast.3), custom_call_target="tpu_custom_call" | custom-call | flops 536870912 | bytes 4194304 | tf_op jit(solution)/shard_map/project_acts/pallas_call | solution.py:124
  3.6 3.0 %collective-permute-start = (f32[2,128,128]{2,1,0:T(8,128)S(1)}, f32[2,128,128]{2,1,0:T(8,128)S(1)}, u32[]{:S(2)}, u32[]{:S(2)}) collective-permute-start(f32[2,128,128]{2,1,0:T(8,128)S(1)} %get-tuple-element.14.acts), channel_id=1, source_target_pairs={{0,2},{2,0},{1,3},{3,1},{4,6},{6,4},{5,7},{7,5},{8,10},{10,8},{9,1... | collective-permute-start | bytes 393224 | tf_op jit(solution)/shard_map/ppermute | solution.py:274
  6.6 0.1 collective-permute-start.3
  6.7 0.0 copy-done
  6.7 0.0 copy-done.2
  6.7 0.0 copy-done.1
  6.7 7.0 %project_grads.1 = (f32[2,128,128]{2,1,0:T(8,128)S(1)}, f32[2,128,128]{2,1,0:T(8,128)S(1)}) custom-call(s32[112]{0:T(128)S(1)} %copy-done.1, s32[112]{0:T(128)S(1)} %copy-done.2, bf16[32,4096]{1,0:T(8,128)(2,1)S(1)} %copy-done, bf16[1024,7168]{1,0:T(8,128)(2,1)} %bitcast.2), custom_call_target="tpu_custom_call" | custom-call | flops 1879048192 | bytes 14680064 | tf_op jit(solution)/shard_map/project_grads/pallas_call | solution.py:124
  13.7 0.0 collective-permute-done.refs_0_
  13.7 0.4 %kron.2 = f32[4,4096]{1,0:T(4,128)S(1)} custom-call(f32[2,128,128]{2,1,0:T(8,128)S(1)} %get-tuple-element.14.acts, f32[2,128,128]{2,1,0:T(8,128)S(1)} %get-tuple-element.15.grads, f32[2,128,128]{2,1,0:T(8,128)S(1)} %collective-permute-done.refs_0_), custom_call_target="tpu_custom_call" | custom-call | tf_op jit(solution)/shard_map/kron/pallas_call | solution.py:175
  14.1 0.1 collective-permute-start.1
  14.2 0.0 collective-permute-done.3.refs_0_
  14.2 0.4 %kron.3 = f32[4,4096]{1,0:T(4,128)S(1)} custom-call(f32[2,128,128]{2,1,0:T(8,128)S(1)} %get-tuple-element.17.acts, f32[2,128,128]{2,1,0:T(8,128)S(1)} %get-tuple-element.18.grads, f32[2,128,128]{2,1,0:T(8,128)S(1)} %collective-permute-done.3.refs_0_), custom_call_target="tpu_custom_call" | custom-call | tf_op jit(solution)/shard_map/kron/pallas_call | solution.py:175
  14.6 0.6 %collective-permute-start.4 = (f32[4,4096]{1,0:T(4,128)S(1)}, f32[4,4096]{1,0:T(4,128)S(1)}, u32[]{:S(2)}, u32[]{:S(2)}) collective-permute-start(f32[4,4096]{1,0:T(4,128)S(1)} %kron.3), channel_id=1, source_target_pairs={{0,1},{1,0},{2,3},{3,2},{4,5},{5,4},{6,7},{7,6},{8,9},{9,8},{10,11... | collective-permute-start | bytes 196616 | tf_op jit(solution)/shard_map/ppermute | solution.py:294
  15.2 0.3 collective-permute-done.1
  15.5 2.0 %collective-permute-start.2 = (f32[4,4096]{1,0:T(4,128)S(1)}, f32[4,4096]{1,0:T(4,128)S(1)}, u32[]{:S(2)}, u32[]{:S(2)}) collective-permute-start(f32[4,4096]{1,0:T(4,128)S(1)} %add.6.here), channel_id=1, source_target_pairs={{0,2},{2,0},{1,3},{3,1},{4,6},{6,4},{5,7},{7,5},{8,10},{10,8},{9,1... | collective-permute-start | bytes 196616 | tf_op jit(solution)/shard_map/ppermute | solution.py:295
  17.5 0.0 collective-permute-done.4
  17.5 0.6 %collective-permute-start.5 = (f32[4,4096]{1,0:T(4,128)S(1)}, f32[4,4096]{1,0:T(4,128)S(1)}, u32[]{:S(2)}, u32[]{:S(2)}) collective-permute-start(f32[4,4096]{1,0:T(4,128)S(1)} %add.7.here), channel_id=1, source_target_pairs={{0,2},{2,0},{1,3},{3,1},{4,6},{6,4},{5,7},{7,5},{8,10},{10,8},{9,1... | collective-permute-start | bytes 196616 | tf_op jit(solution)/shard_map/ppermute | solution.py:295
  18.1 1.8 %collective-permute-done.2.there = f32[4,4096]{1,0:T(4,128)S(1)} collective-permute-done((f32[4,4096]{1,0:T(4,128)S(1)}, f32[4,4096]{1,0:T(4,128)S(1)}, u32[]{:S(2)}, u32[]{:S(2)}) %collective-permute-start.2) | collective-permute-done | bytes 65568 | tf_op jit(solution)/shard_map/ppermute | solution.py:295
  20.0 2.2 %collective-permute-start.6 = (f32[8,1024]{1,0:T(8,128)S(1)}, f32[8,1024]{1,0:T(8,128)S(1)}, u32[]{:S(2)}, u32[]{:S(2)}) collective-permute-start(f32[8,1024]{1,0:T(8,128)S(1)} %get-tuple-element.20), channel_id=1, source_target_pairs={{0,4},{4,8},{8,12},{12,0},{1,5},{5,9},{9,13},{13,1},{2,6},{6,10},{... | collective-permute-start | bytes 98312 | tf_op jit(solution)/shard_map/ppermute | solution.py:300
  22.2 2.6 %collective-permute-start.8 = (f32[8,1024]{1,0:T(8,128)S(1)}, f32[8,1024]{1,0:T(8,128)S(1)}, u32[]{:S(2)}, u32[]{:S(2)}) collective-permute-start(f32[8,1024]{1,0:T(8,128)S(1)} %get-tuple-element.22), channel_id=1, source_target_pairs={{0,8},{4,12},{8,0},{12,4},{1,9},{5,13},{9,1},{13,5},{2,10},{6,14},... | collective-permute-start | bytes 98312 | tf_op jit(solution)/shard_map/ppermute | solution.py:300
  24.8 1.3 %collective-permute-start.10 = (f32[8,1024]{1,0:T(8,128)S(1)}, f32[8,1024]{1,0:T(8,128)S(1)}, u32[]{:S(2)}, u32[]{:S(2)}) collective-permute-start(f32[8,1024]{1,0:T(8,128)S(1)} %get-tuple-element.24), channel_id=1, source_target_pairs={{0,12},{4,0},{8,4},{12,8},{1,13},{5,1},{9,5},{13,9},{2,14},{6,2},{... | collective-permute-start | bytes 98312 | tf_op jit(solution)/shard_map/ppermute | solution.py:300
  26.1 0.0 collective-permute-done.5.there
  26.1 0.7 %collective-permute-start.7 = (f32[8,1024]{1,0:T(8,128)S(1)}, f32[8,1024]{1,0:T(8,128)S(1)}, u32[]{:S(2)}, u32[]{:S(2)}) collective-permute-start(f32[8,1024]{1,0:T(8,128)S(1)} %get-tuple-element.21), channel_id=1, source_target_pairs={{0,4},{4,8},{8,12},{12,0},{1,5},{5,9},{9,13},{13,1},{2,6},{6,10},{... | collective-permute-start | bytes 98312 | tf_op jit(solution)/shard_map/ppermute | solution.py:300
  26.9 0.3 collective-permute-start.9
  27.2 0.0 collective-permute-done.6.refs_2_
  27.2 2.8 %collective-permute-start.11 = (f32[8,1024]{1,0:T(8,128)S(1)}, f32[8,1024]{1,0:T(8,128)S(1)}, u32[]{:S(2)}, u32[]{:S(2)}) collective-permute-start(f32[8,1024]{1,0:T(8,128)S(1)} %get-tuple-element.25), channel_id=1, source_target_pairs={{0,12},{4,0},{8,4},{12,8},{1,13},{5,1},{9,5},{13,9},{2,14},{6,2},{... | collective-permute-start | bytes 98312 | tf_op jit(solution)/shard_map/ppermute | solution.py:300
  30.0 0.0 collective-permute-done.8.refs_4_
  30.0 0.0 collective-permute-done.10.refs_6_
  30.0 2.0 %collective-permute-done.7.refs_3_ = f32[8,1024]{1,0:T(8,128)S(1)} collective-permute-done((f32[8,1024]{1,0:T(8,128)S(1)}, f32[8,1024]{1,0:T(8,128)S(1)}, u32[]{:S(2)}, u32[]{:S(2)}) %collective-permute-start.7) | collective-permute-done | bytes 32800 | tf_op jit(solution)/shard_map/ppermute | solution.py:300
  32.0 0.5 %collective-permute-done.9.refs_5_ = f32[8,1024]{1,0:T(8,128)S(1)} collective-permute-done((f32[8,1024]{1,0:T(8,128)S(1)}, f32[8,1024]{1,0:T(8,128)S(1)}, u32[]{:S(2)}, u32[]{:S(2)}) %collective-permute-start.9) | collective-permute-done | bytes 32800 | tf_op jit(solution)/shard_map/ppermute | solution.py:300
  32.5 0.0 collective-permute-done.11.refs_7_
  32.5 2.5 %fisher.1 = (f32[8,1024]{1,0:T(8,128)}, f32[1024,1024]{1,0:T(8,128)}) custom-call(f32[8,1024]{1,0:T(8,128)S(1)} %get-tuple-element.16.refs_0_, f32[8,1024]{1,0:T(8,128)S(1)} %get-tuple-element.19.refs_1_, f32[8,1024]{1,0:T(8,128)S(1)} %collective-permute-done.6.refs_2_, f32[8,1024]{1,0:T(8,128)S(1)} %collective-permute-done.7.refs_3_, ...), custom_call_target="tpu_custom_call" | custom-call | tf_op jit(solution)/shard_map/fisher/pallas_call | solution.py:247
  (4 shorter events, 0.1 us)
Async XLA Ops:
  0.6 6.0 %copy-start = (bf16[32,4096]{1,0:T(8,128)(2,1)S(1)}, bf16[32,4096]{1,0:T(8,128)(2,1)}, u32[]{:S(2)}) copy-start(bf16[32,4096]{1,0:T(8,128)(2,1)} %table.3) | copy-start | bytes 786436
  0.6 6.0 %copy-start.2 = (s32[112]{0:T(128)S(1)}, s32[112]{0:T(128)}, u32[]{:S(2)}) copy-start(s32[112]{0:T(128)} %signs.3) | copy-start | bytes 1348
  0.7 6.0 %copy-start.1 = (s32[112]{0:T(128)S(1)}, s32[112]{0:T(128)}, u32[]{:S(2)}) copy-start(s32[112]{0:T(128)} %ids.3) | copy-start | bytes 1348
  3.6 10.1 %collective-permute-start = (f32[2,128,128]{2,1,0:T(8,128)S(1)}, f32[2,128,128]{2,1,0:T(8,128)S(1)}, u32[]{:S(2)}, u32[]{:S(2)}) collective-permute-start(f32[2,128,128]{2,1,0:T(8,128)S(1)} %get-tuple-element.14.acts), channel_id=1, source_target_pairs={{0,2},{2,0},{1,3},{3,1},{4,6},{6,4},{5,7},{7,5},{8,10},{10,8},{9,1... | collective-permute-start | bytes 393224 | tf_op jit(solution)/shard_map/ppermute | solution.py:274
  6.6 7.6 %collective-permute-start.3 = (f32[2,128,128]{2,1,0:T(8,128)S(1)}, f32[2,128,128]{2,1,0:T(8,128)S(1)}, u32[]{:S(2)}, u32[]{:S(2)}) collective-permute-start(f32[2,128,128]{2,1,0:T(8,128)S(1)} %get-tuple-element.17.acts), channel_id=1, source_target_pairs={{0,2},{2,0},{1,3},{3,1},{4,6},{6,4},{5,7},{7,5},{8,10},{10,8},{9,1... | collective-permute-start | bytes 393224 | tf_op jit(solution)/shard_map/ppermute | solution.py:274
  14.1 1.3 %collective-permute-start.1 = (f32[4,4096]{1,0:T(4,128)S(1)}, f32[4,4096]{1,0:T(4,128)S(1)}, u32[]{:S(2)}, u32[]{:S(2)}) collective-permute-start(f32[4,4096]{1,0:T(4,128)S(1)} %kron.2), channel_id=1, source_target_pairs={{0,1},{1,0},{2,3},{3,2},{4,5},{5,4},{6,7},{7,6},{8,9},{9,8},{10,11... | collective-permute-start | bytes 196616 | tf_op jit(solution)/shard_map/ppermute | solution.py:294
  14.6 2.9 %collective-permute-start.4 = (f32[4,4096]{1,0:T(4,128)S(1)}, f32[4,4096]{1,0:T(4,128)S(1)}, u32[]{:S(2)}, u32[]{:S(2)}) collective-permute-start(f32[4,4096]{1,0:T(4,128)S(1)} %kron.3), channel_id=1, source_target_pairs={{0,1},{1,0},{2,3},{3,2},{4,5},{5,4},{6,7},{7,6},{8,9},{9,8},{10,11... | collective-permute-start | bytes 196616 | tf_op jit(solution)/shard_map/ppermute | solution.py:294
  15.5 4.5 %collective-permute-start.2 = (f32[4,4096]{1,0:T(4,128)S(1)}, f32[4,4096]{1,0:T(4,128)S(1)}, u32[]{:S(2)}, u32[]{:S(2)}) collective-permute-start(f32[4,4096]{1,0:T(4,128)S(1)} %add.6.here), channel_id=1, source_target_pairs={{0,2},{2,0},{1,3},{3,1},{4,6},{6,4},{5,7},{7,5},{8,10},{10,8},{9,1... | collective-permute-start | bytes 196616 | tf_op jit(solution)/shard_map/ppermute | solution.py:295
  17.5 8.6 %collective-permute-start.5 = (f32[4,4096]{1,0:T(4,128)S(1)}, f32[4,4096]{1,0:T(4,128)S(1)}, u32[]{:S(2)}, u32[]{:S(2)}) collective-permute-start(f32[4,4096]{1,0:T(4,128)S(1)} %add.7.here), channel_id=1, source_target_pairs={{0,2},{2,0},{1,3},{3,1},{4,6},{6,4},{5,7},{7,5},{8,10},{10,8},{9,1... | collective-permute-start | bytes 196616 | tf_op jit(solution)/shard_map/ppermute | solution.py:295
  20.0 7.2 %collective-permute-start.6 = (f32[8,1024]{1,0:T(8,128)S(1)}, f32[8,1024]{1,0:T(8,128)S(1)}, u32[]{:S(2)}, u32[]{:S(2)}) collective-permute-start(f32[8,1024]{1,0:T(8,128)S(1)} %get-tuple-element.20), channel_id=1, source_target_pairs={{0,4},{4,8},{8,12},{12,0},{1,5},{5,9},{9,13},{13,1},{2,6},{6,10},{... | collective-permute-start | bytes 98312 | tf_op jit(solution)/shard_map/ppermute | solution.py:300
  22.2 7.9 %collective-permute-start.8 = (f32[8,1024]{1,0:T(8,128)S(1)}, f32[8,1024]{1,0:T(8,128)S(1)}, u32[]{:S(2)}, u32[]{:S(2)}) collective-permute-start(f32[8,1024]{1,0:T(8,128)S(1)} %get-tuple-element.22), channel_id=1, source_target_pairs={{0,8},{4,12},{8,0},{12,4},{1,9},{5,13},{9,1},{13,5},{2,10},{6,14},... | collective-permute-start | bytes 98312 | tf_op jit(solution)/shard_map/ppermute | solution.py:300
  24.8 5.3 %collective-permute-start.10 = (f32[8,1024]{1,0:T(8,128)S(1)}, f32[8,1024]{1,0:T(8,128)S(1)}, u32[]{:S(2)}, u32[]{:S(2)}) collective-permute-start(f32[8,1024]{1,0:T(8,128)S(1)} %get-tuple-element.24), channel_id=1, source_target_pairs={{0,12},{4,0},{8,4},{12,8},{1,13},{5,1},{9,5},{13,9},{2,14},{6,2},{... | collective-permute-start | bytes 98312 | tf_op jit(solution)/shard_map/ppermute | solution.py:300
  26.1 5.9 %collective-permute-start.7 = (f32[8,1024]{1,0:T(8,128)S(1)}, f32[8,1024]{1,0:T(8,128)S(1)}, u32[]{:S(2)}, u32[]{:S(2)}) collective-permute-start(f32[8,1024]{1,0:T(8,128)S(1)} %get-tuple-element.21), channel_id=1, source_target_pairs={{0,4},{4,8},{8,12},{12,0},{1,5},{5,9},{9,13},{13,1},{2,6},{6,10},{... | collective-permute-start | bytes 98312 | tf_op jit(solution)/shard_map/ppermute | solution.py:300
  26.9 5.6 %collective-permute-start.9 = (f32[8,1024]{1,0:T(8,128)S(1)}, f32[8,1024]{1,0:T(8,128)S(1)}, u32[]{:S(2)}, u32[]{:S(2)}) collective-permute-start(f32[8,1024]{1,0:T(8,128)S(1)} %get-tuple-element.23), channel_id=1, source_target_pairs={{0,8},{4,12},{8,0},{12,4},{1,9},{5,13},{9,1},{13,5},{2,10},{6,14},... | collective-permute-start | bytes 98312 | tf_op jit(solution)/shard_map/ppermute | solution.py:300
  27.2 5.3 %collective-permute-start.11 = (f32[8,1024]{1,0:T(8,128)S(1)}, f32[8,1024]{1,0:T(8,128)S(1)}, u32[]{:S(2)}, u32[]{:S(2)}) collective-permute-start(f32[8,1024]{1,0:T(8,128)S(1)} %get-tuple-element.25), channel_id=1, source_target_pairs={{0,12},{4,0},{8,4},{12,8},{1,13},{5,1},{9,5},{13,9},{2,14},{6,2},{... | collective-permute-start | bytes 98312 | tf_op jit(solution)/shard_map/ppermute | solution.py:300

commit v5 on v4

--- a/solution.py
+++ b/solution.py
@@ -11,10 +11,6 @@
 BLOCK = 64
 LANES = 128
 VMEM_BYTES = 48 * 1024 * 1024
-PLANE = ("tensor", "seq")
-
-
-HALVES = 2
 
 
 def chunks_of(width, most):
@@ -57,7 +53,7 @@
 
 
 def project_kernel(widths, fetch, ids, signs, table, rows_ref, *refs):
-    outs, (spread, signed, matrix, held, total, sems, *own) = refs[:HALVES], refs[HALVES:]
+    out, spread, signed, matrix, held, total, sems, *own = refs
     copies, starts, start = [], [], 0
     for c, width in enumerate(widths):
         columns = pl.ds(start, width)
@@ -97,12 +93,10 @@
             total[...] = part
         else:
             total[...] += part
-    pairs, _, tokens = outs[0].shape
-    for h, out in enumerate(outs):
-        for pair in range(pairs):
-            for side in range(2):
-                example = 2 * (h * pairs + pair) + side
-                out[pair, pl.ds(side * PROJ, PROJ), :] = total[:, pl.ds(example * tokens, tokens)]
+    pairs, _, tokens = out.shape
+    for pair in range(pairs):
+        for side in range(2):
+            out[pair, pl.ds(side * PROJ, PROJ), :] = total[:, pl.ds((2 * pair + side) * tokens, tokens)]
 
 
 def project(values, ids, signs, table, fetch, most, name):
@@ -123,9 +117,9 @@
         operands = [pltpu.with_memory_space_constraint(each, pltpu.HBM) for each in operands]
     return pl.pallas_call(
         functools.partial(project_kernel, widths, fetch),
-        out_shape=[jax.ShapeDtypeStruct((count // 2 // HALVES, LANES, tokens), jnp.float32)] * HALVES,
+        out_shape=jax.ShapeDtypeStruct((count // 2, LANES, tokens), jnp.float32),
         in_specs=[hbm] * 4 if fetch else [smem, smem, vmem, hbm],
-        out_specs=[vmem] * HALVES,
+        out_specs=vmem,
         scratch_shapes=[
             pltpu.VMEM((entries * (BLOCK + 8), LANES), jnp.float32),
             pltpu.VMEM((2 * entries * BLOCK, LANES), jnp.bfloat16),
@@ -143,8 +137,9 @@
     )(*operands)
 
 
-def kron_kernel(acts, grads, *refs):
-    summands, out, products = refs[:-2], refs[-2], refs[-1]
+def kron_kernel(cuts, acts, grads, *refs):
+    parts = cuts[1]
+    summands, outs, rows, products = refs[: -parts - 2], refs[-parts - 2 : -2], refs[-2], refs[-1]
     pairs = acts.shape[0]
     for pair in range(pairs):
         act = acts[pair]
@@ -161,66 +156,98 @@
     lower = lax.broadcasted_iota(jnp.int32, (count, LANES), 1) < PROJ
     even = lax.broadcasted_iota(jnp.int32, (count, LANES), 0) % 2 == 0
     here = even == lower
-    for tile in range(out.shape[1] // LANES):
+    tiles = rows.shape[2] // LANES // cuts[0]
+    for tile in range(PROJ * PROJ // LANES):
         both = []
         for p in (2 * tile, 2 * tile + 1):
             v = products[pl.ds(p, count, stride=PROJ), :]
             both.append(jnp.where(here, v, pltpu.roll(v, PROJ, 1)))
-        out[:, pl.ds(tile * LANES, LANES)] = jnp.where(lower, both[0], both[1])
-
-
-def kron_of(act_parts, grads):
+        block, part, within = tile // tiles // parts, tile // tiles % parts, tile % tiles
+        rows[part, :, pl.ds((block * tiles + within) * LANES, LANES)] = jnp.where(lower, both[0], both[1])
+    for k, out in enumerate(outs):
+        part = lax.rem(lax.axis_index("seq") + k, parts) if parts > 1 else 0
+        out[...] = rows[part]
+
+
+def kron_of(act_parts, grads, cuts):
     pairs = grads.shape[0]
+    parts = cuts[1]
+    width = PROJ * PROJ // parts
     vmem = pl.BlockSpec(memory_space=pltpu.VMEM)
     return pl.pallas_call(
-        kron_kernel,
-        out_shape=jax.ShapeDtypeStruct((2 * pairs, PROJ * PROJ), jnp.float32),
+        functools.partial(kron_kernel, cuts),
+        out_shape=[jax.ShapeDtypeStruct((2 * pairs, width), jnp.float32)] * parts,
         in_specs=[vmem] * (1 + len(act_parts)),
-        out_specs=vmem,
-        scratch_shapes=[pltpu.VMEM((pairs * LANES, LANES), jnp.float32)],
+        out_specs=[vmem] * parts,
+        scratch_shapes=[
+            pltpu.VMEM((parts, 2 * pairs, width), jnp.float32),
+            pltpu.VMEM((pairs * LANES, LANES), jnp.float32),
+        ],
         compiler_params=pltpu.CompilerParams(vmem_limit_bytes=VMEM_BYTES),
         name="kron",
     )(act_parts[0], grads, *act_parts[1:])
 
 
-def place_in_plane():
-    return lax.axis_index("tensor") * lax.axis_size("seq") + lax.axis_index("seq")
-
-
-def pieces_kernel(here, there, *parcels):
+def parcels_kernel(here, there, *parcels):
     count = here.shape[0]
     dp = len(parcels)
     width = parcels[0].shape[1]
-    start = pl.multiple_of(place_in_plane() * width, LANES)
-    row = here[:, pl.ds(start, width)] + there[:, pl.ds(start, width)]
+    core, chip = lax.axis_index("seq"), lax.axis_index("tensor") * 2
+    blocks = [chip + core, chip + 1 - core]
     for k, parcel in enumerate(parcels):
-        parcel[pl.ds(0, count), :] = row
-        other = lax.rem(lax.axis_index("dp") + k, dp)
-        start = pl.multiple_of(other * width, LANES)
-        parcel[pl.ds(count, count), :] = here[:, pl.ds(start, width)] + there[:, pl.ds(start, width)]
-
-
-def pieces_of(here, there, dp):
+        for step, block in enumerate(blocks + [lax.rem(lax.axis_index("dp") + k, dp)]):
+            lanes = pl.ds(pl.multiple_of(block * width, LANES), width)
+            parcel[pl.ds(step * count, count), :] = here[:, lanes] + there[:, lanes]
+
+
+def parcels_of(here, there, dp):
     count, width = here.shape
     vmem = pl.BlockSpec(memory_space=pltpu.VMEM)
     return pl.pallas_call(
-        pieces_kernel,
-        out_shape=[jax.ShapeDtypeStruct((2 * count, width // dp), jnp.float32)] * dp,
+        parcels_kernel,
+        out_shape=[jax.ShapeDtypeStruct((3 * count, width // dp), jnp.float32)] * dp,
         in_specs=[vmem] * 2,
         out_specs=[vmem] * dp,
         compiler_params=pltpu.CompilerParams(vmem_limit_bytes=VMEM_BYTES),
-        name="pieces",
+        name="parcels",
     )(here, there)
 
 
-def fisher_kernel(scale, *refs):
+def bundle_kernel(*refs):
+    parcels, out = refs[:-1], refs[-1]
+    rows = 2 * parcels[0].shape[0] // 3
+    for k, parcel in enumerate(parcels):
+        out[pl.ds(k * rows, rows), :] = parcel[pl.ds(rows // 2, rows), :]
+
+
+def bundle_of(parcels):
+    rows, width = parcels[0].shape
+    vmem = pl.BlockSpec(memory_space=pltpu.VMEM)
+    return pl.pallas_call(
+        bundle_kernel,
+        out_shape=jax.ShapeDtypeStruct((2 * rows // 3 * len(parcels), width), jnp.float32),
+        in_specs=[vmem] * len(parcels),
+        out_specs=vmem,
+        compiler_params=pltpu.CompilerParams(vmem_limit_bytes=VMEM_BYTES),
+        name="bundle",
+    )(*parcels)
+
+
+def fisher_kernel(scale, bundle, *refs):
     parcels, (mine, out, made, kept, left, right, sems) = refs[:-7], refs[-7:]
-    rows = parcels[0].shape[0] // 2
+    rows = parcels[0].shape[0] // 3
+    part = parcels[0].shape[1]
+    core = lax.axis_index("seq")
+    own = pl.ds(pl.multiple_of(core * part, LANES), part)
+    others = pl.ds(pl.multiple_of((1 - core) * part, LANES), part)
     for k, parcel in enumerate(parcels):
-        left[pl.ds(k * rows, rows), :] = parcel[pl.ds(0, rows), :]
-        right[pl.ds(k * rows, rows), :] = parcel[pl.ds(rows, rows), :]
+        into = pl.ds(k * rows, rows)
+        left[into, own] = parcel[pl.ds(0, rows), :]
+        left[into, others] = bundle[pl.ds(2 * k * rows, rows), :]
+        right[into, own] = parcel[pl.ds(2 * rows, rows), :]
+        right[into, others] = bundle[pl.ds((2 * k + 1) * rows, rows), :]
     blocks, _, width = made.shape
-    kept[...] = left[pl.ds(0, kept.shape[0]), :]
+    kept[...] = left[pl.ds(0, rows), :]
     copies = [pltpu.make_async_copy(kept, mine, sems.at[blocks])]
     copies[0].start()
     l1, l2, l3 = split3(left[...])
@@ -238,49 +265,51 @@
         copy.wait()
 
 
-def fisher_block(parcels):
-    rows, width = parcels[0].shape
-    rows //= 2
+def fisher_block(parcels, bundle):
+    rows, part = parcels[0].shape
+    rows //= 3
+    width = 2 * part
     total = rows * len(parcels)
     blocks = 4
     hbm = pl.BlockSpec(memory_space=pltpu.HBM)
     return pl.pallas_call(
         functools.partial(fisher_kernel, 1.0 / total),
         out_shape=[
-            jax.ShapeDtypeStruct((rows * HALVES, width), jnp.float32),
+            jax.ShapeDtypeStruct((rows, width), jnp.float32),
             jax.ShapeDtypeStruct((width, width), jnp.float32),
         ],
-        in_specs=[pl.BlockSpec(memory_space=pltpu.VMEM)] * len(parcels),
+        in_specs=[pl.BlockSpec(memory_space=pltpu.VMEM)] * (1 + len(parcels)),
         out_specs=[hbm] * 2,
         scratch_shapes=[
             pltpu.VMEM((blocks, width, width // blocks), jnp.float32),
-            pltpu.VMEM((rows * HALVES, width), jnp.float32),
+            pltpu.VMEM((rows, width), jnp.float32),
             pltpu.VMEM((total, width), jnp.float32),
             pltpu.VMEM((total, width), jnp.float32),
             pltpu.SemaphoreType.DMA((blocks + 1,)),
         ],
         compiler_params=pltpu.CompilerParams(vmem_limit_bytes=VMEM_BYTES),
         name="fisher",
-    )(*parcels)
+    )(bundle, *parcels)
 
 
 def local(acts, grads, in_ids, in_signs, out_ids, out_signs, in_table, out_table):
     tensor, seq, dp = (lax.axis_size(name) for name in ("tensor", "seq", "dp"))
     shards = tensor * seq
+    small = tensor == 2 and seq == 2 and dp == 4
     swap = [(0, 1), (1, 0)]
 
-    act_halves = project(acts, in_ids, in_signs, in_table, True, 512, "project_acts")
+    act = project(acts, in_ids, in_signs, in_table, True, 512, "project_acts")
     if tensor == 2:
-        act_halves = [[act, lax.ppermute(act, "tensor", swap)] for act in act_halves]
+        act_parts = [act, lax.ppermute(act, "tensor", swap)]
     else:
-        act_halves = [[lax.psum(act, "tensor")] for act in act_halves]
-    grad_halves = project(grads, out_ids, out_signs, out_table, False, 1024, "project_grads")
-    krons = [kron_of(parts, grad) for parts, grad in zip(act_halves, grad_halves)]
-
-    if tensor != 2 or seq != 2 or shards != dp:
-        kron = lax.psum(jnp.concatenate(krons, axis=0), PLANE)
+        act_parts = [lax.psum(act, "tensor")]
+    grad = project(grads, out_ids, out_signs, out_table, False, 1024, "project_grads")
+    krons = kron_of(act_parts, grad, (shards, seq) if small else (1, 1))
+
+    if not small:
+        kron = lax.psum(krons[0], ("tensor", "seq"))
         width = kron.shape[1] // shards
-        place = place_in_plane()
+        place = lax.axis_index("tensor") * seq + lax.axis_index("seq")
         mine = lax.dynamic_slice_in_dim(kron, place * width, width, 1)
         every = lax.all_gather(kron, "dp", axis=0, tiled=True)
         left = lax.dynamic_slice_in_dim(every, place * width, width, 1)
@@ -291,14 +320,11 @@
         ) / left.shape[0]
         return mine, fisher
 
-    krons = [kron + lax.ppermute(kron, "seq", swap) for kron in krons]
-    there = [lax.ppermute(kron, "tensor", swap) for kron in krons]
-    halves = [pieces_of(kron, other, dp) for kron, other in zip(krons, there)]
-    parcels = [parcel[0] for parcel in halves]
+    part = krons[0] + lax.ppermute(krons[1], "seq", swap)
+    parcels = list(parcels_of(part, lax.ppermute(part, "tensor", swap), dp))
     for k in range(1, dp):
-        for parcel in halves:
-            parcels.append(lax.ppermute(parcel[k], "dp", [(d, (d + k) % dp) for d in range(dp)]))
-    mine, fisher = fisher_block(parcels)
+        parcels[k] = lax.ppermute(parcels[k], "dp", [(d, (d + k) % dp) for d in range(dp)])
+    mine, fisher = fisher_block(parcels, lax.ppermute(bundle_of(parcels), "seq", swap))
     return mine, fisher
 
 

time: 35.2 us -> 32.3 us (0.918)
  starting transfers between devices: 16.4 us -> 9.77 us
  waiting for transfers between devices: 4.59 us -> 8.58 us
    ppermute x12 -> x7, starting transfers between devices: 16.4 us -> 9.77 us  [the longest x3 5.57 us: local(): lax.ppermute(parcels[k], 'dp', [(d, (d + k) % dp) for d in range(dp)])]
    ppermute x12 -> x7, waiting for transfers between devices: 4.59 us -> 8.58 us  [the longest x1 3.27 us: local(): parcels = list(parcels_of(part, lax.ppermute(part, 'tensor', swap), dp))]
    pallas_call x4 -> x3, Pallas kernels: 0.85 us -> 0.61 us  [the longest x1 0.58 us: kron_of(): pl.pallas_call(functools.partial(kron_kernel, cuts), out_shape=[jax.Shape...]
  transfers between devices with their start and end apart: 12 -> 7, of which waited for: 4 -> 6; matrix products, arithmetic and copies ran while one was open for 0% -> 0% of each run, Pallas kernels for 22% -> 22%
where the time goes in v5:
time: 32.3 us; the launch traced here: 32.2 us
  Pallas kernels  13.1 us (41%)
  starting transfers between devices  9.77 us (30%)
  waiting for transfers between devices  8.58 us (27%)
  between operations  0.71 us (2%)
    pallas_call x2, Pallas kernels, project(): pl.pallas_call(functools.partial(project_kernel, widths, fetch), out_shap...  9.93 us
    ppermute x3, starting transfers between devices, local(): lax.ppermute(parcels[k], 'dp', [(d, (d + k) % dp) for d in range(dp)])  5.57 us
    ppermute x1, waiting for transfers between devices, local(): parcels = list(parcels_of(part, lax.ppermute(part, 'tensor', swap), dp))  3.27 us
    ppermute x1, starting transfers between devices, local(): act_parts = [act, lax.ppermute(act, 'tensor', swap)]  3 us
    ppermute x3, waiting for transfers between devices, local(): lax.ppermute(parcels[k], 'dp', [(d, (d + k) % dp) for d in range(dp)])  2.73 us
    pallas_call x1, Pallas kernels, fisher_block(): pl.pallas_call(functools.partial(fisher_kernel, 1.0 / total), out_shape=[...  2.55 us
    ppermute x1, waiting for transfers between devices, local(): lax.ppermute(bundle_of(parcels), 'seq', swap)  1.33 us
    ppermute x1, waiting for transfers between devices, local(): part = krons[0] + lax.ppermute(krons[1], 'seq', swap)  1.24 us
  transfers between devices with their start and end apart: 7, of which 6 were waited for; matrix products, arithmetic and copies ran while one was open for 0% of the time, Pallas kernels for 22%

profile of v5, /device:TPU:0, one launch (start us, length us, event | category | flops | bytes accessed | tf_op | source)
XLA Modules:
  0.0 32.2 jit_solution(11189451709202374845)
XLA Ops:
  0.6 0.0 copy-start
  0.6 0.0 copy-start.2
  0.7 0.0 copy-start.1
  0.7 2.9 %project_acts.1.acts = f32[4,128,128]{2,1,0:T(8,128)S(1)} custom-call(s32[32]{0:T(128)} %ids.2, s32[32]{0:T(128)} %signs.2, bf16[32,4096]{1,0:T(8,128)(2,1)} %table.2, bf16[1024,2048]{1,0:T(8,128)(2,1)} %bitcast.3), custom_call_target="tpu_custom_call" | custom-call | flops 536870912 | bytes 4194304 | tf_op jit(solution)/shard_map/project_acts/pallas_call | solution.py:118
  3.6 3.0 %collective-permute-start = (f32[4,128,128]{2,1,0:T(8,128)S(1)}, f32[4,128,128]{2,1,0:T(8,128)S(1)}, u32[]{:S(2)}, u32[]{:S(2)}) collective-permute-start(f32[4,128,128]{2,1,0:T(8,128)S(1)} %project_acts.1.acts), channel_id=1, source_target_pairs={{0,2},{2,0},{1,3},{3,1},{4,6},{6,4},{5,7},{7,5},{8,10},{10,8},{9,1... | collective-permute-start | bytes 786440 | tf_op jit(solution)/shard_map/ppermute | solution.py:303
  6.6 0.0 copy-done
  6.6 0.0 copy-done.2
  6.6 0.0 copy-done.1
  6.6 7.0 %project_grads.1.grads = f32[4,128,128]{2,1,0:T(8,128)S(1)} custom-call(s32[112]{0:T(128)S(1)} %copy-done.1, s32[112]{0:T(128)S(1)} %copy-done.2, bf16[32,4096]{1,0:T(8,128)(2,1)S(1)} %copy-done, bf16[1024,7168]{1,0:T(8,128)(2,1)} %bitcast.2), custom_call_target="tpu_custom_call" | custom-call | flops 1879048192 | bytes 14680064 | tf_op jit(solution)/shard_map/project_grads/pallas_call | solution.py:118
  13.6 0.0 collective-permute-done.refs_0_
  13.6 0.6 %kron.1 = (f32[8,2048]{1,0:T(8,128)S(1)}, f32[8,2048]{1,0:T(8,128)S(1)}) custom-call(f32[4,128,128]{2,1,0:T(8,128)S(1)} %project_acts.1.acts, f32[4,128,128]{2,1,0:T(8,128)S(1)} %project_grads.1.grads, f32[4,128,128]{2,1,0:T(8,128)S(1)} %collective-permute-done.refs_0_), custom_call_target="tpu_custom_call" | custom-call | tf_op jit(solution)/shard_map/kron/pallas_call | solution.py:177
  14.2 0.1 collective-permute-start.1
  14.3 1.2 %collective-permute-done.1 = f32[8,2048]{1,0:T(8,128)S(1)} collective-permute-done((f32[8,2048]{1,0:T(8,128)S(1)}, f32[8,2048]{1,0:T(8,128)S(1)}, u32[]{:S(2)}, u32[]{:S(2)}) %collective-permute-start.1) | collective-permute-done | bytes 65568 | tf_op jit(solution)/shard_map/ppermute | solution.py:323
  15.5 1.1 %collective-permute-start.2 = (f32[8,2048]{1,0:T(8,128)S(1)}, f32[8,2048]{1,0:T(8,128)S(1)}, u32[]{:S(2)}, u32[]{:S(2)}) collective-permute-start(f32[8,2048]{1,0:T(8,128)S(1)} %add.3.here), channel_id=1, source_target_pairs={{0,2},{2,0},{1,3},{3,1},{4,6},{6,4},{5,7},{7,5},{8,10},{10,8},{9,1... | collective-permute-start | bytes 196616 | tf_op jit(solution)/shard_map/ppermute | solution.py:324
  16.6 3.3 %collective-permute-done.2.there = f32[8,2048]{1,0:T(8,128)S(1)} collective-permute-done((f32[8,2048]{1,0:T(8,128)S(1)}, f32[8,2048]{1,0:T(8,128)S(1)}, u32[]{:S(2)}, u32[]{:S(2)}) %collective-permute-start.2) | collective-permute-done | bytes 65568 | tf_op jit(solution)/shard_map/ppermute | solution.py:324
  19.9 1.6 %collective-permute-start.3 = (f32[24,512]{1,0:T(8,128)S(1)}, f32[24,512]{1,0:T(8,128)S(1)}, u32[]{:S(2)}, u32[]{:S(2)}) collective-permute-start(f32[24,512]{1,0:T(8,128)S(1)} %get-tuple-element.11), channel_id=1, source_target_pairs={{0,4},{4,8},{8,12},{12,0},{1,5},{5,9},{9,13},{13,1},{2,6},{6,10},{... | collective-permute-start | bytes 147464 | tf_op jit(solution)/shard_map/ppermute | solution.py:326
  21.5 2.6 %collective-permute-start.4 = (f32[24,512]{1,0:T(8,128)S(1)}, f32[24,512]{1,0:T(8,128)S(1)}, u32[]{:S(2)}, u32[]{:S(2)}) collective-permute-start(f32[24,512]{1,0:T(8,128)S(1)} %get-tuple-element.12), channel_id=1, source_target_pairs={{0,8},{4,12},{8,0},{12,4},{1,9},{5,13},{9,1},{13,5},{2,10},{6,14},... | collective-permute-start | bytes 147464 | tf_op jit(solution)/shard_map/ppermute | solution.py:326
  24.1 1.4 %collective-permute-start.5 = (f32[24,512]{1,0:T(8,128)S(1)}, f32[24,512]{1,0:T(8,128)S(1)}, u32[]{:S(2)}, u32[]{:S(2)}) collective-permute-start(f32[24,512]{1,0:T(8,128)S(1)} %get-tuple-element.13), channel_id=1, source_target_pairs={{0,12},{4,0},{8,4},{12,8},{1,13},{5,1},{9,5},{13,9},{2,14},{6,2},{... | collective-permute-start | bytes 147464 | tf_op jit(solution)/shard_map/ppermute | solution.py:326
  25.5 0.8 %collective-permute-done.3.refs_1_ = f32[24,512]{1,0:T(8,128)S(1)} collective-permute-done((f32[24,512]{1,0:T(8,128)S(1)}, f32[24,512]{1,0:T(8,128)S(1)}, u32[]{:S(2)}, u32[]{:S(2)}) %collective-permute-start.3) | collective-permute-done | bytes 49184 | tf_op jit(solution)/shard_map/ppermute | solution.py:326
  26.3 0.6 %collective-permute-done.4.refs_2_ = f32[24,512]{1,0:T(8,128)S(1)} collective-permute-done((f32[24,512]{1,0:T(8,128)S(1)}, f32[24,512]{1,0:T(8,128)S(1)}, u32[]{:S(2)}, u32[]{:S(2)}) %collective-permute-start.4) | collective-permute-done | bytes 49184 | tf_op jit(solution)/shard_map/ppermute | solution.py:326
  26.9 1.3 %collective-permute-done.5.refs_3_ = f32[24,512]{1,0:T(8,128)S(1)} collective-permute-done((f32[24,512]{1,0:T(8,128)S(1)}, f32[24,512]{1,0:T(8,128)S(1)}, u32[]{:S(2)}, u32[]{:S(2)}) %collective-permute-start.5) | collective-permute-done | bytes 49184 | tf_op jit(solution)/shard_map/ppermute | solution.py:326
  28.2 0.1 collective-permute-start.6
  28.3 1.3 %collective-permute-done.6.bundle = f32[64,512]{1,0:T(8,128)S(1)} collective-permute-done((f32[64,512]{1,0:T(8,128)S(1)}, f32[64,512]{1,0:T(8,128)S(1)}, u32[]{:S(2)}, u32[]{:S(2)}) %collective-permute-start.6) | collective-permute-done | bytes 131104 | tf_op jit(solution)/shard_map/ppermute | solution.py:327
  29.6 2.5 %fisher.1 = (f32[8,1024]{1,0:T(8,128)}, f32[1024,1024]{1,0:T(8,128)}) custom-call(f32[64,512]{1,0:T(8,128)S(1)} %collective-permute-done.6.bundle, f32[24,512]{1,0:T(8,128)S(1)} %get-tuple-element.10.refs_0_, f32[24,512]{1,0:T(8,128)S(1)} %collective-permute-done.3.refs_1_, f32[24,512]{1,0:T(8,128)S(1)} %collective-permute-done.4.refs_2_, ...), custom_call_target="tpu_custom_call" | custom-call | tf_op jit(solution)/shard_map/fisher/pallas_call | solution.py:275
  (3 shorter events, 0.0 us)
Async XLA Ops:
  0.6 6.0 %copy-start = (bf16[32,4096]{1,0:T(8,128)(2,1)S(1)}, bf16[32,4096]{1,0:T(8,128)(2,1)}, u32[]{:S(2)}) copy-start(bf16[32,4096]{1,0:T(8,128)(2,1)} %table.3) | copy-start | bytes 786436
  0.6 5.9 %copy-start.2 = (s32[112]{0:T(128)S(1)}, s32[112]{0:T(128)}, u32[]{:S(2)}) copy-start(s32[112]{0:T(128)} %signs.3) | copy-start | bytes 1348
  0.7 5.9 %copy-start.1 = (s32[112]{0:T(128)S(1)}, s32[112]{0:T(128)}, u32[]{:S(2)}) copy-start(s32[112]{0:T(128)} %ids.3) | copy-start | bytes 1348
  3.6 10.0 %collective-permute-start = (f32[4,128,128]{2,1,0:T(8,128)S(1)}, f32[4,128,128]{2,1,0:T(8,128)S(1)}, u32[]{:S(2)}, u32[]{:S(2)}) collective-permute-start(f32[4,128,128]{2,1,0:T(8,128)S(1)} %project_acts.1.acts), channel_id=1, source_target_pairs={{0,2},{2,0},{1,3},{3,1},{4,6},{6,4},{5,7},{7,5},{8,10},{10,8},{9,1... | collective-permute-start | bytes 786440 | tf_op jit(solution)/shard_map/ppermute | solution.py:303
  14.2 1.3 %collective-permute-start.1 = (f32[8,2048]{1,0:T(8,128)S(1)}, f32[8,2048]{1,0:T(8,128)S(1)}, u32[]{:S(2)}, u32[]{:S(2)}) collective-permute-start(f32[8,2048]{1,0:T(8,128)S(1)} %get-tuple-element.9), channel_id=1, source_target_pairs={{0,1},{1,0},{2,3},{3,2},{4,5},{5,4},{6,7},{7,6},{8,9},{9,8},{10,11... | collective-permute-start | bytes 196616 | tf_op jit(solution)/shard_map/ppermute | solution.py:323
  15.5 4.3 %collective-permute-start.2 = (f32[8,2048]{1,0:T(8,128)S(1)}, f32[8,2048]{1,0:T(8,128)S(1)}, u32[]{:S(2)}, u32[]{:S(2)}) collective-permute-start(f32[8,2048]{1,0:T(8,128)S(1)} %add.3.here), channel_id=1, source_target_pairs={{0,2},{2,0},{1,3},{3,1},{4,6},{6,4},{5,7},{7,5},{8,10},{10,8},{9,1... | collective-permute-start | bytes 196616 | tf_op jit(solution)/shard_map/ppermute | solution.py:324
  19.9 6.4 %collective-permute-start.3 = (f32[24,512]{1,0:T(8,128)S(1)}, f32[24,512]{1,0:T(8,128)S(1)}, u32[]{:S(2)}, u32[]{:S(2)}) collective-permute-start(f32[24,512]{1,0:T(8,128)S(1)} %get-tuple-element.11), channel_id=1, source_target_pairs={{0,4},{4,8},{8,12},{12,0},{1,5},{5,9},{9,13},{13,1},{2,6},{6,10},{... | collective-permute-start | bytes 147464 | tf_op jit(solution)/shard_map/ppermute | solution.py:326
  21.5 5.3 %collective-permute-start.4 = (f32[24,512]{1,0:T(8,128)S(1)}, f32[24,512]{1,0:T(8,128)S(1)}, u32[]{:S(2)}, u32[]{:S(2)}) collective-permute-start(f32[24,512]{1,0:T(8,128)S(1)} %get-tuple-element.12), channel_id=1, source_target_pairs={{0,8},{4,12},{8,0},{12,4},{1,9},{5,13},{9,1},{13,5},{2,10},{6,14},... | collective-permute-start | bytes 147464 | tf_op jit(solution)/shard_map/ppermute | solution.py:326
  24.1 4.1 %collective-permute-start.5 = (f32[24,512]{1,0:T(8,128)S(1)}, f32[24,512]{1,0:T(8,128)S(1)}, u32[]{:S(2)}, u32[]{:S(2)}) collective-permute-start(f32[24,512]{1,0:T(8,128)S(1)} %get-tuple-element.13), channel_id=1, source_target_pairs={{0,12},{4,0},{8,4},{12,8},{1,13},{5,1},{9,5},{13,9},{2,14},{6,2},{... | collective-permute-start | bytes 147464 | tf_op jit(solution)/shard_map/ppermute | solution.py:326
  28.2 1.4 %collective-permute-start.6 = (f32[64,512]{1,0:T(8,128)S(1)}, f32[64,512]{1,0:T(8,128)S(1)}, u32[]{:S(2)}, u32[]{:S(2)}) collective-permute-start(f32[64,512]{1,0:T(8,128)S(1)} %bundle.1), channel_id=1, source_target_pairs={{0,1},{1,0},{2,3},{3,2},{4,5},{5,4},{6,7},{7,6},{8,9},{9,8},{10,11... | collective-permute-start | bytes 393224 | tf_op jit(solution)/shard_map/ppermute | solution.py:327

commit v6 on v5

--- a/solution.py
+++ b/solution.py
@@ -188,16 +188,14 @@
     )(act_parts[0], grads, *act_parts[1:])
 
 
-def parcels_kernel(here, there, *parcels):
+def parcels_kernel(here, there, out):
     count = here.shape[0]
-    dp = len(parcels)
-    width = parcels[0].shape[1]
+    width = out.shape[1]
     core, chip = lax.axis_index("seq"), lax.axis_index("tensor") * 2
-    blocks = [chip + core, chip + 1 - core]
-    for k, parcel in enumerate(parcels):
-        for step, block in enumerate(blocks + [lax.rem(lax.axis_index("dp") + k, dp)]):
+    for d in range(out.shape[0] // (3 * count)):
+        for step, block in enumerate((chip + core, chip + 1 - core, d)):
             lanes = pl.ds(pl.multiple_of(block * width, LANES), width)
-            parcel[pl.ds(step * count, count), :] = here[:, lanes] + there[:, lanes]
+            out[pl.ds((3 * d + step) * count, count), :] = here[:, lanes] + there[:, lanes]
 
 
 def parcels_of(here, there, dp):
@@ -205,49 +203,44 @@
     vmem = pl.BlockSpec(memory_space=pltpu.VMEM)
     return pl.pallas_call(
         parcels_kernel,
-        out_shape=[jax.ShapeDtypeStruct((3 * count, width // dp), jnp.float32)] * dp,
+        out_shape=jax.ShapeDtypeStruct((3 * count * dp, width // dp), jnp.float32),
         in_specs=[vmem] * 2,
-        out_specs=[vmem] * dp,
+        out_specs=vmem,
         compiler_params=pltpu.CompilerParams(vmem_limit_bytes=VMEM_BYTES),
         name="parcels",
     )(here, there)
 
 
-def bundle_kernel(*refs):
-    parcels, out = refs[:-1], refs[-1]
-    rows = 2 * parcels[0].shape[0] // 3
-    for k, parcel in enumerate(parcels):
-        out[pl.ds(k * rows, rows), :] = parcel[pl.ds(rows // 2, rows), :]
-
-
-def bundle_of(parcels):
-    rows, width = parcels[0].shape
+def bundle_kernel(rows, parcels, out):
+    for d in range(parcels.shape[0] // (3 * rows)):
+        out[pl.ds(2 * d * rows, 2 * rows), :] = parcels[pl.ds((3 * d + 1) * rows, 2 * rows), :]
+
+
+def bundle_of(parcels, rows):
     vmem = pl.BlockSpec(memory_space=pltpu.VMEM)
     return pl.pallas_call(
-        bundle_kernel,
-        out_shape=jax.ShapeDtypeStruct((2 * rows // 3 * len(parcels), width), jnp.float32),
-        in_specs=[vmem] * len(parcels),
+        functools.partial(bundle_kernel, rows),
+        out_shape=jax.ShapeDtypeStruct((2 * parcels.shape[0] // 3, parcels.shape[1]), jnp.float32),
+        in_specs=[vmem],
         out_specs=vmem,
         compiler_params=pltpu.CompilerParams(vmem_limit_bytes=VMEM_BYTES),
         name="bundle",
-    )(*parcels)
-
-
-def fisher_kernel(scale, bundle, *refs):
-    parcels, (mine, out, made, kept, left, right, sems) = refs[:-7], refs[-7:]
-    rows = parcels[0].shape[0] // 3
-    part = parcels[0].shape[1]
+    )(parcels)
+
+
+def fisher_kernel(scale, bundle, parcels, mine, out, made, kept, left, right, sems):
+    rows, part = kept.shape[0], parcels.shape[1]
     core = lax.axis_index("seq")
     own = pl.ds(pl.multiple_of(core * part, LANES), part)
     others = pl.ds(pl.multiple_of((1 - core) * part, LANES), part)
-    for k, parcel in enumerate(parcels):
-        into = pl.ds(k * rows, rows)
-        left[into, own] = parcel[pl.ds(0, rows), :]
-        left[into, others] = bundle[pl.ds(2 * k * rows, rows), :]
-        right[into, own] = parcel[pl.ds(2 * rows, rows), :]
-        right[into, others] = bundle[pl.ds((2 * k + 1) * rows, rows), :]
+    for d in range(left.shape[0] // rows):
+        into = pl.ds(d * rows, rows)
+        left[into, own] = parcels[pl.ds(3 * d * rows, rows), :]
+        left[into, others] = bundle[pl.ds(2 * d * rows, rows), :]
+        right[into, own] = parcels[pl.ds((3 * d + 2) * rows, rows), :]
+        right[into, others] = bundle[pl.ds((2 * d + 1) * rows, rows), :]
     blocks, _, width = made.shape
-    kept[...] = left[pl.ds(0, rows), :]
+    kept[...] = left[pl.ds(pl.multiple_of(lax.axis_index("dp") * rows, rows), rows), :]
     copies = [pltpu.make_async_copy(kept, mine, sems.at[blocks])]
     copies[0].start()
     l1, l2, l3 = split3(left[...])
@@ -265,11 +258,9 @@
         copy.wait()
 
 
-def fisher_block(parcels, bundle):
-    rows, part = parcels[0].shape
-    rows //= 3
-    width = 2 * part
-    total = rows * len(parcels)
+def fisher_block(parcels, bundle, rows):
+    total = parcels.shape[0] // 3
+    width = 2 * parcels.shape[1]
     blocks = 4
     hbm = pl.BlockSpec(memory_space=pltpu.HBM)
     return pl.pallas_call(
@@ -278,7 +269,7 @@
             jax.ShapeDtypeStruct((rows, width), jnp.float32),
             jax.ShapeDtypeStruct((width, width), jnp.float32),
         ],
-        in_specs=[pl.BlockSpec(memory_space=pltpu.VMEM)] * (1 + len(parcels)),
+        in_specs=[pl.BlockSpec(memory_space=pltpu.VMEM)] * 2,
         out_specs=[hbm] * 2,
         scratch_shapes=[
             pltpu.VMEM((blocks, width, width // blocks), jnp.float32),
@@ -289,7 +280,7 @@
         ],
         compiler_params=pltpu.CompilerParams(vmem_limit_bytes=VMEM_BYTES),
         name="fisher",
-    )(bundle, *parcels)
+    )(bundle, parcels)
 
 
 def local(acts, grads, in_ids, in_signs, out_ids, out_signs, in_table, out_table):
@@ -321,10 +312,10 @@
         return mine, fisher
 
     part = krons[0] + lax.ppermute(krons[1], "seq", swap)
-    parcels = list(parcels_of(part, lax.ppermute(part, "tensor", swap), dp))
-    for k in range(1, dp):
-        parcels[k] = lax.ppermute(parcels[k], "dp", [(d, (d + k) % dp) for d in range(dp)])
-    mine, fisher = fisher_block(parcels, lax.ppermute(bundle_of(parcels), "seq", swap))
+    parcels = parcels_of(part, lax.ppermute(part, "tensor", swap), dp)
+    parcels = lax.all_to_all(parcels, "dp", 0, 0, tiled=True)
+    rows = part.shape[0]
+    mine, fisher = fisher_block(parcels, lax.ppermute(bundle_of(parcels, rows), "seq", swap), rows)
     return mine, fisher
 
 

time: 32.3 us -> 35.5 us (1.099)
  blocking collectives: 0 us -> 11.5 us
  starting transfers between devices: 9.77 us -> 4.2 us
  waiting for transfers between devices: 8.58 us -> 5.85 us
    all_to_all x0 -> x1, blocking collectives: none -> 11.5 us  [local(): parcels = lax.all_to_all(parcels, 'dp', 0, 0, tiled=True)]
    ppermute x5 -> x2, starting transfers between devices: 6.7 us -> 1.13 us  [the longest x1 1.06 us: local(): parcels = parcels_of(part, lax.ppermute(part, 'tensor', swap), dp)]
    ppermute x5 -> x2, waiting for transfers between devices: 7.34 us -> 4.61 us  [the longest x1 3.27 us: local(): parcels = parcels_of(part, lax.ppermute(part, 'tensor', swap), dp)]
  transfers between devices with their start and end apart: 7 -> 4, of which waited for: 6 -> 3; matrix products, arithmetic and copies ran while one was open for 0% -> 0% of each run, Pallas kernels for 22% -> 20%
where the time goes in v6:
time: 35.5 us; the launch traced here: 35.4 us
  Pallas kernels  13.1 us (37%)
  blocking collectives  11.5 us (32%)
  waiting for transfers between devices  5.85 us (16%)
  starting transfers between devices  4.2 us (12%)
  between operations  0.72 us (2%)
    all_to_all x1, blocking collectives, local(): parcels = lax.all_to_all(parcels, 'dp', 0, 0, tiled=True)  11.5 us
    pallas_call x2, Pallas kernels, project(): pl.pallas_call(functools.partial(project_kernel, widths, fetch), out_shap...  9.93 us
    ppermute x1, waiting for transfers between devices, local(): parcels = parcels_of(part, lax.ppermute(part, 'tensor', swap), dp)  3.27 us
    ppermute x1, starting transfers between devices, local(): act_parts = [act, lax.ppermute(act, 'tensor', swap)]  3 us
    pallas_call x1, Pallas kernels, fisher_block(): pl.pallas_call(functools.partial(fisher_kernel, 1.0 / total), out_shape=[...  2.55 us
    ppermute x1, waiting for transfers between devices, local(): lax.ppermute(bundle_of(parcels, rows), 'seq', swap)  1.33 us
    ppermute x1, waiting for transfers between devices, local(): part = krons[0] + lax.ppermute(krons[1], 'seq', swap)  1.24 us
    ppermute x1, starting transfers between devices, local(): parcels = parcels_of(part, lax.ppermute(part, 'tensor', swap), dp)  1.06 us
  transfers between devices with their start and end apart: 4, of which 3 were waited for; matrix products, arithmetic and copies ran while one was open for 0% of the time, Pallas kernels for 20%

profile of v6, /device:TPU:0, one launch (start us, length us, event | category | flops | bytes accessed | tf_op | source)
XLA Modules:
  0.0 35.4 jit_solution(3170499592288702454)
XLA Ops:
  0.6 0.0 copy-start
  0.6 0.0 copy-start.2
  0.7 0.0 copy-start.1
  0.7 2.9 %project_acts.1.acts = f32[4,128,128]{2,1,0:T(8,128)S(1)} custom-call(s32[32]{0:T(128)} %ids.2, s32[32]{0:T(128)} %signs.2, bf16[32,4096]{1,0:T(8,128)(2,1)} %table.2, bf16[1024,2048]{1,0:T(8,128)(2,1)} %bitcast.8), custom_call_target="tpu_custom_call" | custom-call | flops 536870912 | bytes 4194304 | tf_op jit(solution)/shard_map/project_acts/pallas_call | solution.py:118
  3.6 3.0 %collective-permute-start = (f32[4,128,128]{2,1,0:T(8,128)S(1)}, f32[4,128,128]{2,1,0:T(8,128)S(1)}, u32[]{:S(2)}, u32[]{:S(2)}) collective-permute-start(f32[4,128,128]{2,1,0:T(8,128)S(1)} %project_acts.1.acts), channel_id=1, source_target_pairs={{0,2},{2,0},{1,3},{3,1},{4,6},{6,4},{5,7},{7,5},{8,10},{10,8},{9,1... | collective-permute-start | bytes 786440 | tf_op jit(solution)/shard_map/ppermute | solution.py:294
  6.6 0.0 copy-done
  6.6 0.0 copy-done.2
  6.6 0.0 copy-done.1
  6.6 7.0 %project_grads.1.grads = f32[4,128,128]{2,1,0:T(8,128)S(1)} custom-call(s32[112]{0:T(128)S(1)} %copy-done.1, s32[112]{0:T(128)S(1)} %copy-done.2, bf16[32,4096]{1,0:T(8,128)(2,1)S(1)} %copy-done, bf16[1024,7168]{1,0:T(8,128)(2,1)} %bitcast.7), custom_call_target="tpu_custom_call" | custom-call | flops 1879048192 | bytes 14680064 | tf_op jit(solution)/shard_map/project_grads/pallas_call | solution.py:118
  13.6 0.0 collective-permute-done.refs_0_
  13.6 0.6 %kron.1 = (f32[8,2048]{1,0:T(8,128)S(1)}, f32[8,2048]{1,0:T(8,128)S(1)}) custom-call(f32[4,128,128]{2,1,0:T(8,128)S(1)} %project_acts.1.acts, f32[4,128,128]{2,1,0:T(8,128)S(1)} %project_grads.1.grads, f32[4,128,128]{2,1,0:T(8,128)S(1)} %collective-permute-done.refs_0_), custom_call_target="tpu_custom_call" | custom-call | tf_op jit(solution)/shard_map/kron/pallas_call | solution.py:177
  14.2 0.1 collective-permute-start.1
  14.3 1.2 %collective-permute-done.1 = f32[8,2048]{1,0:T(8,128)S(1)} collective-permute-done((f32[8,2048]{1,0:T(8,128)S(1)}, f32[8,2048]{1,0:T(8,128)S(1)}, u32[]{:S(2)}, u32[]{:S(2)}) %collective-permute-start.1) | collective-permute-done | bytes 65568 | tf_op jit(solution)/shard_map/ppermute | solution.py:314
  15.5 1.1 %collective-permute-start.2 = (f32[8,2048]{1,0:T(8,128)S(1)}, f32[8,2048]{1,0:T(8,128)S(1)}, u32[]{:S(2)}, u32[]{:S(2)}) collective-permute-start(f32[8,2048]{1,0:T(8,128)S(1)} %add.3.here), channel_id=1, source_target_pairs={{0,2},{2,0},{1,3},{3,1},{4,6},{6,4},{5,7},{7,5},{8,10},{10,8},{9,1... | collective-permute-start | bytes 196616 | tf_op jit(solution)/shard_map/ppermute | solution.py:315
  16.6 3.3 %collective-permute-done.2.there = f32[8,2048]{1,0:T(8,128)S(1)} collective-permute-done((f32[8,2048]{1,0:T(8,128)S(1)}, f32[8,2048]{1,0:T(8,128)S(1)}, u32[]{:S(2)}, u32[]{:S(2)}) %collective-permute-start.2) | collective-permute-done | bytes 65568 | tf_op jit(solution)/shard_map/ppermute | solution.py:315
  19.9 11.5 %all_to_all.11 = f32[4,24,512]{2,1,0:T(8,128)S(1)} all-to-all(f32[4,24,512]{2,1,0:T(8,128)S(1)} %bitcast.6), channel_id=1, replica_groups=mesh['groups'=2,'dp'=4,'tensor'=2,'seq'=2] {'dp'}, dimensions={0} | all-to-all | bytes 393216 | tf_op jit(solution)/shard_map/all_to_all | solution.py:316
  31.4 0.1 collective-permute-start.3
  31.5 1.3 %collective-permute-done.3.bundle = f32[64,512]{1,0:T(8,128)S(1)} collective-permute-done((f32[64,512]{1,0:T(8,128)S(1)}, f32[64,512]{1,0:T(8,128)S(1)}, u32[]{:S(2)}, u32[]{:S(2)}) %collective-permute-start.3) | collective-permute-done | bytes 131104 | tf_op jit(solution)/shard_map/ppermute | solution.py:318
  32.8 2.5 %fisher.1 = (f32[8,1024]{1,0:T(8,128)}, f32[1024,1024]{1,0:T(8,128)}) custom-call(f32[64,512]{1,0:T(8,128)S(1)} %collective-permute-done.3.bundle, f32[96,512]{1,0:T(8,128)S(1)} %bitcast.5), custom_call_target="tpu_custom_call" | custom-call | tf_op jit(solution)/shard_map/fisher/pallas_call | solution.py:266
  (3 shorter events, 0.0 us)
Async XLA Ops:
  0.6 6.0 %copy-start = (bf16[32,4096]{1,0:T(8,128)(2,1)S(1)}, bf16[32,4096]{1,0:T(8,128)(2,1)}, u32[]{:S(2)}) copy-start(bf16[32,4096]{1,0:T(8,128)(2,1)} %table.3) | copy-start | bytes 786436
  0.6 5.9 %copy-start.2 = (s32[112]{0:T(128)S(1)}, s32[112]{0:T(128)}, u32[]{:S(2)}) copy-start(s32[112]{0:T(128)} %signs.3) | copy-start | bytes 1348
  0.7 5.9 %copy-start.1 = (s32[112]{0:T(128)S(1)}, s32[112]{0:T(128)}, u32[]{:S(2)}) copy-start(s32[112]{0:T(128)} %ids.3) | copy-start | bytes 1348
  3.6 10.0 %collective-permute-start = (f32[4,128,128]{2,1,0:T(8,128)S(1)}, f32[4,128,128]{2,1,0:T(8,128)S(1)}, u32[]{:S(2)}, u32[]{:S(2)}) collective-permute-start(f32[4,128,128]{2,1,0:T(8,128)S(1)} %project_acts.1.acts), channel_id=1, source_target_pairs={{0,2},{2,0},{1,3},{3,1},{4,6},{6,4},{5,7},{7,5},{8,10},{10,8},{9,1... | collective-permute-start | bytes 786440 | tf_op jit(solution)/shard_map/ppermute | solution.py:294
  14.2 1.3 %collective-permute-start.1 = (f32[8,2048]{1,0:T(8,128)S(1)}, f32[8,2048]{1,0:T(8,128)S(1)}, u32[]{:S(2)}, u32[]{:S(2)}) collective-permute-start(f32[8,2048]{1,0:T(8,128)S(1)} %get-tuple-element.5), channel_id=1, source_target_pairs={{0,1},{1,0},{2,3},{3,2},{4,5},{5,4},{6,7},{7,6},{8,9},{9,8},{10,11... | collective-permute-start | bytes 196616 | tf_op jit(solution)/shard_map/ppermute | solution.py:314
  15.5 4.3 %collective-permute-start.2 = (f32[8,2048]{1,0:T(8,128)S(1)}, f32[8,2048]{1,0:T(8,128)S(1)}, u32[]{:S(2)}, u32[]{:S(2)}) collective-permute-start(f32[8,2048]{1,0:T(8,128)S(1)} %add.3.here), channel_id=1, source_target_pairs={{0,2},{2,0},{1,3},{3,1},{4,6},{6,4},{5,7},{7,5},{8,10},{10,8},{9,1... | collective-permute-start | bytes 196616 | tf_op jit(solution)/shard_map/ppermute | solution.py:315
  31.4 1.4 %collective-permute-start.3 = (f32[64,512]{1,0:T(8,128)S(1)}, f32[64,512]{1,0:T(8,128)S(1)}, u32[]{:S(2)}, u32[]{:S(2)}) collective-permute-start(f32[64,512]{1,0:T(8,128)S(1)} %bundle.1), channel_id=1, source_target_pairs={{0,1},{1,0},{2,3},{3,2},{4,5},{5,4},{6,7},{7,6},{8,9},{9,8},{10,11... | collective-permute-start | bytes 393224 | tf_op jit(solution)/shard_map/ppermute | solution.py:318

commit v7 on v5

--- a/solution.py
+++ b/solution.py
@@ -14,15 +14,14 @@
 
 
 def chunks_of(width, most):
-    if width >= 4 * most:
-        inner = width - most
-        ends = [most // 2] * 2
-    else:
-        inner, ends = width, []
+    if width < 4 * most:
+        most = LANES
+    ends = most // 2 // LANES * LANES
+    inner = width - 2 * ends
     chunk = most
     while inner % chunk:
         chunk -= LANES
-    return ends[:1] + [chunk] * (inner // chunk) + ends[1:]
+    return [ends] * (ends > 0) + [chunk] * (inner // chunk) + [ends] * (ends > 0)
 
 
 def split3(x):
@@ -68,8 +67,8 @@
         for copy in small:
             copy.start()
         table, ids, signs = own
-    for copy in copies:
-        copy.start()
+    for c, copy in enumerate(copies):
+        copy.start(priority=c % 2)
     if fetch:
         small[0].wait()
     spread_table(table, spread, signed)
@@ -195,7 +194,7 @@
     core, chip = lax.axis_index("seq"), lax.axis_index("tensor") * 2
     blocks = [chip + core, chip + 1 - core]
     for k, parcel in enumerate(parcels):
-        for step, block in enumerate(blocks + [lax.rem(lax.axis_index("dp") + k, dp)]):
+        for step, block in enumerate(blocks + [lax.axis_index("dp") ^ k]):
             lanes = pl.ds(pl.multiple_of(block * width, LANES), width)
             parcel[pl.ds(step * count, count), :] = here[:, lanes] + there[:, lanes]
 
@@ -260,7 +259,7 @@
         copies.append(
             pltpu.make_async_copy(made.at[block], out.at[:, pl.ds(block * width, width)], sems.at[block])
         )
-        copies[-1].start()
+        copies[-1].start(priority=block % 2)
     for copy in copies:
         copy.wait()
 
@@ -322,8 +321,9 @@
 
     part = krons[0] + lax.ppermute(krons[1], "seq", swap)
     parcels = list(parcels_of(part, lax.ppermute(part, "tensor", swap), dp))
-    for k in range(1, dp):
-        parcels[k] = lax.ppermute(parcels[k], "dp", [(d, (d + k) % dp) for d in range(dp)])
+    parcels = parcels[:1] + [
+        lax.ppermute(parcels[k], "dp", [(d, d ^ k) for d in range(dp)]) for k in (2, 3, 1)
+    ]
     mine, fisher = fisher_block(parcels, lax.ppermute(bundle_of(parcels), "seq", swap))
     return mine, fisher
 

time: 32.3 us -> 34.9 us (1.080)
  waiting for transfers between devices: 8.58 us -> 11.2 us
  Pallas kernels: 13.1 us -> 15.4 us
  starting transfers between devices: 9.77 us -> 7.48 us
    pallas_call x2, Pallas kernels: 9.93 us -> 12.2 us  [project(): pl.pallas_call(functools.partial(project_kernel, widths, fetch), out_shap...]
    ppermute x3, waiting for transfers between devices: 2.73 us -> 4.39 us  [local(): lax.ppermute(parcels[k], 'dp', [(d, d ^ k) for d in range(dp)])]
    ppermute x3, starting transfers between devices: 5.57 us -> 4.23 us  [local(): lax.ppermute(parcels[k], 'dp', [(d, d ^ k) for d in range(dp)])]
    ppermute x1, waiting for transfers between devices: 3.27 us -> 4.22 us  [local(): parcels = list(parcels_of(part, lax.ppermute(part, 'tensor', swap), dp))]
    ppermute x1, starting transfers between devices: 1.06 us -> 0.11 us  [local(): parcels = list(parcels_of(part, lax.ppermute(part, 'tensor', swap), dp))]
  transfers between devices with their start and end apart: 7 -> 7, of which waited for: 6 -> 5; matrix products, arithmetic and copies ran while one was open for 0% -> 0% of each run, Pallas kernels for 22% -> 26%
where the time goes in v7:
time: 34.9 us; the launch traced here: 34.8 us
  Pallas kernels  15.4 us (44%)
  waiting for transfers between devices  11.2 us (32%)
  starting transfers between devices  7.48 us (21%)
  between operations  0.72 us (2%)
    pallas_call x2, Pallas kernels, project(): pl.pallas_call(functools.partial(project_kernel, widths, fetch), out_shap...  12.2 us
    ppermute x3, waiting for transfers between devices, local(): lax.ppermute(parcels[k], 'dp', [(d, d ^ k) for d in range(dp)])  4.39 us
    ppermute x3, starting transfers between devices, local(): lax.ppermute(parcels[k], 'dp', [(d, d ^ k) for d in range(dp)])  4.23 us
    ppermute x1, waiting for transfers between devices, local(): parcels = list(parcels_of(part, lax.ppermute(part, 'tensor', swap), dp))  4.22 us
    ppermute x1, starting transfers between devices, local(): act_parts = [act, lax.ppermute(act, 'tensor', swap)]  3 us
    pallas_call x1, Pallas kernels, fisher_block(): pl.pallas_call(functools.partial(fisher_kernel, 1.0 / total), out_shape=[...  2.55 us
    ppermute x1, waiting for transfers between devices, local(): lax.ppermute(bundle_of(parcels), 'seq', swap)  1.33 us
    ppermute x1, waiting for transfers between devices, local(): part = krons[0] + lax.ppermute(krons[1], 'seq', swap)  1.24 us
  transfers between devices with their start and end apart: 7, of which 5 were waited for; matrix products, arithmetic and copies ran while one was open for 0% of the time, Pallas kernels for 26%

profile of v7, /device:TPU:0, one launch (start us, length us, event | category | flops | bytes accessed | tf_op | source)
XLA Modules:
  0.0 34.8 jit_solution(6022493963515276029)
XLA Ops:
  0.6 0.0 copy-start
  0.6 0.0 copy-start.2
  0.7 0.0 copy-start.1
  0.7 3.4 %project_acts.1.acts = f32[4,128,128]{2,1,0:T(8,128)S(1)} custom-call(s32[32]{0:T(128)} %ids.2, s32[32]{0:T(128)} %signs.2, bf16[32,4096]{1,0:T(8,128)(2,1)} %table.2, bf16[1024,2048]{1,0:T(8,128)(2,1)} %bitcast.3), custom_call_target="tpu_custom_call" | custom-call | flops 536870912 | bytes 4194304 | tf_op jit(solution)/shard_map/project_acts/pallas_call | solution.py:117
  4.0 3.0 %collective-permute-start = (f32[4,128,128]{2,1,0:T(8,128)S(1)}, f32[4,128,128]{2,1,0:T(8,128)S(1)}, u32[]{:S(2)}, u32[]{:S(2)}) collective-permute-start(f32[4,128,128]{2,1,0:T(8,128)S(1)} %project_acts.1.acts), channel_id=1, source_target_pairs={{0,2},{2,0},{1,3},{3,1},{4,6},{6,4},{5,7},{7,5},{8,10},{10,8},{9,1... | collective-permute-start | bytes 786440 | tf_op jit(solution)/shard_map/ppermute | solution.py:302
  7.0 0.0 copy-done
  7.0 0.0 copy-done.2
  7.0 0.0 copy-done.1
  7.0 8.9 %project_grads.1.grads = f32[4,128,128]{2,1,0:T(8,128)S(1)} custom-call(s32[112]{0:T(128)S(1)} %copy-done.1, s32[112]{0:T(128)S(1)} %copy-done.2, bf16[32,4096]{1,0:T(8,128)(2,1)S(1)} %copy-done, bf16[1024,7168]{1,0:T(8,128)(2,1)} %bitcast.2), custom_call_target="tpu_custom_call" | custom-call | flops 1879048192 | bytes 14680064 | tf_op jit(solution)/shard_map/project_grads/pallas_call | solution.py:117
  15.9 0.0 collective-permute-done.refs_0_
  15.9 0.6 %kron.1 = (f32[8,2048]{1,0:T(8,128)S(1)}, f32[8,2048]{1,0:T(8,128)S(1)}) custom-call(f32[4,128,128]{2,1,0:T(8,128)S(1)} %project_acts.1.acts, f32[4,128,128]{2,1,0:T(8,128)S(1)} %project_grads.1.grads, f32[4,128,128]{2,1,0:T(8,128)S(1)} %collective-permute-done.refs_0_), custom_call_target="tpu_custom_call" | custom-call | tf_op jit(solution)/shard_map/kron/pallas_call | solution.py:176
  16.5 0.1 collective-permute-start.1
  16.6 1.2 %collective-permute-done.1 = f32[8,2048]{1,0:T(8,128)S(1)} collective-permute-done((f32[8,2048]{1,0:T(8,128)S(1)}, f32[8,2048]{1,0:T(8,128)S(1)}, u32[]{:S(2)}, u32[]{:S(2)}) %collective-permute-start.1) | collective-permute-done | bytes 65568 | tf_op jit(solution)/shard_map/ppermute | solution.py:322
  17.8 0.1 collective-permute-start.2
  17.9 4.2 %collective-permute-done.2.there = f32[8,2048]{1,0:T(8,128)S(1)} collective-permute-done((f32[8,2048]{1,0:T(8,128)S(1)}, f32[8,2048]{1,0:T(8,128)S(1)}, u32[]{:S(2)}, u32[]{:S(2)}) %collective-permute-start.2) | collective-permute-done | bytes 65568 | tf_op jit(solution)/shard_map/ppermute | solution.py:323
  22.2 2.6 %collective-permute-start.3 = (f32[24,512]{1,0:T(8,128)S(1)}, f32[24,512]{1,0:T(8,128)S(1)}, u32[]{:S(2)}, u32[]{:S(2)}) collective-permute-start(f32[24,512]{1,0:T(8,128)S(1)} %get-tuple-element.11), channel_id=1, source_target_pairs={{0,8},{4,12},{8,0},{12,4},{1,9},{5,13},{9,1},{13,5},{2,10},{6,14},... | collective-permute-start | bytes 147464 | tf_op jit(solution)/shard_map/ppermute | solution.py:325
  24.8 1.4 %collective-permute-start.4 = (f32[24,512]{1,0:T(8,128)S(1)}, f32[24,512]{1,0:T(8,128)S(1)}, u32[]{:S(2)}, u32[]{:S(2)}) collective-permute-start(f32[24,512]{1,0:T(8,128)S(1)} %get-tuple-element.12), channel_id=1, source_target_pairs={{0,12},{4,8},{8,4},{12,0},{1,13},{5,9},{9,5},{13,1},{2,14},{6,10},... | collective-permute-start | bytes 147464 | tf_op jit(solution)/shard_map/ppermute | solution.py:325
  26.2 0.2 collective-permute-start.5
  26.4 1.0 %collective-permute-done.3.refs_1_ = f32[24,512]{1,0:T(8,128)S(1)} collective-permute-done((f32[24,512]{1,0:T(8,128)S(1)}, f32[24,512]{1,0:T(8,128)S(1)}, u32[]{:S(2)}, u32[]{:S(2)}) %collective-permute-start.3) | collective-permute-done | bytes 49184 | tf_op jit(solution)/shard_map/ppermute | solution.py:325
  27.4 3.4 %collective-permute-done.4.refs_2_ = f32[24,512]{1,0:T(8,128)S(1)} collective-permute-done((f32[24,512]{1,0:T(8,128)S(1)}, f32[24,512]{1,0:T(8,128)S(1)}, u32[]{:S(2)}, u32[]{:S(2)}) %collective-permute-start.4) | collective-permute-done | bytes 49184 | tf_op jit(solution)/shard_map/ppermute | solution.py:325
  30.8 0.0 collective-permute-done.5.refs_3_
  30.8 0.1 collective-permute-start.6
  30.9 1.3 %collective-permute-done.6.bundle = f32[64,512]{1,0:T(8,128)S(1)} collective-permute-done((f32[64,512]{1,0:T(8,128)S(1)}, f32[64,512]{1,0:T(8,128)S(1)}, u32[]{:S(2)}, u32[]{:S(2)}) %collective-permute-start.6) | collective-permute-done | bytes 131104 | tf_op jit(solution)/shard_map/ppermute | solution.py:327
  32.2 2.5 %fisher.1 = (f32[8,1024]{1,0:T(8,128)}, f32[1024,1024]{1,0:T(8,128)}) custom-call(f32[64,512]{1,0:T(8,128)S(1)} %collective-permute-done.6.bundle, f32[24,512]{1,0:T(8,128)S(1)} %get-tuple-element.10.refs_0_, f32[24,512]{1,0:T(8,128)S(1)} %collective-permute-done.3.refs_1_, f32[24,512]{1,0:T(8,128)S(1)} %collective-permute-done.4.refs_2_, ...), custom_call_target="tpu_custom_call" | custom-call | tf_op jit(solution)/shard_map/fisher/pallas_call | solution.py:274
  (3 shorter events, 0.0 us)
Async XLA Ops:
  0.6 6.4 %copy-start = (bf16[32,4096]{1,0:T(8,128)(2,1)S(1)}, bf16[32,4096]{1,0:T(8,128)(2,1)}, u32[]{:S(2)}) copy-start(bf16[32,4096]{1,0:T(8,128)(2,1)} %table.3) | copy-start | bytes 786436
  0.6 6.4 %copy-start.2 = (s32[112]{0:T(128)S(1)}, s32[112]{0:T(128)}, u32[]{:S(2)}) copy-start(s32[112]{0:T(128)} %signs.3) | copy-start | bytes 1348
  0.7 6.4 %copy-start.1 = (s32[112]{0:T(128)S(1)}, s32[112]{0:T(128)}, u32[]{:S(2)}) copy-start(s32[112]{0:T(128)} %ids.3) | copy-start | bytes 1348
  4.0 11.9 %collective-permute-start = (f32[4,128,128]{2,1,0:T(8,128)S(1)}, f32[4,128,128]{2,1,0:T(8,128)S(1)}, u32[]{:S(2)}, u32[]{:S(2)}) collective-permute-start(f32[4,128,128]{2,1,0:T(8,128)S(1)} %project_acts.1.acts), channel_id=1, source_target_pairs={{0,2},{2,0},{1,3},{3,1},{4,6},{6,4},{5,7},{7,5},{8,10},{10,8},{9,1... | collective-permute-start | bytes 786440 | tf_op jit(solution)/shard_map/ppermute | solution.py:302
  16.5 1.3 %collective-permute-start.1 = (f32[8,2048]{1,0:T(8,128)S(1)}, f32[8,2048]{1,0:T(8,128)S(1)}, u32[]{:S(2)}, u32[]{:S(2)}) collective-permute-start(f32[8,2048]{1,0:T(8,128)S(1)} %get-tuple-element.9), channel_id=1, source_target_pairs={{0,1},{1,0},{2,3},{3,2},{4,5},{5,4},{6,7},{7,6},{8,9},{9,8},{10,11... | collective-permute-start | bytes 196616 | tf_op jit(solution)/shard_map/ppermute | solution.py:322
  17.8 4.3 %collective-permute-start.2 = (f32[8,2048]{1,0:T(8,128)S(1)}, f32[8,2048]{1,0:T(8,128)S(1)}, u32[]{:S(2)}, u32[]{:S(2)}) collective-permute-start(f32[8,2048]{1,0:T(8,128)S(1)} %add.3.here), channel_id=1, source_target_pairs={{0,2},{2,0},{1,3},{3,1},{4,6},{6,4},{5,7},{7,5},{8,10},{10,8},{9,1... | collective-permute-start | bytes 196616 | tf_op jit(solution)/shard_map/ppermute | solution.py:323
  22.2 5.2 %collective-permute-start.3 = (f32[24,512]{1,0:T(8,128)S(1)}, f32[24,512]{1,0:T(8,128)S(1)}, u32[]{:S(2)}, u32[]{:S(2)}) collective-permute-start(f32[24,512]{1,0:T(8,128)S(1)} %get-tuple-element.11), channel_id=1, source_target_pairs={{0,8},{4,12},{8,0},{12,4},{1,9},{5,13},{9,1},{13,5},{2,10},{6,14},... | collective-permute-start | bytes 147464 | tf_op jit(solution)/shard_map/ppermute | solution.py:325
  24.8 6.0 %collective-permute-start.4 = (f32[24,512]{1,0:T(8,128)S(1)}, f32[24,512]{1,0:T(8,128)S(1)}, u32[]{:S(2)}, u32[]{:S(2)}) collective-permute-start(f32[24,512]{1,0:T(8,128)S(1)} %get-tuple-element.12), channel_id=1, source_target_pairs={{0,12},{4,8},{8,4},{12,0},{1,13},{5,9},{9,5},{13,1},{2,14},{6,10},... | collective-permute-start | bytes 147464 | tf_op jit(solution)/shard_map/ppermute | solution.py:325
  26.2 4.6 %collective-permute-start.5 = (f32[24,512]{1,0:T(8,128)S(1)}, f32[24,512]{1,0:T(8,128)S(1)}, u32[]{:S(2)}, u32[]{:S(2)}) collective-permute-start(f32[24,512]{1,0:T(8,128)S(1)} %get-tuple-element.13), channel_id=1, source_target_pairs={{0,4},{4,0},{8,12},{12,8},{1,5},{5,1},{9,13},{13,9},{2,6},{6,2},{1... | collective-permute-start | bytes 147464 | tf_op jit(solution)/shard_map/ppermute | solution.py:325
  30.8 1.4 %collective-permute-start.6 = (f32[64,512]{1,0:T(8,128)S(1)}, f32[64,512]{1,0:T(8,128)S(1)}, u32[]{:S(2)}, u32[]{:S(2)}) collective-permute-start(f32[64,512]{1,0:T(8,128)S(1)} %bundle.1), channel_id=1, source_target_pairs={{0,1},{1,0},{2,3},{3,2},{4,5},{5,4},{6,7},{7,6},{8,9},{9,8},{10,11... | collective-permute-start | bytes 393224 | tf_op jit(solution)/shard_map/ppermute | solution.py:327

commit v8 on v7

--- a/solution.py
+++ b/solution.py
@@ -10,6 +10,7 @@
 PROJ = 64
 BLOCK = 64
 LANES = 128
+PLANE = ("tensor", "seq")
 VMEM_BYTES = 48 * 1024 * 1024
 
 
@@ -67,8 +68,8 @@
         for copy in small:
             copy.start()
         table, ids, signs = own
-    for c, copy in enumerate(copies):
-        copy.start(priority=c % 2)
+    for copy in copies:
+        copy.start()
     if fetch:
         small[0].wait()
     spread_table(table, spread, signed)
@@ -136,9 +137,8 @@
     )(*operands)
 
 
-def kron_kernel(cuts, acts, grads, *refs):
-    parts = cuts[1]
-    summands, outs, rows, products = refs[: -parts - 2], refs[-parts - 2 : -2], refs[-2], refs[-1]
+def kron_kernel(acts, grads, *refs):
+    summands, out, products = refs[:-2], refs[-2], refs[-1]
     pairs = acts.shape[0]
     for pair in range(pairs):
         act = acts[pair]
@@ -155,33 +155,23 @@
     lower = lax.broadcasted_iota(jnp.int32, (count, LANES), 1) < PROJ
     even = lax.broadcasted_iota(jnp.int32, (count, LANES), 0) % 2 == 0
     here = even == lower
-    tiles = rows.shape[2] // LANES // cuts[0]
-    for tile in range(PROJ * PROJ // LANES):
+    for tile in range(out.shape[1] // LANES):
         both = []
         for p in (2 * tile, 2 * tile + 1):
             v = products[pl.ds(p, count, stride=PROJ), :]
             both.append(jnp.where(here, v, pltpu.roll(v, PROJ, 1)))
-        block, part, within = tile // tiles // parts, tile // tiles % parts, tile % tiles
-        rows[part, :, pl.ds((block * tiles + within) * LANES, LANES)] = jnp.where(lower, both[0], both[1])
-    for k, out in enumerate(outs):
-        part = lax.rem(lax.axis_index("seq") + k, parts) if parts > 1 else 0
-        out[...] = rows[part]
-
-
-def kron_of(act_parts, grads, cuts):
+        out[:, pl.ds(tile * LANES, LANES)] = jnp.where(lower, both[0], both[1])
+
+
+def kron_of(act_parts, grads):
     pairs = grads.shape[0]
-    parts = cuts[1]
-    width = PROJ * PROJ // parts
     vmem = pl.BlockSpec(memory_space=pltpu.VMEM)
     return pl.pallas_call(
-        functools.partial(kron_kernel, cuts),
-        out_shape=[jax.ShapeDtypeStruct((2 * pairs, width), jnp.float32)] * parts,
+        kron_kernel,
+        out_shape=jax.ShapeDtypeStruct((2 * pairs, PROJ * PROJ), jnp.float32),
         in_specs=[vmem] * (1 + len(act_parts)),
-        out_specs=[vmem] * parts,
-        scratch_shapes=[
-            pltpu.VMEM((parts, 2 * pairs, width), jnp.float32),
-            pltpu.VMEM((pairs * LANES, LANES), jnp.float32),
-        ],
+        out_specs=vmem,
+        scratch_shapes=[pltpu.VMEM((pairs * LANES, LANES), jnp.float32)],
         compiler_params=pltpu.CompilerParams(vmem_limit_bytes=VMEM_BYTES),
         name="kron",
     )(act_parts[0], grads, *act_parts[1:])
@@ -189,12 +179,10 @@
 
 def parcels_kernel(here, there, *parcels):
     count = here.shape[0]
-    dp = len(parcels)
     width = parcels[0].shape[1]
-    core, chip = lax.axis_index("seq"), lax.axis_index("tensor") * 2
-    blocks = [chip + core, chip + 1 - core]
+    chip = lax.axis_index("tensor") * 2
     for k, parcel in enumerate(parcels):
-        for step, block in enumerate(blocks + [lax.axis_index("dp") ^ k]):
+        for step, block in enumerate((chip, chip + 1, lax.axis_index("dp") ^ k)):
             lanes = pl.ds(pl.multiple_of(block * width, LANES), width)
             parcel[pl.ds(step * count, count), :] = here[:, lanes] + there[:, lanes]
 
@@ -214,9 +202,10 @@
 
 def bundle_kernel(*refs):
     parcels, out = refs[:-1], refs[-1]
-    rows = 2 * parcels[0].shape[0] // 3
+    rows = parcels[0].shape[0] // 3
     for k, parcel in enumerate(parcels):
-        out[pl.ds(k * rows, rows), :] = parcel[pl.ds(rows // 2, rows), :]
+        out[pl.ds(2 * k * rows, rows), :] = parcel[pl.ds(0, rows), :]
+        out[pl.ds((2 * k + 1) * rows, rows), :] = parcel[pl.ds(2 * rows, rows), :]
 
 
 def bundle_of(parcels):
@@ -234,17 +223,20 @@
 
 def fisher_kernel(scale, bundle, *refs):
     parcels, (mine, out, made, kept, left, right, sems) = refs[:-7], refs[-7:]
-    rows = parcels[0].shape[0] // 3
-    part = parcels[0].shape[1]
-    core = lax.axis_index("seq")
-    own = pl.ds(pl.multiple_of(core * part, LANES), part)
-    others = pl.ds(pl.multiple_of((1 - core) * part, LANES), part)
-    for k, parcel in enumerate(parcels):
-        into = pl.ds(k * rows, rows)
-        left[into, own] = parcel[pl.ds(0, rows), :]
-        left[into, others] = bundle[pl.ds(2 * k * rows, rows), :]
-        right[into, own] = parcel[pl.ds(2 * rows, rows), :]
-        right[into, others] = bundle[pl.ds((2 * k + 1) * rows, rows), :]
+    rows = kept.shape[0]
+
+    @pl.when(lax.axis_index("seq") == 0)
+    def _():
+        for k in range(len(parcels)):
+            left[pl.ds(k * rows, rows), :] = bundle[pl.ds(2 * k * rows, rows), :]
+            right[pl.ds(k * rows, rows), :] = bundle[pl.ds((2 * k + 1) * rows, rows), :]
+
+    @pl.when(lax.axis_index("seq") == 1)
+    def _():
+        for k, parcel in enumerate(parcels):
+            left[pl.ds(k * rows, rows), :] = parcel[pl.ds(rows, rows), :]
+            right[pl.ds(k * rows, rows), :] = parcel[pl.ds(2 * rows, rows), :]
+
     blocks, _, width = made.shape
     kept[...] = left[pl.ds(0, rows), :]
     copies = [pltpu.make_async_copy(kept, mine, sems.at[blocks])]
@@ -259,15 +251,14 @@
         copies.append(
             pltpu.make_async_copy(made.at[block], out.at[:, pl.ds(block * width, width)], sems.at[block])
         )
-        copies[-1].start(priority=block % 2)
+        copies[-1].start()
     for copy in copies:
         copy.wait()
 
 
 def fisher_block(parcels, bundle):
-    rows, part = parcels[0].shape
+    rows, width = parcels[0].shape
     rows //= 3
-    width = 2 * part
     total = rows * len(parcels)
     blocks = 4
     hbm = pl.BlockSpec(memory_space=pltpu.HBM)
@@ -295,18 +286,17 @@
     tensor, seq, dp = (lax.axis_size(name) for name in ("tensor", "seq", "dp"))
     shards = tensor * seq
     small = tensor == 2 and seq == 2 and dp == 4
-    swap = [(0, 1), (1, 0)]
 
     act = project(acts, in_ids, in_signs, in_table, True, 512, "project_acts")
     if tensor == 2:
-        act_parts = [act, lax.ppermute(act, "tensor", swap)]
+        act_parts = [act, lax.ppermute(act, "tensor", [(0, 1), (1, 0)])]
     else:
         act_parts = [lax.psum(act, "tensor")]
     grad = project(grads, out_ids, out_signs, out_table, False, 1024, "project_grads")
-    krons = kron_of(act_parts, grad, (shards, seq) if small else (1, 1))
+    kron = kron_of(act_parts, grad)
 
     if not small:
-        kron = lax.psum(krons[0], ("tensor", "seq"))
+        kron = lax.psum(kron, PLANE)
         width = kron.shape[1] // shards
         place = lax.axis_index("tensor") * seq + lax.axis_index("seq")
         mine = lax.dynamic_slice_in_dim(kron, place * width, width, 1)
@@ -319,12 +309,18 @@
         ) / left.shape[0]
         return mine, fisher
 
-    part = krons[0] + lax.ppermute(krons[1], "seq", swap)
-    parcels = list(parcels_of(part, lax.ppermute(part, "tensor", swap), dp))
+    kron = kron + lax.ppermute(kron, PLANE, [(0, 1), (2, 3)])
+    parcels = list(parcels_of(kron, lax.ppermute(kron, PLANE, [(1, 3), (3, 1)]), dp))
     parcels = parcels[:1] + [
-        lax.ppermute(parcels[k], "dp", [(d, d ^ k) for d in range(dp)]) for k in (2, 3, 1)
+        lax.ppermute(
+            parcels[k],
+            ("dp",) + PLANE,
+            [(shards * d + place, shards * (d ^ k) + place) for d in range(dp) for place in (1, 3)],
+        )
+        for k in (2, 3, 1)
     ]
-    mine, fisher = fisher_block(parcels, lax.ppermute(bundle_of(parcels), "seq", swap))
+    bundle = lax.ppermute(bundle_of(parcels), PLANE, [(1, 0), (3, 2)])
+    mine, fisher = fisher_block(parcels, bundle)
     return mine, fisher
 
 

time: 34.9 us -> 40.4 us (1.16)
  waiting for transfers between devices: 11.2 us -> 17.9 us
  Pallas kernels: 15.4 us -> 13.1 us
  starting transfers between devices: 7.48 us -> 8.43 us
    ppermute x7, waiting for transfers between devices: 11.2 us -> 17.9 us  [the longest x1 16.9 us: local(): bundle = lax.ppermute(bundle_of(parcels), PLANE, [(1, 0), (3, 2)])]
    pallas_call x2, Pallas kernels: 12.2 us -> 9.93 us  [project(): pl.pallas_call(functools.partial(project_kernel, widths, fetch), out_shap...]
    ppermute x7, starting transfers between devices: 7.48 us -> 8.43 us  [the longest x1 3 us: local(): act_parts = [act, lax.ppermute(act, 'tensor', [(0, 1), (1, 0)])]]
  transfers between devices with their start and end apart: 7 -> 7, of which waited for: 5 -> 2; matrix products, arithmetic and copies ran while one was open for 0% -> 0% of each run, Pallas kernels for 26% -> 17%
where the time goes in v8:
time: 40.4 us; the launch traced here: 40.2 us
  waiting for transfers between devices  17.9 us (44%)
  Pallas kernels  13.1 us (32%)
  starting transfers between devices  8.43 us (21%)
  between operations  0.79 us (2%)
    ppermute x1, waiting for transfers between devices, local(): bundle = lax.ppermute(bundle_of(parcels), PLANE, [(1, 0), (3, 2)])  16.9 us
    pallas_call x2, Pallas kernels, project(): pl.pallas_call(functools.partial(project_kernel, widths, fetch), out_shap...  9.93 us
    ppermute x1, starting transfers between devices, local(): act_parts = [act, lax.ppermute(act, 'tensor', [(0, 1), (1, 0)])]  3 us
    pallas_call x1, Pallas kernels, fisher_block(): pl.pallas_call(functools.partial(fisher_kernel, 1.0 / total), out_shape=[...  2.54 us
    ppermute x3, starting transfers between devices, local(): lax.ppermute(parcels[k], ('dp',) + PLANE, [(shards * d + place, shards *...  2 us
    ppermute x1, starting transfers between devices, local(): kron = kron + lax.ppermute(kron, PLANE, [(0, 1), (2, 3)])  1.46 us
    ppermute x1, starting transfers between devices, local(): bundle = lax.ppermute(bundle_of(parcels), PLANE, [(1, 0), (3, 2)])  1.29 us
    ppermute x1, waiting for transfers between devices, local(): kron = kron + lax.ppermute(kron, PLANE, [(0, 1), (2, 3)])  0.96 us
  transfers between devices with their start and end apart: 7, of which 2 were waited for; matrix products, arithmetic and copies ran while one was open for 0% of the time, Pallas kernels for 17%

profile of v8, /device:TPU:0, one launch (start us, length us, event | category | flops | bytes accessed | tf_op | source)
XLA Modules:
  0.0 40.2 jit_solution(6917831030898233345)
XLA Ops:
  0.6 0.0 copy-start
  0.6 0.0 copy-start.2
  0.7 0.0 copy-start.1
  0.7 2.9 %project_acts.1.acts = f32[4,128,128]{2,1,0:T(8,128)S(1)} custom-call(s32[32]{0:T(128)} %ids.2, s32[32]{0:T(128)} %signs.2, bf16[32,4096]{1,0:T(8,128)(2,1)} %table.2, bf16[1024,2048]{1,0:T(8,128)(2,1)} %bitcast.3), custom_call_target="tpu_custom_call" | custom-call | flops 536870912 | bytes 4194304 | tf_op jit(solution)/shard_map/project_acts/pallas_call | solution.py:118
  3.6 3.0 %collective-permute-start = (f32[4,128,128]{2,1,0:T(8,128)S(1)}, f32[4,128,128]{2,1,0:T(8,128)S(1)}, u32[]{:S(2)}, u32[]{:S(2)}) collective-permute-start(f32[4,128,128]{2,1,0:T(8,128)S(1)} %project_acts.1.acts), channel_id=1, source_target_pairs={{0,2},{2,0},{1,3},{3,1},{4,6},{6,4},{5,7},{7,5},{8,10},{10,8},{9,1... | collective-permute-start | bytes 786440 | tf_op jit(solution)/shard_map/ppermute | solution.py:292
  6.6 0.0 copy-done
  6.6 0.0 copy-done.2
  6.6 0.0 copy-done.1
  6.6 7.0 %project_grads.1.grads = f32[4,128,128]{2,1,0:T(8,128)S(1)} custom-call(s32[112]{0:T(128)S(1)} %copy-done.1, s32[112]{0:T(128)S(1)} %copy-done.2, bf16[32,4096]{1,0:T(8,128)(2,1)S(1)} %copy-done, bf16[1024,7168]{1,0:T(8,128)(2,1)} %bitcast.2), custom_call_target="tpu_custom_call" | custom-call | flops 1879048192 | bytes 14680064 | tf_op jit(solution)/shard_map/project_grads/pallas_call | solution.py:118
  13.6 0.0 collective-permute-done.refs_0_
  13.6 0.6 %kron.1 = f32[8,4096]{1,0:T(8,128)S(1)} custom-call(f32[4,128,128]{2,1,0:T(8,128)S(1)} %project_acts.1.acts, f32[4,128,128]{2,1,0:T(8,128)S(1)} %project_grads.1.grads, f32[4,128,128]{2,1,0:T(8,128)S(1)} %collective-permute-done.refs_0_), custom_call_target="tpu_custom_call" | custom-call | tf_op jit(solution)/shard_map/kron/pallas_call | solution.py:169
  14.2 1.5 %collective-permute-start.1 = (f32[8,4096]{1,0:T(8,128)S(1)}, f32[8,4096]{1,0:T(8,128)S(1)}, u32[]{:S(2)}, u32[]{:S(2)}) collective-permute-start(f32[8,4096]{1,0:T(8,128)S(1)} %kron.1), channel_id=1, source_target_pairs={{0,1},{2,3},{4,5},{6,7},{8,9},{10,11},{12,13},{14,15},{16,17},{18,... | collective-permute-start | bytes 393224 | tf_op jit(solution)/shard_map/ppermute | solution.py:312
  15.7 1.0 %collective-permute-done.1 = f32[8,4096]{1,0:T(8,128)S(1)} collective-permute-done((f32[8,4096]{1,0:T(8,128)S(1)}, f32[8,4096]{1,0:T(8,128)S(1)}, u32[]{:S(2)}, u32[]{:S(2)}) %collective-permute-start.1) | collective-permute-done | bytes 131104 | tf_op jit(solution)/shard_map/ppermute | solution.py:312
  16.7 0.7 %collective-permute-start.2 = (f32[8,4096]{1,0:T(8,128)S(1)}, f32[8,4096]{1,0:T(8,128)S(1)}, u32[]{:S(2)}, u32[]{:S(2)}) collective-permute-start(f32[8,4096]{1,0:T(8,128)S(1)} %add.3.here), channel_id=1, source_target_pairs={{1,3},{3,1},{5,7},{7,5},{9,11},{11,9},{13,15},{15,13},{17,19},{19,... | collective-permute-start | bytes 393224 | tf_op jit(solution)/shard_map/ppermute | solution.py:313
  17.3 0.0 collective-permute-done.2.there
  17.4 0.7 %collective-permute-start.3 = (f32[24,1024]{1,0:T(8,128)S(1)}, f32[24,1024]{1,0:T(8,128)S(1)}, u32[]{:S(2)}, u32[]{:S(2)}) collective-permute-start(f32[24,1024]{1,0:T(8,128)S(1)} %get-tuple-element.7), channel_id=1, source_target_pairs={{1,9},{3,11},{5,13},{7,15},{9,1},{11,3},{13,5},{15,7},{17,25},{19,... | collective-permute-start | bytes 294920 | tf_op jit(solution)/shard_map/ppermute | solution.py:315
  18.1 0.7 %collective-permute-start.4 = (f32[24,1024]{1,0:T(8,128)S(1)}, f32[24,1024]{1,0:T(8,128)S(1)}, u32[]{:S(2)}, u32[]{:S(2)}) collective-permute-start(f32[24,1024]{1,0:T(8,128)S(1)} %get-tuple-element.8), channel_id=1, source_target_pairs={{1,13},{3,15},{5,9},{7,11},{9,5},{11,7},{13,1},{15,3},{17,29},{19,... | collective-permute-start | bytes 294920 | tf_op jit(solution)/shard_map/ppermute | solution.py:315
  18.7 0.7 %collective-permute-start.5 = (f32[24,1024]{1,0:T(8,128)S(1)}, f32[24,1024]{1,0:T(8,128)S(1)}, u32[]{:S(2)}, u32[]{:S(2)}) collective-permute-start(f32[24,1024]{1,0:T(8,128)S(1)} %get-tuple-element.9), channel_id=1, source_target_pairs={{1,5},{3,7},{5,1},{7,3},{9,13},{11,15},{13,9},{15,11},{17,21},{19,... | collective-permute-start | bytes 294920 | tf_op jit(solution)/shard_map/ppermute | solution.py:315
  19.4 0.0 collective-permute-done.3.refs_1_
  19.4 0.0 collective-permute-done.4.refs_2_
  19.4 0.0 collective-permute-done.5.refs_3_
  19.5 1.3 %collective-permute-start.6 = (f32[64,1024]{1,0:T(8,128)S(1)}, f32[64,1024]{1,0:T(8,128)S(1)}, u32[]{:S(2)}, u32[]{:S(2)}) collective-permute-start(f32[64,1024]{1,0:T(8,128)S(1)} %bundle.1), channel_id=1, source_target_pairs={{1,0},{3,2},{5,4},{7,6},{9,8},{11,10},{13,12},{15,14},{17,16},{19,... | collective-permute-start | bytes 786440 | tf_op jit(solution)/shard_map/ppermute | solution.py:322
  20.8 16.9 %collective-permute-done.6.bundle = f32[64,1024]{1,0:T(8,128)S(1)} collective-permute-done((f32[64,1024]{1,0:T(8,128)S(1)}, f32[64,1024]{1,0:T(8,128)S(1)}, u32[]{:S(2)}, u32[]{:S(2)}) %collective-permute-start.6) | collective-permute-done | bytes 262176 | tf_op jit(solution)/shard_map/ppermute | solution.py:322
  37.7 2.5 %fisher.1 = (f32[8,1024]{1,0:T(8,128)}, f32[1024,1024]{1,0:T(8,128)}) custom-call(f32[64,1024]{1,0:T(8,128)S(1)} %collective-permute-done.6.bundle, f32[24,1024]{1,0:T(8,128)S(1)} %get-tuple-element.6.refs_0_, f32[24,1024]{1,0:T(8,128)S(1)} %collective-permute-done.3.refs_1_, f32[24,1024]{1,0:T(8,128)S(1)} %collective-permute-done.4.refs_2_, ...), custom_call_target="tpu_custom_call" | custom-call | tf_op jit(solution)/shard_map/fisher/pallas_call | solution.py:265
  (3 shorter events, 0.1 us)
Async XLA Ops:
  0.6 6.0 %copy-start = (bf16[32,4096]{1,0:T(8,128)(2,1)S(1)}, bf16[32,4096]{1,0:T(8,128)(2,1)}, u32[]{:S(2)}) copy-start(bf16[32,4096]{1,0:T(8,128)(2,1)} %table.3) | copy-start | bytes 786436
  0.6 5.9 %copy-start.2 = (s32[112]{0:T(128)S(1)}, s32[112]{0:T(128)}, u32[]{:S(2)}) copy-start(s32[112]{0:T(128)} %signs.3) | copy-start | bytes 1348
  0.7 5.9 %copy-start.1 = (s32[112]{0:T(128)S(1)}, s32[112]{0:T(128)}, u32[]{:S(2)}) copy-start(s32[112]{0:T(128)} %ids.3) | copy-start | bytes 1348
  3.6 10.0 %collective-permute-start = (f32[4,128,128]{2,1,0:T(8,128)S(1)}, f32[4,128,128]{2,1,0:T(8,128)S(1)}, u32[]{:S(2)}, u32[]{:S(2)}) collective-permute-start(f32[4,128,128]{2,1,0:T(8,128)S(1)} %project_acts.1.acts), channel_id=1, source_target_pairs={{0,2},{2,0},{1,3},{3,1},{4,6},{6,4},{5,7},{7,5},{8,10},{10,8},{9,1... | collective-permute-start | bytes 786440 | tf_op jit(solution)/shard_map/ppermute | solution.py:292
  14.2 2.4 %collective-permute-start.1 = (f32[8,4096]{1,0:T(8,128)S(1)}, f32[8,4096]{1,0:T(8,128)S(1)}, u32[]{:S(2)}, u32[]{:S(2)}) collective-permute-start(f32[8,4096]{1,0:T(8,128)S(1)} %kron.1), channel_id=1, source_target_pairs={{0,1},{2,3},{4,5},{6,7},{8,9},{10,11},{12,13},{14,15},{16,17},{18,... | collective-permute-start | bytes 393224 | tf_op jit(solution)/shard_map/ppermute | solution.py:312
  16.7 0.7 %collective-permute-start.2 = (f32[8,4096]{1,0:T(8,128)S(1)}, f32[8,4096]{1,0:T(8,128)S(1)}, u32[]{:S(2)}, u32[]{:S(2)}) collective-permute-start(f32[8,4096]{1,0:T(8,128)S(1)} %add.3.here), channel_id=1, source_target_pairs={{1,3},{3,1},{5,7},{7,5},{9,11},{11,9},{13,15},{15,13},{17,19},{19,... | collective-permute-start | bytes 393224 | tf_op jit(solution)/shard_map/ppermute | solution.py:313
  17.4 2.0 %collective-permute-start.3 = (f32[24,1024]{1,0:T(8,128)S(1)}, f32[24,1024]{1,0:T(8,128)S(1)}, u32[]{:S(2)}, u32[]{:S(2)}) collective-permute-start(f32[24,1024]{1,0:T(8,128)S(1)} %get-tuple-element.7), channel_id=1, source_target_pairs={{1,9},{3,11},{5,13},{7,15},{9,1},{11,3},{13,5},{15,7},{17,25},{19,... | collective-permute-start | bytes 294920 | tf_op jit(solution)/shard_map/ppermute | solution.py:315
  18.1 1.4 %collective-permute-start.4 = (f32[24,1024]{1,0:T(8,128)S(1)}, f32[24,1024]{1,0:T(8,128)S(1)}, u32[]{:S(2)}, u32[]{:S(2)}) collective-permute-start(f32[24,1024]{1,0:T(8,128)S(1)} %get-tuple-element.8), channel_id=1, source_target_pairs={{1,13},{3,15},{5,9},{7,11},{9,5},{11,7},{13,1},{15,3},{17,29},{19,... | collective-permute-start | bytes 294920 | tf_op jit(solution)/shard_map/ppermute | solution.py:315
  18.7 0.7 %collective-permute-start.5 = (f32[24,1024]{1,0:T(8,128)S(1)}, f32[24,1024]{1,0:T(8,128)S(1)}, u32[]{:S(2)}, u32[]{:S(2)}) collective-permute-start(f32[24,1024]{1,0:T(8,128)S(1)} %get-tuple-element.9), channel_id=1, source_target_pairs={{1,5},{3,7},{5,1},{7,3},{9,13},{11,15},{13,9},{15,11},{17,21},{19,... | collective-permute-start | bytes 294920 | tf_op jit(solution)/shard_map/ppermute | solution.py:315
  19.5 18.2 %collective-permute-start.6 = (f32[64,1024]{1,0:T(8,128)S(1)}, f32[64,1024]{1,0:T(8,128)S(1)}, u32[]{:S(2)}, u32[]{:S(2)}) collective-permute-start(f32[64,1024]{1,0:T(8,128)S(1)} %bundle.1), channel_id=1, source_target_pairs={{1,0},{3,2},{5,4},{7,6},{9,8},{11,10},{13,12},{15,14},{17,16},{19,... | collective-permute-start | bytes 786440 | tf_op jit(solution)/shard_map/ppermute | solution.py:322

commit v9 on v8

--- a/solution.py
+++ b/solution.py
@@ -309,17 +309,21 @@
         ) / left.shape[0]
         return mine, fisher
 
-    kron = kron + lax.ppermute(kron, PLANE, [(0, 1), (2, 3)])
-    parcels = list(parcels_of(kron, lax.ppermute(kron, PLANE, [(1, 3), (3, 1)]), dp))
+    kron = kron + lax.ppermute(kron, PLANE, [(0, 1), (1, 0), (2, 3), (3, 2)])
+    parcels = list(parcels_of(kron, lax.ppermute(kron, PLANE, [(0, 0), (1, 3), (2, 2), (3, 1)]), dp))
     parcels = parcels[:1] + [
         lax.ppermute(
             parcels[k],
             ("dp",) + PLANE,
-            [(shards * d + place, shards * (d ^ k) + place) for d in range(dp) for place in (1, 3)],
+            [
+                (shards * d + place, shards * (d ^ k * (place % 2)) + place)
+                for d in range(dp)
+                for place in range(shards)
+            ],
         )
         for k in (2, 3, 1)
     ]
-    bundle = lax.ppermute(bundle_of(parcels), PLANE, [(1, 0), (3, 2)])
+    bundle = lax.ppermute(bundle_of(parcels), PLANE, [(0, 1), (1, 0), (2, 3), (3, 2)])
     mine, fisher = fisher_block(parcels, bundle)
     return mine, fisher
 

time: 40.4 us -> 38.1 us (0.943)
  waiting for transfers between devices: 17.9 us -> 2.51 us
  starting transfers between devices: 8.43 us -> 21.5 us
    ppermute x3, waiting for transfers between devices: 17.8 us -> 2.5 us  [the longest x1 1.33 us: local(): kron = kron + lax.ppermute(kron, PLANE, [(0, 1), (1, 0), (2, 3), (3, 2)])]
    ppermute x3, starting transfers between devices: 3.42 us -> 16.5 us  [the longest x1 15.7 us: local(): lax.ppermute(bundle_of(parcels), PLANE, [(0, 1), (1, 0), (2, 3), (3, 2)])]
  transfers between devices with their start and end apart: 7 -> 7, of which waited for: 2 -> 2; matrix products, arithmetic and copies ran while one was open for 0% -> 0% of each run, Pallas kernels for 17% -> 19%
where the time goes in v9:
time: 38.1 us; the launch traced here: 37.9 us
  starting transfers between devices  21.5 us (56%)
  Pallas kernels  13.1 us (34%)
  waiting for transfers between devices  2.51 us (7%)
  between operations  0.78 us (2%)
    ppermute x1, starting transfers between devices, local(): lax.ppermute(bundle_of(parcels), PLANE, [(0, 1), (1, 0), (2, 3), (3, 2)])  15.7 us
    pallas_call x2, Pallas kernels, project(): pl.pallas_call(functools.partial(project_kernel, widths, fetch), out_shap...  9.93 us
    ppermute x1, starting transfers between devices, local(): act_parts = [act, lax.ppermute(act, 'tensor', [(0, 1), (1, 0)])]  3 us
    pallas_call x1, Pallas kernels, fisher_block(): pl.pallas_call(functools.partial(fisher_kernel, 1.0 / total), out_shape=[...  2.54 us
    ppermute x3, starting transfers between devices, local(): lax.ppermute(parcels[k], ('dp',) + PLANE, [(shards * d + place, shards *...  2 us
    ppermute x1, waiting for transfers between devices, local(): kron = kron + lax.ppermute(kron, PLANE, [(0, 1), (1, 0), (2, 3), (3, 2)])  1.33 us
    ppermute x1, waiting for transfers between devices, local(): lax.ppermute(bundle_of(parcels), PLANE, [(0, 1), (1, 0), (2, 3), (3, 2)])  1.16 us
  transfers between devices with their start and end apart: 7, of which 2 were waited for; matrix products, arithmetic and copies ran while one was open for 0% of the time, Pallas kernels for 19%

profile of v9, /device:TPU:0, one launch (start us, length us, event | category | flops | bytes accessed | tf_op | source)
XLA Modules:
  0.0 37.9 jit_solution(1273639608318296403)
XLA Ops:
  0.6 0.0 copy-start
  0.6 0.0 copy-start.2
  0.7 0.0 copy-start.1
  0.7 2.9 %project_acts.1.acts = f32[4,128,128]{2,1,0:T(8,128)S(1)} custom-call(s32[32]{0:T(128)} %ids.2, s32[32]{0:T(128)} %signs.2, bf16[32,4096]{1,0:T(8,128)(2,1)} %table.2, bf16[1024,2048]{1,0:T(8,128)(2,1)} %bitcast.3), custom_call_target="tpu_custom_call" | custom-call | flops 536870912 | bytes 4194304 | tf_op jit(solution)/shard_map/project_acts/pallas_call | solution.py:118
  3.6 3.0 %collective-permute-start = (f32[4,128,128]{2,1,0:T(8,128)S(1)}, f32[4,128,128]{2,1,0:T(8,128)S(1)}, u32[]{:S(2)}, u32[]{:S(2)}) collective-permute-start(f32[4,128,128]{2,1,0:T(8,128)S(1)} %project_acts.1.acts), channel_id=1, source_target_pairs={{0,2},{2,0},{1,3},{3,1},{4,6},{6,4},{5,7},{7,5},{8,10},{10,8},{9,1... | collective-permute-start | bytes 786440 | tf_op jit(solution)/shard_map/ppermute | solution.py:292
  6.6 0.0 copy-done
  6.6 0.0 copy-done.2
  6.6 0.0 copy-done.1
  6.6 7.0 %project_grads.1.grads = f32[4,128,128]{2,1,0:T(8,128)S(1)} custom-call(s32[112]{0:T(128)S(1)} %copy-done.1, s32[112]{0:T(128)S(1)} %copy-done.2, bf16[32,4096]{1,0:T(8,128)(2,1)S(1)} %copy-done, bf16[1024,7168]{1,0:T(8,128)(2,1)} %bitcast.2), custom_call_target="tpu_custom_call" | custom-call | flops 1879048192 | bytes 14680064 | tf_op jit(solution)/shard_map/project_grads/pallas_call | solution.py:118
  13.6 0.0 collective-permute-done.refs_0_
  13.6 0.6 %kron.1 = f32[8,4096]{1,0:T(8,128)S(1)} custom-call(f32[4,128,128]{2,1,0:T(8,128)S(1)} %project_acts.1.acts, f32[4,128,128]{2,1,0:T(8,128)S(1)} %project_grads.1.grads, f32[4,128,128]{2,1,0:T(8,128)S(1)} %collective-permute-done.refs_0_), custom_call_target="tpu_custom_call" | custom-call | tf_op jit(solution)/shard_map/kron/pallas_call | solution.py:169
  14.2 0.1 collective-permute-start.1
  14.3 1.3 %collective-permute-done.1 = f32[8,4096]{1,0:T(8,128)S(1)} collective-permute-done((f32[8,4096]{1,0:T(8,128)S(1)}, f32[8,4096]{1,0:T(8,128)S(1)}, u32[]{:S(2)}, u32[]{:S(2)}) %collective-permute-start.1) | collective-permute-done | bytes 131104 | tf_op jit(solution)/shard_map/ppermute | solution.py:312
  15.6 0.7 %collective-permute-start.2 = (f32[8,4096]{1,0:T(8,128)S(1)}, f32[8,4096]{1,0:T(8,128)S(1)}, u32[]{:S(2)}, u32[]{:S(2)}) collective-permute-start(f32[8,4096]{1,0:T(8,128)S(1)} %add.3.here), channel_id=1, source_target_pairs={{0,0},{1,3},{2,2},{3,1},{4,4},{5,7},{6,6},{7,5},{8,8},{9,11},{10,1... | collective-permute-start | bytes 393224 | tf_op jit(solution)/shard_map/ppermute | solution.py:313
  16.3 0.0 collective-permute-done.2.there
  16.4 0.7 %collective-permute-start.3 = (f32[24,1024]{1,0:T(8,128)S(1)}, f32[24,1024]{1,0:T(8,128)S(1)}, u32[]{:S(2)}, u32[]{:S(2)}) collective-permute-start(f32[24,1024]{1,0:T(8,128)S(1)} %get-tuple-element.7), channel_id=1, source_target_pairs={{0,0},{1,9},{2,2},{3,11},{4,4},{5,13},{6,6},{7,15},{8,8},{9,1},{10... | collective-permute-start | bytes 294920 | tf_op jit(solution)/shard_map/ppermute | solution.py:315
  17.1 0.7 %collective-permute-start.4 = (f32[24,1024]{1,0:T(8,128)S(1)}, f32[24,1024]{1,0:T(8,128)S(1)}, u32[]{:S(2)}, u32[]{:S(2)}) collective-permute-start(f32[24,1024]{1,0:T(8,128)S(1)} %get-tuple-element.8), channel_id=1, source_target_pairs={{0,0},{1,13},{2,2},{3,15},{4,4},{5,9},{6,6},{7,11},{8,8},{9,5},{10... | collective-permute-start | bytes 294920 | tf_op jit(solution)/shard_map/ppermute | solution.py:315
  17.7 0.7 %collective-permute-start.5 = (f32[24,1024]{1,0:T(8,128)S(1)}, f32[24,1024]{1,0:T(8,128)S(1)}, u32[]{:S(2)}, u32[]{:S(2)}) collective-permute-start(f32[24,1024]{1,0:T(8,128)S(1)} %get-tuple-element.9), channel_id=1, source_target_pairs={{0,0},{1,5},{2,2},{3,7},{4,4},{5,1},{6,6},{7,3},{8,8},{9,13},{10,1... | collective-permute-start | bytes 294920 | tf_op jit(solution)/shard_map/ppermute | solution.py:315
  18.4 0.0 collective-permute-done.3.refs_1_
  18.4 0.0 collective-permute-done.4.refs_2_
  18.4 0.0 collective-permute-done.5.refs_3_
  18.5 15.7 %collective-permute-start.6 = (f32[64,1024]{1,0:T(8,128)S(1)}, f32[64,1024]{1,0:T(8,128)S(1)}, u32[]{:S(2)}, u32[]{:S(2)}) collective-permute-start(f32[64,1024]{1,0:T(8,128)S(1)} %bundle.1), channel_id=1, source_target_pairs={{0,1},{1,0},{2,3},{3,2},{4,5},{5,4},{6,7},{7,6},{8,9},{9,8},{10,11... | collective-permute-start | bytes 786440 | tf_op jit(solution)/shard_map/ppermute | solution.py:326
  34.2 1.2 %collective-permute-done.6.bundle = f32[64,1024]{1,0:T(8,128)S(1)} collective-permute-done((f32[64,1024]{1,0:T(8,128)S(1)}, f32[64,1024]{1,0:T(8,128)S(1)}, u32[]{:S(2)}, u32[]{:S(2)}) %collective-permute-start.6) | collective-permute-done | bytes 262176 | tf_op jit(solution)/shard_map/ppermute | solution.py:326
  35.4 2.5 %fisher.1 = (f32[8,1024]{1,0:T(8,128)}, f32[1024,1024]{1,0:T(8,128)}) custom-call(f32[64,1024]{1,0:T(8,128)S(1)} %collective-permute-done.6.bundle, f32[24,1024]{1,0:T(8,128)S(1)} %get-tuple-element.6.refs_0_, f32[24,1024]{1,0:T(8,128)S(1)} %collective-permute-done.3.refs_1_, f32[24,1024]{1,0:T(8,128)S(1)} %collective-permute-done.4.refs_2_, ...), custom_call_target="tpu_custom_call" | custom-call | tf_op jit(solution)/shard_map/fisher/pallas_call | solution.py:265
  (3 shorter events, 0.1 us)
Async XLA Ops:
  0.6 6.0 %copy-start = (bf16[32,4096]{1,0:T(8,128)(2,1)S(1)}, bf16[32,4096]{1,0:T(8,128)(2,1)}, u32[]{:S(2)}) copy-start(bf16[32,4096]{1,0:T(8,128)(2,1)} %table.3) | copy-start | bytes 786436
  0.6 5.9 %copy-start.2 = (s32[112]{0:T(128)S(1)}, s32[112]{0:T(128)}, u32[]{:S(2)}) copy-start(s32[112]{0:T(128)} %signs.3) | copy-start | bytes 1348
  0.7 5.9 %copy-start.1 = (s32[112]{0:T(128)S(1)}, s32[112]{0:T(128)}, u32[]{:S(2)}) copy-start(s32[112]{0:T(128)} %ids.3) | copy-start | bytes 1348
  3.6 10.0 %collective-permute-start = (f32[4,128,128]{2,1,0:T(8,128)S(1)}, f32[4,128,128]{2,1,0:T(8,128)S(1)}, u32[]{:S(2)}, u32[]{:S(2)}) collective-permute-start(f32[4,128,128]{2,1,0:T(8,128)S(1)} %project_acts.1.acts), channel_id=1, source_target_pairs={{0,2},{2,0},{1,3},{3,1},{4,6},{6,4},{5,7},{7,5},{8,10},{10,8},{9,1... | collective-permute-start | bytes 786440 | tf_op jit(solution)/shard_map/ppermute | solution.py:292
  14.2 1.4 %collective-permute-start.1 = (f32[8,4096]{1,0:T(8,128)S(1)}, f32[8,4096]{1,0:T(8,128)S(1)}, u32[]{:S(2)}, u32[]{:S(2)}) collective-permute-start(f32[8,4096]{1,0:T(8,128)S(1)} %kron.1), channel_id=1, source_target_pairs={{0,1},{1,0},{2,3},{3,2},{4,5},{5,4},{6,7},{7,6},{8,9},{9,8},{10,11... | collective-permute-start | bytes 393224 | tf_op jit(solution)/shard_map/ppermute | solution.py:312
  15.6 0.7 %collective-permute-start.2 = (f32[8,4096]{1,0:T(8,128)S(1)}, f32[8,4096]{1,0:T(8,128)S(1)}, u32[]{:S(2)}, u32[]{:S(2)}) collective-permute-start(f32[8,4096]{1,0:T(8,128)S(1)} %add.3.here), channel_id=1, source_target_pairs={{0,0},{1,3},{2,2},{3,1},{4,4},{5,7},{6,6},{7,5},{8,8},{9,11},{10,1... | collective-permute-start | bytes 393224 | tf_op jit(solution)/shard_map/ppermute | solution.py:313
  16.4 2.0 %collective-permute-start.3 = (f32[24,1024]{1,0:T(8,128)S(1)}, f32[24,1024]{1,0:T(8,128)S(1)}, u32[]{:S(2)}, u32[]{:S(2)}) collective-permute-start(f32[24,1024]{1,0:T(8,128)S(1)} %get-tuple-element.7), channel_id=1, source_target_pairs={{0,0},{1,9},{2,2},{3,11},{4,4},{5,13},{6,6},{7,15},{8,8},{9,1},{10... | collective-permute-start | bytes 294920 | tf_op jit(solution)/shard_map/ppermute | solution.py:315
  17.1 1.4 %collective-permute-start.4 = (f32[24,1024]{1,0:T(8,128)S(1)}, f32[24,1024]{1,0:T(8,128)S(1)}, u32[]{:S(2)}, u32[]{:S(2)}) collective-permute-start(f32[24,1024]{1,0:T(8,128)S(1)} %get-tuple-element.8), channel_id=1, source_target_pairs={{0,0},{1,13},{2,2},{3,15},{4,4},{5,9},{6,6},{7,11},{8,8},{9,5},{10... | collective-permute-start | bytes 294920 | tf_op jit(solution)/shard_map/ppermute | solution.py:315
  17.7 0.7 %collective-permute-start.5 = (f32[24,1024]{1,0:T(8,128)S(1)}, f32[24,1024]{1,0:T(8,128)S(1)}, u32[]{:S(2)}, u32[]{:S(2)}) collective-permute-start(f32[24,1024]{1,0:T(8,128)S(1)} %get-tuple-element.9), channel_id=1, source_target_pairs={{0,0},{1,5},{2,2},{3,7},{4,4},{5,1},{6,6},{7,3},{8,8},{9,13},{10,1... | collective-permute-start | bytes 294920 | tf_op jit(solution)/shard_map/ppermute | solution.py:315
  18.5 16.9 %collective-permute-start.6 = (f32[64,1024]{1,0:T(8,128)S(1)}, f32[64,1024]{1,0:T(8,128)S(1)}, u32[]{:S(2)}, u32[]{:S(2)}) collective-permute-start(f32[64,1024]{1,0:T(8,128)S(1)} %bundle.1), channel_id=1, source_target_pairs={{0,1},{1,0},{2,3},{3,2},{4,5},{5,4},{6,7},{7,6},{8,9},{9,8},{10,11... | collective-permute-start | bytes 786440 | tf_op jit(solution)/shard_map/ppermute | solution.py:326

commit v10 on v5

--- a/solution.py
+++ b/solution.py
@@ -52,8 +52,23 @@
         matrix[pl.ds(j * BLOCK, BLOCK), :] = signed[pl.ds(start, BLOCK), :]
 
 
+def operand(x):
+    x1, x2, x3 = split3(x)
+    return jnp.concatenate([x1, x1, x2, x1, x3, x2], axis=1)
+
+
+def products_with(left, act):
+    a1, a2, a3 = split3(act)
+    right = jnp.concatenate([a1, a2, a1, a3, a1, a2], axis=1)
+    return lax.dot_general(left, right, (((1,), (1,)), ((), ())), preferred_element_type=jnp.float32)
+
+
 def project_kernel(widths, fetch, ids, signs, table, rows_ref, *refs):
-    out, spread, signed, matrix, held, total, sems, *own = refs
+    if fetch:
+        (out,), refs = refs[:1], refs[1:]
+    else:
+        (acts, lefts, products), refs = refs[:3], refs[3:]
+    spread, signed, matrix, held, total, sems, *own = refs
     copies, starts, start = [], [], 0
     for c, width in enumerate(widths):
         columns = pl.ds(start, width)
@@ -93,13 +108,20 @@
             total[...] = part
         else:
             total[...] += part
-    pairs, _, tokens = out.shape
+    pairs, _, tokens = out.shape if fetch else acts.shape
     for pair in range(pairs):
-        for side in range(2):
-            out[pair, pl.ds(side * PROJ, PROJ), :] = total[:, pl.ds((2 * pair + side) * tokens, tokens)]
-
-
-def project(values, ids, signs, table, fetch, most, name):
+        sides = [total[:, pl.ds((2 * pair + side) * tokens, tokens)] for side in range(2)]
+        if fetch:
+            for side in range(2):
+                out[pair, pl.ds(side * PROJ, PROJ), :] = sides[side]
+        else:
+            left = operand(jnp.concatenate(sides, axis=0))
+            lefts[pair] = left
+            products[pl.ds(pair * LANES, LANES), :] = products_with(left, acts[pair])
+
+
+def project(values, ids, signs, table, acts, most, name):
+    fetch = acts is None
     count, tokens, width = values.shape
     widths = chunks_of(width, most)
     rows = count * tokens
@@ -113,13 +135,20 @@
         pltpu.SMEM(signs.shape, signs.dtype),
     ]
     operands = [ids, signs, table, values.reshape(rows, width)]
+    shapes = [jax.ShapeDtypeStruct((count // 2, LANES, tokens), jnp.float32)]
     if fetch:
         operands = [pltpu.with_memory_space_constraint(each, pltpu.HBM) for each in operands]
+    else:
+        operands.append(acts)
+        shapes = [
+            jax.ShapeDtypeStruct((count // 2, LANES, 6 * tokens), jnp.bfloat16),
+            jax.ShapeDtypeStruct((count // 2 * LANES, LANES), jnp.float32),
+        ]
     return pl.pallas_call(
         functools.partial(project_kernel, widths, fetch),
-        out_shape=jax.ShapeDtypeStruct((count // 2, LANES, tokens), jnp.float32),
-        in_specs=[hbm] * 4 if fetch else [smem, smem, vmem, hbm],
-        out_specs=vmem,
+        out_shape=shapes,
+        in_specs=[hbm] * 4 if fetch else [smem, smem, vmem, hbm, vmem],
+        out_specs=[vmem] * len(shapes),
         scratch_shapes=[
             pltpu.VMEM((entries * (BLOCK + 8), LANES), jnp.float32),
             pltpu.VMEM((2 * entries * BLOCK, LANES), jnp.bfloat16),
@@ -137,21 +166,13 @@
     )(*operands)
 
 
-def kron_kernel(cuts, acts, grads, *refs):
+def kron_kernel(cuts, lefts, own, act, *refs):
     parts = cuts[1]
-    summands, outs, rows, products = refs[: -parts - 2], refs[-parts - 2 : -2], refs[-2], refs[-1]
-    pairs = acts.shape[0]
+    outs, rows, products = refs[:-2], refs[-2], refs[-1]
+    pairs = act.shape[0]
     for pair in range(pairs):
-        act = acts[pair]
-        for other in summands:
-            act = act + other[pair]
-        a1, a2, a3 = split3(act)
-        g1, g2, g3 = split3(grads[pair])
-        left = jnp.concatenate([g1, g1, g2, g1, g3, g2], axis=1)
-        right = jnp.concatenate([a1, a2, a1, a3, a1, a2], axis=1)
-        products[pl.ds(pair * LANES, LANES), :] = lax.dot_general(
-            left, right, (((1,), (1,)), ((), ())), preferred_element_type=jnp.float32
-        )
+        into = pl.ds(pair * LANES, LANES)
+        products[into, :] = own[into, :] + products_with(lefts[pair], act[pair])
     count = 2 * pairs
     lower = lax.broadcasted_iota(jnp.int32, (count, LANES), 1) < PROJ
     even = lax.broadcasted_iota(jnp.int32, (count, LANES), 0) % 2 == 0
@@ -169,15 +190,15 @@
         out[...] = rows[part]
 
 
-def kron_of(act_parts, grads, cuts):
-    pairs = grads.shape[0]
+def kron_of(lefts, own, act, cuts):
+    pairs = lefts.shape[0]
     parts = cuts[1]
     width = PROJ * PROJ // parts
     vmem = pl.BlockSpec(memory_space=pltpu.VMEM)
     return pl.pallas_call(
         functools.partial(kron_kernel, cuts),
         out_shape=[jax.ShapeDtypeStruct((2 * pairs, width), jnp.float32)] * parts,
-        in_specs=[vmem] * (1 + len(act_parts)),
+        in_specs=[vmem] * 3,
         out_specs=[vmem] * parts,
         scratch_shapes=[
             pltpu.VMEM((parts, 2 * pairs, width), jnp.float32),
@@ -185,7 +206,7 @@
         ],
         compiler_params=pltpu.CompilerParams(vmem_limit_bytes=VMEM_BYTES),
         name="kron",
-    )(act_parts[0], grads, *act_parts[1:])
+    )(lefts, own, act)
 
 
 def parcels_kernel(here, there, *parcels):
@@ -233,63 +254,115 @@
     )(*parcels)
 
 
-def fisher_kernel(scale, bundle, *refs):
-    parcels, (mine, out, made, kept, left, right, sems) = refs[:-7], refs[-7:]
+def left_operand(x):
+    x1, x2, x3 = split3(x)
+    return jnp.concatenate([x1, x1, x2, x1, x3, x2, x2, x3], axis=0).T
+
+
+def right_operand(x):
+    x1, x2, x3 = split3(x)
+    return jnp.concatenate([x1, x2, x1, x3, x1, x2, x3, x2], axis=0)
+
+
+def own_halves(parcels):
     rows = parcels[0].shape[0] // 3
+    left = jnp.concatenate([parcel[pl.ds(0, rows), :] for parcel in parcels], axis=0)
+    right = jnp.concatenate([parcel[pl.ds(2 * rows, rows), :] for parcel in parcels], axis=0)
+    return left, right
+
+
+def halves_at(part):
+    core = lax.axis_index("seq")
+    return [pl.ds(pl.multiple_of(place * part, part), part) for place in (core, 1 - core)]
+
+
+TILE = 256
+
+
+def quadrant_kernel(scale, *refs):
+    parcels, (out, made, sems) = refs[:-3], refs[-3:]
     part = parcels[0].shape[1]
-    core = lax.axis_index("seq")
-    own = pl.ds(pl.multiple_of(core * part, LANES), part)
-    others = pl.ds(pl.multiple_of((1 - core) * part, LANES), part)
-    for k, parcel in enumerate(parcels):
-        into = pl.ds(k * rows, rows)
-        left[into, own] = parcel[pl.ds(0, rows), :]
-        left[into, others] = bundle[pl.ds(2 * k * rows, rows), :]
-        right[into, own] = parcel[pl.ds(2 * rows, rows), :]
-        right[into, others] = bundle[pl.ds((2 * k + 1) * rows, rows), :]
-    blocks, _, width = made.shape
-    kept[...] = left[pl.ds(0, rows), :]
-    copies = [pltpu.make_async_copy(kept, mine, sems.at[blocks])]
-    copies[0].start()
-    l1, l2, l3 = split3(left[...])
-    r1, r2, r3 = split3(right[...] * scale)
-    left_parts = jnp.concatenate([l1, l1, l2, l1, l3, l2, l2, l3], axis=0).T
-    right_parts = jnp.concatenate([r1, r2, r1, r3, r1, r2, r3, r2], axis=0)
-    for block in range(blocks):
-        columns = slice(block * width, (block + 1) * width)
-        made[block] = jnp.dot(left_parts, right_parts[:, columns], preferred_element_type=jnp.float32)
-        copies.append(
-            pltpu.make_async_copy(made.at[block], out.at[:, pl.ds(block * width, width)], sems.at[block])
-        )
+    left, right = own_halves(parcels)
+    left, right = left_operand(left), right_operand(right * scale)
+    here, _ = halves_at(part)
+    copies = []
+    for k in range(part // TILE):
+        rows = slice(k * TILE, (k + 1) * TILE)
+        made[rows, :] = jnp.dot(left[rows], right, preferred_element_type=jnp.float32)
+        into = pl.ds(pl.multiple_of(lax.axis_index("seq") * part + k * TILE, TILE), TILE)
+        copies.append(pltpu.make_async_copy(made.at[rows], out.at[into, here], sems.at[k]))
         copies[-1].start()
     for copy in copies:
         copy.wait()
 
 
-def fisher_block(parcels, bundle):
+def fisher_kernel(scale, begun, bundle, *refs):
+    del begun
+    parcels, (mine, out, made, kept, sems) = refs[:-5], refs[-5:]
+    rows, part = parcels[0].shape[0] // 3, parcels[0].shape[1]
+    here, there = halves_at(part)
+    kept[:, here] = parcels[0][pl.ds(0, rows), :]
+    kept[:, there] = bundle[pl.ds(0, rows), :]
+    copies = [pltpu.make_async_copy(kept, mine, sems.at[0])]
+    copies[0].start()
+    left, right = own_halves(parcels)
+    count = len(parcels)
+    other_left = jnp.concatenate([bundle[pl.ds(2 * k * rows, rows), :] for k in range(count)], axis=0)
+    other_right = jnp.concatenate([bundle[pl.ds((2 * k + 1) * rows, rows), :] for k in range(count)], axis=0)
+    left, other_left = left_operand(left), left_operand(other_left)
+    right, other_right = right_operand(right * scale), right_operand(other_right * scale)
+    for k, (a, b, into) in enumerate(
+        (
+            (other_left, right, (there, here)),
+            (other_left, other_right, (there, there)),
+            (left, other_right, (here, there)),
+        )
+    ):
+        made[k] = jnp.dot(a, b, preferred_element_type=jnp.float32)
+        copies.append(pltpu.make_async_copy(made.at[k], out.at[into], sems.at[k + 1]))
+        copies[-1].start()
+    for copy in copies:
+        copy.wait()
+
+
+def quadrant_of(parcels):
+    rows, part = parcels[0].shape
+    total = rows // 3 * len(parcels)
+    return pl.pallas_call(
+        functools.partial(quadrant_kernel, 1.0 / total),
+        out_shape=jax.ShapeDtypeStruct((2 * part, 2 * part), jnp.float32),
+        in_specs=[pl.BlockSpec(memory_space=pltpu.VMEM)] * len(parcels),
+        out_specs=pl.BlockSpec(memory_space=pltpu.HBM),
+        scratch_shapes=[pltpu.VMEM((part, part), jnp.float32), pltpu.SemaphoreType.DMA((part // TILE,))],
+        compiler_params=pltpu.CompilerParams(vmem_limit_bytes=VMEM_BYTES),
+        cost_estimate=pl.CostEstimate(flops=2**28, bytes_accessed=4 * part * part, transcendentals=0),
+        name="quadrant",
+    )(*parcels)
+
+
+def fisher_block(begun, parcels, bundle):
     rows, part = parcels[0].shape
     rows //= 3
     width = 2 * part
-    total = rows * len(parcels)
-    blocks = 4
     hbm = pl.BlockSpec(memory_space=pltpu.HBM)
-    return pl.pallas_call(
-        functools.partial(fisher_kernel, 1.0 / total),
+    vmem = pl.BlockSpec(memory_space=pltpu.VMEM)
+    return pl.pallas_call(
+        functools.partial(fisher_kernel, 1.0 / (rows * len(parcels))),
         out_shape=[
             jax.ShapeDtypeStruct((rows, width), jnp.float32),
             jax.ShapeDtypeStruct((width, width), jnp.float32),
         ],
-        in_specs=[pl.BlockSpec(memory_space=pltpu.VMEM)] * (1 + len(parcels)),
+        in_specs=[hbm] + [vmem] * (1 + len(parcels)),
         out_specs=[hbm] * 2,
         scratch_shapes=[
-            pltpu.VMEM((blocks, width, width // blocks), jnp.float32),
+            pltpu.VMEM((3, part, part), jnp.float32),
             pltpu.VMEM((rows, width), jnp.float32),
-            pltpu.VMEM((total, width), jnp.float32),
-            pltpu.VMEM((total, width), jnp.float32),
-            pltpu.SemaphoreType.DMA((blocks + 1,)),
+            pltpu.SemaphoreType.DMA((4,)),
         ],
+        input_output_aliases={0: 1},
         compiler_params=pltpu.CompilerParams(vmem_limit_bytes=VMEM_BYTES),
         name="fisher",
-    )(bundle, *parcels)
+    )(begun, bundle, *parcels)
 
 
 def local(acts, grads, in_ids, in_signs, out_ids, out_signs, in_table, out_table):
@@ -298,13 +371,14 @@
     small = tensor == 2 and seq == 2 and dp == 4
     swap = [(0, 1), (1, 0)]
 
-    act = project(acts, in_ids, in_signs, in_table, True, 512, "project_acts")
+    (act,) = project(acts, in_ids, in_signs, in_table, None, 512, "project_acts")
     if tensor == 2:
-        act_parts = [act, lax.ppermute(act, "tensor", swap)]
+        other = lax.ppermute(act, "tensor", swap)
     else:
-        act_parts = [lax.psum(act, "tensor")]
-    grad = project(grads, out_ids, out_signs, out_table, False, 1024, "project_grads")
-    krons = kron_of(act_parts, grad, (shards, seq) if small else (1, 1))
+        act = lax.psum(act, "tensor")
+        other = jnp.zeros_like(act)
+    lefts, own = project(grads, out_ids, out_signs, out_table, act, 1024, "project_grads")
+    krons = kron_of(lefts, own, other, (shards, seq) if small else (1, 1))
 
     if not small:
         kron = lax.psum(krons[0], ("tensor", "seq"))
@@ -324,7 +398,8 @@
     parcels = list(parcels_of(part, lax.ppermute(part, "tensor", swap), dp))
     for k in range(1, dp):
         parcels[k] = lax.ppermute(parcels[k], "dp", [(d, (d + k) % dp) for d in range(dp)])
-    mine, fisher = fisher_block(parcels, lax.ppermute(bundle_of(parcels), "seq", swap))
+    bundle = lax.ppermute(bundle_of(parcels), "seq", swap)
+    mine, fisher = fisher_block(quadrant_of(parcels), parcels, bundle)
     return mine, fisher
 
 

time: 32.3 us -> 32.1 us (level)
  Pallas kernels: 13.1 us -> 14.1 us
  waiting for transfers between devices: 8.58 us -> 7.58 us
    ppermute x2, waiting for transfers between devices: 1.34 us -> 0.08 us  [the longest x1 0.08 us: local(): bundle = lax.ppermute(bundle_of(parcels), 'seq', swap)]
    pallas_call x1 -> x2, Pallas kernels: 2.55 us -> 3.28 us  [the longest x1 2.02 us: fisher_block(): pl.pallas_call(functools.partial(fisher_kernel, 1.0 / (rows * len(parcels...]
  transfers between devices with their start and end apart: 7 -> 7, of which waited for: 6 -> 6; matrix products, arithmetic and copies ran while one was open for 0% -> 0% of each run, Pallas kernels for 22% -> 27%
where the time goes in v10:
time: 32.1 us; the launch traced here: 31.9 us
  Pallas kernels  14.1 us (44%)
  starting transfers between devices  9.52 us (30%)
  waiting for transfers between devices  7.58 us (24%)
  between operations  0.72 us (2%)
    pallas_call x2, Pallas kernels, project(): pl.pallas_call(functools.partial(project_kernel, widths, fetch), out_shap...  10.2 us
    ppermute x3, starting transfers between devices, local(): lax.ppermute(parcels[k], 'dp', [(d, (d + k) % dp) for d in range(dp)])  5.57 us
    ppermute x1, waiting for transfers between devices, local(): parcels = list(parcels_of(part, lax.ppermute(part, 'tensor', swap), dp))  3.53 us
    ppermute x1, starting transfers between devices, local(): other = lax.ppermute(act, 'tensor', swap)  3 us
    ppermute x3, waiting for transfers between devices, local(): lax.ppermute(parcels[k], 'dp', [(d, (d + k) % dp) for d in range(dp)])  2.73 us
    pallas_call x1, Pallas kernels, fisher_block(): pl.pallas_call(functools.partial(fisher_kernel, 1.0 / (rows * len(parcels...  2.02 us
    pallas_call x1, Pallas kernels, quadrant_of(): pl.pallas_call(functools.partial(quadrant_kernel, 1.0 / total), out_shape...  1.25 us
    ppermute x1, waiting for transfers between devices, local(): part = krons[0] + lax.ppermute(krons[1], 'seq', swap)  1.24 us
  transfers between devices with their start and end apart: 7, of which 6 were waited for; matrix products, arithmetic and copies ran while one was open for 0% of the time, Pallas kernels for 27%

profile of v10, /device:TPU:0, one launch (start us, length us, event | category | flops | bytes accessed | tf_op | source)
XLA Modules:
  0.0 31.9 jit_solution(575218097906275030)
XLA Ops:
  0.6 0.0 copy-start
  0.6 0.0 copy-start.2
  0.7 0.0 copy-start.1
  0.7 2.9 %project_acts.1.refs_0_ = f32[4,128,128]{2,1,0:T(8,128)S(1)} custom-call(s32[32]{0:T(128)} %ids.2, s32[32]{0:T(128)} %signs.2, bf16[32,4096]{1,0:T(8,128)(2,1)} %table.2, bf16[1024,2048]{1,0:T(8,128)(2,1)} %bitcast.3), custom_call_target="tpu_custom_call" | custom-call | flops 536870912 | bytes 4194304 | tf_op jit(solution)/shard_map/project_acts/pallas_call | solution.py:147
  3.6 3.0 %collective-permute-start = (f32[4,128,128]{2,1,0:T(8,128)S(1)}, f32[4,128,128]{2,1,0:T(8,128)S(1)}, u32[]{:S(2)}, u32[]{:S(2)}) collective-permute-start(f32[4,128,128]{2,1,0:T(8,128)S(1)} %project_acts.1.refs_0_), channel_id=1, source_target_pairs={{0,2},{2,0},{1,3},{3,1},{4,6},{6,4},{5,7},{7,5},{8,10},{10,8},{9,1... | collective-permute-start | bytes 786440 | tf_op jit(solution)/shard_map/ppermute | solution.py:376
  6.6 0.0 copy-done
  6.6 0.0 copy-done.2
  6.6 0.0 copy-done.1
  6.6 7.3 %project_grads.1 = (bf16[4,128,768]{2,1,0:T(8,128)(2,1)S(1)}, f32[512,128]{1,0:T(8,128)S(1)}) custom-call(s32[112]{0:T(128)S(1)} %copy-done.1, s32[112]{0:T(128)S(1)} %copy-done.2, bf16[32,4096]{1,0:T(8,128)(2,1)S(1)} %copy-done, bf16[1024,7168]{1,0:T(8,128)(2,1)} %bitcast.2, f32[4,128,128]{2,1,0:T(8,128)S(1)} %project_acts.1.refs_0_), custom_call_target="tpu_custom_call" | custom-call | flops 1879048192 | bytes 14680064 | tf_op jit(solution)/shard_map/project_grads/pallas_call | solution.py:147
  13.9 0.0 collective-permute-done.act
  13.9 0.6 %kron.1 = (f32[8,2048]{1,0:T(8,128)S(1)}, f32[8,2048]{1,0:T(8,128)S(1)}) custom-call(bf16[4,128,768]{2,1,0:T(8,128)(2,1)S(1)} %get-tuple-element.10.lefts, f32[512,128]{1,0:T(8,128)S(1)} %get-tuple-element.11.own, f32[4,128,128]{2,1,0:T(8,128)S(1)} %collective-permute-done.act), custom_call_target="tpu_custom_call" | custom-call | tf_op jit(solution)/shard_map/kron/pallas_call | solution.py:198
  14.5 0.1 collective-permute-start.1
  14.6 1.2 %collective-permute-done.1 = f32[8,2048]{1,0:T(8,128)S(1)} collective-permute-done((f32[8,2048]{1,0:T(8,128)S(1)}, f32[8,2048]{1,0:T(8,128)S(1)}, u32[]{:S(2)}, u32[]{:S(2)}) %collective-permute-start.1) | collective-permute-done | bytes 65568 | tf_op jit(solution)/shard_map/ppermute | solution.py:397
  15.8 0.8 %collective-permute-start.2 = (f32[8,2048]{1,0:T(8,128)S(1)}, f32[8,2048]{1,0:T(8,128)S(1)}, u32[]{:S(2)}, u32[]{:S(2)}) collective-permute-start(f32[8,2048]{1,0:T(8,128)S(1)} %add.3.here), channel_id=1, source_target_pairs={{0,2},{2,0},{1,3},{3,1},{4,6},{6,4},{5,7},{7,5},{8,10},{10,8},{9,1... | collective-permute-start | bytes 196616 | tf_op jit(solution)/shard_map/ppermute | solution.py:398
  16.6 3.5 %collective-permute-done.2.there = f32[8,2048]{1,0:T(8,128)S(1)} collective-permute-done((f32[8,2048]{1,0:T(8,128)S(1)}, f32[8,2048]{1,0:T(8,128)S(1)}, u32[]{:S(2)}, u32[]{:S(2)}) %collective-permute-start.2) | collective-permute-done | bytes 65568 | tf_op jit(solution)/shard_map/ppermute | solution.py:398
  20.2 1.6 %collective-permute-start.3 = (f32[24,512]{1,0:T(8,128)S(1)}, f32[24,512]{1,0:T(8,128)S(1)}, u32[]{:S(2)}, u32[]{:S(2)}) collective-permute-start(f32[24,512]{1,0:T(8,128)S(1)} %get-tuple-element.15), channel_id=1, source_target_pairs={{0,4},{4,8},{8,12},{12,0},{1,5},{5,9},{9,13},{13,1},{2,6},{6,10},{... | collective-permute-start | bytes 147464 | tf_op jit(solution)/shard_map/ppermute | solution.py:400
  21.8 2.6 %collective-permute-start.4 = (f32[24,512]{1,0:T(8,128)S(1)}, f32[24,512]{1,0:T(8,128)S(1)}, u32[]{:S(2)}, u32[]{:S(2)}) collective-permute-start(f32[24,512]{1,0:T(8,128)S(1)} %get-tuple-element.16), channel_id=1, source_target_pairs={{0,8},{4,12},{8,0},{12,4},{1,9},{5,13},{9,1},{13,5},{2,10},{6,14},... | collective-permute-start | bytes 147464 | tf_op jit(solution)/shard_map/ppermute | solution.py:400
  24.4 1.4 %collective-permute-start.5 = (f32[24,512]{1,0:T(8,128)S(1)}, f32[24,512]{1,0:T(8,128)S(1)}, u32[]{:S(2)}, u32[]{:S(2)}) collective-permute-start(f32[24,512]{1,0:T(8,128)S(1)} %get-tuple-element.17), channel_id=1, source_target_pairs={{0,12},{4,0},{8,4},{12,8},{1,13},{5,1},{9,5},{13,9},{2,14},{6,2},{... | collective-permute-start | bytes 147464 | tf_op jit(solution)/shard_map/ppermute | solution.py:400
  25.7 0.8 %collective-permute-done.3.refs_1_ = f32[24,512]{1,0:T(8,128)S(1)} collective-permute-done((f32[24,512]{1,0:T(8,128)S(1)}, f32[24,512]{1,0:T(8,128)S(1)}, u32[]{:S(2)}, u32[]{:S(2)}) %collective-permute-start.3) | collective-permute-done | bytes 49184 | tf_op jit(solution)/shard_map/ppermute | solution.py:400
  26.6 0.6 %collective-permute-done.4.refs_2_ = f32[24,512]{1,0:T(8,128)S(1)} collective-permute-done((f32[24,512]{1,0:T(8,128)S(1)}, f32[24,512]{1,0:T(8,128)S(1)}, u32[]{:S(2)}, u32[]{:S(2)}) %collective-permute-start.4) | collective-permute-done | bytes 49184 | tf_op jit(solution)/shard_map/ppermute | solution.py:400
  27.1 1.3 %collective-permute-done.5.refs_3_ = f32[24,512]{1,0:T(8,128)S(1)} collective-permute-done((f32[24,512]{1,0:T(8,128)S(1)}, f32[24,512]{1,0:T(8,128)S(1)}, u32[]{:S(2)}, u32[]{:S(2)}) %collective-permute-start.5) | collective-permute-done | bytes 49184 | tf_op jit(solution)/shard_map/ppermute | solution.py:400
  28.5 0.1 collective-permute-start.6
  28.6 1.3 %quadrant.1.begun = f32[1024,1024]{1,0:T(8,128)} custom-call(f32[24,512]{1,0:T(8,128)S(1)} %get-tuple-element.14.refs_0_, f32[24,512]{1,0:T(8,128)S(1)} %collective-permute-done.3.refs_1_, f32[24,512]{1,0:T(8,128)S(1)} %collective-permute-done.4.refs_2_, f32[24,512]{1,0:T(8,128)S(1)} %collective-permute-done.5.refs_3_), custom_call_target="tpu_custom_call" | custom-call | flops 268435456 | bytes 1048576 | tf_op jit(solution)/shard_map/quadrant/pallas_call | solution.py:331
  29.8 0.1 collective-permute-done.6.bundle
  29.9 2.0 %fisher.1 = (f32[8,1024]{1,0:T(8,128)}, f32[1024,1024]{1,0:T(8,128)}) custom-call(f32[1024,1024]{1,0:T(8,128)} %quadrant.1.begun, f32[64,512]{1,0:T(8,128)S(1)} %collective-permute-done.6.bundle, f32[24,512]{1,0:T(8,128)S(1)} %get-tuple-element.14.refs_0_, f32[24,512]{1,0:T(8,128)S(1)} %collective-permute-done.3.refs_1_, ...), custom_call_target="tpu_custom_call", output_to_operand_aliasing={{1}: (0, {})} | custom-call | tf_op jit(solution)/shard_map/fisher/pallas_call | solution.py:349
  (3 shorter events, 0.0 us)
Async XLA Ops:
  0.6 6.0 %copy-start = (bf16[32,4096]{1,0:T(8,128)(2,1)S(1)}, bf16[32,4096]{1,0:T(8,128)(2,1)}, u32[]{:S(2)}) copy-start(bf16[32,4096]{1,0:T(8,128)(2,1)} %table.3) | copy-start | bytes 786436
  0.6 5.9 %copy-start.2 = (s32[112]{0:T(128)S(1)}, s32[112]{0:T(128)}, u32[]{:S(2)}) copy-start(s32[112]{0:T(128)} %signs.3) | copy-start | bytes 1348
  0.7 5.9 %copy-start.1 = (s32[112]{0:T(128)S(1)}, s32[112]{0:T(128)}, u32[]{:S(2)}) copy-start(s32[112]{0:T(128)} %ids.3) | copy-start | bytes 1348
  3.6 10.3 %collective-permute-start = (f32[4,128,128]{2,1,0:T(8,128)S(1)}, f32[4,128,128]{2,1,0:T(8,128)S(1)}, u32[]{:S(2)}, u32[]{:S(2)}) collective-permute-start(f32[4,128,128]{2,1,0:T(8,128)S(1)} %project_acts.1.refs_0_), channel_id=1, source_target_pairs={{0,2},{2,0},{1,3},{3,1},{4,6},{6,4},{5,7},{7,5},{8,10},{10,8},{9,1... | collective-permute-start | bytes 786440 | tf_op jit(solution)/shard_map/ppermute | solution.py:376
  14.5 1.3 %collective-permute-start.1 = (f32[8,2048]{1,0:T(8,128)S(1)}, f32[8,2048]{1,0:T(8,128)S(1)}, u32[]{:S(2)}, u32[]{:S(2)}) collective-permute-start(f32[8,2048]{1,0:T(8,128)S(1)} %get-tuple-element.13), channel_id=1, source_target_pairs={{0,1},{1,0},{2,3},{3,2},{4,5},{5,4},{6,7},{7,6},{8,9},{9,8},{10,11... | collective-permute-start | bytes 196616 | tf_op jit(solution)/shard_map/ppermute | solution.py:397
  15.8 4.3 %collective-permute-start.2 = (f32[8,2048]{1,0:T(8,128)S(1)}, f32[8,2048]{1,0:T(8,128)S(1)}, u32[]{:S(2)}, u32[]{:S(2)}) collective-permute-start(f32[8,2048]{1,0:T(8,128)S(1)} %add.3.here), channel_id=1, source_target_pairs={{0,2},{2,0},{1,3},{3,1},{4,6},{6,4},{5,7},{7,5},{8,10},{10,8},{9,1... | collective-permute-start | bytes 196616 | tf_op jit(solution)/shard_map/ppermute | solution.py:398
  20.2 6.4 %collective-permute-start.3 = (f32[24,512]{1,0:T(8,128)S(1)}, f32[24,512]{1,0:T(8,128)S(1)}, u32[]{:S(2)}, u32[]{:S(2)}) collective-permute-start(f32[24,512]{1,0:T(8,128)S(1)} %get-tuple-element.15), channel_id=1, source_target_pairs={{0,4},{4,8},{8,12},{12,0},{1,5},{5,9},{9,13},{13,1},{2,6},{6,10},{... | collective-permute-start | bytes 147464 | tf_op jit(solution)/shard_map/ppermute | solution.py:400
  21.8 5.3 %collective-permute-start.4 = (f32[24,512]{1,0:T(8,128)S(1)}, f32[24,512]{1,0:T(8,128)S(1)}, u32[]{:S(2)}, u32[]{:S(2)}) collective-permute-start(f32[24,512]{1,0:T(8,128)S(1)} %get-tuple-element.16), channel_id=1, source_target_pairs={{0,8},{4,12},{8,0},{12,4},{1,9},{5,13},{9,1},{13,5},{2,10},{6,14},... | collective-permute-start | bytes 147464 | tf_op jit(solution)/shard_map/ppermute | solution.py:400
  24.4 4.1 %collective-permute-start.5 = (f32[24,512]{1,0:T(8,128)S(1)}, f32[24,512]{1,0:T(8,128)S(1)}, u32[]{:S(2)}, u32[]{:S(2)}) collective-permute-start(f32[24,512]{1,0:T(8,128)S(1)} %get-tuple-element.17), channel_id=1, source_target_pairs={{0,12},{4,0},{8,4},{12,8},{1,13},{5,1},{9,5},{13,9},{2,14},{6,2},{... | collective-permute-start | bytes 147464 | tf_op jit(solution)/shard_map/ppermute | solution.py:400
  28.5 1.4 %collective-permute-start.6 = (f32[64,512]{1,0:T(8,128)S(1)}, f32[64,512]{1,0:T(8,128)S(1)}, u32[]{:S(2)}, u32[]{:S(2)}) collective-permute-start(f32[64,512]{1,0:T(8,128)S(1)} %bundle.1), channel_id=1, source_target_pairs={{0,1},{1,0},{2,3},{3,2},{4,5},{5,4},{6,7},{7,6},{8,9},{9,8},{10,11... | collective-permute-start | bytes 393224 | tf_op jit(solution)/shard_map/ppermute | solution.py:401

commit v11 on v10

--- a/solution.py
+++ b/solution.py
@@ -10,6 +10,7 @@
 PROJ = 64
 BLOCK = 64
 LANES = 128
+STRIDE = 72
 VMEM_BYTES = 48 * 1024 * 1024
 
 
@@ -33,23 +34,33 @@
     return high, mid, low
 
 
-def spread_table(table, spread, signed):
+def spread_table(table, spread):
     entries = table.shape[0]
-    stride = spread.shape[0] // entries
     for row in range(0, BLOCK, 2):
         both = table[:, row * PROJ : row * PROJ + LANES].astype(jnp.float32)
-        spread[pl.ds(row, entries, stride=stride), :] = both
-        spread[pl.ds(row + 1, entries, stride=stride), :] = pltpu.roll(both, PROJ, 1)
+        spread[pl.ds(row, entries, stride=STRIDE), :] = both
+        spread[pl.ds(row + 1, entries, stride=STRIDE), :] = pltpu.roll(both, PROJ, 1)
+
+
+def sign_table(spread, signed):
+    entries = spread.shape[0] // STRIDE
     for entry in range(entries):
-        block = spread[pl.ds(entry * stride, BLOCK), :].astype(jnp.bfloat16)
+        block = spread[pl.ds(entry * STRIDE, BLOCK), :].astype(jnp.bfloat16)
         signed[pl.ds((entries + entry) * BLOCK, BLOCK), :] = block
         signed[pl.ds(entry * BLOCK, BLOCK), :] = -block
 
 
-def lay_blocks(ids, signs, entries, signed, matrix, first, last):
+def lay_blocks(ids, signs, spread, signed, matrix, first, last):
+    entries = spread.shape[0] // STRIDE
     for j in range(first, last):
-        start = pl.multiple_of((signs[j] * entries + ids[j]) * BLOCK, BLOCK)
-        matrix[pl.ds(j * BLOCK, BLOCK), :] = signed[pl.ds(start, BLOCK), :]
+        if signed is None:
+            start = pl.multiple_of(ids[j] * STRIDE, 8)
+            sign = (2 * signs[j] - 1).astype(jnp.float32)
+            block = (spread[pl.ds(start, BLOCK), :] * sign).astype(jnp.bfloat16)
+        else:
+            start = pl.multiple_of((signs[j] * entries + ids[j]) * BLOCK, BLOCK)
+            block = signed[pl.ds(start, BLOCK), :]
+        matrix[pl.ds(j * BLOCK, BLOCK), :] = block
 
 
 def operand(x):
@@ -87,11 +98,15 @@
         copy.start()
     if fetch:
         small[0].wait()
-    spread_table(table, spread, signed)
+    spread_table(table, spread)
+    if fetch:
+        signed = None
+    else:
+        sign_table(spread, signed)
     if fetch:
         small[1].wait()
         small[2].wait()
-    lay = functools.partial(lay_blocks, ids, signs, table.shape[0], signed, matrix)
+    lay = functools.partial(lay_blocks, ids, signs, spread, signed, matrix)
     lay(0, widths[0] // BLOCK)
     for c, copy in enumerate(copies):
         columns = pl.ds(starts[c], widths[c])
@@ -150,7 +165,7 @@
         in_specs=[hbm] * 4 if fetch else [smem, smem, vmem, hbm, vmem],
         out_specs=[vmem] * len(shapes),
         scratch_shapes=[
-            pltpu.VMEM((entries * (BLOCK + 8), LANES), jnp.float32),
+            pltpu.VMEM((entries * STRIDE, LANES), jnp.float32),
             pltpu.VMEM((2 * entries * BLOCK, LANES), jnp.bfloat16),
             pltpu.VMEM((width, LANES), jnp.bfloat16),
             pltpu.VMEM((rows, width), jnp.bfloat16),
@@ -171,8 +186,9 @@
     outs, rows, products = refs[:-2], refs[-2], refs[-1]
     pairs = act.shape[0]
     for pair in range(pairs):
-        into = pl.ds(pair * LANES, LANES)
-        products[into, :] = own[into, :] + products_with(lefts[pair], act[pair])
+        both = own[pl.ds(pair * LANES, LANES), :] + products_with(lefts[pair], act[pair])
+        for side in range(2):
+            products[pl.ds((2 * pair + side) * STRIDE, PROJ), :] = both[side * PROJ : (side + 1) * PROJ]
     count = 2 * pairs
     lower = lax.broadcasted_iota(jnp.int32, (count, LANES), 1) < PROJ
     even = lax.broadcasted_iota(jnp.int32, (count, LANES), 0) % 2 == 0
@@ -181,7 +197,7 @@
     for tile in range(PROJ * PROJ // LANES):
         both = []
         for p in (2 * tile, 2 * tile + 1):
-            v = products[pl.ds(p, count, stride=PROJ), :]
+            v = products[pl.ds(p, count, stride=STRIDE), :]
             both.append(jnp.where(here, v, pltpu.roll(v, PROJ, 1)))
         block, part, within = tile // tiles // parts, tile // tiles % parts, tile % tiles
         rows[part, :, pl.ds((block * tiles + within) * LANES, LANES)] = jnp.where(lower, both[0], both[1])
@@ -202,7 +218,7 @@
         out_specs=[vmem] * parts,
         scratch_shapes=[
             pltpu.VMEM((parts, 2 * pairs, width), jnp.float32),
-            pltpu.VMEM((pairs * LANES, LANES), jnp.float32),
+            pltpu.VMEM((2 * pairs * STRIDE, LANES), jnp.float32),
         ],
         compiler_params=pltpu.CompilerParams(vmem_limit_bytes=VMEM_BYTES),
         name="kron",
@@ -211,12 +227,11 @@
 
 def parcels_kernel(here, there, *parcels):
     count = here.shape[0]
-    dp = len(parcels)
     width = parcels[0].shape[1]
     core, chip = lax.axis_index("seq"), lax.axis_index("tensor") * 2
     blocks = [chip + core, chip + 1 - core]
     for k, parcel in enumerate(parcels):
-        for step, block in enumerate(blocks + [lax.rem(lax.axis_index("dp") + k, dp)]):
+        for step, block in enumerate(blocks + [lax.axis_index("dp") ^ k]):
             lanes = pl.ds(pl.multiple_of(block * width, LANES), width)
             parcel[pl.ds(step * count, count), :] = here[:, lanes] + there[:, lanes]
 
@@ -280,10 +295,11 @@
 
 
 def quadrant_kernel(scale, *refs):
-    parcels, (out, made, sems) = refs[:-3], refs[-3:]
+    parcels, (out, left_ref, right_ref, made, sems) = refs[:-5], refs[-5:]
     part = parcels[0].shape[1]
     left, right = own_halves(parcels)
     left, right = left_operand(left), right_operand(right * scale)
+    left_ref[...], right_ref[...] = left, right
     here, _ = halves_at(part)
     copies = []
     for k in range(part // TILE):
@@ -296,7 +312,7 @@
         copy.wait()
 
 
-def fisher_kernel(scale, begun, bundle, *refs):
+def fisher_kernel(scale, begun, left, right, bundle, *refs):
     del begun
     parcels, (mine, out, made, kept, sems) = refs[:-5], refs[-5:]
     rows, part = parcels[0].shape[0] // 3, parcels[0].shape[1]
@@ -305,12 +321,11 @@
     kept[:, there] = bundle[pl.ds(0, rows), :]
     copies = [pltpu.make_async_copy(kept, mine, sems.at[0])]
     copies[0].start()
-    left, right = own_halves(parcels)
     count = len(parcels)
     other_left = jnp.concatenate([bundle[pl.ds(2 * k * rows, rows), :] for k in range(count)], axis=0)
     other_right = jnp.concatenate([bundle[pl.ds((2 * k + 1) * rows, rows), :] for k in range(count)], axis=0)
-    left, other_left = left_operand(left), left_operand(other_left)
-    right, other_right = right_operand(right * scale), right_operand(other_right * scale)
+    left, other_left = left[...], left_operand(other_left)
+    right, other_right = right[...], right_operand(other_right * scale)
     for k, (a, b, into) in enumerate(
         (
             (other_left, right, (there, here)),
@@ -328,11 +343,16 @@
 def quadrant_of(parcels):
     rows, part = parcels[0].shape
     total = rows // 3 * len(parcels)
+    vmem = pl.BlockSpec(memory_space=pltpu.VMEM)
     return pl.pallas_call(
         functools.partial(quadrant_kernel, 1.0 / total),
-        out_shape=jax.ShapeDtypeStruct((2 * part, 2 * part), jnp.float32),
-        in_specs=[pl.BlockSpec(memory_space=pltpu.VMEM)] * len(parcels),
-        out_specs=pl.BlockSpec(memory_space=pltpu.HBM),
+        out_shape=[
+            jax.ShapeDtypeStruct((2 * part, 2 * part), jnp.float32),
+            jax.ShapeDtypeStruct((part, 8 * total), jnp.bfloat16),
+            jax.ShapeDtypeStruct((8 * total, part), jnp.bfloat16),
+        ],
+        in_specs=[vmem] * len(parcels),
+        out_specs=[pl.BlockSpec(memory_space=pltpu.HBM), vmem, vmem],
         scratch_shapes=[pltpu.VMEM((part, part), jnp.float32), pltpu.SemaphoreType.DMA((part // TILE,))],
         compiler_params=pltpu.CompilerParams(vmem_limit_bytes=VMEM_BYTES),
         cost_estimate=pl.CostEstimate(flops=2**28, bytes_accessed=4 * part * part, transcendentals=0),
@@ -352,7 +372,7 @@
             jax.ShapeDtypeStruct((rows, width), jnp.float32),
             jax.ShapeDtypeStruct((width, width), jnp.float32),
         ],
-        in_specs=[hbm] + [vmem] * (1 + len(parcels)),
+        in_specs=[hbm] + [vmem] * (3 + len(parcels)),
         out_specs=[hbm] * 2,
         scratch_shapes=[
             pltpu.VMEM((3, part, part), jnp.float32),
@@ -362,7 +382,7 @@
         input_output_aliases={0: 1},
         compiler_params=pltpu.CompilerParams(vmem_limit_bytes=VMEM_BYTES),
         name="fisher",
-    )(begun, bundle, *parcels)
+    )(*begun, bundle, *parcels)
 
 
 def local(acts, grads, in_ids, in_signs, out_ids, out_signs, in_table, out_table):
@@ -397,7 +417,7 @@
     part = krons[0] + lax.ppermute(krons[1], "seq", swap)
     parcels = list(parcels_of(part, lax.ppermute(part, "tensor", swap), dp))
     for k in range(1, dp):
-        parcels[k] = lax.ppermute(parcels[k], "dp", [(d, (d + k) % dp) for d in range(dp)])
+        parcels[k] = lax.ppermute(parcels[k], "dp", [(d, d ^ k) for d in range(dp)])
     bundle = lax.ppermute(bundle_of(parcels), "seq", swap)
     mine, fisher = fisher_block(quadrant_of(parcels), parcels, bundle)
     return mine, fisher

time: 32.1 us -> 33.8 us (1.053)
  waiting for transfers between devices: 7.58 us -> 10.5 us
  starting transfers between devices: 9.52 us -> 8.41 us
    ppermute x3, waiting for transfers between devices: 2.73 us -> 5.66 us  [local(): parcels[k] = lax.ppermute(parcels[k], 'dp', [(d, d ^ k) for d in range(dp)])]
    ppermute x3, starting transfers between devices: 5.57 us -> 4.45 us  [local(): parcels[k] = lax.ppermute(parcels[k], 'dp', [(d, d ^ k) for d in range(dp)])]
  transfers between devices with their start and end apart: 7 -> 7, of which waited for: 6 -> 6; matrix products, arithmetic and copies ran while one was open for 0% -> 0% of each run, Pallas kernels for 27% -> 25%
where the time goes in v11:
time: 33.8 us; the launch traced here: 33.6 us
  Pallas kernels  14 us (41%)
  waiting for transfers between devices  10.5 us (31%)
  starting transfers between devices  8.41 us (25%)
  between operations  0.72 us (2%)
    pallas_call x2, Pallas kernels, project(): pl.pallas_call(functools.partial(project_kernel, widths, fetch), out_shap...  10.2 us
    ppermute x3, waiting for transfers between devices, local(): parcels[k] = lax.ppermute(parcels[k], 'dp', [(d, d ^ k) for d in range(dp)])  5.66 us
    ppermute x3, starting transfers between devices, local(): parcels[k] = lax.ppermute(parcels[k], 'dp', [(d, d ^ k) for d in range(dp)])  4.45 us
    ppermute x1, waiting for transfers between devices, local(): parcels = list(parcels_of(part, lax.ppermute(part, 'tensor', swap), dp))  3.53 us
    ppermute x1, starting transfers between devices, local(): other = lax.ppermute(act, 'tensor', swap)  3.01 us
    pallas_call x1, Pallas kernels, fisher_block(): pl.pallas_call(functools.partial(fisher_kernel, 1.0 / (rows * len(parcels...  2.02 us
    pallas_call x1, Pallas kernels, quadrant_of(): pl.pallas_call(functools.partial(quadrant_kernel, 1.0 / total), out_shape...  1.25 us
    ppermute x1, waiting for transfers between devices, local(): part = krons[0] + lax.ppermute(krons[1], 'seq', swap)  1.24 us
  transfers between devices with their start and end apart: 7, of which 6 were waited for; matrix products, arithmetic and copies ran while one was open for 0% of the time, Pallas kernels for 25%

profile of v11, /device:TPU:0, one launch (start us, length us, event | category | flops | bytes accessed | tf_op | source)
XLA Modules:
  0.0 33.6 jit_solution(12253693653923202203)
XLA Ops:
  0.6 0.0 copy-start
  0.6 0.0 copy-start.2
  0.7 0.0 copy-start.1
  0.7 2.9 %project_acts.1.refs_0_ = f32[4,128,128]{2,1,0:T(8,128)S(1)} custom-call(s32[32]{0:T(128)} %ids.2, s32[32]{0:T(128)} %signs.2, bf16[32,4096]{1,0:T(8,128)(2,1)} %table.2, bf16[1024,2048]{1,0:T(8,128)(2,1)} %bitcast.3), custom_call_target="tpu_custom_call" | custom-call | flops 536870912 | bytes 4194304 | tf_op jit(solution)/shard_map/project_acts/pallas_call | solution.py:162
  3.5 3.0 %collective-permute-start = (f32[4,128,128]{2,1,0:T(8,128)S(1)}, f32[4,128,128]{2,1,0:T(8,128)S(1)}, u32[]{:S(2)}, u32[]{:S(2)}) collective-permute-start(f32[4,128,128]{2,1,0:T(8,128)S(1)} %project_acts.1.refs_0_), channel_id=1, source_target_pairs={{0,2},{2,0},{1,3},{3,1},{4,6},{6,4},{5,7},{7,5},{8,10},{10,8},{9,1... | collective-permute-start | bytes 786440 | tf_op jit(solution)/shard_map/ppermute | solution.py:396
  6.6 0.0 copy-done
  6.6 0.0 copy-done.2
  6.6 0.0 copy-done.1
  6.6 7.3 %project_grads.1 = (bf16[4,128,768]{2,1,0:T(8,128)(2,1)S(1)}, f32[512,128]{1,0:T(8,128)S(1)}) custom-call(s32[112]{0:T(128)S(1)} %copy-done.1, s32[112]{0:T(128)S(1)} %copy-done.2, bf16[32,4096]{1,0:T(8,128)(2,1)S(1)} %copy-done, bf16[1024,7168]{1,0:T(8,128)(2,1)} %bitcast.2, f32[4,128,128]{2,1,0:T(8,128)S(1)} %project_acts.1.refs_0_), custom_call_target="tpu_custom_call" | custom-call | flops 1879048192 | bytes 14680064 | tf_op jit(solution)/shard_map/project_grads/pallas_call | solution.py:162
  13.8 0.0 collective-permute-done.act
  13.9 0.5 %kron.1 = (f32[8,2048]{1,0:T(8,128)S(1)}, f32[8,2048]{1,0:T(8,128)S(1)}) custom-call(bf16[4,128,768]{2,1,0:T(8,128)(2,1)S(1)} %get-tuple-element.13.lefts, f32[512,128]{1,0:T(8,128)S(1)} %get-tuple-element.14.own, f32[4,128,128]{2,1,0:T(8,128)S(1)} %collective-permute-done.act), custom_call_target="tpu_custom_call" | custom-call | tf_op jit(solution)/shard_map/kron/pallas_call | solution.py:214
  14.4 0.1 collective-permute-start.1
  14.5 1.2 %collective-permute-done.1 = f32[8,2048]{1,0:T(8,128)S(1)} collective-permute-done((f32[8,2048]{1,0:T(8,128)S(1)}, f32[8,2048]{1,0:T(8,128)S(1)}, u32[]{:S(2)}, u32[]{:S(2)}) %collective-permute-start.1) | collective-permute-done | bytes 65568 | tf_op jit(solution)/shard_map/ppermute | solution.py:417
  15.7 0.8 %collective-permute-start.2 = (f32[8,2048]{1,0:T(8,128)S(1)}, f32[8,2048]{1,0:T(8,128)S(1)}, u32[]{:S(2)}, u32[]{:S(2)}) collective-permute-start(f32[8,2048]{1,0:T(8,128)S(1)} %add.3.here), channel_id=1, source_target_pairs={{0,2},{2,0},{1,3},{3,1},{4,6},{6,4},{5,7},{7,5},{8,10},{10,8},{9,1... | collective-permute-start | bytes 196616 | tf_op jit(solution)/shard_map/ppermute | solution.py:418
  16.5 3.5 %collective-permute-done.2.there = f32[8,2048]{1,0:T(8,128)S(1)} collective-permute-done((f32[8,2048]{1,0:T(8,128)S(1)}, f32[8,2048]{1,0:T(8,128)S(1)}, u32[]{:S(2)}, u32[]{:S(2)}) %collective-permute-start.2) | collective-permute-done | bytes 65568 | tf_op jit(solution)/shard_map/ppermute | solution.py:418
  20.1 1.6 %collective-permute-start.3 = (f32[24,512]{1,0:T(8,128)S(1)}, f32[24,512]{1,0:T(8,128)S(1)}, u32[]{:S(2)}, u32[]{:S(2)}) collective-permute-start(f32[24,512]{1,0:T(8,128)S(1)} %get-tuple-element.18), channel_id=1, source_target_pairs={{0,4},{4,0},{8,12},{12,8},{1,5},{5,1},{9,13},{13,9},{2,6},{6,2},{1... | collective-permute-start | bytes 147464 | tf_op jit(solution)/shard_map/ppermute | solution.py:420
  21.7 2.6 %collective-permute-start.4 = (f32[24,512]{1,0:T(8,128)S(1)}, f32[24,512]{1,0:T(8,128)S(1)}, u32[]{:S(2)}, u32[]{:S(2)}) collective-permute-start(f32[24,512]{1,0:T(8,128)S(1)} %get-tuple-element.19), channel_id=1, source_target_pairs={{0,8},{4,12},{8,0},{12,4},{1,9},{5,13},{9,1},{13,5},{2,10},{6,14},... | collective-permute-start | bytes 147464 | tf_op jit(solution)/shard_map/ppermute | solution.py:420
  24.3 0.2 collective-permute-start.5
  24.5 0.2 collective-permute-done.3.refs_1_
  24.7 3.1 %collective-permute-done.4.refs_2_ = f32[24,512]{1,0:T(8,128)S(1)} collective-permute-done((f32[24,512]{1,0:T(8,128)S(1)}, f32[24,512]{1,0:T(8,128)S(1)}, u32[]{:S(2)}, u32[]{:S(2)}) %collective-permute-start.4) | collective-permute-done | bytes 49184 | tf_op jit(solution)/shard_map/ppermute | solution.py:420
  27.8 2.4 %collective-permute-done.5.refs_3_ = f32[24,512]{1,0:T(8,128)S(1)} collective-permute-done((f32[24,512]{1,0:T(8,128)S(1)}, f32[24,512]{1,0:T(8,128)S(1)}, u32[]{:S(2)}, u32[]{:S(2)}) %collective-permute-start.5) | collective-permute-done | bytes 49184 | tf_op jit(solution)/shard_map/ppermute | solution.py:420
  30.2 0.1 collective-permute-start.6
  30.3 1.3 %quadrant.1 = (f32[1024,1024]{1,0:T(8,128)}, bf16[512,256]{1,0:T(8,128)(2,1)S(1)}, bf16[256,512]{1,0:T(8,128)(2,1)S(1)}) custom-call(f32[24,512]{1,0:T(8,128)S(1)} %get-tuple-element.17.refs_0_, f32[24,512]{1,0:T(8,128)S(1)} %collective-permute-done.3.refs_1_, f32[24,512]{1,0:T(8,128)S(1)} %collective-permute-done.4.refs_2_, ...), custom_call_target="tpu_custom_call" | custom-call | flops 268435456 | bytes 1048576 | tf_op jit(solution)/shard_map/quadrant/pallas_call | solution.py:347
  31.5 0.1 collective-permute-done.6.bundle
  31.6 2.0 %fisher.1 = (f32[8,1024]{1,0:T(8,128)}, f32[1024,1024]{1,0:T(8,128)}) custom-call(f32[1024,1024]{1,0:T(8,128)} %get-tuple-element.21.begun, bf16[512,256]{1,0:T(8,128)(2,1)S(1)} %get-tuple-element.22.left, bf16[256,512]{1,0:T(8,128)(2,1)S(1)} %get-tuple-element.23.right, ...), custom_call_target="tpu_custom_call", output_to_operand_aliasing={{1}: (0, {})} | custom-call | tf_op jit(solution)/shard_map/fisher/pallas_call | solution.py:369
  (3 shorter events, 0.0 us)
Async XLA Ops:
  0.6 5.9 %copy-start = (bf16[32,4096]{1,0:T(8,128)(2,1)S(1)}, bf16[32,4096]{1,0:T(8,128)(2,1)}, u32[]{:S(2)}) copy-start(bf16[32,4096]{1,0:T(8,128)(2,1)} %table.3) | copy-start | bytes 786436
  0.6 5.9 %copy-start.2 = (s32[112]{0:T(128)S(1)}, s32[112]{0:T(128)}, u32[]{:S(2)}) copy-start(s32[112]{0:T(128)} %signs.3) | copy-start | bytes 1348
  0.7 5.9 %copy-start.1 = (s32[112]{0:T(128)S(1)}, s32[112]{0:T(128)}, u32[]{:S(2)}) copy-start(s32[112]{0:T(128)} %ids.3) | copy-start | bytes 1348
  3.5 10.3 %collective-permute-start = (f32[4,128,128]{2,1,0:T(8,128)S(1)}, f32[4,128,128]{2,1,0:T(8,128)S(1)}, u32[]{:S(2)}, u32[]{:S(2)}) collective-permute-start(f32[4,128,128]{2,1,0:T(8,128)S(1)} %project_acts.1.refs_0_), channel_id=1, source_target_pairs={{0,2},{2,0},{1,3},{3,1},{4,6},{6,4},{5,7},{7,5},{8,10},{10,8},{9,1... | collective-permute-start | bytes 786440 | tf_op jit(solution)/shard_map/ppermute | solution.py:396
  14.4 1.3 %collective-permute-start.1 = (f32[8,2048]{1,0:T(8,128)S(1)}, f32[8,2048]{1,0:T(8,128)S(1)}, u32[]{:S(2)}, u32[]{:S(2)}) collective-permute-start(f32[8,2048]{1,0:T(8,128)S(1)} %get-tuple-element.16), channel_id=1, source_target_pairs={{0,1},{1,0},{2,3},{3,2},{4,5},{5,4},{6,7},{7,6},{8,9},{9,8},{10,11... | collective-permute-start | bytes 196616 | tf_op jit(solution)/shard_map/ppermute | solution.py:417
  15.7 4.3 %collective-permute-start.2 = (f32[8,2048]{1,0:T(8,128)S(1)}, f32[8,2048]{1,0:T(8,128)S(1)}, u32[]{:S(2)}, u32[]{:S(2)}) collective-permute-start(f32[8,2048]{1,0:T(8,128)S(1)} %add.3.here), channel_id=1, source_target_pairs={{0,2},{2,0},{1,3},{3,1},{4,6},{6,4},{5,7},{7,5},{8,10},{10,8},{9,1... | collective-permute-start | bytes 196616 | tf_op jit(solution)/shard_map/ppermute | solution.py:418
  20.1 4.6 %collective-permute-start.3 = (f32[24,512]{1,0:T(8,128)S(1)}, f32[24,512]{1,0:T(8,128)S(1)}, u32[]{:S(2)}, u32[]{:S(2)}) collective-permute-start(f32[24,512]{1,0:T(8,128)S(1)} %get-tuple-element.18), channel_id=1, source_target_pairs={{0,4},{4,0},{8,12},{12,8},{1,5},{5,1},{9,13},{13,9},{2,6},{6,2},{1... | collective-permute-start | bytes 147464 | tf_op jit(solution)/shard_map/ppermute | solution.py:420
  21.7 6.0 %collective-permute-start.4 = (f32[24,512]{1,0:T(8,128)S(1)}, f32[24,512]{1,0:T(8,128)S(1)}, u32[]{:S(2)}, u32[]{:S(2)}) collective-permute-start(f32[24,512]{1,0:T(8,128)S(1)} %get-tuple-element.19), channel_id=1, source_target_pairs={{0,8},{4,12},{8,0},{12,4},{1,9},{5,13},{9,1},{13,5},{2,10},{6,14},... | collective-permute-start | bytes 147464 | tf_op jit(solution)/shard_map/ppermute | solution.py:420
  24.3 5.9 %collective-permute-start.5 = (f32[24,512]{1,0:T(8,128)S(1)}, f32[24,512]{1,0:T(8,128)S(1)}, u32[]{:S(2)}, u32[]{:S(2)}) collective-permute-start(f32[24,512]{1,0:T(8,128)S(1)} %get-tuple-element.20), channel_id=1, source_target_pairs={{0,12},{4,8},{8,4},{12,0},{1,13},{5,9},{9,5},{13,1},{2,14},{6,10},... | collective-permute-start | bytes 147464 | tf_op jit(solution)/shard_map/ppermute | solution.py:420
  30.2 1.4 %collective-permute-start.6 = (f32[64,512]{1,0:T(8,128)S(1)}, f32[64,512]{1,0:T(8,128)S(1)}, u32[]{:S(2)}, u32[]{:S(2)}) collective-permute-start(f32[64,512]{1,0:T(8,128)S(1)} %bundle.1), channel_id=1, source_target_pairs={{0,1},{1,0},{2,3},{3,2},{4,5},{5,4},{6,7},{7,6},{8,9},{9,8},{10,11... | collective-permute-start | bytes 393224 | tf_op jit(solution)/shard_map/ppermute | solution.py:421

commit v12 on v11

--- a/solution.py
+++ b/solution.py
@@ -14,16 +14,11 @@
 VMEM_BYTES = 48 * 1024 * 1024
 
 
-def chunks_of(width, most):
-    if width >= 4 * most:
-        inner = width - most
-        ends = [most // 2] * 2
-    else:
-        inner, ends = width, []
+def chunk_of(width, most):
     chunk = most
-    while inner % chunk:
+    while width % chunk:
         chunk -= LANES
-    return ends[:1] + [chunk] * (inner // chunk) + ends[1:]
+    return chunk
 
 
 def split3(x):
@@ -44,15 +39,24 @@
 
 def sign_table(spread, signed):
     entries = spread.shape[0] // STRIDE
-    for entry in range(entries):
-        block = spread[pl.ds(entry * STRIDE, BLOCK), :].astype(jnp.bfloat16)
-        signed[pl.ds((entries + entry) * BLOCK, BLOCK), :] = block
-        signed[pl.ds(entry * BLOCK, BLOCK), :] = -block
-
-
-def lay_blocks(ids, signs, spread, signed, matrix, first, last):
+    most = 4 if entries % 4 == 0 else 1
+
+    def some(step, carry):
+        for part in range(most):
+            entry = step * most + part
+            start = pl.multiple_of(entry * STRIDE, 8)
+            block = spread[pl.ds(start, BLOCK), :].astype(jnp.bfloat16)
+            signed[pl.ds(pl.multiple_of((entries + entry) * BLOCK, BLOCK), BLOCK), :] = block
+            signed[pl.ds(pl.multiple_of(entry * BLOCK, BLOCK), BLOCK), :] = -block
+        return carry
+
+    lax.fori_loop(0, entries // most, some, 0)
+
+
+def lay_blocks(ids, signs, spread, signed, matrix, first, count):
     entries = spread.shape[0] // STRIDE
-    for j in range(first, last):
+    for part in range(count):
+        j = first + part
         if signed is None:
             start = pl.multiple_of(ids[j] * STRIDE, 8)
             sign = (2 * signs[j] - 1).astype(jnp.float32)
@@ -60,7 +64,7 @@
         else:
             start = pl.multiple_of((signs[j] * entries + ids[j]) * BLOCK, BLOCK)
             block = signed[pl.ds(start, BLOCK), :]
-        matrix[pl.ds(j * BLOCK, BLOCK), :] = block
+        matrix[pl.ds(part * BLOCK, BLOCK), :] = block
 
 
 def operand(x):
@@ -74,28 +78,28 @@
     return lax.dot_general(left, right, (((1,), (1,)), ((), ())), preferred_element_type=jnp.float32)
 
 
-def project_kernel(widths, fetch, ids, signs, table, rows_ref, *refs):
+def project_kernel(fetch, ids, signs, table, rows_ref, *refs):
     if fetch:
         (out,), refs = refs[:1], refs[1:]
     else:
         (acts, lefts, products), refs = refs[:3], refs[3:]
     spread, signed, matrix, held, total, sems, *own = refs
-    copies, starts, start = [], [], 0
-    for c, width in enumerate(widths):
-        columns = pl.ds(start, width)
-        copies.append(pltpu.make_async_copy(rows_ref.at[:, columns], held.at[:, columns], sems.at[c]))
-        starts.append(start)
-        start += width
+    chunks, _, chunk = held.shape
+
+    def copy_of(c):
+        columns = pl.ds(pl.multiple_of(c * chunk, LANES), chunk)
+        return pltpu.make_async_copy(rows_ref.at[:, columns], held.at[c], sems.at[c])
+
     if fetch:
         small = [
-            pltpu.make_async_copy(source, kept, sems.at[len(widths) + k])
+            pltpu.make_async_copy(source, kept, sems.at[chunks + k])
             for k, (source, kept) in enumerate(zip((table, ids, signs), own))
         ]
         for copy in small:
             copy.start()
         table, ids, signs = own
-    for copy in copies:
-        copy.start()
+    for c in range(chunks):
+        copy_of(c).start()
     if fetch:
         small[0].wait()
     spread_table(table, spread)
@@ -106,23 +110,22 @@
     if fetch:
         small[1].wait()
         small[2].wait()
-    lay = functools.partial(lay_blocks, ids, signs, spread, signed, matrix)
-    lay(0, widths[0] // BLOCK)
-    for c, copy in enumerate(copies):
-        columns = pl.ds(starts[c], widths[c])
-        copy.wait()
-        if c + 1 < len(widths):
-            lay(starts[c + 1] // BLOCK, (starts[c + 1] + widths[c + 1]) // BLOCK)
+    lay = functools.partial(lay_blocks, ids, signs, spread, signed)
+    blocks = chunk // BLOCK
+    total[...] = jnp.zeros_like(total)
+    lay(matrix.at[0], 0, blocks)
+
+    def some(c, carry):
+        copy_of(c).wait()
+        now = lax.rem(c, 2)
         part = lax.dot_general(
-            matrix[columns, :PROJ],
-            held[:, columns],
-            (((0,), (1,)), ((), ())),
-            preferred_element_type=jnp.float32,
+            matrix[now, :, :PROJ], held[c], (((0,), (1,)), ((), ())), preferred_element_type=jnp.float32
         )
-        if c == 0:
-            total[...] = part
-        else:
-            total[...] += part
+        lay(matrix.at[1 - now], lax.min(c + 1, chunks - 1) * blocks, blocks)
+        total[...] += part
+        return carry
+
+    lax.fori_loop(0, chunks, some, 0)
     pairs, _, tokens = out.shape if fetch else acts.shape
     for pair in range(pairs):
         sides = [total[:, pl.ds((2 * pair + side) * tokens, tokens)] for side in range(2)]
@@ -138,7 +141,8 @@
 def project(values, ids, signs, table, acts, most, name):
     fetch = acts is None
     count, tokens, width = values.shape
-    widths = chunks_of(width, most)
+    chunk = chunk_of(width, most)
+    chunks = width // chunk
     rows = count * tokens
     entries = table.shape[0]
     smem = pl.BlockSpec(memory_space=pltpu.SMEM)
@@ -160,17 +164,17 @@
             jax.ShapeDtypeStruct((count // 2 * LANES, LANES), jnp.float32),
         ]
     return pl.pallas_call(
-        functools.partial(project_kernel, widths, fetch),
+        functools.partial(project_kernel, fetch),
         out_shape=shapes,
         in_specs=[hbm] * 4 if fetch else [smem, smem, vmem, hbm, vmem],
         out_specs=[vmem] * len(shapes),
         scratch_shapes=[
             pltpu.VMEM((entries * STRIDE, LANES), jnp.float32),
             pltpu.VMEM((2 * entries * BLOCK, LANES), jnp.bfloat16),
-            pltpu.VMEM((width, LANES), jnp.bfloat16),
-            pltpu.VMEM((rows, width), jnp.bfloat16),
+            pltpu.VMEM((2, chunk, LANES), jnp.bfloat16),
+            pltpu.VMEM((chunks, rows, chunk), jnp.bfloat16),
             pltpu.VMEM((PROJ, rows), jnp.float32),
-            pltpu.SemaphoreType.DMA((len(widths) + 3,)),
+            pltpu.SemaphoreType.DMA((chunks + 3,)),
         ]
         + (own if fetch else []),
         compiler_params=pltpu.CompilerParams(vmem_limit_bytes=VMEM_BYTES),
@@ -227,11 +231,12 @@
 
 def parcels_kernel(here, there, *parcels):
     count = here.shape[0]
+    dp = len(parcels)
     width = parcels[0].shape[1]
     core, chip = lax.axis_index("seq"), lax.axis_index("tensor") * 2
     blocks = [chip + core, chip + 1 - core]
     for k, parcel in enumerate(parcels):
-        for step, block in enumerate(blocks + [lax.axis_index("dp") ^ k]):
+        for step, block in enumerate(blocks + [lax.rem(lax.axis_index("dp") + k, dp)]):
             lanes = pl.ds(pl.multiple_of(block * width, LANES), width)
             parcel[pl.ds(step * count, count), :] = here[:, lanes] + there[:, lanes]
 
@@ -417,7 +422,7 @@
     part = krons[0] + lax.ppermute(krons[1], "seq", swap)
     parcels = list(parcels_of(part, lax.ppermute(part, "tensor", swap), dp))
     for k in range(1, dp):
-        parcels[k] = lax.ppermute(parcels[k], "dp", [(d, d ^ k) for d in range(dp)])
+        parcels[k] = lax.ppermute(parcels[k], "dp", [(d, (d + k) % dp) for d in range(dp)])
     bundle = lax.ppermute(bundle_of(parcels), "seq", swap)
     mine, fisher = fisher_block(quadrant_of(parcels), parcels, bundle)
     return mine, fisher

time: 33.8 us -> 33.3 us (0.985)
  waiting for transfers between devices: 10.5 us -> 8.28 us
  Pallas kernels: 14 us -> 15.3 us
  starting transfers between devices: 8.41 us -> 8.82 us
    ppermute x3, waiting for transfers between devices: 5.66 us -> 2.74 us  [local(): lax.ppermute(parcels[k], 'dp', [(d, (d + k) % dp) for d in range(dp)])]
    pallas_call x2, Pallas kernels: 10.2 us -> 11.4 us  [project(): pl.pallas_call(functools.partial(project_kernel, fetch), out_shape=shapes...]
    ppermute x3, starting transfers between devices: 4.45 us -> 5.56 us  [local(): lax.ppermute(parcels[k], 'dp', [(d, (d + k) % dp) for d in range(dp)])]
    ppermute x1, starting transfers between devices: 0.8 us -> 0.11 us  [local(): parcels = list(parcels_of(part, lax.ppermute(part, 'tensor', swap), dp))]
    ppermute x1, waiting for transfers between devices: 3.53 us -> 4.22 us  [local(): parcels = list(parcels_of(part, lax.ppermute(part, 'tensor', swap), dp))]
  transfers between devices with their start and end apart: 7 -> 7, of which waited for: 6 -> 6; matrix products, arithmetic and copies ran while one was open for 0% -> 0% of each run, Pallas kernels for 25% -> 28%
where the time goes in v12:
time: 33.3 us; the launch traced here: 33.1 us
  Pallas kernels  15.3 us (46%)
  starting transfers between devices  8.82 us (26%)
  waiting for transfers between devices  8.28 us (25%)
  between operations  0.72 us (2%)
    pallas_call x2, Pallas kernels, project(): pl.pallas_call(functools.partial(project_kernel, fetch), out_shape=shapes...  11.4 us
    ppermute x3, starting transfers between devices, local(): lax.ppermute(parcels[k], 'dp', [(d, (d + k) % dp) for d in range(dp)])  5.56 us
    ppermute x1, waiting for transfers between devices, local(): parcels = list(parcels_of(part, lax.ppermute(part, 'tensor', swap), dp))  4.22 us
    ppermute x1, starting transfers between devices, local(): other = lax.ppermute(act, 'tensor', swap)  3.02 us
    ppermute x3, waiting for transfers between devices, local(): lax.ppermute(parcels[k], 'dp', [(d, (d + k) % dp) for d in range(dp)])  2.74 us
    pallas_call x1, Pallas kernels, fisher_block(): pl.pallas_call(functools.partial(fisher_kernel, 1.0 / (rows * len(parcels...  2.02 us
    pallas_call x1, Pallas kernels, quadrant_of(): pl.pallas_call(functools.partial(quadrant_kernel, 1.0 / total), out_shape...  1.25 us
    ppermute x1, waiting for transfers between devices, local(): part = krons[0] + lax.ppermute(krons[1], 'seq', swap)  1.24 us
  transfers between devices with their start and end apart: 7, of which 6 were waited for; matrix products, arithmetic and copies ran while one was open for 0% of the time, Pallas kernels for 28%

profile of v12, /device:TPU:0, one launch (start us, length us, event | category | flops | bytes accessed | tf_op | source)
XLA Modules:
  0.0 33.1 jit_solution(2232754310277903602)
XLA Ops:
  0.6 0.0 copy-start
  0.6 0.0 copy-start.2
  0.7 0.0 copy-start.1
  0.7 3.3 %project_acts.1.refs_0_ = f32[4,128,128]{2,1,0:T(8,128)S(1)} custom-call(s32[32]{0:T(128)} %ids.2, s32[32]{0:T(128)} %signs.2, bf16[32,4096]{1,0:T(8,128)(2,1)} %table.2, bf16[1024,2048]{1,0:T(8,128)(2,1)} %bitcast.3), custom_call_target="tpu_custom_call" | custom-call | flops 536870912 | bytes 4194304 | tf_op jit(solution)/shard_map/project_acts/pallas_call | solution.py:166
  3.9 3.0 %collective-permute-start = (f32[4,128,128]{2,1,0:T(8,128)S(1)}, f32[4,128,128]{2,1,0:T(8,128)S(1)}, u32[]{:S(2)}, u32[]{:S(2)}) collective-permute-start(f32[4,128,128]{2,1,0:T(8,128)S(1)} %project_acts.1.refs_0_), channel_id=1, source_target_pairs={{0,2},{2,0},{1,3},{3,1},{4,6},{6,4},{5,7},{7,5},{8,10},{10,8},{9,1... | collective-permute-start | bytes 786440 | tf_op jit(solution)/shard_map/ppermute | solution.py:401
  7.0 0.0 copy-done
  7.0 0.0 copy-done.2
  7.0 0.0 copy-done.1
  7.0 8.2 %project_grads.1 = (bf16[4,128,768]{2,1,0:T(8,128)(2,1)S(1)}, f32[512,128]{1,0:T(8,128)S(1)}) custom-call(s32[112]{0:T(128)S(1)} %copy-done.1, s32[112]{0:T(128)S(1)} %copy-done.2, bf16[32,4096]{1,0:T(8,128)(2,1)S(1)} %copy-done, bf16[1024,7168]{1,0:T(8,128)(2,1)} %bitcast.2, f32[4,128,128]{2,1,0:T(8,128)S(1)} %project_acts.1.refs_0_), custom_call_target="tpu_custom_call" | custom-call | flops 1879048192 | bytes 14680064 | tf_op jit(solution)/shard_map/project_grads/pallas_call | solution.py:166
  15.1 0.0 collective-permute-done.act
  15.2 0.5 %kron.1 = (f32[8,2048]{1,0:T(8,128)S(1)}, f32[8,2048]{1,0:T(8,128)S(1)}) custom-call(bf16[4,128,768]{2,1,0:T(8,128)(2,1)S(1)} %get-tuple-element.13.lefts, f32[512,128]{1,0:T(8,128)S(1)} %get-tuple-element.14.own, f32[4,128,128]{2,1,0:T(8,128)S(1)} %collective-permute-done.act), custom_call_target="tpu_custom_call" | custom-call | tf_op jit(solution)/shard_map/kron/pallas_call | solution.py:218
  15.7 0.1 collective-permute-start.1
  15.8 1.2 %collective-permute-done.1 = f32[8,2048]{1,0:T(8,128)S(1)} collective-permute-done((f32[8,2048]{1,0:T(8,128)S(1)}, f32[8,2048]{1,0:T(8,128)S(1)}, u32[]{:S(2)}, u32[]{:S(2)}) %collective-permute-start.1) | collective-permute-done | bytes 65568 | tf_op jit(solution)/shard_map/ppermute | solution.py:422
  17.0 0.1 collective-permute-start.2
  17.1 4.2 %collective-permute-done.2.there = f32[8,2048]{1,0:T(8,128)S(1)} collective-permute-done((f32[8,2048]{1,0:T(8,128)S(1)}, f32[8,2048]{1,0:T(8,128)S(1)}, u32[]{:S(2)}, u32[]{:S(2)}) %collective-permute-start.2) | collective-permute-done | bytes 65568 | tf_op jit(solution)/shard_map/ppermute | solution.py:423
  21.4 1.6 %collective-permute-start.3 = (f32[24,512]{1,0:T(8,128)S(1)}, f32[24,512]{1,0:T(8,128)S(1)}, u32[]{:S(2)}, u32[]{:S(2)}) collective-permute-start(f32[24,512]{1,0:T(8,128)S(1)} %get-tuple-element.18), channel_id=1, source_target_pairs={{0,4},{4,8},{8,12},{12,0},{1,5},{5,9},{9,13},{13,1},{2,6},{6,10},{... | collective-permute-start | bytes 147464 | tf_op jit(solution)/shard_map/ppermute | solution.py:425
  23.0 2.6 %collective-permute-start.4 = (f32[24,512]{1,0:T(8,128)S(1)}, f32[24,512]{1,0:T(8,128)S(1)}, u32[]{:S(2)}, u32[]{:S(2)}) collective-permute-start(f32[24,512]{1,0:T(8,128)S(1)} %get-tuple-element.19), channel_id=1, source_target_pairs={{0,8},{4,12},{8,0},{12,4},{1,9},{5,13},{9,1},{13,5},{2,10},{6,14},... | collective-permute-start | bytes 147464 | tf_op jit(solution)/shard_map/ppermute | solution.py:425
  25.6 1.3 %collective-permute-start.5 = (f32[24,512]{1,0:T(8,128)S(1)}, f32[24,512]{1,0:T(8,128)S(1)}, u32[]{:S(2)}, u32[]{:S(2)}) collective-permute-start(f32[24,512]{1,0:T(8,128)S(1)} %get-tuple-element.20), channel_id=1, source_target_pairs={{0,12},{4,0},{8,4},{12,8},{1,13},{5,1},{9,5},{13,9},{2,14},{6,2},{... | collective-permute-start | bytes 147464 | tf_op jit(solution)/shard_map/ppermute | solution.py:425
  26.9 0.8 %collective-permute-done.3.refs_1_ = f32[24,512]{1,0:T(8,128)S(1)} collective-permute-done((f32[24,512]{1,0:T(8,128)S(1)}, f32[24,512]{1,0:T(8,128)S(1)}, u32[]{:S(2)}, u32[]{:S(2)}) %collective-permute-start.3) | collective-permute-done | bytes 49184 | tf_op jit(solution)/shard_map/ppermute | solution.py:425
  27.8 0.6 %collective-permute-done.4.refs_2_ = f32[24,512]{1,0:T(8,128)S(1)} collective-permute-done((f32[24,512]{1,0:T(8,128)S(1)}, f32[24,512]{1,0:T(8,128)S(1)}, u32[]{:S(2)}, u32[]{:S(2)}) %collective-permute-start.4) | collective-permute-done | bytes 49184 | tf_op jit(solution)/shard_map/ppermute | solution.py:425
  28.3 1.3 %collective-permute-done.5.refs_3_ = f32[24,512]{1,0:T(8,128)S(1)} collective-permute-done((f32[24,512]{1,0:T(8,128)S(1)}, f32[24,512]{1,0:T(8,128)S(1)}, u32[]{:S(2)}, u32[]{:S(2)}) %collective-permute-start.5) | collective-permute-done | bytes 49184 | tf_op jit(solution)/shard_map/ppermute | solution.py:425
  29.7 0.1 collective-permute-start.6
  29.8 1.3 %quadrant.1 = (f32[1024,1024]{1,0:T(8,128)}, bf16[512,256]{1,0:T(8,128)(2,1)S(1)}, bf16[256,512]{1,0:T(8,128)(2,1)S(1)}) custom-call(f32[24,512]{1,0:T(8,128)S(1)} %get-tuple-element.17.refs_0_, f32[24,512]{1,0:T(8,128)S(1)} %collective-permute-done.3.refs_1_, f32[24,512]{1,0:T(8,128)S(1)} %collective-permute-done.4.refs_2_, ...), custom_call_target="tpu_custom_call" | custom-call | flops 268435456 | bytes 1048576 | tf_op jit(solution)/shard_map/quadrant/pallas_call | solution.py:352
  31.0 0.1 collective-permute-done.6.bundle
  31.1 2.0 %fisher.1 = (f32[8,1024]{1,0:T(8,128)}, f32[1024,1024]{1,0:T(8,128)}) custom-call(f32[1024,1024]{1,0:T(8,128)} %get-tuple-element.21.begun, bf16[512,256]{1,0:T(8,128)(2,1)S(1)} %get-tuple-element.22.left, bf16[256,512]{1,0:T(8,128)(2,1)S(1)} %get-tuple-element.23.right, ...), custom_call_target="tpu_custom_call", output_to_operand_aliasing={{1}: (0, {})} | custom-call | tf_op jit(solution)/shard_map/fisher/pallas_call | solution.py:374
  (3 shorter events, 0.0 us)
Async XLA Ops:
  0.6 6.3 %copy-start = (bf16[32,4096]{1,0:T(8,128)(2,1)S(1)}, bf16[32,4096]{1,0:T(8,128)(2,1)}, u32[]{:S(2)}) copy-start(bf16[32,4096]{1,0:T(8,128)(2,1)} %table.3) | copy-start | bytes 786436
  0.6 6.3 %copy-start.2 = (s32[112]{0:T(128)S(1)}, s32[112]{0:T(128)}, u32[]{:S(2)}) copy-start(s32[112]{0:T(128)} %signs.3) | copy-start | bytes 1348
  0.7 6.3 %copy-start.1 = (s32[112]{0:T(128)S(1)}, s32[112]{0:T(128)}, u32[]{:S(2)}) copy-start(s32[112]{0:T(128)} %ids.3) | copy-start | bytes 1348
  3.9 11.2 %collective-permute-start = (f32[4,128,128]{2,1,0:T(8,128)S(1)}, f32[4,128,128]{2,1,0:T(8,128)S(1)}, u32[]{:S(2)}, u32[]{:S(2)}) collective-permute-start(f32[4,128,128]{2,1,0:T(8,128)S(1)} %project_acts.1.refs_0_), channel_id=1, source_target_pairs={{0,2},{2,0},{1,3},{3,1},{4,6},{6,4},{5,7},{7,5},{8,10},{10,8},{9,1... | collective-permute-start | bytes 786440 | tf_op jit(solution)/shard_map/ppermute | solution.py:401
  15.7 1.3 %collective-permute-start.1 = (f32[8,2048]{1,0:T(8,128)S(1)}, f32[8,2048]{1,0:T(8,128)S(1)}, u32[]{:S(2)}, u32[]{:S(2)}) collective-permute-start(f32[8,2048]{1,0:T(8,128)S(1)} %get-tuple-element.16), channel_id=1, source_target_pairs={{0,1},{1,0},{2,3},{3,2},{4,5},{5,4},{6,7},{7,6},{8,9},{9,8},{10,11... | collective-permute-start | bytes 196616 | tf_op jit(solution)/shard_map/ppermute | solution.py:422
  17.0 4.3 %collective-permute-start.2 = (f32[8,2048]{1,0:T(8,128)S(1)}, f32[8,2048]{1,0:T(8,128)S(1)}, u32[]{:S(2)}, u32[]{:S(2)}) collective-permute-start(f32[8,2048]{1,0:T(8,128)S(1)} %add.3.here), channel_id=1, source_target_pairs={{0,2},{2,0},{1,3},{3,1},{4,6},{6,4},{5,7},{7,5},{8,10},{10,8},{9,1... | collective-permute-start | bytes 196616 | tf_op jit(solution)/shard_map/ppermute | solution.py:423
  21.4 6.4 %collective-permute-start.3 = (f32[24,512]{1,0:T(8,128)S(1)}, f32[24,512]{1,0:T(8,128)S(1)}, u32[]{:S(2)}, u32[]{:S(2)}) collective-permute-start(f32[24,512]{1,0:T(8,128)S(1)} %get-tuple-element.18), channel_id=1, source_target_pairs={{0,4},{4,8},{8,12},{12,0},{1,5},{5,9},{9,13},{13,1},{2,6},{6,10},{... | collective-permute-start | bytes 147464 | tf_op jit(solution)/shard_map/ppermute | solution.py:425
  23.0 5.3 %collective-permute-start.4 = (f32[24,512]{1,0:T(8,128)S(1)}, f32[24,512]{1,0:T(8,128)S(1)}, u32[]{:S(2)}, u32[]{:S(2)}) collective-permute-start(f32[24,512]{1,0:T(8,128)S(1)} %get-tuple-element.19), channel_id=1, source_target_pairs={{0,8},{4,12},{8,0},{12,4},{1,9},{5,13},{9,1},{13,5},{2,10},{6,14},... | collective-permute-start | bytes 147464 | tf_op jit(solution)/shard_map/ppermute | solution.py:425
  25.6 4.1 %collective-permute-start.5 = (f32[24,512]{1,0:T(8,128)S(1)}, f32[24,512]{1,0:T(8,128)S(1)}, u32[]{:S(2)}, u32[]{:S(2)}) collective-permute-start(f32[24,512]{1,0:T(8,128)S(1)} %get-tuple-element.20), channel_id=1, source_target_pairs={{0,12},{4,0},{8,4},{12,8},{1,13},{5,1},{9,5},{13,9},{2,14},{6,2},{... | collective-permute-start | bytes 147464 | tf_op jit(solution)/shard_map/ppermute | solution.py:425
  29.7 1.4 %collective-permute-start.6 = (f32[64,512]{1,0:T(8,128)S(1)}, f32[64,512]{1,0:T(8,128)S(1)}, u32[]{:S(2)}, u32[]{:S(2)}) collective-permute-start(f32[64,512]{1,0:T(8,128)S(1)} %bundle.1), channel_id=1, source_target_pairs={{0,1},{1,0},{2,3},{3,2},{4,5},{5,4},{6,7},{7,6},{8,9},{9,8},{10,11... | collective-permute-start | bytes 393224 | tf_op jit(solution)/shard_map/ppermute | solution.py:426

commit v13 on v11

--- a/solution.py
+++ b/solution.py
@@ -202,7 +202,7 @@
         block, part, within = tile // tiles // parts, tile // tiles % parts, tile % tiles
         rows[part, :, pl.ds((block * tiles + within) * LANES, LANES)] = jnp.where(lower, both[0], both[1])
     for k, out in enumerate(outs):
-        part = lax.rem(lax.axis_index("seq") + k, parts) if parts > 1 else 0
+        part = lax.rem(lax.axis_index("seq") + k % 2, parts) if parts > 1 else 0
         out[...] = rows[part]
 
 
@@ -210,12 +210,13 @@
     pairs = lefts.shape[0]
     parts = cuts[1]
     width = PROJ * PROJ // parts
+    outs = 4 if parts > 1 else 1
     vmem = pl.BlockSpec(memory_space=pltpu.VMEM)
     return pl.pallas_call(
         functools.partial(kron_kernel, cuts),
-        out_shape=[jax.ShapeDtypeStruct((2 * pairs, width), jnp.float32)] * parts,
+        out_shape=[jax.ShapeDtypeStruct((2 * pairs, width), jnp.float32)] * outs,
         in_specs=[vmem] * 3,
-        out_specs=[vmem] * parts,
+        out_specs=[vmem] * outs,
         scratch_shapes=[
             pltpu.VMEM((parts, 2 * pairs, width), jnp.float32),
             pltpu.VMEM((2 * pairs * STRIDE, LANES), jnp.float32),
@@ -225,28 +226,33 @@
     )(lefts, own, act)
 
 
-def parcels_kernel(here, there, *parcels):
-    count = here.shape[0]
+def parcels_kernel(parts, *refs):
+    summands, parcels = refs[:parts], refs[parts:]
+    count = summands[0].shape[0]
+    dp = len(parcels)
     width = parcels[0].shape[1]
     core, chip = lax.axis_index("seq"), lax.axis_index("tensor") * 2
     blocks = [chip + core, chip + 1 - core]
     for k, parcel in enumerate(parcels):
-        for step, block in enumerate(blocks + [lax.axis_index("dp") ^ k]):
+        for step, block in enumerate(blocks + [lax.rem(lax.axis_index("dp") + k, dp)]):
             lanes = pl.ds(pl.multiple_of(block * width, LANES), width)
-            parcel[pl.ds(step * count, count), :] = here[:, lanes] + there[:, lanes]
-
-
-def parcels_of(here, there, dp):
-    count, width = here.shape
-    vmem = pl.BlockSpec(memory_space=pltpu.VMEM)
-    return pl.pallas_call(
-        parcels_kernel,
+            row = summands[0][:, lanes]
+            for other in summands[1:]:
+                row = row + other[:, lanes]
+            parcel[pl.ds(step * count, count), :] = row
+
+
+def parcels_of(summands, dp):
+    count, width = summands[0].shape
+    vmem = pl.BlockSpec(memory_space=pltpu.VMEM)
+    return pl.pallas_call(
+        functools.partial(parcels_kernel, len(summands)),
         out_shape=[jax.ShapeDtypeStruct((3 * count, width // dp), jnp.float32)] * dp,
-        in_specs=[vmem] * 2,
+        in_specs=[vmem] * len(summands),
         out_specs=[vmem] * dp,
         compiler_params=pltpu.CompilerParams(vmem_limit_bytes=VMEM_BYTES),
         name="parcels",
-    )(here, there)
+    )(*summands)
 
 
 def bundle_kernel(*refs):
@@ -414,10 +420,12 @@
         ) / left.shape[0]
         return mine, fisher
 
-    part = krons[0] + lax.ppermute(krons[1], "seq", swap)
-    parcels = list(parcels_of(part, lax.ppermute(part, "tensor", swap), dp))
+    across = lax.ppermute(krons[1], ("tensor", "seq"), [(p, 3 - p) for p in range(shards)])
+    beside = lax.ppermute(krons[2], "tensor", swap)
+    mate = lax.ppermute(krons[3], "seq", swap)
+    parcels = list(parcels_of([across, beside, mate, krons[0]], dp))
     for k in range(1, dp):
-        parcels[k] = lax.ppermute(parcels[k], "dp", [(d, d ^ k) for d in range(dp)])
+        parcels[k] = lax.ppermute(parcels[k], "dp", [(d, (d + k) % dp) for d in range(dp)])
     bundle = lax.ppermute(bundle_of(parcels), "seq", swap)
     mine, fisher = fisher_block(quadrant_of(parcels), parcels, bundle)
     return mine, fisher

time: 33.8 us -> 31.8 us (0.941)
  waiting for transfers between devices: 10.5 us -> 6.34 us
  starting transfers between devices: 8.41 us -> 10.6 us
    ppermute x5 -> x6, waiting for transfers between devices: 10.4 us -> 6.27 us  [the longest x3 2.89 us: local(): lax.ppermute(parcels[k], 'dp', [(d, (d + k) % dp) for d in range(dp)])]
    ppermute x5 -> x6, starting transfers between devices: 5.33 us -> 7.49 us  [the longest x3 5.57 us: local(): lax.ppermute(parcels[k], 'dp', [(d, (d + k) % dp) for d in range(dp)])]
  transfers between devices with their start and end apart: 7 -> 8, of which waited for: 6 -> 6; matrix products, arithmetic and copies ran while one was open for 0% -> 0% of each run, Pallas kernels for 25% -> 27%
where the time goes in v13:
time: 31.8 us; the launch traced here: 31.6 us
  Pallas kernels  14 us (44%)
  starting transfers between devices  10.6 us (33%)
  waiting for transfers between devices  6.34 us (20%)
  between operations  0.72 us (2%)
    pallas_call x2, Pallas kernels, project(): pl.pallas_call(functools.partial(project_kernel, widths, fetch), out_shap...  10.2 us
    ppermute x3, starting transfers between devices, local(): lax.ppermute(parcels[k], 'dp', [(d, (d + k) % dp) for d in range(dp)])  5.57 us
    ppermute x1, starting transfers between devices, local(): other = lax.ppermute(act, 'tensor', swap)  3 us
    ppermute x3, waiting for transfers between devices, local(): lax.ppermute(parcels[k], 'dp', [(d, (d + k) % dp) for d in range(dp)])  2.89 us
    ppermute x1, waiting for transfers between devices, local(): lax.ppermute(krons[1], ('tensor', 'seq'), [(p, 3 - p) for p in range(shar...  2.53 us
    pallas_call x1, Pallas kernels, fisher_block(): pl.pallas_call(functools.partial(fisher_kernel, 1.0 / (rows * len(parcels...  2.02 us
    pallas_call x1, Pallas kernels, quadrant_of(): pl.pallas_call(functools.partial(quadrant_kernel, 1.0 / total), out_shape...  1.25 us
    ppermute x1, starting transfers between devices, local(): beside = lax.ppermute(krons[2], 'tensor', swap)  1.16 us
  transfers between devices with their start and end apart: 8, of which 6 were waited for; matrix products, arithmetic and copies ran while one was open for 0% of the time, Pallas kernels for 27%

profile of v13, /device:TPU:0, one launch (start us, length us, event | category | flops | bytes accessed | tf_op | source)
XLA Modules:
  0.0 31.6 jit_solution(11618754841849969813)
XLA Ops:
  0.6 0.0 copy-start
  0.6 0.0 copy-start.2
  0.7 0.0 copy-start.1
  0.7 2.9 %project_acts.1.refs_0_ = f32[4,128,128]{2,1,0:T(8,128)S(1)} custom-call(s32[32]{0:T(128)} %ids.2, s32[32]{0:T(128)} %signs.2, bf16[32,4096]{1,0:T(8,128)(2,1)} %table.2, bf16[1024,2048]{1,0:T(8,128)(2,1)} %bitcast.3), custom_call_target="tpu_custom_call" | custom-call | flops 536870912 | bytes 4194304 | tf_op jit(solution)/shard_map/project_acts/pallas_call | solution.py:162
  3.5 3.0 %collective-permute-start = (f32[4,128,128]{2,1,0:T(8,128)S(1)}, f32[4,128,128]{2,1,0:T(8,128)S(1)}, u32[]{:S(2)}, u32[]{:S(2)}) collective-permute-start(f32[4,128,128]{2,1,0:T(8,128)S(1)} %project_acts.1.refs_0_), channel_id=1, source_target_pairs={{0,2},{2,0},{1,3},{3,1},{4,6},{6,4},{5,7},{7,5},{8,10},{10,8},{9,1... | collective-permute-start | bytes 786440 | tf_op jit(solution)/shard_map/ppermute | solution.py:402
  6.6 0.0 copy-done
  6.6 0.0 copy-done.2
  6.6 0.0 copy-done.1
  6.6 7.3 %project_grads.1 = (bf16[4,128,768]{2,1,0:T(8,128)(2,1)S(1)}, f32[512,128]{1,0:T(8,128)S(1)}) custom-call(s32[112]{0:T(128)S(1)} %copy-done.1, s32[112]{0:T(128)S(1)} %copy-done.2, bf16[32,4096]{1,0:T(8,128)(2,1)S(1)} %copy-done, bf16[1024,7168]{1,0:T(8,128)(2,1)} %bitcast.2, f32[4,128,128]{2,1,0:T(8,128)S(1)} %project_acts.1.refs_0_), custom_call_target="tpu_custom_call" | custom-call | flops 1879048192 | bytes 14680064 | tf_op jit(solution)/shard_map/project_grads/pallas_call | solution.py:162
  13.8 0.0 collective-permute-done.act
  13.9 0.5 %kron.1 = (f32[8,2048]{1,0:T(8,128)S(1)}, f32[8,2048]{1,0:T(8,128)S(1)}, f32[8,2048]{1,0:T(8,128)S(1)}, f32[8,2048]{1,0:T(8,128)S(1)}) custom-call(bf16[4,128,768]{2,1,0:T(8,128)(2,1)S(1)} %get-tuple-element.15.lefts, f32[512,128]{1,0:T(8,128)S(1)} %get-tuple-element.16.own, f32[4,128,128]{2,1,0:T(8,128)S(1)} %collective-permute-done.act), custom_call_target="tpu_custom_call" | custom-call | tf_op jit(solution)/shard_map/kron/pallas_call | solution.py:215
  14.4 0.1 collective-permute-start.1
  14.5 1.2 %collective-permute-start.2 = (f32[8,2048]{1,0:T(8,128)S(1)}, f32[8,2048]{1,0:T(8,128)S(1)}, u32[]{:S(2)}, u32[]{:S(2)}) collective-permute-start(f32[8,2048]{1,0:T(8,128)S(1)} %get-tuple-element.18), channel_id=1, source_target_pairs={{0,2},{2,0},{1,3},{3,1},{4,6},{6,4},{5,7},{7,5},{8,10},{10,8},{9,1... | collective-permute-start | bytes 196616 | tf_op jit(solution)/shard_map/ppermute | solution.py:424
  15.6 0.7 %collective-permute-start.3 = (f32[8,2048]{1,0:T(8,128)S(1)}, f32[8,2048]{1,0:T(8,128)S(1)}, u32[]{:S(2)}, u32[]{:S(2)}) collective-permute-start(f32[8,2048]{1,0:T(8,128)S(1)} %get-tuple-element.19), channel_id=1, source_target_pairs={{0,1},{1,0},{2,3},{3,2},{4,5},{5,4},{6,7},{7,6},{8,9},{9,8},{10,11... | collective-permute-start | bytes 196616 | tf_op jit(solution)/shard_map/ppermute | solution.py:425
  16.3 2.5 %collective-permute-done.1.refs_0_ = f32[8,2048]{1,0:T(8,128)S(1)} collective-permute-done((f32[8,2048]{1,0:T(8,128)S(1)}, f32[8,2048]{1,0:T(8,128)S(1)}, u32[]{:S(2)}, u32[]{:S(2)}) %collective-permute-start.1) | collective-permute-done | bytes 65568 | tf_op jit(solution)/shard_map/ppermute | solution.py:423
  18.8 0.8 %collective-permute-done.2.refs_1_ = f32[8,2048]{1,0:T(8,128)S(1)} collective-permute-done((f32[8,2048]{1,0:T(8,128)S(1)}, f32[8,2048]{1,0:T(8,128)S(1)}, u32[]{:S(2)}, u32[]{:S(2)}) %collective-permute-start.2) | collective-permute-done | bytes 65568 | tf_op jit(solution)/shard_map/ppermute | solution.py:424
  19.7 0.0 collective-permute-done.3.refs_2_
  19.7 1.6 %collective-permute-start.4 = (f32[24,512]{1,0:T(8,128)S(1)}, f32[24,512]{1,0:T(8,128)S(1)}, u32[]{:S(2)}, u32[]{:S(2)}) collective-permute-start(f32[24,512]{1,0:T(8,128)S(1)} %get-tuple-element.22), channel_id=1, source_target_pairs={{0,4},{4,8},{8,12},{12,0},{1,5},{5,9},{9,13},{13,1},{2,6},{6,10},{... | collective-permute-start | bytes 147464 | tf_op jit(solution)/shard_map/ppermute | solution.py:428
  21.4 2.6 %collective-permute-start.5 = (f32[24,512]{1,0:T(8,128)S(1)}, f32[24,512]{1,0:T(8,128)S(1)}, u32[]{:S(2)}, u32[]{:S(2)}) collective-permute-start(f32[24,512]{1,0:T(8,128)S(1)} %get-tuple-element.23), channel_id=1, source_target_pairs={{0,8},{4,12},{8,0},{12,4},{1,9},{5,13},{9,1},{13,5},{2,10},{6,14},... | collective-permute-start | bytes 147464 | tf_op jit(solution)/shard_map/ppermute | solution.py:428
  24.0 1.3 %collective-permute-start.6 = (f32[24,512]{1,0:T(8,128)S(1)}, f32[24,512]{1,0:T(8,128)S(1)}, u32[]{:S(2)}, u32[]{:S(2)}) collective-permute-start(f32[24,512]{1,0:T(8,128)S(1)} %get-tuple-element.24), channel_id=1, source_target_pairs={{0,12},{4,0},{8,4},{12,8},{1,13},{5,1},{9,5},{13,9},{2,14},{6,2},{... | collective-permute-start | bytes 147464 | tf_op jit(solution)/shard_map/ppermute | solution.py:428
  25.3 0.4 %collective-permute-done.4.refs_1_ = f32[24,512]{1,0:T(8,128)S(1)} collective-permute-done((f32[24,512]{1,0:T(8,128)S(1)}, f32[24,512]{1,0:T(8,128)S(1)}, u32[]{:S(2)}, u32[]{:S(2)}) %collective-permute-start.4) | collective-permute-done | bytes 49184 | tf_op jit(solution)/shard_map/ppermute | solution.py:428
  25.7 2.1 %collective-permute-done.5.refs_2_ = f32[24,512]{1,0:T(8,128)S(1)} collective-permute-done((f32[24,512]{1,0:T(8,128)S(1)}, f32[24,512]{1,0:T(8,128)S(1)}, u32[]{:S(2)}, u32[]{:S(2)}) %collective-permute-start.5) | collective-permute-done | bytes 49184 | tf_op jit(solution)/shard_map/ppermute | solution.py:428
  27.8 0.4 %collective-permute-done.6.refs_3_ = f32[24,512]{1,0:T(8,128)S(1)} collective-permute-done((f32[24,512]{1,0:T(8,128)S(1)}, f32[24,512]{1,0:T(8,128)S(1)}, u32[]{:S(2)}, u32[]{:S(2)}) %collective-permute-start.6) | collective-permute-done | bytes 49184 | tf_op jit(solution)/shard_map/ppermute | solution.py:428
  28.2 0.1 collective-permute-start.7
  28.3 1.3 %quadrant.1 = (f32[1024,1024]{1,0:T(8,128)}, bf16[512,256]{1,0:T(8,128)(2,1)S(1)}, bf16[256,512]{1,0:T(8,128)(2,1)S(1)}) custom-call(f32[24,512]{1,0:T(8,128)S(1)} %get-tuple-element.21.refs_0_, f32[24,512]{1,0:T(8,128)S(1)} %collective-permute-done.4.refs_1_, f32[24,512]{1,0:T(8,128)S(1)} %collective-permute-done.5.refs_2_, ...), custom_call_target="tpu_custom_call" | custom-call | flops 268435456 | bytes 1048576 | tf_op jit(solution)/shard_map/quadrant/pallas_call | solution.py:353
  29.5 0.1 collective-permute-done.7.bundle
  29.6 2.0 %fisher.1 = (f32[8,1024]{1,0:T(8,128)}, f32[1024,1024]{1,0:T(8,128)}) custom-call(f32[1024,1024]{1,0:T(8,128)} %get-tuple-element.25.begun, bf16[512,256]{1,0:T(8,128)(2,1)S(1)} %get-tuple-element.26.left, bf16[256,512]{1,0:T(8,128)(2,1)S(1)} %get-tuple-element.27.right, ...), custom_call_target="tpu_custom_call", output_to_operand_aliasing={{1}: (0, {})} | custom-call | tf_op jit(solution)/shard_map/fisher/pallas_call | solution.py:375
  (2 shorter events, 0.0 us)
Async XLA Ops:
  0.6 5.9 %copy-start = (bf16[32,4096]{1,0:T(8,128)(2,1)S(1)}, bf16[32,4096]{1,0:T(8,128)(2,1)}, u32[]{:S(2)}) copy-start(bf16[32,4096]{1,0:T(8,128)(2,1)} %table.3) | copy-start | bytes 786436
  0.6 5.9 %copy-start.2 = (s32[112]{0:T(128)S(1)}, s32[112]{0:T(128)}, u32[]{:S(2)}) copy-start(s32[112]{0:T(128)} %signs.3) | copy-start | bytes 1348
  0.7 5.9 %copy-start.1 = (s32[112]{0:T(128)S(1)}, s32[112]{0:T(128)}, u32[]{:S(2)}) copy-start(s32[112]{0:T(128)} %ids.3) | copy-start | bytes 1348
  3.5 10.3 %collective-permute-start = (f32[4,128,128]{2,1,0:T(8,128)S(1)}, f32[4,128,128]{2,1,0:T(8,128)S(1)}, u32[]{:S(2)}, u32[]{:S(2)}) collective-permute-start(f32[4,128,128]{2,1,0:T(8,128)S(1)} %project_acts.1.refs_0_), channel_id=1, source_target_pairs={{0,2},{2,0},{1,3},{3,1},{4,6},{6,4},{5,7},{7,5},{8,10},{10,8},{9,1... | collective-permute-start | bytes 786440 | tf_op jit(solution)/shard_map/ppermute | solution.py:402
  14.4 4.5 %collective-permute-start.1 = (f32[8,2048]{1,0:T(8,128)S(1)}, f32[8,2048]{1,0:T(8,128)S(1)}, u32[]{:S(2)}, u32[]{:S(2)}) collective-permute-start(f32[8,2048]{1,0:T(8,128)S(1)} %get-tuple-element.17), channel_id=1, source_target_pairs={{0,3},{1,2},{2,1},{3,0},{4,7},{5,6},{6,5},{7,4},{8,11},{9,10},{10,... | collective-permute-start | bytes 196616 | tf_op jit(solution)/shard_map/ppermute | solution.py:423
  14.5 5.2 %collective-permute-start.2 = (f32[8,2048]{1,0:T(8,128)S(1)}, f32[8,2048]{1,0:T(8,128)S(1)}, u32[]{:S(2)}, u32[]{:S(2)}) collective-permute-start(f32[8,2048]{1,0:T(8,128)S(1)} %get-tuple-element.18), channel_id=1, source_target_pairs={{0,2},{2,0},{1,3},{3,1},{4,6},{6,4},{5,7},{7,5},{8,10},{10,8},{9,1... | collective-permute-start | bytes 196616 | tf_op jit(solution)/shard_map/ppermute | solution.py:424
  15.6 4.1 %collective-permute-start.3 = (f32[8,2048]{1,0:T(8,128)S(1)}, f32[8,2048]{1,0:T(8,128)S(1)}, u32[]{:S(2)}, u32[]{:S(2)}) collective-permute-start(f32[8,2048]{1,0:T(8,128)S(1)} %get-tuple-element.19), channel_id=1, source_target_pairs={{0,1},{1,0},{2,3},{3,2},{4,5},{5,4},{6,7},{7,6},{8,9},{9,8},{10,11... | collective-permute-start | bytes 196616 | tf_op jit(solution)/shard_map/ppermute | solution.py:425
  19.7 5.9 %collective-permute-start.4 = (f32[24,512]{1,0:T(8,128)S(1)}, f32[24,512]{1,0:T(8,128)S(1)}, u32[]{:S(2)}, u32[]{:S(2)}) collective-permute-start(f32[24,512]{1,0:T(8,128)S(1)} %get-tuple-element.22), channel_id=1, source_target_pairs={{0,4},{4,8},{8,12},{12,0},{1,5},{5,9},{9,13},{13,1},{2,6},{6,10},{... | collective-permute-start | bytes 147464 | tf_op jit(solution)/shard_map/ppermute | solution.py:428
  21.4 6.5 %collective-permute-start.5 = (f32[24,512]{1,0:T(8,128)S(1)}, f32[24,512]{1,0:T(8,128)S(1)}, u32[]{:S(2)}, u32[]{:S(2)}) collective-permute-start(f32[24,512]{1,0:T(8,128)S(1)} %get-tuple-element.23), channel_id=1, source_target_pairs={{0,8},{4,12},{8,0},{12,4},{1,9},{5,13},{9,1},{13,5},{2,10},{6,14},... | collective-permute-start | bytes 147464 | tf_op jit(solution)/shard_map/ppermute | solution.py:428
  24.0 4.2 %collective-permute-start.6 = (f32[24,512]{1,0:T(8,128)S(1)}, f32[24,512]{1,0:T(8,128)S(1)}, u32[]{:S(2)}, u32[]{:S(2)}) collective-permute-start(f32[24,512]{1,0:T(8,128)S(1)} %get-tuple-element.24), channel_id=1, source_target_pairs={{0,12},{4,0},{8,4},{12,8},{1,13},{5,1},{9,5},{13,9},{2,14},{6,2},{... | collective-permute-start | bytes 147464 | tf_op jit(solution)/shard_map/ppermute | solution.py:428
  28.2 1.4 %collective-permute-start.7 = (f32[64,512]{1,0:T(8,128)S(1)}, f32[64,512]{1,0:T(8,128)S(1)}, u32[]{:S(2)}, u32[]{:S(2)}) collective-permute-start(f32[64,512]{1,0:T(8,128)S(1)} %bundle.1), channel_id=1, source_target_pairs={{0,1},{1,0},{2,3},{3,2},{4,5},{5,4},{6,7},{7,6},{8,9},{9,8},{10,11... | collective-permute-start | bytes 393224 | tf_op jit(solution)/shard_map/ppermute | solution.py:429

commit v14 on v13

--- a/solution.py
+++ b/solution.py
@@ -75,11 +75,7 @@
 
 
 def project_kernel(widths, fetch, ids, signs, table, rows_ref, *refs):
-    if fetch:
-        (out,), refs = refs[:1], refs[1:]
-    else:
-        (acts, lefts, products), refs = refs[:3], refs[3:]
-    spread, signed, matrix, held, total, sems, *own = refs
+    out, spread, signed, matrix, held, total, sems, *own = refs
     copies, starts, start = [], [], 0
     for c, width in enumerate(widths):
         columns = pl.ds(start, width)
@@ -123,20 +119,13 @@
             total[...] = part
         else:
             total[...] += part
-    pairs, _, tokens = out.shape if fetch else acts.shape
+    pairs, _, tokens = out.shape
     for pair in range(pairs):
-        sides = [total[:, pl.ds((2 * pair + side) * tokens, tokens)] for side in range(2)]
-        if fetch:
-            for side in range(2):
-                out[pair, pl.ds(side * PROJ, PROJ), :] = sides[side]
-        else:
-            left = operand(jnp.concatenate(sides, axis=0))
-            lefts[pair] = left
-            products[pl.ds(pair * LANES, LANES), :] = products_with(left, acts[pair])
-
-
-def project(values, ids, signs, table, acts, most, name):
-    fetch = acts is None
+        for side in range(2):
+            out[pair, pl.ds(side * PROJ, PROJ), :] = total[:, pl.ds((2 * pair + side) * tokens, tokens)]
+
+
+def project(values, ids, signs, table, fetch, most, name):
     count, tokens, width = values.shape
     widths = chunks_of(width, most)
     rows = count * tokens
@@ -150,20 +139,13 @@
         pltpu.SMEM(signs.shape, signs.dtype),
     ]
     operands = [ids, signs, table, values.reshape(rows, width)]
-    shapes = [jax.ShapeDtypeStruct((count // 2, LANES, tokens), jnp.float32)]
     if fetch:
         operands = [pltpu.with_memory_space_constraint(each, pltpu.HBM) for each in operands]
-    else:
-        operands.append(acts)
-        shapes = [
-            jax.ShapeDtypeStruct((count // 2, LANES, 6 * tokens), jnp.bfloat16),
-            jax.ShapeDtypeStruct((count // 2 * LANES, LANES), jnp.float32),
-        ]
     return pl.pallas_call(
         functools.partial(project_kernel, widths, fetch),
-        out_shape=shapes,
-        in_specs=[hbm] * 4 if fetch else [smem, smem, vmem, hbm, vmem],
-        out_specs=[vmem] * len(shapes),
+        out_shape=jax.ShapeDtypeStruct((count // 2, LANES, tokens), jnp.float32),
+        in_specs=[hbm] * 4 if fetch else [smem, smem, vmem, hbm],
+        out_specs=vmem,
         scratch_shapes=[
             pltpu.VMEM((entries * STRIDE, LANES), jnp.float32),
             pltpu.VMEM((2 * entries * BLOCK, LANES), jnp.bfloat16),
@@ -181,12 +163,12 @@
     )(*operands)
 
 
-def kron_kernel(cuts, lefts, own, act, *refs):
+def kron_kernel(cuts, grads, own, act, *refs):
     parts = cuts[1]
     outs, rows, products = refs[:-2], refs[-2], refs[-1]
     pairs = act.shape[0]
     for pair in range(pairs):
-        both = own[pl.ds(pair * LANES, LANES), :] + products_with(lefts[pair], act[pair])
+        both = products_with(operand(grads[pair]), own[pair] + act[pair])
         for side in range(2):
             products[pl.ds((2 * pair + side) * STRIDE, PROJ), :] = both[side * PROJ : (side + 1) * PROJ]
     count = 2 * pairs
@@ -206,8 +188,8 @@
         out[...] = rows[part]
 
 
-def kron_of(lefts, own, act, cuts):
-    pairs = lefts.shape[0]
+def kron_of(grads, own, act, cuts):
+    pairs = grads.shape[0]
     parts = cuts[1]
     width = PROJ * PROJ // parts
     outs = 4 if parts > 1 else 1
@@ -223,7 +205,7 @@
         ],
         compiler_params=pltpu.CompilerParams(vmem_limit_bytes=VMEM_BYTES),
         name="kron",
-    )(lefts, own, act)
+    )(grads, own, act)
 
 
 def parcels_kernel(parts, *refs):
@@ -330,17 +312,17 @@
     count = len(parcels)
     other_left = jnp.concatenate([bundle[pl.ds(2 * k * rows, rows), :] for k in range(count)], axis=0)
     other_right = jnp.concatenate([bundle[pl.ds((2 * k + 1) * rows, rows), :] for k in range(count)], axis=0)
-    left, other_left = left[...], left_operand(other_left)
     right, other_right = right[...], right_operand(other_right * scale)
-    for k, (a, b, into) in enumerate(
-        (
-            (other_left, right, (there, here)),
-            (other_left, other_right, (there, there)),
-            (left, other_right, (here, there)),
-        )
-    ):
-        made[k] = jnp.dot(a, b, preferred_element_type=jnp.float32)
-        copies.append(pltpu.make_async_copy(made.at[k], out.at[into], sems.at[k + 1]))
+    for k in range(part // TILE):
+        piece = slice(k * TILE, (k + 1) * TILE)
+        made[0, piece, :] = jnp.dot(left[piece, :], other_right, preferred_element_type=jnp.float32)
+        into = pl.ds(pl.multiple_of(lax.axis_index("seq") * part + k * TILE, TILE), TILE)
+        copies.append(pltpu.make_async_copy(made.at[0, piece], out.at[into, there], sems.at[k + 1]))
+        copies[-1].start()
+    other_left = left_operand(other_left)
+    for k, (operand_right, into) in enumerate(((other_right, there), (right, here))):
+        made[k + 1] = jnp.dot(other_left, operand_right, preferred_element_type=jnp.float32)
+        copies.append(pltpu.make_async_copy(made.at[k + 1], out.at[there, into], sems.at[part // TILE + k + 1]))
         copies[-1].start()
     for copy in copies:
         copy.wait()
@@ -383,7 +365,7 @@
         scratch_shapes=[
             pltpu.VMEM((3, part, part), jnp.float32),
             pltpu.VMEM((rows, width), jnp.float32),
-            pltpu.SemaphoreType.DMA((4,)),
+            pltpu.SemaphoreType.DMA((part // TILE + 3,)),
         ],
         input_output_aliases={0: 1},
         compiler_params=pltpu.CompilerParams(vmem_limit_bytes=VMEM_BYTES),
@@ -397,14 +379,14 @@
     small = tensor == 2 and seq == 2 and dp == 4
     swap = [(0, 1), (1, 0)]
 
-    (act,) = project(acts, in_ids, in_signs, in_table, None, 512, "project_acts")
+    act = project(acts, in_ids, in_signs, in_table, True, 512, "project_acts")
     if tensor == 2:
         other = lax.ppermute(act, "tensor", swap)
     else:
         act = lax.psum(act, "tensor")
         other = jnp.zeros_like(act)
-    lefts, own = project(grads, out_ids, out_signs, out_table, act, 1024, "project_grads")
-    krons = kron_of(lefts, own, other, (shards, seq) if small else (1, 1))
+    grad = project(grads, out_ids, out_signs, out_table, False, 1024, "project_grads")
+    krons = kron_of(grad, act, other, (shards, seq) if small else (1, 1))
 
     if not small:
         kron = lax.psum(krons[0], ("tensor", "seq"))

time: 31.8 us -> 31.5 us (level)
  transfers between devices with their start and end apart: 8 -> 8, of which waited for: 6 -> 6; matrix products, arithmetic and copies ran while one was open for 0% -> 0% of each run, Pallas kernels for 27% -> 26%
where the time goes in v14:
time: 31.5 us; the launch traced here: 31.3 us
  Pallas kernels  13.7 us (43%)
  starting transfers between devices  10.6 us (34%)
  waiting for transfers between devices  6.37 us (20%)
  between operations  0.72 us (2%)
    pallas_call x2, Pallas kernels, project(): pl.pallas_call(functools.partial(project_kernel, widths, fetch), out_shap...  9.89 us
    ppermute x3, starting transfers between devices, local(): lax.ppermute(parcels[k], 'dp', [(d, (d + k) % dp) for d in range(dp)])  5.56 us
    ppermute x1, starting transfers between devices, local(): other = lax.ppermute(act, 'tensor', swap)  3.01 us
    ppermute x3, waiting for transfers between devices, local(): lax.ppermute(parcels[k], 'dp', [(d, (d + k) % dp) for d in range(dp)])  2.89 us
    ppermute x1, waiting for transfers between devices, local(): lax.ppermute(krons[1], ('tensor', 'seq'), [(p, 3 - p) for p in range(shar...  2.53 us
    pallas_call x1, Pallas kernels, fisher_block(): pl.pallas_call(functools.partial(fisher_kernel, 1.0 / (rows * len(parcels...  1.95 us
    pallas_call x1, Pallas kernels, quadrant_of(): pl.pallas_call(functools.partial(quadrant_kernel, 1.0 / total), out_shape...  1.25 us
    ppermute x1, starting transfers between devices, local(): beside = lax.ppermute(krons[2], 'tensor', swap)  1.17 us
  transfers between devices with their start and end apart: 8, of which 6 were waited for; matrix products, arithmetic and copies ran while one was open for 0% of the time, Pallas kernels for 26%

profile of v14, /device:TPU:0, one launch (start us, length us, event | category | flops | bytes accessed | tf_op | source)
XLA Modules:
  0.0 31.3 jit_solution(8002299397659477231)
XLA Ops:
  0.6 0.0 copy-start
  0.6 0.0 copy-start.2
  0.7 0.0 copy-start.1
  0.7 2.9 %project_acts.1.own = f32[4,128,128]{2,1,0:T(8,128)S(1)} custom-call(s32[32]{0:T(128)} %ids.3, s32[32]{0:T(128)} %signs.3, bf16[32,4096]{1,0:T(8,128)(2,1)} %table.3, bf16[1024,2048]{1,0:T(8,128)(2,1)} %bitcast.3), custom_call_target="tpu_custom_call" | custom-call | flops 536870912 | bytes 4194304 | tf_op jit(solution)/shard_map/project_acts/pallas_call | solution.py:144
  3.5 3.0 %collective-permute-start = (f32[4,128,128]{2,1,0:T(8,128)S(1)}, f32[4,128,128]{2,1,0:T(8,128)S(1)}, u32[]{:S(2)}, u32[]{:S(2)}) collective-permute-start(f32[4,128,128]{2,1,0:T(8,128)S(1)} %project_acts.1.own), channel_id=1, source_target_pairs={{0,2},{2,0},{1,3},{3,1},{4,6},{6,4},{5,7},{7,5},{8,10},{10,8},{9,1... | collective-permute-start | bytes 786440 | tf_op jit(solution)/shard_map/ppermute | solution.py:384
  6.6 0.0 copy-done
  6.6 0.0 copy-done.2
  6.6 0.0 copy-done.1
  6.6 7.0 %project_grads.1.grads = f32[4,128,128]{2,1,0:T(8,128)S(1)} custom-call(s32[112]{0:T(128)S(1)} %copy-done.1, s32[112]{0:T(128)S(1)} %copy-done.2, bf16[32,4096]{1,0:T(8,128)(2,1)S(1)} %copy-done, bf16[1024,7168]{1,0:T(8,128)(2,1)} %bitcast.2), custom_call_target="tpu_custom_call" | custom-call | flops 1879048192 | bytes 14680064 | tf_op jit(solution)/shard_map/project_grads/pallas_call | solution.py:144
  13.6 0.0 collective-permute-done.act
  13.6 0.5 %kron.1 = (f32[8,2048]{1,0:T(8,128)S(1)}, f32[8,2048]{1,0:T(8,128)S(1)}, f32[8,2048]{1,0:T(8,128)S(1)}, f32[8,2048]{1,0:T(8,128)S(1)}) custom-call(f32[4,128,128]{2,1,0:T(8,128)S(1)} %project_grads.1.grads, f32[4,128,128]{2,1,0:T(8,128)S(1)} %project_acts.1.own, f32[4,128,128]{2,1,0:T(8,128)S(1)} %collective-permute-done.act), custom_call_target="tpu_custom_call" | custom-call | tf_op jit(solution)/shard_map/kron/pallas_call | solution.py:197
  14.1 0.1 collective-permute-start.1
  14.2 1.2 %collective-permute-start.2 = (f32[8,2048]{1,0:T(8,128)S(1)}, f32[8,2048]{1,0:T(8,128)S(1)}, u32[]{:S(2)}, u32[]{:S(2)}) collective-permute-start(f32[8,2048]{1,0:T(8,128)S(1)} %get-tuple-element.14), channel_id=1, source_target_pairs={{0,2},{2,0},{1,3},{3,1},{4,6},{6,4},{5,7},{7,5},{8,10},{10,8},{9,1... | collective-permute-start | bytes 196616 | tf_op jit(solution)/shard_map/ppermute | solution.py:406
  15.4 0.7 %collective-permute-start.3 = (f32[8,2048]{1,0:T(8,128)S(1)}, f32[8,2048]{1,0:T(8,128)S(1)}, u32[]{:S(2)}, u32[]{:S(2)}) collective-permute-start(f32[8,2048]{1,0:T(8,128)S(1)} %get-tuple-element.15), channel_id=1, source_target_pairs={{0,1},{1,0},{2,3},{3,2},{4,5},{5,4},{6,7},{7,6},{8,9},{9,8},{10,11... | collective-permute-start | bytes 196616 | tf_op jit(solution)/shard_map/ppermute | solution.py:407
  16.1 2.5 %collective-permute-done.1.refs_0_ = f32[8,2048]{1,0:T(8,128)S(1)} collective-permute-done((f32[8,2048]{1,0:T(8,128)S(1)}, f32[8,2048]{1,0:T(8,128)S(1)}, u32[]{:S(2)}, u32[]{:S(2)}) %collective-permute-start.1) | collective-permute-done | bytes 65568 | tf_op jit(solution)/shard_map/ppermute | solution.py:405
  18.6 0.9 %collective-permute-done.2.refs_1_ = f32[8,2048]{1,0:T(8,128)S(1)} collective-permute-done((f32[8,2048]{1,0:T(8,128)S(1)}, f32[8,2048]{1,0:T(8,128)S(1)}, u32[]{:S(2)}, u32[]{:S(2)}) %collective-permute-start.2) | collective-permute-done | bytes 65568 | tf_op jit(solution)/shard_map/ppermute | solution.py:406
  19.5 0.0 collective-permute-done.3.refs_2_
  19.5 1.6 %collective-permute-start.4 = (f32[24,512]{1,0:T(8,128)S(1)}, f32[24,512]{1,0:T(8,128)S(1)}, u32[]{:S(2)}, u32[]{:S(2)}) collective-permute-start(f32[24,512]{1,0:T(8,128)S(1)} %get-tuple-element.18), channel_id=1, source_target_pairs={{0,4},{4,8},{8,12},{12,0},{1,5},{5,9},{9,13},{13,1},{2,6},{6,10},{... | collective-permute-start | bytes 147464 | tf_op jit(solution)/shard_map/ppermute | solution.py:410
  21.1 2.6 %collective-permute-start.5 = (f32[24,512]{1,0:T(8,128)S(1)}, f32[24,512]{1,0:T(8,128)S(1)}, u32[]{:S(2)}, u32[]{:S(2)}) collective-permute-start(f32[24,512]{1,0:T(8,128)S(1)} %get-tuple-element.19), channel_id=1, source_target_pairs={{0,8},{4,12},{8,0},{12,4},{1,9},{5,13},{9,1},{13,5},{2,10},{6,14},... | collective-permute-start | bytes 147464 | tf_op jit(solution)/shard_map/ppermute | solution.py:410
  23.7 1.3 %collective-permute-start.6 = (f32[24,512]{1,0:T(8,128)S(1)}, f32[24,512]{1,0:T(8,128)S(1)}, u32[]{:S(2)}, u32[]{:S(2)}) collective-permute-start(f32[24,512]{1,0:T(8,128)S(1)} %get-tuple-element.20), channel_id=1, source_target_pairs={{0,12},{4,0},{8,4},{12,8},{1,13},{5,1},{9,5},{13,9},{2,14},{6,2},{... | collective-permute-start | bytes 147464 | tf_op jit(solution)/shard_map/ppermute | solution.py:410
  25.1 0.4 %collective-permute-done.4.refs_1_ = f32[24,512]{1,0:T(8,128)S(1)} collective-permute-done((f32[24,512]{1,0:T(8,128)S(1)}, f32[24,512]{1,0:T(8,128)S(1)}, u32[]{:S(2)}, u32[]{:S(2)}) %collective-permute-start.4) | collective-permute-done | bytes 49184 | tf_op jit(solution)/shard_map/ppermute | solution.py:410
  25.4 2.1 %collective-permute-done.5.refs_2_ = f32[24,512]{1,0:T(8,128)S(1)} collective-permute-done((f32[24,512]{1,0:T(8,128)S(1)}, f32[24,512]{1,0:T(8,128)S(1)}, u32[]{:S(2)}, u32[]{:S(2)}) %collective-permute-start.5) | collective-permute-done | bytes 49184 | tf_op jit(solution)/shard_map/ppermute | solution.py:410
  27.6 0.4 %collective-permute-done.6.refs_3_ = f32[24,512]{1,0:T(8,128)S(1)} collective-permute-done((f32[24,512]{1,0:T(8,128)S(1)}, f32[24,512]{1,0:T(8,128)S(1)}, u32[]{:S(2)}, u32[]{:S(2)}) %collective-permute-start.6) | collective-permute-done | bytes 49184 | tf_op jit(solution)/shard_map/ppermute | solution.py:410
  28.0 0.1 collective-permute-start.7
  28.0 1.3 %quadrant.1 = (f32[1024,1024]{1,0:T(8,128)}, bf16[512,256]{1,0:T(8,128)(2,1)S(1)}, bf16[256,512]{1,0:T(8,128)(2,1)S(1)}) custom-call(f32[24,512]{1,0:T(8,128)S(1)} %get-tuple-element.17.refs_0_, f32[24,512]{1,0:T(8,128)S(1)} %collective-permute-done.4.refs_1_, f32[24,512]{1,0:T(8,128)S(1)} %collective-permute-done.5.refs_2_, ...), custom_call_target="tpu_custom_call" | custom-call | flops 268435456 | bytes 1048576 | tf_op jit(solution)/shard_map/quadrant/pallas_call | solution.py:335
  29.3 0.1 collective-permute-done.7.bundle
  29.4 1.9 %fisher.1 = (f32[8,1024]{1,0:T(8,128)}, f32[1024,1024]{1,0:T(8,128)}) custom-call(f32[1024,1024]{1,0:T(8,128)} %get-tuple-element.21.begun, bf16[512,256]{1,0:T(8,128)(2,1)S(1)} %get-tuple-element.22.left, bf16[256,512]{1,0:T(8,128)(2,1)S(1)} %get-tuple-element.23.right, ...), custom_call_target="tpu_custom_call", output_to_operand_aliasing={{1}: (0, {})} | custom-call | tf_op jit(solution)/shard_map/fisher/pallas_call | solution.py:357
  (2 shorter events, 0.0 us)
Async XLA Ops:
  0.6 5.9 %copy-start = (bf16[32,4096]{1,0:T(8,128)(2,1)S(1)}, bf16[32,4096]{1,0:T(8,128)(2,1)}, u32[]{:S(2)}) copy-start(bf16[32,4096]{1,0:T(8,128)(2,1)} %table.2) | copy-start | bytes 786436
  0.6 5.9 %copy-start.2 = (s32[112]{0:T(128)S(1)}, s32[112]{0:T(128)}, u32[]{:S(2)}) copy-start(s32[112]{0:T(128)} %signs.2) | copy-start | bytes 1348
  0.7 5.9 %copy-start.1 = (s32[112]{0:T(128)S(1)}, s32[112]{0:T(128)}, u32[]{:S(2)}) copy-start(s32[112]{0:T(128)} %ids.2) | copy-start | bytes 1348
  3.5 10.1 %collective-permute-start = (f32[4,128,128]{2,1,0:T(8,128)S(1)}, f32[4,128,128]{2,1,0:T(8,128)S(1)}, u32[]{:S(2)}, u32[]{:S(2)}) collective-permute-start(f32[4,128,128]{2,1,0:T(8,128)S(1)} %project_acts.1.own), channel_id=1, source_target_pairs={{0,2},{2,0},{1,3},{3,1},{4,6},{6,4},{5,7},{7,5},{8,10},{10,8},{9,1... | collective-permute-start | bytes 786440 | tf_op jit(solution)/shard_map/ppermute | solution.py:384
  14.1 4.5 %collective-permute-start.1 = (f32[8,2048]{1,0:T(8,128)S(1)}, f32[8,2048]{1,0:T(8,128)S(1)}, u32[]{:S(2)}, u32[]{:S(2)}) collective-permute-start(f32[8,2048]{1,0:T(8,128)S(1)} %get-tuple-element.13), channel_id=1, source_target_pairs={{0,3},{1,2},{2,1},{3,0},{4,7},{5,6},{6,5},{7,4},{8,11},{9,10},{10,... | collective-permute-start | bytes 196616 | tf_op jit(solution)/shard_map/ppermute | solution.py:405
  14.2 5.2 %collective-permute-start.2 = (f32[8,2048]{1,0:T(8,128)S(1)}, f32[8,2048]{1,0:T(8,128)S(1)}, u32[]{:S(2)}, u32[]{:S(2)}) collective-permute-start(f32[8,2048]{1,0:T(8,128)S(1)} %get-tuple-element.14), channel_id=1, source_target_pairs={{0,2},{2,0},{1,3},{3,1},{4,6},{6,4},{5,7},{7,5},{8,10},{10,8},{9,1... | collective-permute-start | bytes 196616 | tf_op jit(solution)/shard_map/ppermute | solution.py:406
  15.4 4.1 %collective-permute-start.3 = (f32[8,2048]{1,0:T(8,128)S(1)}, f32[8,2048]{1,0:T(8,128)S(1)}, u32[]{:S(2)}, u32[]{:S(2)}) collective-permute-start(f32[8,2048]{1,0:T(8,128)S(1)} %get-tuple-element.15), channel_id=1, source_target_pairs={{0,1},{1,0},{2,3},{3,2},{4,5},{5,4},{6,7},{7,6},{8,9},{9,8},{10,11... | collective-permute-start | bytes 196616 | tf_op jit(solution)/shard_map/ppermute | solution.py:407
  19.5 5.9 %collective-permute-start.4 = (f32[24,512]{1,0:T(8,128)S(1)}, f32[24,512]{1,0:T(8,128)S(1)}, u32[]{:S(2)}, u32[]{:S(2)}) collective-permute-start(f32[24,512]{1,0:T(8,128)S(1)} %get-tuple-element.18), channel_id=1, source_target_pairs={{0,4},{4,8},{8,12},{12,0},{1,5},{5,9},{9,13},{13,1},{2,6},{6,10},{... | collective-permute-start | bytes 147464 | tf_op jit(solution)/shard_map/ppermute | solution.py:410
  21.1 6.5 %collective-permute-start.5 = (f32[24,512]{1,0:T(8,128)S(1)}, f32[24,512]{1,0:T(8,128)S(1)}, u32[]{:S(2)}, u32[]{:S(2)}) collective-permute-start(f32[24,512]{1,0:T(8,128)S(1)} %get-tuple-element.19), channel_id=1, source_target_pairs={{0,8},{4,12},{8,0},{12,4},{1,9},{5,13},{9,1},{13,5},{2,10},{6,14},... | collective-permute-start | bytes 147464 | tf_op jit(solution)/shard_map/ppermute | solution.py:410
  23.7 4.2 %collective-permute-start.6 = (f32[24,512]{1,0:T(8,128)S(1)}, f32[24,512]{1,0:T(8,128)S(1)}, u32[]{:S(2)}, u32[]{:S(2)}) collective-permute-start(f32[24,512]{1,0:T(8,128)S(1)} %get-tuple-element.20), channel_id=1, source_target_pairs={{0,12},{4,0},{8,4},{12,8},{1,13},{5,1},{9,5},{13,9},{2,14},{6,2},{... | collective-permute-start | bytes 147464 | tf_op jit(solution)/shard_map/ppermute | solution.py:410
  28.0 1.4 %collective-permute-start.7 = (f32[64,512]{1,0:T(8,128)S(1)}, f32[64,512]{1,0:T(8,128)S(1)}, u32[]{:S(2)}, u32[]{:S(2)}) collective-permute-start(f32[64,512]{1,0:T(8,128)S(1)} %bundle.1), channel_id=1, source_target_pairs={{0,1},{1,0},{2,3},{3,2},{4,5},{5,4},{6,7},{7,6},{8,9},{9,8},{10,11... | collective-permute-start | bytes 393224 | tf_op jit(solution)/shard_map/ppermute | solution.py:411

commit v15 on v14

--- a/solution.py
+++ b/solution.py
@@ -15,15 +15,16 @@
 
 
 def chunks_of(width, most):
-    if width >= 4 * most:
-        inner = width - most
-        ends = [most // 2] * 2
-    else:
-        inner, ends = width, []
+    if width < 4 * most or most % (4 * LANES):
+        chunk = most
+        while width % chunk:
+            chunk -= LANES
+        return [chunk] * (width // chunk)
+    inner = width - most
     chunk = most
     while inner % chunk:
         chunk -= LANES
-    return ends[:1] + [chunk] * (inner // chunk) + ends[1:]
+    return [most // 2] + [chunk] * (inner // chunk) + [most // 4] * 2
 
 
 def split3(x):
@@ -74,35 +75,28 @@
     return lax.dot_general(left, right, (((1,), (1,)), ((), ())), preferred_element_type=jnp.float32)
 
 
-def project_kernel(widths, fetch, ids, signs, table, rows_ref, *refs):
-    out, spread, signed, matrix, held, total, sems, *own = refs
+def project_kernel(widths, ids, signs, table, rows_ref, out, *refs):
+    spread, matrix, held, total, own_table, own_ids, own_signs, sems, *signed = refs
+    signed = signed[0] if signed else None
     copies, starts, start = [], [], 0
     for c, width in enumerate(widths):
         columns = pl.ds(start, width)
         copies.append(pltpu.make_async_copy(rows_ref.at[:, columns], held.at[:, columns], sems.at[c]))
         starts.append(start)
         start += width
-    if fetch:
-        small = [
-            pltpu.make_async_copy(source, kept, sems.at[len(widths) + k])
-            for k, (source, kept) in enumerate(zip((table, ids, signs), own))
-        ]
-        for copy in small:
-            copy.start()
-        table, ids, signs = own
-    for copy in copies:
+    small = [
+        pltpu.make_async_copy(source, kept, sems.at[len(widths) + k])
+        for k, (source, kept) in enumerate(((table, own_table), (ids, own_ids), (signs, own_signs)))
+    ]
+    for copy in small + copies:
         copy.start()
-    if fetch:
-        small[0].wait()
-    spread_table(table, spread)
-    if fetch:
-        signed = None
-    else:
+    small[0].wait()
+    spread_table(own_table, spread)
+    if signed is not None:
         sign_table(spread, signed)
-    if fetch:
-        small[1].wait()
-        small[2].wait()
-    lay = functools.partial(lay_blocks, ids, signs, spread, signed, matrix)
+    small[1].wait()
+    small[2].wait()
+    lay = functools.partial(lay_blocks, own_ids, own_signs, spread, signed, matrix)
     lay(0, widths[0] // BLOCK)
     for c, copy in enumerate(copies):
         columns = pl.ds(starts[c], widths[c])
@@ -117,44 +111,43 @@
         )
         if c == 0:
             total[...] = part
-        else:
+        elif c + 1 < len(widths):
             total[...] += part
+    part = total[...] + part if len(widths) > 1 else part
     pairs, _, tokens = out.shape
     for pair in range(pairs):
         for side in range(2):
-            out[pair, pl.ds(side * PROJ, PROJ), :] = total[:, pl.ds((2 * pair + side) * tokens, tokens)]
-
-
-def project(values, ids, signs, table, fetch, most, name):
+            example = 2 * pair + side
+            out[pair, pl.ds(side * PROJ, PROJ), :] = part[:, example * tokens : (example + 1) * tokens]
+
+
+def project(values, ids, signs, table, most, name):
     count, tokens, width = values.shape
     widths = chunks_of(width, most)
     rows = count * tokens
     entries = table.shape[0]
-    smem = pl.BlockSpec(memory_space=pltpu.SMEM)
-    vmem = pl.BlockSpec(memory_space=pltpu.VMEM)
-    hbm = pl.BlockSpec(memory_space=pltpu.HBM)
-    own = [
-        pltpu.VMEM(table.shape, table.dtype),
-        pltpu.SMEM(ids.shape, ids.dtype),
-        pltpu.SMEM(signs.shape, signs.dtype),
+    blocks = ids.shape[0]
+    operands = [
+        pltpu.with_memory_space_constraint(each, pltpu.HBM)
+        for each in (ids, signs, table, values.reshape(rows, width))
     ]
-    operands = [ids, signs, table, values.reshape(rows, width)]
-    if fetch:
-        operands = [pltpu.with_memory_space_constraint(each, pltpu.HBM) for each in operands]
-    return pl.pallas_call(
-        functools.partial(project_kernel, widths, fetch),
+    signed = [pltpu.VMEM((2 * entries * BLOCK, LANES), jnp.bfloat16)] if blocks > entries else []
+    return pl.pallas_call(
+        functools.partial(project_kernel, widths),
         out_shape=jax.ShapeDtypeStruct((count // 2, LANES, tokens), jnp.float32),
-        in_specs=[hbm] * 4 if fetch else [smem, smem, vmem, hbm],
-        out_specs=vmem,
+        in_specs=[pl.BlockSpec(memory_space=pltpu.HBM)] * 4,
+        out_specs=pl.BlockSpec(memory_space=pltpu.VMEM),
         scratch_shapes=[
             pltpu.VMEM((entries * STRIDE, LANES), jnp.float32),
-            pltpu.VMEM((2 * entries * BLOCK, LANES), jnp.bfloat16),
             pltpu.VMEM((width, LANES), jnp.bfloat16),
             pltpu.VMEM((rows, width), jnp.bfloat16),
             pltpu.VMEM((PROJ, rows), jnp.float32),
+            pltpu.VMEM(table.shape, table.dtype),
+            pltpu.SMEM(ids.shape, ids.dtype),
+            pltpu.SMEM(signs.shape, signs.dtype),
             pltpu.SemaphoreType.DMA((len(widths) + 3,)),
         ]
-        + (own if fetch else []),
+        + signed,
         compiler_params=pltpu.CompilerParams(vmem_limit_bytes=VMEM_BYTES),
         cost_estimate=pl.CostEstimate(
             flops=2 * rows * width * LANES, bytes_accessed=2 * rows * width, transcendentals=0
@@ -379,13 +372,13 @@
     small = tensor == 2 and seq == 2 and dp == 4
     swap = [(0, 1), (1, 0)]
 
-    act = project(acts, in_ids, in_signs, in_table, True, 512, "project_acts")
+    act = project(acts, in_ids, in_signs, in_table, 512, "project_acts")
     if tensor == 2:
         other = lax.ppermute(act, "tensor", swap)
     else:
         act = lax.psum(act, "tensor")
         other = jnp.zeros_like(act)
-    grad = project(grads, out_ids, out_signs, out_table, False, 1024, "project_grads")
+    grad = project(grads, out_ids, out_signs, out_table, 1024, "project_grads")
     krons = kron_of(grad, act, other, (shards, seq) if small else (1, 1))
 
     if not small:

time: 31.5 us -> 31.5 us (level)
  Pallas kernels: 13.7 us -> 13.1 us
  waiting for transfers between devices: 6.37 us -> 6.88 us
    ppermute x1, waiting for transfers between devices: 0.87 us -> 1.54 us  [local(): beside = lax.ppermute(krons[2], 'tensor', swap)]
    pallas_call x2, Pallas kernels: 9.89 us -> 9.38 us  [project(): pl.pallas_call(functools.partial(project_kernel, widths), out_shape=jax.S...]
    ppermute x1, starting transfers between devices: 0.68 us -> 0.21 us  [local(): mate = lax.ppermute(krons[3], 'seq', swap)]
    ppermute x1, starting transfers between devices: 1.17 us -> 1.52 us  [local(): beside = lax.ppermute(krons[2], 'tensor', swap)]
  transfers between devices with their start and end apart: 8 -> 8, of which waited for: 6 -> 6; matrix products, arithmetic and copies ran while one was open for 0% -> 0% of each run, Pallas kernels for 26% -> 25%
where the time goes in v15:
time: 31.5 us; the launch traced here: 31.4 us
  Pallas kernels  13.1 us (42%)
  starting transfers between devices  10.7 us (34%)
  waiting for transfers between devices  6.88 us (22%)
  between operations  0.69 us (2%)
    pallas_call x2, Pallas kernels, project(): pl.pallas_call(functools.partial(project_kernel, widths), out_shape=jax.S...  9.38 us
    ppermute x3, starting transfers between devices, local(): lax.ppermute(parcels[k], 'dp', [(d, (d + k) % dp) for d in range(dp)])  5.65 us
    ppermute x1, starting transfers between devices, local(): other = lax.ppermute(act, 'tensor', swap)  3 us
    ppermute x3, waiting for transfers between devices, local(): lax.ppermute(parcels[k], 'dp', [(d, (d + k) % dp) for d in range(dp)])  2.87 us
    ppermute x1, waiting for transfers between devices, local(): lax.ppermute(krons[1], ('tensor', 'seq'), [(p, 3 - p) for p in range(shar...  2.4 us
    pallas_call x1, Pallas kernels, fisher_block(): pl.pallas_call(functools.partial(fisher_kernel, 1.0 / (rows * len(parcels...  1.94 us
    ppermute x1, waiting for transfers between devices, local(): beside = lax.ppermute(krons[2], 'tensor', swap)  1.54 us
    ppermute x1, starting transfers between devices, local(): beside = lax.ppermute(krons[2], 'tensor', swap)  1.52 us
  transfers between devices with their start and end apart: 8, of which 6 were waited for; matrix products, arithmetic and copies ran while one was open for 0% of the time, Pallas kernels for 25%

profile of v15, /device:TPU:0, one launch (start us, length us, event | category | flops | bytes accessed | tf_op | source)
XLA Modules:
  0.0 31.4 jit_solution(3203655519734699497)
XLA Ops:
  0.6 2.9 %project_acts.1.own = f32[4,128,128]{2,1,0:T(8,128)S(1)} custom-call(s32[32]{0:T(128)} %ids.3, s32[32]{0:T(128)} %signs.3, bf16[32,4096]{1,0:T(8,128)(2,1)} %table.3, bf16[1024,2048]{1,0:T(8,128)(2,1)} %bitcast.3), custom_call_target="tpu_custom_call" | custom-call | flops 536870912 | bytes 4194304 | tf_op jit(solution)/shard_map/project_acts/pallas_call | solution.py:135
  3.6 3.0 %collective-permute-start = (f32[4,128,128]{2,1,0:T(8,128)S(1)}, f32[4,128,128]{2,1,0:T(8,128)S(1)}, u32[]{:S(2)}, u32[]{:S(2)}) collective-permute-start(f32[4,128,128]{2,1,0:T(8,128)S(1)} %project_acts.1.own), channel_id=1, source_target_pairs={{0,2},{2,0},{1,3},{3,1},{4,6},{6,4},{5,7},{7,5},{8,10},{10,8},{9,1... | collective-permute-start | bytes 786440 | tf_op jit(solution)/shard_map/ppermute | solution.py:377
  6.6 6.5 %project_grads.1.grads = f32[4,128,128]{2,1,0:T(8,128)S(1)} custom-call(s32[112]{0:T(128)} %ids.2, s32[112]{0:T(128)} %signs.2, bf16[32,4096]{1,0:T(8,128)(2,1)} %table.2, bf16[1024,7168]{1,0:T(8,128)(2,1)} %bitcast.2), custom_call_target="tpu_custom_call" | custom-call | flops 1879048192 | bytes 14680064 | tf_op jit(solution)/shard_map/project_grads/pallas_call | solution.py:135
  13.0 0.0 collective-permute-done.act
  13.0 0.5 %kron.1 = (f32[8,2048]{1,0:T(8,128)S(1)}, f32[8,2048]{1,0:T(8,128)S(1)}, f32[8,2048]{1,0:T(8,128)S(1)}, f32[8,2048]{1,0:T(8,128)S(1)}) custom-call(f32[4,128,128]{2,1,0:T(8,128)S(1)} %project_grads.1.grads, f32[4,128,128]{2,1,0:T(8,128)S(1)} %project_acts.1.own, f32[4,128,128]{2,1,0:T(8,128)S(1)} %collective-permute-done.act), custom_call_target="tpu_custom_call" | custom-call | tf_op jit(solution)/shard_map/kron/pallas_call | solution.py:190
  13.6 0.2 collective-permute-start.1
  13.8 1.5 %collective-permute-start.2 = (f32[8,2048]{1,0:T(8,128)S(1)}, f32[8,2048]{1,0:T(8,128)S(1)}, u32[]{:S(2)}, u32[]{:S(2)}) collective-permute-start(f32[8,2048]{1,0:T(8,128)S(1)} %get-tuple-element.14), channel_id=1, source_target_pairs={{0,2},{2,0},{1,3},{3,1},{4,6},{6,4},{5,7},{7,5},{8,10},{10,8},{9,1... | collective-permute-start | bytes 196616 | tf_op jit(solution)/shard_map/ppermute | solution.py:399
  15.3 0.2 collective-permute-start.3
  15.5 2.4 %collective-permute-done.1.refs_0_ = f32[8,2048]{1,0:T(8,128)S(1)} collective-permute-done((f32[8,2048]{1,0:T(8,128)S(1)}, f32[8,2048]{1,0:T(8,128)S(1)}, u32[]{:S(2)}, u32[]{:S(2)}) %collective-permute-start.1) | collective-permute-done | bytes 65568 | tf_op jit(solution)/shard_map/ppermute | solution.py:398
  17.9 1.5 %collective-permute-done.2.refs_1_ = f32[8,2048]{1,0:T(8,128)S(1)} collective-permute-done((f32[8,2048]{1,0:T(8,128)S(1)}, f32[8,2048]{1,0:T(8,128)S(1)}, u32[]{:S(2)}, u32[]{:S(2)}) %collective-permute-start.2) | collective-permute-done | bytes 65568 | tf_op jit(solution)/shard_map/ppermute | solution.py:399
  19.4 0.0 collective-permute-done.3.refs_2_
  19.5 1.7 %collective-permute-start.4 = (f32[24,512]{1,0:T(8,128)S(1)}, f32[24,512]{1,0:T(8,128)S(1)}, u32[]{:S(2)}, u32[]{:S(2)}) collective-permute-start(f32[24,512]{1,0:T(8,128)S(1)} %get-tuple-element.18), channel_id=1, source_target_pairs={{0,4},{4,8},{8,12},{12,0},{1,5},{5,9},{9,13},{13,1},{2,6},{6,10},{... | collective-permute-start | bytes 147464 | tf_op jit(solution)/shard_map/ppermute | solution.py:403
  21.2 2.6 %collective-permute-start.5 = (f32[24,512]{1,0:T(8,128)S(1)}, f32[24,512]{1,0:T(8,128)S(1)}, u32[]{:S(2)}, u32[]{:S(2)}) collective-permute-start(f32[24,512]{1,0:T(8,128)S(1)} %get-tuple-element.19), channel_id=1, source_target_pairs={{0,8},{4,12},{8,0},{12,4},{1,9},{5,13},{9,1},{13,5},{2,10},{6,14},... | collective-permute-start | bytes 147464 | tf_op jit(solution)/shard_map/ppermute | solution.py:403
  23.8 1.3 %collective-permute-start.6 = (f32[24,512]{1,0:T(8,128)S(1)}, f32[24,512]{1,0:T(8,128)S(1)}, u32[]{:S(2)}, u32[]{:S(2)}) collective-permute-start(f32[24,512]{1,0:T(8,128)S(1)} %get-tuple-element.20), channel_id=1, source_target_pairs={{0,12},{4,0},{8,4},{12,8},{1,13},{5,1},{9,5},{13,9},{2,14},{6,2},{... | collective-permute-start | bytes 147464 | tf_op jit(solution)/shard_map/ppermute | solution.py:403
  25.1 0.3 collective-permute-done.4.refs_1_
  25.4 2.2 %collective-permute-done.5.refs_2_ = f32[24,512]{1,0:T(8,128)S(1)} collective-permute-done((f32[24,512]{1,0:T(8,128)S(1)}, f32[24,512]{1,0:T(8,128)S(1)}, u32[]{:S(2)}, u32[]{:S(2)}) %collective-permute-start.5) | collective-permute-done | bytes 49184 | tf_op jit(solution)/shard_map/ppermute | solution.py:403
  27.6 0.4 %collective-permute-done.6.refs_3_ = f32[24,512]{1,0:T(8,128)S(1)} collective-permute-done((f32[24,512]{1,0:T(8,128)S(1)}, f32[24,512]{1,0:T(8,128)S(1)}, u32[]{:S(2)}, u32[]{:S(2)}) %collective-permute-start.6) | collective-permute-done | bytes 49184 | tf_op jit(solution)/shard_map/ppermute | solution.py:403
  28.0 0.1 collective-permute-start.7
  28.1 1.3 %quadrant.1 = (f32[1024,1024]{1,0:T(8,128)}, bf16[512,256]{1,0:T(8,128)(2,1)S(1)}, bf16[256,512]{1,0:T(8,128)(2,1)S(1)}) custom-call(f32[24,512]{1,0:T(8,128)S(1)} %get-tuple-element.17.refs_0_, f32[24,512]{1,0:T(8,128)S(1)} %collective-permute-done.4.refs_1_, f32[24,512]{1,0:T(8,128)S(1)} %collective-permute-done.5.refs_2_, ...), custom_call_target="tpu_custom_call" | custom-call | flops 268435456 | bytes 1048576 | tf_op jit(solution)/shard_map/quadrant/pallas_call | solution.py:328
  29.3 0.1 collective-permute-done.7.bundle
  29.4 1.9 %fisher.1 = (f32[8,1024]{1,0:T(8,128)}, f32[1024,1024]{1,0:T(8,128)}) custom-call(f32[1024,1024]{1,0:T(8,128)} %get-tuple-element.21.begun, bf16[512,256]{1,0:T(8,128)(2,1)S(1)} %get-tuple-element.22.left, bf16[256,512]{1,0:T(8,128)(2,1)S(1)} %get-tuple-element.23.right, ...), custom_call_target="tpu_custom_call", output_to_operand_aliasing={{1}: (0, {})} | custom-call | tf_op jit(solution)/shard_map/fisher/pallas_call | solution.py:350
  (2 shorter events, 0.0 us)
Async XLA Ops:
  3.6 9.5 %collective-permute-start = (f32[4,128,128]{2,1,0:T(8,128)S(1)}, f32[4,128,128]{2,1,0:T(8,128)S(1)}, u32[]{:S(2)}, u32[]{:S(2)}) collective-permute-start(f32[4,128,128]{2,1,0:T(8,128)S(1)} %project_acts.1.own), channel_id=1, source_target_pairs={{0,2},{2,0},{1,3},{3,1},{4,6},{6,4},{5,7},{7,5},{8,10},{10,8},{9,1... | collective-permute-start | bytes 786440 | tf_op jit(solution)/shard_map/ppermute | solution.py:377
  13.6 4.3 %collective-permute-start.1 = (f32[8,2048]{1,0:T(8,128)S(1)}, f32[8,2048]{1,0:T(8,128)S(1)}, u32[]{:S(2)}, u32[]{:S(2)}) collective-permute-start(f32[8,2048]{1,0:T(8,128)S(1)} %get-tuple-element.13), channel_id=1, source_target_pairs={{0,3},{1,2},{2,1},{3,0},{4,7},{5,6},{6,5},{7,4},{8,11},{9,10},{10,... | collective-permute-start | bytes 196616 | tf_op jit(solution)/shard_map/ppermute | solution.py:398
  13.8 5.7 %collective-permute-start.2 = (f32[8,2048]{1,0:T(8,128)S(1)}, f32[8,2048]{1,0:T(8,128)S(1)}, u32[]{:S(2)}, u32[]{:S(2)}) collective-permute-start(f32[8,2048]{1,0:T(8,128)S(1)} %get-tuple-element.14), channel_id=1, source_target_pairs={{0,2},{2,0},{1,3},{3,1},{4,6},{6,4},{5,7},{7,5},{8,10},{10,8},{9,1... | collective-permute-start | bytes 196616 | tf_op jit(solution)/shard_map/ppermute | solution.py:399
  15.3 4.1 %collective-permute-start.3 = (f32[8,2048]{1,0:T(8,128)S(1)}, f32[8,2048]{1,0:T(8,128)S(1)}, u32[]{:S(2)}, u32[]{:S(2)}) collective-permute-start(f32[8,2048]{1,0:T(8,128)S(1)} %get-tuple-element.15), channel_id=1, source_target_pairs={{0,1},{1,0},{2,3},{3,2},{4,5},{5,4},{6,7},{7,6},{8,9},{9,8},{10,11... | collective-permute-start | bytes 196616 | tf_op jit(solution)/shard_map/ppermute | solution.py:400
  19.5 5.9 %collective-permute-start.4 = (f32[24,512]{1,0:T(8,128)S(1)}, f32[24,512]{1,0:T(8,128)S(1)}, u32[]{:S(2)}, u32[]{:S(2)}) collective-permute-start(f32[24,512]{1,0:T(8,128)S(1)} %get-tuple-element.18), channel_id=1, source_target_pairs={{0,4},{4,8},{8,12},{12,0},{1,5},{5,9},{9,13},{13,1},{2,6},{6,10},{... | collective-permute-start | bytes 147464 | tf_op jit(solution)/shard_map/ppermute | solution.py:403
  21.2 6.4 %collective-permute-start.5 = (f32[24,512]{1,0:T(8,128)S(1)}, f32[24,512]{1,0:T(8,128)S(1)}, u32[]{:S(2)}, u32[]{:S(2)}) collective-permute-start(f32[24,512]{1,0:T(8,128)S(1)} %get-tuple-element.19), channel_id=1, source_target_pairs={{0,8},{4,12},{8,0},{12,4},{1,9},{5,13},{9,1},{13,5},{2,10},{6,14},... | collective-permute-start | bytes 147464 | tf_op jit(solution)/shard_map/ppermute | solution.py:403
  23.8 4.2 %collective-permute-start.6 = (f32[24,512]{1,0:T(8,128)S(1)}, f32[24,512]{1,0:T(8,128)S(1)}, u32[]{:S(2)}, u32[]{:S(2)}) collective-permute-start(f32[24,512]{1,0:T(8,128)S(1)} %get-tuple-element.20), channel_id=1, source_target_pairs={{0,12},{4,0},{8,4},{12,8},{1,13},{5,1},{9,5},{13,9},{2,14},{6,2},{... | collective-permute-start | bytes 147464 | tf_op jit(solution)/shard_map/ppermute | solution.py:403
  28.0 1.4 %collective-permute-start.7 = (f32[64,512]{1,0:T(8,128)S(1)}, f32[64,512]{1,0:T(8,128)S(1)}, u32[]{:S(2)}, u32[]{:S(2)}) collective-permute-start(f32[64,512]{1,0:T(8,128)S(1)} %bundle.1), channel_id=1, source_target_pairs={{0,1},{1,0},{2,3},{3,2},{4,5},{5,4},{6,7},{7,6},{8,9},{9,8},{10,11... | collective-permute-start | bytes 393224 | tf_op jit(solution)/shard_map/ppermute | solution.py:404

commit v16 on v15

--- a/solution.py
+++ b/solution.py
@@ -75,9 +75,10 @@
     return lax.dot_general(left, right, (((1,), (1,)), ((), ())), preferred_element_type=jnp.float32)
 
 
-def project_kernel(widths, ids, signs, table, rows_ref, out, *refs):
+def project_kernel(widths, streamed, ids, signs, table, rows_ref, out, *refs):
     spread, matrix, held, total, own_table, own_ids, own_signs, sems, *signed = refs
     signed = signed[0] if signed else None
+    half = held.shape[0] // 2
     copies, starts, start = [], [], 0
     for c, width in enumerate(widths):
         columns = pl.ds(start, width)
@@ -103,25 +104,39 @@
         copy.wait()
         if c + 1 < len(widths):
             lay(starts[c + 1] // BLOCK, (starts[c + 1] + widths[c + 1]) // BLOCK)
-        part = lax.dot_general(
-            matrix[columns, :PROJ],
-            held[:, columns],
-            (((0,), (1,)), ((), ())),
-            preferred_element_type=jnp.float32,
-        )
-        if c == 0:
-            total[...] = part
-        elif c + 1 < len(widths):
-            total[...] += part
-    part = total[...] + part if len(widths) > 1 else part
+        if streamed:
+            parts = [
+                jnp.dot(held[pl.ds(k * half, half), columns], matrix[columns, :], preferred_element_type=jnp.float32)
+                for k in range(2)
+            ]
+        else:
+            parts = [
+                lax.dot_general(
+                    matrix[columns, :PROJ],
+                    held[pl.ds(k * half, half), columns],
+                    (((0,), (1,)), ((), ())),
+                    preferred_element_type=jnp.float32,
+                )
+                for k in range(2)
+            ]
+        if c > 0:
+            parts = [total[k] + part for k, part in enumerate(parts)]
+        if c + 1 < len(widths):
+            for k, part in enumerate(parts):
+                total[k] = part
     pairs, _, tokens = out.shape
     for pair in range(pairs):
         for side in range(2):
             example = 2 * pair + side
-            out[pair, pl.ds(side * PROJ, PROJ), :] = part[:, example * tokens : (example + 1) * tokens]
-
-
-def project(values, ids, signs, table, most, name):
+            k, start = example * tokens // half, example * tokens % half
+            if streamed:
+                mine = parts[k][start : start + tokens, :].T[:PROJ, :]
+            else:
+                mine = parts[k][:, start : start + tokens]
+            out[pair, pl.ds(side * PROJ, PROJ), :] = mine
+
+
+def project(values, ids, signs, table, most, streamed, name):
     count, tokens, width = values.shape
     widths = chunks_of(width, most)
     rows = count * tokens
@@ -133,7 +148,7 @@
     ]
     signed = [pltpu.VMEM((2 * entries * BLOCK, LANES), jnp.bfloat16)] if blocks > entries else []
     return pl.pallas_call(
-        functools.partial(project_kernel, widths),
+        functools.partial(project_kernel, widths, streamed),
         out_shape=jax.ShapeDtypeStruct((count // 2, LANES, tokens), jnp.float32),
         in_specs=[pl.BlockSpec(memory_space=pltpu.HBM)] * 4,
         out_specs=pl.BlockSpec(memory_space=pltpu.VMEM),
@@ -141,7 +156,7 @@
             pltpu.VMEM((entries * STRIDE, LANES), jnp.float32),
             pltpu.VMEM((width, LANES), jnp.bfloat16),
             pltpu.VMEM((rows, width), jnp.bfloat16),
-            pltpu.VMEM((PROJ, rows), jnp.float32),
+            pltpu.VMEM((2, rows // 2, LANES) if streamed else (2, PROJ, rows // 2), jnp.float32),
             pltpu.VMEM(table.shape, table.dtype),
             pltpu.SMEM(ids.shape, ids.dtype),
             pltpu.SMEM(signs.shape, signs.dtype),
@@ -372,13 +387,13 @@
     small = tensor == 2 and seq == 2 and dp == 4
     swap = [(0, 1), (1, 0)]
 
-    act = project(acts, in_ids, in_signs, in_table, 512, "project_acts")
+    act = project(acts, in_ids, in_signs, in_table, 512, True, "project_acts")
     if tensor == 2:
         other = lax.ppermute(act, "tensor", swap)
     else:
         act = lax.psum(act, "tensor")
         other = jnp.zeros_like(act)
-    grad = project(grads, out_ids, out_signs, out_table, 1024, "project_grads")
+    grad = project(grads, out_ids, out_signs, out_table, 1024, False, "project_grads")
     krons = kron_of(grad, act, other, (shards, seq) if small else (1, 1))
 
     if not small:

time: 31.5 us -> 31.8 us (level)
  Pallas kernels: 13.1 us -> 13.5 us
  transfers between devices with their start and end apart: 8 -> 8, of which waited for: 6 -> 6; matrix products, arithmetic and copies ran while one was open for 0% -> 0% of each run, Pallas kernels for 25% -> 24%
where the time goes in v16:
time: 31.8 us; the launch traced here: 31.7 us
  Pallas kernels  13.5 us (42%)
  starting transfers between devices  10.6 us (33%)
  waiting for transfers between devices  6.87 us (22%)
  between operations  0.69 us (2%)
    pallas_call x2, Pallas kernels, project(): pl.pallas_call(functools.partial(project_kernel, widths, streamed), out_s...  9.7 us
    ppermute x3, starting transfers between devices, local(): lax.ppermute(parcels[k], 'dp', [(d, (d + k) % dp) for d in range(dp)])  5.65 us
    ppermute x1, starting transfers between devices, local(): other = lax.ppermute(act, 'tensor', swap)  3 us
    ppermute x3, waiting for transfers between devices, local(): lax.ppermute(parcels[k], 'dp', [(d, (d + k) % dp) for d in range(dp)])  2.86 us
    ppermute x1, waiting for transfers between devices, local(): lax.ppermute(krons[1], ('tensor', 'seq'), [(p, 3 - p) for p in range(shar...  2.4 us
    pallas_call x1, Pallas kernels, fisher_block(): pl.pallas_call(functools.partial(fisher_kernel, 1.0 / (rows * len(parcels...  1.94 us
    ppermute x1, waiting for transfers between devices, local(): beside = lax.ppermute(krons[2], 'tensor', swap)  1.54 us
    ppermute x1, starting transfers between devices, local(): beside = lax.ppermute(krons[2], 'tensor', swap)  1.5 us
  transfers between devices with their start and end apart: 8, of which 6 were waited for; matrix products, arithmetic and copies ran while one was open for 0% of the time, Pallas kernels for 24%

profile of v16, /device:TPU:0, one launch (start us, length us, event | category | flops | bytes accessed | tf_op | source)
XLA Modules:
  0.0 31.7 jit_solution(11078886826728922205)
XLA Ops:
  0.6 3.2 %project_acts.1.own = f32[4,128,128]{2,1,0:T(8,128)S(1)} custom-call(s32[32]{0:T(128)} %ids.3, s32[32]{0:T(128)} %signs.3, bf16[32,4096]{1,0:T(8,128)(2,1)} %table.3, bf16[1024,2048]{1,0:T(8,128)(2,1)} %bitcast.3), custom_call_target="tpu_custom_call" | custom-call | flops 536870912 | bytes 4194304 | tf_op jit(solution)/shard_map/project_acts/pallas_call | solution.py:150
  3.9 3.0 %collective-permute-start = (f32[4,128,128]{2,1,0:T(8,128)S(1)}, f32[4,128,128]{2,1,0:T(8,128)S(1)}, u32[]{:S(2)}, u32[]{:S(2)}) collective-permute-start(f32[4,128,128]{2,1,0:T(8,128)S(1)} %project_acts.1.own), channel_id=1, source_target_pairs={{0,2},{2,0},{1,3},{3,1},{4,6},{6,4},{5,7},{7,5},{8,10},{10,8},{9,1... | collective-permute-start | bytes 786440 | tf_op jit(solution)/shard_map/ppermute | solution.py:392
  6.9 6.4 %project_grads.1.grads = f32[4,128,128]{2,1,0:T(8,128)S(1)} custom-call(s32[112]{0:T(128)} %ids.2, s32[112]{0:T(128)} %signs.2, bf16[32,4096]{1,0:T(8,128)(2,1)} %table.2, bf16[1024,7168]{1,0:T(8,128)(2,1)} %bitcast.2), custom_call_target="tpu_custom_call" | custom-call | flops 1879048192 | bytes 14680064 | tf_op jit(solution)/shard_map/project_grads/pallas_call | solution.py:150
  13.3 0.0 collective-permute-done.act
  13.4 0.5 %kron.1 = (f32[8,2048]{1,0:T(8,128)S(1)}, f32[8,2048]{1,0:T(8,128)S(1)}, f32[8,2048]{1,0:T(8,128)S(1)}, f32[8,2048]{1,0:T(8,128)S(1)}) custom-call(f32[4,128,128]{2,1,0:T(8,128)S(1)} %project_grads.1.grads, f32[4,128,128]{2,1,0:T(8,128)S(1)} %project_acts.1.own, f32[4,128,128]{2,1,0:T(8,128)S(1)} %collective-permute-done.act), custom_call_target="tpu_custom_call" | custom-call | tf_op jit(solution)/shard_map/kron/pallas_call | solution.py:205
  13.9 0.2 collective-permute-start.1
  14.1 1.5 %collective-permute-start.2 = (f32[8,2048]{1,0:T(8,128)S(1)}, f32[8,2048]{1,0:T(8,128)S(1)}, u32[]{:S(2)}, u32[]{:S(2)}) collective-permute-start(f32[8,2048]{1,0:T(8,128)S(1)} %get-tuple-element.14), channel_id=1, source_target_pairs={{0,2},{2,0},{1,3},{3,1},{4,6},{6,4},{5,7},{7,5},{8,10},{10,8},{9,1... | collective-permute-start | bytes 196616 | tf_op jit(solution)/shard_map/ppermute | solution.py:414
  15.6 0.2 collective-permute-start.3
  15.8 2.4 %collective-permute-done.1.refs_0_ = f32[8,2048]{1,0:T(8,128)S(1)} collective-permute-done((f32[8,2048]{1,0:T(8,128)S(1)}, f32[8,2048]{1,0:T(8,128)S(1)}, u32[]{:S(2)}, u32[]{:S(2)}) %collective-permute-start.1) | collective-permute-done | bytes 65568 | tf_op jit(solution)/shard_map/ppermute | solution.py:413
  18.2 1.5 %collective-permute-done.2.refs_1_ = f32[8,2048]{1,0:T(8,128)S(1)} collective-permute-done((f32[8,2048]{1,0:T(8,128)S(1)}, f32[8,2048]{1,0:T(8,128)S(1)}, u32[]{:S(2)}, u32[]{:S(2)}) %collective-permute-start.2) | collective-permute-done | bytes 65568 | tf_op jit(solution)/shard_map/ppermute | solution.py:414
  19.7 0.0 collective-permute-done.3.refs_2_
  19.8 1.7 %collective-permute-start.4 = (f32[24,512]{1,0:T(8,128)S(1)}, f32[24,512]{1,0:T(8,128)S(1)}, u32[]{:S(2)}, u32[]{:S(2)}) collective-permute-start(f32[24,512]{1,0:T(8,128)S(1)} %get-tuple-element.18), channel_id=1, source_target_pairs={{0,4},{4,8},{8,12},{12,0},{1,5},{5,9},{9,13},{13,1},{2,6},{6,10},{... | collective-permute-start | bytes 147464 | tf_op jit(solution)/shard_map/ppermute | solution.py:418
  21.5 2.6 %collective-permute-start.5 = (f32[24,512]{1,0:T(8,128)S(1)}, f32[24,512]{1,0:T(8,128)S(1)}, u32[]{:S(2)}, u32[]{:S(2)}) collective-permute-start(f32[24,512]{1,0:T(8,128)S(1)} %get-tuple-element.19), channel_id=1, source_target_pairs={{0,8},{4,12},{8,0},{12,4},{1,9},{5,13},{9,1},{13,5},{2,10},{6,14},... | collective-permute-start | bytes 147464 | tf_op jit(solution)/shard_map/ppermute | solution.py:418
  24.1 1.3 %collective-permute-start.6 = (f32[24,512]{1,0:T(8,128)S(1)}, f32[24,512]{1,0:T(8,128)S(1)}, u32[]{:S(2)}, u32[]{:S(2)}) collective-permute-start(f32[24,512]{1,0:T(8,128)S(1)} %get-tuple-element.20), channel_id=1, source_target_pairs={{0,12},{4,0},{8,4},{12,8},{1,13},{5,1},{9,5},{13,9},{2,14},{6,2},{... | collective-permute-start | bytes 147464 | tf_op jit(solution)/shard_map/ppermute | solution.py:418
  25.4 0.3 collective-permute-done.4.refs_1_
  25.7 2.2 %collective-permute-done.5.refs_2_ = f32[24,512]{1,0:T(8,128)S(1)} collective-permute-done((f32[24,512]{1,0:T(8,128)S(1)}, f32[24,512]{1,0:T(8,128)S(1)}, u32[]{:S(2)}, u32[]{:S(2)}) %collective-permute-start.5) | collective-permute-done | bytes 49184 | tf_op jit(solution)/shard_map/ppermute | solution.py:418
  27.9 0.4 %collective-permute-done.6.refs_3_ = f32[24,512]{1,0:T(8,128)S(1)} collective-permute-done((f32[24,512]{1,0:T(8,128)S(1)}, f32[24,512]{1,0:T(8,128)S(1)}, u32[]{:S(2)}, u32[]{:S(2)}) %collective-permute-start.6) | collective-permute-done | bytes 49184 | tf_op jit(solution)/shard_map/ppermute | solution.py:418
  28.3 0.1 collective-permute-start.7
  28.4 1.3 %quadrant.1 = (f32[1024,1024]{1,0:T(8,128)}, bf16[512,256]{1,0:T(8,128)(2,1)S(1)}, bf16[256,512]{1,0:T(8,128)(2,1)S(1)}) custom-call(f32[24,512]{1,0:T(8,128)S(1)} %get-tuple-element.17.refs_0_, f32[24,512]{1,0:T(8,128)S(1)} %collective-permute-done.4.refs_1_, f32[24,512]{1,0:T(8,128)S(1)} %collective-permute-done.5.refs_2_, ...), custom_call_target="tpu_custom_call" | custom-call | flops 268435456 | bytes 1048576 | tf_op jit(solution)/shard_map/quadrant/pallas_call | solution.py:343
  29.6 0.1 collective-permute-done.7.bundle
  29.7 1.9 %fisher.1 = (f32[8,1024]{1,0:T(8,128)}, f32[1024,1024]{1,0:T(8,128)}) custom-call(f32[1024,1024]{1,0:T(8,128)} %get-tuple-element.21.begun, bf16[512,256]{1,0:T(8,128)(2,1)S(1)} %get-tuple-element.22.left, bf16[256,512]{1,0:T(8,128)(2,1)S(1)} %get-tuple-element.23.right, ...), custom_call_target="tpu_custom_call", output_to_operand_aliasing={{1}: (0, {})} | custom-call | tf_op jit(solution)/shard_map/fisher/pallas_call | solution.py:365
  (2 shorter events, 0.0 us)
Async XLA Ops:
  3.9 9.5 %collective-permute-start = (f32[4,128,128]{2,1,0:T(8,128)S(1)}, f32[4,128,128]{2,1,0:T(8,128)S(1)}, u32[]{:S(2)}, u32[]{:S(2)}) collective-permute-start(f32[4,128,128]{2,1,0:T(8,128)S(1)} %project_acts.1.own), channel_id=1, source_target_pairs={{0,2},{2,0},{1,3},{3,1},{4,6},{6,4},{5,7},{7,5},{8,10},{10,8},{9,1... | collective-permute-start | bytes 786440 | tf_op jit(solution)/shard_map/ppermute | solution.py:392
  13.9 4.3 %collective-permute-start.1 = (f32[8,2048]{1,0:T(8,128)S(1)}, f32[8,2048]{1,0:T(8,128)S(1)}, u32[]{:S(2)}, u32[]{:S(2)}) collective-permute-start(f32[8,2048]{1,0:T(8,128)S(1)} %get-tuple-element.13), channel_id=1, source_target_pairs={{0,3},{1,2},{2,1},{3,0},{4,7},{5,6},{6,5},{7,4},{8,11},{9,10},{10,... | collective-permute-start | bytes 196616 | tf_op jit(solution)/shard_map/ppermute | solution.py:413
  14.1 5.6 %collective-permute-start.2 = (f32[8,2048]{1,0:T(8,128)S(1)}, f32[8,2048]{1,0:T(8,128)S(1)}, u32[]{:S(2)}, u32[]{:S(2)}) collective-permute-start(f32[8,2048]{1,0:T(8,128)S(1)} %get-tuple-element.14), channel_id=1, source_target_pairs={{0,2},{2,0},{1,3},{3,1},{4,6},{6,4},{5,7},{7,5},{8,10},{10,8},{9,1... | collective-permute-start | bytes 196616 | tf_op jit(solution)/shard_map/ppermute | solution.py:414
  15.6 4.1 %collective-permute-start.3 = (f32[8,2048]{1,0:T(8,128)S(1)}, f32[8,2048]{1,0:T(8,128)S(1)}, u32[]{:S(2)}, u32[]{:S(2)}) collective-permute-start(f32[8,2048]{1,0:T(8,128)S(1)} %get-tuple-element.15), channel_id=1, source_target_pairs={{0,1},{1,0},{2,3},{3,2},{4,5},{5,4},{6,7},{7,6},{8,9},{9,8},{10,11... | collective-permute-start | bytes 196616 | tf_op jit(solution)/shard_map/ppermute | solution.py:415
  19.8 5.9 %collective-permute-start.4 = (f32[24,512]{1,0:T(8,128)S(1)}, f32[24,512]{1,0:T(8,128)S(1)}, u32[]{:S(2)}, u32[]{:S(2)}) collective-permute-start(f32[24,512]{1,0:T(8,128)S(1)} %get-tuple-element.18), channel_id=1, source_target_pairs={{0,4},{4,8},{8,12},{12,0},{1,5},{5,9},{9,13},{13,1},{2,6},{6,10},{... | collective-permute-start | bytes 147464 | tf_op jit(solution)/shard_map/ppermute | solution.py:418
  21.5 6.4 %collective-permute-start.5 = (f32[24,512]{1,0:T(8,128)S(1)}, f32[24,512]{1,0:T(8,128)S(1)}, u32[]{:S(2)}, u32[]{:S(2)}) collective-permute-start(f32[24,512]{1,0:T(8,128)S(1)} %get-tuple-element.19), channel_id=1, source_target_pairs={{0,8},{4,12},{8,0},{12,4},{1,9},{5,13},{9,1},{13,5},{2,10},{6,14},... | collective-permute-start | bytes 147464 | tf_op jit(solution)/shard_map/ppermute | solution.py:418
  24.1 4.2 %collective-permute-start.6 = (f32[24,512]{1,0:T(8,128)S(1)}, f32[24,512]{1,0:T(8,128)S(1)}, u32[]{:S(2)}, u32[]{:S(2)}) collective-permute-start(f32[24,512]{1,0:T(8,128)S(1)} %get-tuple-element.20), channel_id=1, source_target_pairs={{0,12},{4,0},{8,4},{12,8},{1,13},{5,1},{9,5},{13,9},{2,14},{6,2},{... | collective-permute-start | bytes 147464 | tf_op jit(solution)/shard_map/ppermute | solution.py:418
  28.3 1.4 %collective-permute-start.7 = (f32[64,512]{1,0:T(8,128)S(1)}, f32[64,512]{1,0:T(8,128)S(1)}, u32[]{:S(2)}, u32[]{:S(2)}) collective-permute-start(f32[64,512]{1,0:T(8,128)S(1)} %bundle.1), channel_id=1, source_target_pairs={{0,1},{1,0},{2,3},{3,2},{4,5},{5,4},{6,7},{7,6},{8,9},{9,8},{10,11... | collective-permute-start | bytes 393224 | tf_op jit(solution)/shard_map/ppermute | solution.py:419

commit v17 on v15

--- a/solution.py
+++ b/solution.py
@@ -11,6 +11,7 @@
 BLOCK = 64
 LANES = 128
 STRIDE = 72
+TABLE_COPIES = 4
 VMEM_BYTES = 48 * 1024 * 1024
 
 
@@ -35,9 +36,9 @@
     return high, mid, low
 
 
-def spread_table(table, spread):
+def spread_table(table, spread, first, last):
     entries = table.shape[0]
-    for row in range(0, BLOCK, 2):
+    for row in range(first, last, 2):
         both = table[:, row * PROJ : row * PROJ + LANES].astype(jnp.float32)
         spread[pl.ds(row, entries, stride=STRIDE), :] = both
         spread[pl.ds(row + 1, entries, stride=STRIDE), :] = pltpu.roll(both, PROJ, 1)
@@ -84,18 +85,22 @@
         copies.append(pltpu.make_async_copy(rows_ref.at[:, columns], held.at[:, columns], sems.at[c]))
         starts.append(start)
         start += width
+    quarter = BLOCK // TABLE_COPIES
+    parts = [pl.ds(k * quarter * PROJ, quarter * PROJ) for k in range(TABLE_COPIES)]
+    small = [(table.at[:, part], own_table.at[:, part]) for part in parts]
+    small += [(ids, own_ids), (signs, own_signs)]
     small = [
-        pltpu.make_async_copy(source, kept, sems.at[len(widths) + k])
-        for k, (source, kept) in enumerate(((table, own_table), (ids, own_ids), (signs, own_signs)))
+        pltpu.make_async_copy(source, kept, sems.at[len(widths) + k]) for k, (source, kept) in enumerate(small)
     ]
     for copy in small + copies:
         copy.start()
-    small[0].wait()
-    spread_table(own_table, spread)
+    for k in range(TABLE_COPIES):
+        small[k].wait()
+        spread_table(own_table, spread, k * quarter, (k + 1) * quarter)
     if signed is not None:
         sign_table(spread, signed)
-    small[1].wait()
-    small[2].wait()
+    for copy in small[TABLE_COPIES:]:
+        copy.wait()
     lay = functools.partial(lay_blocks, own_ids, own_signs, spread, signed, matrix)
     lay(0, widths[0] // BLOCK)
     for c, copy in enumerate(copies):
@@ -145,7 +150,7 @@
             pltpu.VMEM(table.shape, table.dtype),
             pltpu.SMEM(ids.shape, ids.dtype),
             pltpu.SMEM(signs.shape, signs.dtype),
-            pltpu.SemaphoreType.DMA((len(widths) + 3,)),
+            pltpu.SemaphoreType.DMA((len(widths) + TABLE_COPIES + 2,)),
         ]
         + signed,
         compiler_params=pltpu.CompilerParams(vmem_limit_bytes=VMEM_BYTES),

time: 31.5 us -> 31.6 us (level)
  no operation moved by 1% of the time
where the time goes in v17:
time: 31.6 us; the launch traced here: 31.4 us
  Pallas kernels  13.3 us (42%)
  starting transfers between devices  10.6 us (34%)
  waiting for transfers between devices  6.88 us (22%)
  between operations  0.69 us (2%)
    pallas_call x2, Pallas kernels, project(): pl.pallas_call(functools.partial(project_kernel, widths), out_shape=jax.S...  9.56 us
    ppermute x3, starting transfers between devices, local(): lax.ppermute(parcels[k], 'dp', [(d, (d + k) % dp) for d in range(dp)])  5.57 us
    ppermute x1, starting transfers between devices, local(): other = lax.ppermute(act, 'tensor', swap)  3 us
    ppermute x3, waiting for transfers between devices, local(): lax.ppermute(parcels[k], 'dp', [(d, (d + k) % dp) for d in range(dp)])  2.87 us
    ppermute x1, waiting for transfers between devices, local(): lax.ppermute(krons[1], ('tensor', 'seq'), [(p, 3 - p) for p in range(shar...  2.48 us
    pallas_call x1, Pallas kernels, fisher_block(): pl.pallas_call(functools.partial(fisher_kernel, 1.0 / (rows * len(parcels...  1.94 us
    ppermute x1, starting transfers between devices, local(): beside = lax.ppermute(krons[2], 'tensor', swap)  1.51 us
    ppermute x1, waiting for transfers between devices, local(): beside = lax.ppermute(krons[2], 'tensor', swap)  1.45 us
  transfers between devices with their start and end apart: 8, of which 6 were waited for; matrix products, arithmetic and copies ran while one was open for 0% of the time, Pallas kernels for 25%

profile of v17, /device:TPU:0, one launch (start us, length us, event | category | flops | bytes accessed | tf_op | source)
XLA Modules:
  0.0 31.4 jit_solution(7868958147245509027)
XLA Ops:
  0.6 3.0 %project_acts.1.own = f32[4,128,128]{2,1,0:T(8,128)S(1)} custom-call(s32[32]{0:T(128)} %ids.3, s32[32]{0:T(128)} %signs.3, bf16[32,4096]{1,0:T(8,128)(2,1)} %table.3, bf16[1024,2048]{1,0:T(8,128)(2,1)} %bitcast.3), custom_call_target="tpu_custom_call" | custom-call | flops 536870912 | bytes 4194304 | tf_op jit(solution)/shard_map/project_acts/pallas_call | solution.py:140
  3.7 3.0 %collective-permute-start = (f32[4,128,128]{2,1,0:T(8,128)S(1)}, f32[4,128,128]{2,1,0:T(8,128)S(1)}, u32[]{:S(2)}, u32[]{:S(2)}) collective-permute-start(f32[4,128,128]{2,1,0:T(8,128)S(1)} %project_acts.1.own), channel_id=1, source_target_pairs={{0,2},{2,0},{1,3},{3,1},{4,6},{6,4},{5,7},{7,5},{8,10},{10,8},{9,1... | collective-permute-start | bytes 786440 | tf_op jit(solution)/shard_map/ppermute | solution.py:382
  6.7 6.5 %project_grads.1.grads = f32[4,128,128]{2,1,0:T(8,128)S(1)} custom-call(s32[112]{0:T(128)} %ids.2, s32[112]{0:T(128)} %signs.2, bf16[32,4096]{1,0:T(8,128)(2,1)} %table.2, bf16[1024,7168]{1,0:T(8,128)(2,1)} %bitcast.2), custom_call_target="tpu_custom_call" | custom-call | flops 1879048192 | bytes 14680064 | tf_op jit(solution)/shard_map/project_grads/pallas_call | solution.py:140
  13.2 0.0 collective-permute-done.act
  13.2 0.5 %kron.1 = (f32[8,2048]{1,0:T(8,128)S(1)}, f32[8,2048]{1,0:T(8,128)S(1)}, f32[8,2048]{1,0:T(8,128)S(1)}, f32[8,2048]{1,0:T(8,128)S(1)}) custom-call(f32[4,128,128]{2,1,0:T(8,128)S(1)} %project_grads.1.grads, f32[4,128,128]{2,1,0:T(8,128)S(1)} %project_acts.1.own, f32[4,128,128]{2,1,0:T(8,128)S(1)} %collective-permute-done.act), custom_call_target="tpu_custom_call" | custom-call | tf_op jit(solution)/shard_map/kron/pallas_call | solution.py:195
  13.7 0.1 collective-permute-start.1
  13.9 1.5 %collective-permute-start.2 = (f32[8,2048]{1,0:T(8,128)S(1)}, f32[8,2048]{1,0:T(8,128)S(1)}, u32[]{:S(2)}, u32[]{:S(2)}) collective-permute-start(f32[8,2048]{1,0:T(8,128)S(1)} %get-tuple-element.14), channel_id=1, source_target_pairs={{0,2},{2,0},{1,3},{3,1},{4,6},{6,4},{5,7},{7,5},{8,10},{10,8},{9,1... | collective-permute-start | bytes 196616 | tf_op jit(solution)/shard_map/ppermute | solution.py:404
  15.4 0.3 collective-permute-start.3
  15.7 2.5 %collective-permute-done.1.refs_0_ = f32[8,2048]{1,0:T(8,128)S(1)} collective-permute-done((f32[8,2048]{1,0:T(8,128)S(1)}, f32[8,2048]{1,0:T(8,128)S(1)}, u32[]{:S(2)}, u32[]{:S(2)}) %collective-permute-start.1) | collective-permute-done | bytes 65568 | tf_op jit(solution)/shard_map/ppermute | solution.py:403
  18.1 1.5 %collective-permute-done.2.refs_1_ = f32[8,2048]{1,0:T(8,128)S(1)} collective-permute-done((f32[8,2048]{1,0:T(8,128)S(1)}, f32[8,2048]{1,0:T(8,128)S(1)}, u32[]{:S(2)}, u32[]{:S(2)}) %collective-permute-start.2) | collective-permute-done | bytes 65568 | tf_op jit(solution)/shard_map/ppermute | solution.py:404
  19.6 0.0 collective-permute-done.3.refs_2_
  19.6 1.6 %collective-permute-start.4 = (f32[24,512]{1,0:T(8,128)S(1)}, f32[24,512]{1,0:T(8,128)S(1)}, u32[]{:S(2)}, u32[]{:S(2)}) collective-permute-start(f32[24,512]{1,0:T(8,128)S(1)} %get-tuple-element.18), channel_id=1, source_target_pairs={{0,4},{4,8},{8,12},{12,0},{1,5},{5,9},{9,13},{13,1},{2,6},{6,10},{... | collective-permute-start | bytes 147464 | tf_op jit(solution)/shard_map/ppermute | solution.py:408
  21.3 2.6 %collective-permute-start.5 = (f32[24,512]{1,0:T(8,128)S(1)}, f32[24,512]{1,0:T(8,128)S(1)}, u32[]{:S(2)}, u32[]{:S(2)}) collective-permute-start(f32[24,512]{1,0:T(8,128)S(1)} %get-tuple-element.19), channel_id=1, source_target_pairs={{0,8},{4,12},{8,0},{12,4},{1,9},{5,13},{9,1},{13,5},{2,10},{6,14},... | collective-permute-start | bytes 147464 | tf_op jit(solution)/shard_map/ppermute | solution.py:408
  23.9 1.4 %collective-permute-start.6 = (f32[24,512]{1,0:T(8,128)S(1)}, f32[24,512]{1,0:T(8,128)S(1)}, u32[]{:S(2)}, u32[]{:S(2)}) collective-permute-start(f32[24,512]{1,0:T(8,128)S(1)} %get-tuple-element.20), channel_id=1, source_target_pairs={{0,12},{4,0},{8,4},{12,8},{1,13},{5,1},{9,5},{13,9},{2,14},{6,2},{... | collective-permute-start | bytes 147464 | tf_op jit(solution)/shard_map/ppermute | solution.py:408
  25.2 0.4 %collective-permute-done.4.refs_1_ = f32[24,512]{1,0:T(8,128)S(1)} collective-permute-done((f32[24,512]{1,0:T(8,128)S(1)}, f32[24,512]{1,0:T(8,128)S(1)}, u32[]{:S(2)}, u32[]{:S(2)}) %collective-permute-start.4) | collective-permute-done | bytes 49184 | tf_op jit(solution)/shard_map/ppermute | solution.py:408
  25.7 2.0 %collective-permute-done.5.refs_2_ = f32[24,512]{1,0:T(8,128)S(1)} collective-permute-done((f32[24,512]{1,0:T(8,128)S(1)}, f32[24,512]{1,0:T(8,128)S(1)}, u32[]{:S(2)}, u32[]{:S(2)}) %collective-permute-start.5) | collective-permute-done | bytes 49184 | tf_op jit(solution)/shard_map/ppermute | solution.py:408
  27.7 0.4 %collective-permute-done.6.refs_3_ = f32[24,512]{1,0:T(8,128)S(1)} collective-permute-done((f32[24,512]{1,0:T(8,128)S(1)}, f32[24,512]{1,0:T(8,128)S(1)}, u32[]{:S(2)}, u32[]{:S(2)}) %collective-permute-start.6) | collective-permute-done | bytes 49184 | tf_op jit(solution)/shard_map/ppermute | solution.py:408
  28.1 0.1 collective-permute-start.7
  28.2 1.3 %quadrant.1 = (f32[1024,1024]{1,0:T(8,128)}, bf16[512,256]{1,0:T(8,128)(2,1)S(1)}, bf16[256,512]{1,0:T(8,128)(2,1)S(1)}) custom-call(f32[24,512]{1,0:T(8,128)S(1)} %get-tuple-element.17.refs_0_, f32[24,512]{1,0:T(8,128)S(1)} %collective-permute-done.4.refs_1_, f32[24,512]{1,0:T(8,128)S(1)} %collective-permute-done.5.refs_2_, ...), custom_call_target="tpu_custom_call" | custom-call | flops 268435456 | bytes 1048576 | tf_op jit(solution)/shard_map/quadrant/pallas_call | solution.py:333
  29.4 0.1 collective-permute-done.7.bundle
  29.5 1.9 %fisher.1 = (f32[8,1024]{1,0:T(8,128)}, f32[1024,1024]{1,0:T(8,128)}) custom-call(f32[1024,1024]{1,0:T(8,128)} %get-tuple-element.21.begun, bf16[512,256]{1,0:T(8,128)(2,1)S(1)} %get-tuple-element.22.left, bf16[256,512]{1,0:T(8,128)(2,1)S(1)} %get-tuple-element.23.right, ...), custom_call_target="tpu_custom_call", output_to_operand_aliasing={{1}: (0, {})} | custom-call | tf_op jit(solution)/shard_map/fisher/pallas_call | solution.py:355
  (2 shorter events, 0.0 us)
Async XLA Ops:
  3.7 9.6 %collective-permute-start = (f32[4,128,128]{2,1,0:T(8,128)S(1)}, f32[4,128,128]{2,1,0:T(8,128)S(1)}, u32[]{:S(2)}, u32[]{:S(2)}) collective-permute-start(f32[4,128,128]{2,1,0:T(8,128)S(1)} %project_acts.1.own), channel_id=1, source_target_pairs={{0,2},{2,0},{1,3},{3,1},{4,6},{6,4},{5,7},{7,5},{8,10},{10,8},{9,1... | collective-permute-start | bytes 786440 | tf_op jit(solution)/shard_map/ppermute | solution.py:382
  13.7 4.4 %collective-permute-start.1 = (f32[8,2048]{1,0:T(8,128)S(1)}, f32[8,2048]{1,0:T(8,128)S(1)}, u32[]{:S(2)}, u32[]{:S(2)}) collective-permute-start(f32[8,2048]{1,0:T(8,128)S(1)} %get-tuple-element.13), channel_id=1, source_target_pairs={{0,3},{1,2},{2,1},{3,0},{4,7},{5,6},{6,5},{7,4},{8,11},{9,10},{10,... | collective-permute-start | bytes 196616 | tf_op jit(solution)/shard_map/ppermute | solution.py:403
  13.9 5.7 %collective-permute-start.2 = (f32[8,2048]{1,0:T(8,128)S(1)}, f32[8,2048]{1,0:T(8,128)S(1)}, u32[]{:S(2)}, u32[]{:S(2)}) collective-permute-start(f32[8,2048]{1,0:T(8,128)S(1)} %get-tuple-element.14), channel_id=1, source_target_pairs={{0,2},{2,0},{1,3},{3,1},{4,6},{6,4},{5,7},{7,5},{8,10},{10,8},{9,1... | collective-permute-start | bytes 196616 | tf_op jit(solution)/shard_map/ppermute | solution.py:404
  15.4 4.2 %collective-permute-start.3 = (f32[8,2048]{1,0:T(8,128)S(1)}, f32[8,2048]{1,0:T(8,128)S(1)}, u32[]{:S(2)}, u32[]{:S(2)}) collective-permute-start(f32[8,2048]{1,0:T(8,128)S(1)} %get-tuple-element.15), channel_id=1, source_target_pairs={{0,1},{1,0},{2,3},{3,2},{4,5},{5,4},{6,7},{7,6},{8,9},{9,8},{10,11... | collective-permute-start | bytes 196616 | tf_op jit(solution)/shard_map/ppermute | solution.py:405
  19.6 6.0 %collective-permute-start.4 = (f32[24,512]{1,0:T(8,128)S(1)}, f32[24,512]{1,0:T(8,128)S(1)}, u32[]{:S(2)}, u32[]{:S(2)}) collective-permute-start(f32[24,512]{1,0:T(8,128)S(1)} %get-tuple-element.18), channel_id=1, source_target_pairs={{0,4},{4,8},{8,12},{12,0},{1,5},{5,9},{9,13},{13,1},{2,6},{6,10},{... | collective-permute-start | bytes 147464 | tf_op jit(solution)/shard_map/ppermute | solution.py:408
  21.3 6.4 %collective-permute-start.5 = (f32[24,512]{1,0:T(8,128)S(1)}, f32[24,512]{1,0:T(8,128)S(1)}, u32[]{:S(2)}, u32[]{:S(2)}) collective-permute-start(f32[24,512]{1,0:T(8,128)S(1)} %get-tuple-element.19), channel_id=1, source_target_pairs={{0,8},{4,12},{8,0},{12,4},{1,9},{5,13},{9,1},{13,5},{2,10},{6,14},... | collective-permute-start | bytes 147464 | tf_op jit(solution)/shard_map/ppermute | solution.py:408
  23.9 4.2 %collective-permute-start.6 = (f32[24,512]{1,0:T(8,128)S(1)}, f32[24,512]{1,0:T(8,128)S(1)}, u32[]{:S(2)}, u32[]{:S(2)}) collective-permute-start(f32[24,512]{1,0:T(8,128)S(1)} %get-tuple-element.20), channel_id=1, source_target_pairs={{0,12},{4,0},{8,4},{12,8},{1,13},{5,1},{9,5},{13,9},{2,14},{6,2},{... | collective-permute-start | bytes 147464 | tf_op jit(solution)/shard_map/ppermute | solution.py:408
  28.1 1.4 %collective-permute-start.7 = (f32[64,512]{1,0:T(8,128)S(1)}, f32[64,512]{1,0:T(8,128)S(1)}, u32[]{:S(2)}, u32[]{:S(2)}) collective-permute-start(f32[64,512]{1,0:T(8,128)S(1)} %bundle.1), channel_id=1, source_target_pairs={{0,1},{1,0},{2,3},{3,2},{4,5},{5,4},{6,7},{7,6},{8,9},{9,8},{10,11... | collective-permute-start | bytes 393224 | tf_op jit(solution)/shard_map/ppermute | solution.py:409

commit v18 on v15

--- a/solution.py
+++ b/solution.py
@@ -35,29 +35,30 @@
     return high, mid, low
 
 
+def gap(entries):
+    return entries + 8
+
+
 def spread_table(table, spread):
     entries = table.shape[0]
     for row in range(0, BLOCK, 2):
         both = table[:, row * PROJ : row * PROJ + LANES].astype(jnp.float32)
-        spread[pl.ds(row, entries, stride=STRIDE), :] = both
-        spread[pl.ds(row + 1, entries, stride=STRIDE), :] = pltpu.roll(both, PROJ, 1)
-
-
-def sign_table(spread, signed):
-    entries = spread.shape[0] // STRIDE
+        spread[pl.ds(row * gap(entries), entries), :] = both
+        spread[pl.ds((row + 1) * gap(entries), entries), :] = pltpu.roll(both, PROJ, 1)
+
+
+def sign_table(entries, spread, signed):
     for entry in range(entries):
-        block = spread[pl.ds(entry * STRIDE, BLOCK), :].astype(jnp.bfloat16)
+        block = spread[pl.ds(entry, BLOCK, stride=gap(entries)), :].astype(jnp.bfloat16)
         signed[pl.ds((entries + entry) * BLOCK, BLOCK), :] = block
         signed[pl.ds(entry * BLOCK, BLOCK), :] = -block
 
 
-def lay_blocks(ids, signs, spread, signed, matrix, first, last):
-    entries = spread.shape[0] // STRIDE
+def lay_blocks(ids, signs, entries, spread, signed, matrix, first, last):
     for j in range(first, last):
         if signed is None:
-            start = pl.multiple_of(ids[j] * STRIDE, 8)
             sign = (2 * signs[j] - 1).astype(jnp.float32)
-            block = (spread[pl.ds(start, BLOCK), :] * sign).astype(jnp.bfloat16)
+            block = (spread[pl.ds(ids[j], BLOCK, stride=gap(entries)), :] * sign).astype(jnp.bfloat16)
         else:
             start = pl.multiple_of((signs[j] * entries + ids[j]) * BLOCK, BLOCK)
             block = signed[pl.ds(start, BLOCK), :]
@@ -93,10 +94,10 @@
     small[0].wait()
     spread_table(own_table, spread)
     if signed is not None:
-        sign_table(spread, signed)
+        sign_table(table.shape[0], spread, signed)
     small[1].wait()
     small[2].wait()
-    lay = functools.partial(lay_blocks, own_ids, own_signs, spread, signed, matrix)
+    lay = functools.partial(lay_blocks, own_ids, own_signs, table.shape[0], spread, signed, matrix)
     lay(0, widths[0] // BLOCK)
     for c, copy in enumerate(copies):
         columns = pl.ds(starts[c], widths[c])
@@ -138,7 +139,7 @@
         in_specs=[pl.BlockSpec(memory_space=pltpu.HBM)] * 4,
         out_specs=pl.BlockSpec(memory_space=pltpu.VMEM),
         scratch_shapes=[
-            pltpu.VMEM((entries * STRIDE, LANES), jnp.float32),
+            pltpu.VMEM((BLOCK * gap(entries), LANES), jnp.float32),
             pltpu.VMEM((width, LANES), jnp.bfloat16),
             pltpu.VMEM((rows, width), jnp.bfloat16),
             pltpu.VMEM((PROJ, rows), jnp.float32),

time: 31.5 us -> 31.6 us (level)
  transfers between devices with their start and end apart: 8 -> 8, of which waited for: 6 -> 6; matrix products, arithmetic and copies ran while one was open for 0% -> 0% of each run, Pallas kernels for 25% -> 24%
where the time goes in v18:
time: 31.6 us; the launch traced here: 31.5 us
  Pallas kernels  13.3 us (42%)
  starting transfers between devices  10.7 us (34%)
  waiting for transfers between devices  6.87 us (22%)
  between operations  0.69 us (2%)
    pallas_call x2, Pallas kernels, project(): pl.pallas_call(functools.partial(project_kernel, widths), out_shape=jax.S...  9.52 us
    ppermute x3, starting transfers between devices, local(): lax.ppermute(parcels[k], 'dp', [(d, (d + k) % dp) for d in range(dp)])  5.65 us
    ppermute x1, starting transfers between devices, local(): other = lax.ppermute(act, 'tensor', swap)  3 us
    ppermute x3, waiting for transfers between devices, local(): lax.ppermute(parcels[k], 'dp', [(d, (d + k) % dp) for d in range(dp)])  2.86 us
    ppermute x1, waiting for transfers between devices, local(): lax.ppermute(krons[1], ('tensor', 'seq'), [(p, 3 - p) for p in range(shar...  2.4 us
    pallas_call x1, Pallas kernels, fisher_block(): pl.pallas_call(functools.partial(fisher_kernel, 1.0 / (rows * len(parcels...  1.94 us
    ppermute x1, waiting for transfers between devices, local(): beside = lax.ppermute(krons[2], 'tensor', swap)  1.54 us
    ppermute x1, starting transfers between devices, local(): beside = lax.ppermute(krons[2], 'tensor', swap)  1.51 us
  transfers between devices with their start and end apart: 8, of which 6 were waited for; matrix products, arithmetic and copies ran while one was open for 0% of the time, Pallas kernels for 24%

profile of v18, /device:TPU:0, one launch (start us, length us, event | category | flops | bytes accessed | tf_op | source)
XLA Modules:
  0.0 31.5 jit_solution(258131111537618965)
XLA Ops:
  0.6 3.1 %project_acts.1.own = f32[4,128,128]{2,1,0:T(8,128)S(1)} custom-call(s32[32]{0:T(128)} %ids.3, s32[32]{0:T(128)} %signs.3, bf16[32,4096]{1,0:T(8,128)(2,1)} %table.3, bf16[1024,2048]{1,0:T(8,128)(2,1)} %bitcast.3), custom_call_target="tpu_custom_call" | custom-call | flops 536870912 | bytes 4194304 | tf_op jit(solution)/shard_map/project_acts/pallas_call | solution.py:136
  3.7 3.0 %collective-permute-start = (f32[4,128,128]{2,1,0:T(8,128)S(1)}, f32[4,128,128]{2,1,0:T(8,128)S(1)}, u32[]{:S(2)}, u32[]{:S(2)}) collective-permute-start(f32[4,128,128]{2,1,0:T(8,128)S(1)} %project_acts.1.own), channel_id=1, source_target_pairs={{0,2},{2,0},{1,3},{3,1},{4,6},{6,4},{5,7},{7,5},{8,10},{10,8},{9,1... | collective-permute-start | bytes 786440 | tf_op jit(solution)/shard_map/ppermute | solution.py:378
  6.7 6.5 %project_grads.1.grads = f32[4,128,128]{2,1,0:T(8,128)S(1)} custom-call(s32[112]{0:T(128)} %ids.2, s32[112]{0:T(128)} %signs.2, bf16[32,4096]{1,0:T(8,128)(2,1)} %table.2, bf16[1024,7168]{1,0:T(8,128)(2,1)} %bitcast.2), custom_call_target="tpu_custom_call" | custom-call | flops 1879048192 | bytes 14680064 | tf_op jit(solution)/shard_map/project_grads/pallas_call | solution.py:136
  13.2 0.0 collective-permute-done.act
  13.2 0.5 %kron.1 = (f32[8,2048]{1,0:T(8,128)S(1)}, f32[8,2048]{1,0:T(8,128)S(1)}, f32[8,2048]{1,0:T(8,128)S(1)}, f32[8,2048]{1,0:T(8,128)S(1)}) custom-call(f32[4,128,128]{2,1,0:T(8,128)S(1)} %project_grads.1.grads, f32[4,128,128]{2,1,0:T(8,128)S(1)} %project_acts.1.own, f32[4,128,128]{2,1,0:T(8,128)S(1)} %collective-permute-done.act), custom_call_target="tpu_custom_call" | custom-call | tf_op jit(solution)/shard_map/kron/pallas_call | solution.py:191
  13.7 0.2 collective-permute-start.1
  13.9 1.5 %collective-permute-start.2 = (f32[8,2048]{1,0:T(8,128)S(1)}, f32[8,2048]{1,0:T(8,128)S(1)}, u32[]{:S(2)}, u32[]{:S(2)}) collective-permute-start(f32[8,2048]{1,0:T(8,128)S(1)} %get-tuple-element.14), channel_id=1, source_target_pairs={{0,2},{2,0},{1,3},{3,1},{4,6},{6,4},{5,7},{7,5},{8,10},{10,8},{9,1... | collective-permute-start | bytes 196616 | tf_op jit(solution)/shard_map/ppermute | solution.py:400
  15.4 0.2 collective-permute-start.3
  15.6 2.4 %collective-permute-done.1.refs_0_ = f32[8,2048]{1,0:T(8,128)S(1)} collective-permute-done((f32[8,2048]{1,0:T(8,128)S(1)}, f32[8,2048]{1,0:T(8,128)S(1)}, u32[]{:S(2)}, u32[]{:S(2)}) %collective-permute-start.1) | collective-permute-done | bytes 65568 | tf_op jit(solution)/shard_map/ppermute | solution.py:399
  18.0 1.5 %collective-permute-done.2.refs_1_ = f32[8,2048]{1,0:T(8,128)S(1)} collective-permute-done((f32[8,2048]{1,0:T(8,128)S(1)}, f32[8,2048]{1,0:T(8,128)S(1)}, u32[]{:S(2)}, u32[]{:S(2)}) %collective-permute-start.2) | collective-permute-done | bytes 65568 | tf_op jit(solution)/shard_map/ppermute | solution.py:400
  19.6 0.0 collective-permute-done.3.refs_2_
  19.6 1.7 %collective-permute-start.4 = (f32[24,512]{1,0:T(8,128)S(1)}, f32[24,512]{1,0:T(8,128)S(1)}, u32[]{:S(2)}, u32[]{:S(2)}) collective-permute-start(f32[24,512]{1,0:T(8,128)S(1)} %get-tuple-element.18), channel_id=1, source_target_pairs={{0,4},{4,8},{8,12},{12,0},{1,5},{5,9},{9,13},{13,1},{2,6},{6,10},{... | collective-permute-start | bytes 147464 | tf_op jit(solution)/shard_map/ppermute | solution.py:404
  21.3 2.6 %collective-permute-start.5 = (f32[24,512]{1,0:T(8,128)S(1)}, f32[24,512]{1,0:T(8,128)S(1)}, u32[]{:S(2)}, u32[]{:S(2)}) collective-permute-start(f32[24,512]{1,0:T(8,128)S(1)} %get-tuple-element.19), channel_id=1, source_target_pairs={{0,8},{4,12},{8,0},{12,4},{1,9},{5,13},{9,1},{13,5},{2,10},{6,14},... | collective-permute-start | bytes 147464 | tf_op jit(solution)/shard_map/ppermute | solution.py:404
  23.9 1.4 %collective-permute-start.6 = (f32[24,512]{1,0:T(8,128)S(1)}, f32[24,512]{1,0:T(8,128)S(1)}, u32[]{:S(2)}, u32[]{:S(2)}) collective-permute-start(f32[24,512]{1,0:T(8,128)S(1)} %get-tuple-element.20), channel_id=1, source_target_pairs={{0,12},{4,0},{8,4},{12,8},{1,13},{5,1},{9,5},{13,9},{2,14},{6,2},{... | collective-permute-start | bytes 147464 | tf_op jit(solution)/shard_map/ppermute | solution.py:404
  25.3 0.3 collective-permute-done.4.refs_1_
  25.5 2.2 %collective-permute-done.5.refs_2_ = f32[24,512]{1,0:T(8,128)S(1)} collective-permute-done((f32[24,512]{1,0:T(8,128)S(1)}, f32[24,512]{1,0:T(8,128)S(1)}, u32[]{:S(2)}, u32[]{:S(2)}) %collective-permute-start.5) | collective-permute-done | bytes 49184 | tf_op jit(solution)/shard_map/ppermute | solution.py:404
  27.7 0.4 %collective-permute-done.6.refs_3_ = f32[24,512]{1,0:T(8,128)S(1)} collective-permute-done((f32[24,512]{1,0:T(8,128)S(1)}, f32[24,512]{1,0:T(8,128)S(1)}, u32[]{:S(2)}, u32[]{:S(2)}) %collective-permute-start.6) | collective-permute-done | bytes 49184 | tf_op jit(solution)/shard_map/ppermute | solution.py:404
  28.1 0.1 collective-permute-start.7
  28.2 1.3 %quadrant.1 = (f32[1024,1024]{1,0:T(8,128)}, bf16[512,256]{1,0:T(8,128)(2,1)S(1)}, bf16[256,512]{1,0:T(8,128)(2,1)S(1)}) custom-call(f32[24,512]{1,0:T(8,128)S(1)} %get-tuple-element.17.refs_0_, f32[24,512]{1,0:T(8,128)S(1)} %collective-permute-done.4.refs_1_, f32[24,512]{1,0:T(8,128)S(1)} %collective-permute-done.5.refs_2_, ...), custom_call_target="tpu_custom_call" | custom-call | flops 268435456 | bytes 1048576 | tf_op jit(solution)/shard_map/quadrant/pallas_call | solution.py:329
  29.5 0.1 collective-permute-done.7.bundle
  29.5 1.9 %fisher.1 = (f32[8,1024]{1,0:T(8,128)}, f32[1024,1024]{1,0:T(8,128)}) custom-call(f32[1024,1024]{1,0:T(8,128)} %get-tuple-element.21.begun, bf16[512,256]{1,0:T(8,128)(2,1)S(1)} %get-tuple-element.22.left, bf16[256,512]{1,0:T(8,128)(2,1)S(1)} %get-tuple-element.23.right, ...), custom_call_target="tpu_custom_call", output_to_operand_aliasing={{1}: (0, {})} | custom-call | tf_op jit(solution)/shard_map/fisher/pallas_call | solution.py:351
  (2 shorter events, 0.0 us)
Async XLA Ops:
  3.7 9.5 %collective-permute-start = (f32[4,128,128]{2,1,0:T(8,128)S(1)}, f32[4,128,128]{2,1,0:T(8,128)S(1)}, u32[]{:S(2)}, u32[]{:S(2)}) collective-permute-start(f32[4,128,128]{2,1,0:T(8,128)S(1)} %project_acts.1.own), channel_id=1, source_target_pairs={{0,2},{2,0},{1,3},{3,1},{4,6},{6,4},{5,7},{7,5},{8,10},{10,8},{9,1... | collective-permute-start | bytes 786440 | tf_op jit(solution)/shard_map/ppermute | solution.py:378
  13.7 4.3 %collective-permute-start.1 = (f32[8,2048]{1,0:T(8,128)S(1)}, f32[8,2048]{1,0:T(8,128)S(1)}, u32[]{:S(2)}, u32[]{:S(2)}) collective-permute-start(f32[8,2048]{1,0:T(8,128)S(1)} %get-tuple-element.13), channel_id=1, source_target_pairs={{0,3},{1,2},{2,1},{3,0},{4,7},{5,6},{6,5},{7,4},{8,11},{9,10},{10,... | collective-permute-start | bytes 196616 | tf_op jit(solution)/shard_map/ppermute | solution.py:399
  13.9 5.7 %collective-permute-start.2 = (f32[8,2048]{1,0:T(8,128)S(1)}, f32[8,2048]{1,0:T(8,128)S(1)}, u32[]{:S(2)}, u32[]{:S(2)}) collective-permute-start(f32[8,2048]{1,0:T(8,128)S(1)} %get-tuple-element.14), channel_id=1, source_target_pairs={{0,2},{2,0},{1,3},{3,1},{4,6},{6,4},{5,7},{7,5},{8,10},{10,8},{9,1... | collective-permute-start | bytes 196616 | tf_op jit(solution)/shard_map/ppermute | solution.py:400
  15.4 4.1 %collective-permute-start.3 = (f32[8,2048]{1,0:T(8,128)S(1)}, f32[8,2048]{1,0:T(8,128)S(1)}, u32[]{:S(2)}, u32[]{:S(2)}) collective-permute-start(f32[8,2048]{1,0:T(8,128)S(1)} %get-tuple-element.15), channel_id=1, source_target_pairs={{0,1},{1,0},{2,3},{3,2},{4,5},{5,4},{6,7},{7,6},{8,9},{9,8},{10,11... | collective-permute-start | bytes 196616 | tf_op jit(solution)/shard_map/ppermute | solution.py:401
  19.6 5.9 %collective-permute-start.4 = (f32[24,512]{1,0:T(8,128)S(1)}, f32[24,512]{1,0:T(8,128)S(1)}, u32[]{:S(2)}, u32[]{:S(2)}) collective-permute-start(f32[24,512]{1,0:T(8,128)S(1)} %get-tuple-element.18), channel_id=1, source_target_pairs={{0,4},{4,8},{8,12},{12,0},{1,5},{5,9},{9,13},{13,1},{2,6},{6,10},{... | collective-permute-start | bytes 147464 | tf_op jit(solution)/shard_map/ppermute | solution.py:404
  21.3 6.4 %collective-permute-start.5 = (f32[24,512]{1,0:T(8,128)S(1)}, f32[24,512]{1,0:T(8,128)S(1)}, u32[]{:S(2)}, u32[]{:S(2)}) collective-permute-start(f32[24,512]{1,0:T(8,128)S(1)} %get-tuple-element.19), channel_id=1, source_target_pairs={{0,8},{4,12},{8,0},{12,4},{1,9},{5,13},{9,1},{13,5},{2,10},{6,14},... | collective-permute-start | bytes 147464 | tf_op jit(solution)/shard_map/ppermute | solution.py:404
  23.9 4.2 %collective-permute-start.6 = (f32[24,512]{1,0:T(8,128)S(1)}, f32[24,512]{1,0:T(8,128)S(1)}, u32[]{:S(2)}, u32[]{:S(2)}) collective-permute-start(f32[24,512]{1,0:T(8,128)S(1)} %get-tuple-element.20), channel_id=1, source_target_pairs={{0,12},{4,0},{8,4},{12,8},{1,13},{5,1},{9,5},{13,9},{2,14},{6,2},{... | collective-permute-start | bytes 147464 | tf_op jit(solution)/shard_map/ppermute | solution.py:404
  28.1 1.4 %collective-permute-start.7 = (f32[64,512]{1,0:T(8,128)S(1)}, f32[64,512]{1,0:T(8,128)S(1)}, u32[]{:S(2)}, u32[]{:S(2)}) collective-permute-start(f32[64,512]{1,0:T(8,128)S(1)} %bundle.1), channel_id=1, source_target_pairs={{0,1},{1,0},{2,3},{3,2},{4,5},{5,4},{6,7},{7,6},{8,9},{9,8},{10,11... | collective-permute-start | bytes 393224 | tf_op jit(solution)/shard_map/ppermute | solution.py:405

commit v19 on v15

--- a/solution.py
+++ b/solution.py
@@ -272,50 +272,36 @@
     return [pl.ds(pl.multiple_of(place * part, part), part) for place in (core, 1 - core)]
 
 
-TILE = 256
-
-
 def quadrant_kernel(scale, *refs):
-    parcels, (out, left_ref, right_ref, made, sems) = refs[:-5], refs[-5:]
-    part = parcels[0].shape[1]
-    left, right = own_halves(parcels)
-    left, right = left_operand(left), right_operand(right * scale)
-    left_ref[...], right_ref[...] = left, right
-    here, _ = halves_at(part)
-    copies = []
-    for k in range(part // TILE):
-        rows = slice(k * TILE, (k + 1) * TILE)
-        made[rows, :] = jnp.dot(left[rows], right, preferred_element_type=jnp.float32)
-        into = pl.ds(pl.multiple_of(lax.axis_index("seq") * part + k * TILE, TILE), TILE)
-        copies.append(pltpu.make_async_copy(made.at[rows], out.at[into, here], sems.at[k]))
-        copies[-1].start()
-    for copy in copies:
-        copy.wait()
-
-
-def fisher_kernel(scale, begun, left, right, bundle, *refs):
-    del begun
+    parcels, (quadrant, left, right) = refs[:-3], refs[-3:]
+    own_left, own_right = own_halves(parcels)
+    left[...], right[...] = left_operand(own_left), right_operand(own_right * scale)
+    quadrant[...] = jnp.dot(left[...], right[...], preferred_element_type=jnp.float32)
+
+
+def fisher_kernel(scale, quadrant, left, right, bundle, *refs):
     parcels, (mine, out, made, kept, sems) = refs[:-5], refs[-5:]
     rows, part = parcels[0].shape[0] // 3, parcels[0].shape[1]
     here, there = halves_at(part)
     kept[:, here] = parcels[0][pl.ds(0, rows), :]
     kept[:, there] = bundle[pl.ds(0, rows), :]
-    copies = [pltpu.make_async_copy(kept, mine, sems.at[0])]
-    copies[0].start()
+    copies = [
+        pltpu.make_async_copy(quadrant, out.at[here, here], sems.at[0]),
+        pltpu.make_async_copy(kept, mine, sems.at[1]),
+    ]
+    for copy in copies:
+        copy.start()
     count = len(parcels)
     other_left = jnp.concatenate([bundle[pl.ds(2 * k * rows, rows), :] for k in range(count)], axis=0)
     other_right = jnp.concatenate([bundle[pl.ds((2 * k + 1) * rows, rows), :] for k in range(count)], axis=0)
-    right, other_right = right[...], right_operand(other_right * scale)
-    for k in range(part // TILE):
-        piece = slice(k * TILE, (k + 1) * TILE)
-        made[0, piece, :] = jnp.dot(left[piece, :], other_right, preferred_element_type=jnp.float32)
-        into = pl.ds(pl.multiple_of(lax.axis_index("seq") * part + k * TILE, TILE), TILE)
-        copies.append(pltpu.make_async_copy(made.at[0, piece], out.at[into, there], sems.at[k + 1]))
-        copies[-1].start()
+    other_right = right_operand(other_right * scale)
+    made[0] = jnp.dot(left[...], other_right, preferred_element_type=jnp.float32)
+    copies.append(pltpu.make_async_copy(made.at[0], out.at[here, there], sems.at[2]))
+    copies[-1].start()
     other_left = left_operand(other_left)
-    for k, (operand_right, into) in enumerate(((other_right, there), (right, here))):
+    for k, (operand_right, into) in enumerate(((other_right, there), (right[...], here))):
         made[k + 1] = jnp.dot(other_left, operand_right, preferred_element_type=jnp.float32)
-        copies.append(pltpu.make_async_copy(made.at[k + 1], out.at[there, into], sems.at[part // TILE + k + 1]))
+        copies.append(pltpu.make_async_copy(made.at[k + 1], out.at[there, into], sems.at[k + 3]))
         copies[-1].start()
     for copy in copies:
         copy.wait()
@@ -328,13 +314,12 @@
     return pl.pallas_call(
         functools.partial(quadrant_kernel, 1.0 / total),
         out_shape=[
-            jax.ShapeDtypeStruct((2 * part, 2 * part), jnp.float32),
+            jax.ShapeDtypeStruct((part, part), jnp.float32),
             jax.ShapeDtypeStruct((part, 8 * total), jnp.bfloat16),
             jax.ShapeDtypeStruct((8 * total, part), jnp.bfloat16),
         ],
         in_specs=[vmem] * len(parcels),
-        out_specs=[pl.BlockSpec(memory_space=pltpu.HBM), vmem, vmem],
-        scratch_shapes=[pltpu.VMEM((part, part), jnp.float32), pltpu.SemaphoreType.DMA((part // TILE,))],
+        out_specs=[vmem] * 3,
         compiler_params=pltpu.CompilerParams(vmem_limit_bytes=VMEM_BYTES),
         cost_estimate=pl.CostEstimate(flops=2**28, bytes_accessed=4 * part * part, transcendentals=0),
         name="quadrant",
@@ -353,14 +338,13 @@
             jax.ShapeDtypeStruct((rows, width), jnp.float32),
             jax.ShapeDtypeStruct((width, width), jnp.float32),
         ],
-        in_specs=[hbm] + [vmem] * (3 + len(parcels)),
+        in_specs=[vmem] * (4 + len(parcels)),
         out_specs=[hbm] * 2,
         scratch_shapes=[
             pltpu.VMEM((3, part, part), jnp.float32),
             pltpu.VMEM((rows, width), jnp.float32),
-            pltpu.SemaphoreType.DMA((part // TILE + 3,)),
+            pltpu.SemaphoreType.DMA((5,)),
         ],
-        input_output_aliases={0: 1},
         compiler_params=pltpu.CompilerParams(vmem_limit_bytes=VMEM_BYTES),
         name="fisher",
     )(*begun, bundle, *parcels)

time: 31.5 us -> 31.8 us (level)
  waiting for transfers between devices: 6.88 us -> 7.79 us
  Pallas kernels: 13.1 us -> 12.6 us
    ppermute x1, waiting for transfers between devices: 0.07 us -> 0.99 us  [local(): bundle = lax.ppermute(bundle_of(parcels), 'seq', swap)]
    pallas_call x1, Pallas kernels: 1.25 us -> 0.34 us  [quadrant_of(): pl.pallas_call(functools.partial(quadrant_kernel, 1.0 / total), out_shape...]
    pallas_call x1, Pallas kernels: 1.94 us -> 2.29 us  [fisher_block(): pl.pallas_call(functools.partial(fisher_kernel, 1.0 / (rows * len(parcels...]
  transfers between devices with their start and end apart: 8 -> 8, of which waited for: 6 -> 6; matrix products, arithmetic and copies ran while one was open for 0% -> 0% of each run, Pallas kernels for 25% -> 21%
where the time goes in v19:
time: 31.8 us; the launch traced here: 31.7 us
  Pallas kernels  12.6 us (40%)
  starting transfers between devices  10.6 us (33%)
  waiting for transfers between devices  7.79 us (24%)
  between operations  0.68 us (2%)
    pallas_call x2, Pallas kernels, project(): pl.pallas_call(functools.partial(project_kernel, widths), out_shape=jax.S...  9.37 us
    ppermute x3, starting transfers between devices, local(): lax.ppermute(parcels[k], 'dp', [(d, (d + k) % dp) for d in range(dp)])  5.65 us
    ppermute x1, starting transfers between devices, local(): other = lax.ppermute(act, 'tensor', swap)  3 us
    ppermute x3, waiting for transfers between devices, local(): lax.ppermute(parcels[k], 'dp', [(d, (d + k) % dp) for d in range(dp)])  2.86 us
    ppermute x1, waiting for transfers between devices, local(): lax.ppermute(krons[1], ('tensor', 'seq'), [(p, 3 - p) for p in range(shar...  2.4 us
    pallas_call x1, Pallas kernels, fisher_block(): pl.pallas_call(functools.partial(fisher_kernel, 1.0 / (rows * len(parcels...  2.29 us
    ppermute x1, waiting for transfers between devices, local(): beside = lax.ppermute(krons[2], 'tensor', swap)  1.54 us
    ppermute x1, starting transfers between devices, local(): beside = lax.ppermute(krons[2], 'tensor', swap)  1.52 us
  transfers between devices with their start and end apart: 8, of which 6 were waited for; matrix products, arithmetic and copies ran while one was open for 0% of the time, Pallas kernels for 21%

profile of v19, /device:TPU:0, one launch (start us, length us, event | category | flops | bytes accessed | tf_op | source)
XLA Modules:
  0.0 31.7 jit_solution(5136642043851857677)
XLA Ops:
  0.6 2.9 %project_acts.1.own = f32[4,128,128]{2,1,0:T(8,128)S(1)} custom-call(s32[32]{0:T(128)} %ids.3, s32[32]{0:T(128)} %signs.3, bf16[32,4096]{1,0:T(8,128)(2,1)} %table.3, bf16[1024,2048]{1,0:T(8,128)(2,1)} %bitcast.3), custom_call_target="tpu_custom_call" | custom-call | flops 536870912 | bytes 4194304 | tf_op jit(solution)/shard_map/project_acts/pallas_call | solution.py:135
  3.6 3.0 %collective-permute-start = (f32[4,128,128]{2,1,0:T(8,128)S(1)}, f32[4,128,128]{2,1,0:T(8,128)S(1)}, u32[]{:S(2)}, u32[]{:S(2)}) collective-permute-start(f32[4,128,128]{2,1,0:T(8,128)S(1)} %project_acts.1.own), channel_id=1, source_target_pairs={{0,2},{2,0},{1,3},{3,1},{4,6},{6,4},{5,7},{7,5},{8,10},{10,8},{9,1... | collective-permute-start | bytes 786440 | tf_op jit(solution)/shard_map/ppermute | solution.py:361
  6.6 6.5 %project_grads.1.grads = f32[4,128,128]{2,1,0:T(8,128)S(1)} custom-call(s32[112]{0:T(128)} %ids.2, s32[112]{0:T(128)} %signs.2, bf16[32,4096]{1,0:T(8,128)(2,1)} %table.2, bf16[1024,7168]{1,0:T(8,128)(2,1)} %bitcast.2), custom_call_target="tpu_custom_call" | custom-call | flops 1879048192 | bytes 14680064 | tf_op jit(solution)/shard_map/project_grads/pallas_call | solution.py:135
  13.0 0.0 collective-permute-done.act
  13.0 0.5 %kron.1 = (f32[8,2048]{1,0:T(8,128)S(1)}, f32[8,2048]{1,0:T(8,128)S(1)}, f32[8,2048]{1,0:T(8,128)S(1)}, f32[8,2048]{1,0:T(8,128)S(1)}) custom-call(f32[4,128,128]{2,1,0:T(8,128)S(1)} %project_grads.1.grads, f32[4,128,128]{2,1,0:T(8,128)S(1)} %project_acts.1.own, f32[4,128,128]{2,1,0:T(8,128)S(1)} %collective-permute-done.act), custom_call_target="tpu_custom_call" | custom-call | tf_op jit(solution)/shard_map/kron/pallas_call | solution.py:190
  13.6 0.2 collective-permute-start.1
  13.8 1.5 %collective-permute-start.2 = (f32[8,2048]{1,0:T(8,128)S(1)}, f32[8,2048]{1,0:T(8,128)S(1)}, u32[]{:S(2)}, u32[]{:S(2)}) collective-permute-start(f32[8,2048]{1,0:T(8,128)S(1)} %get-tuple-element.14), channel_id=1, source_target_pairs={{0,2},{2,0},{1,3},{3,1},{4,6},{6,4},{5,7},{7,5},{8,10},{10,8},{9,1... | collective-permute-start | bytes 196616 | tf_op jit(solution)/shard_map/ppermute | solution.py:383
  15.3 0.2 collective-permute-start.3
  15.5 2.4 %collective-permute-done.1.refs_0_ = f32[8,2048]{1,0:T(8,128)S(1)} collective-permute-done((f32[8,2048]{1,0:T(8,128)S(1)}, f32[8,2048]{1,0:T(8,128)S(1)}, u32[]{:S(2)}, u32[]{:S(2)}) %collective-permute-start.1) | collective-permute-done | bytes 65568 | tf_op jit(solution)/shard_map/ppermute | solution.py:382
  17.9 1.5 %collective-permute-done.2.refs_1_ = f32[8,2048]{1,0:T(8,128)S(1)} collective-permute-done((f32[8,2048]{1,0:T(8,128)S(1)}, f32[8,2048]{1,0:T(8,128)S(1)}, u32[]{:S(2)}, u32[]{:S(2)}) %collective-permute-start.2) | collective-permute-done | bytes 65568 | tf_op jit(solution)/shard_map/ppermute | solution.py:383
  19.4 0.0 collective-permute-done.3.refs_2_
  19.5 1.7 %collective-permute-start.4 = (f32[24,512]{1,0:T(8,128)S(1)}, f32[24,512]{1,0:T(8,128)S(1)}, u32[]{:S(2)}, u32[]{:S(2)}) collective-permute-start(f32[24,512]{1,0:T(8,128)S(1)} %get-tuple-element.18), channel_id=1, source_target_pairs={{0,4},{4,8},{8,12},{12,0},{1,5},{5,9},{9,13},{13,1},{2,6},{6,10},{... | collective-permute-start | bytes 147464 | tf_op jit(solution)/shard_map/ppermute | solution.py:387
  21.2 2.6 %collective-permute-start.5 = (f32[24,512]{1,0:T(8,128)S(1)}, f32[24,512]{1,0:T(8,128)S(1)}, u32[]{:S(2)}, u32[]{:S(2)}) collective-permute-start(f32[24,512]{1,0:T(8,128)S(1)} %get-tuple-element.19), channel_id=1, source_target_pairs={{0,8},{4,12},{8,0},{12,4},{1,9},{5,13},{9,1},{13,5},{2,10},{6,14},... | collective-permute-start | bytes 147464 | tf_op jit(solution)/shard_map/ppermute | solution.py:387
  23.8 1.3 %collective-permute-start.6 = (f32[24,512]{1,0:T(8,128)S(1)}, f32[24,512]{1,0:T(8,128)S(1)}, u32[]{:S(2)}, u32[]{:S(2)}) collective-permute-start(f32[24,512]{1,0:T(8,128)S(1)} %get-tuple-element.20), channel_id=1, source_target_pairs={{0,12},{4,0},{8,4},{12,8},{1,13},{5,1},{9,5},{13,9},{2,14},{6,2},{... | collective-permute-start | bytes 147464 | tf_op jit(solution)/shard_map/ppermute | solution.py:387
  25.1 0.3 collective-permute-done.4.refs_1_
  25.4 2.2 %collective-permute-done.5.refs_2_ = f32[24,512]{1,0:T(8,128)S(1)} collective-permute-done((f32[24,512]{1,0:T(8,128)S(1)}, f32[24,512]{1,0:T(8,128)S(1)}, u32[]{:S(2)}, u32[]{:S(2)}) %collective-permute-start.5) | collective-permute-done | bytes 49184 | tf_op jit(solution)/shard_map/ppermute | solution.py:387
  27.6 0.4 %collective-permute-done.6.refs_3_ = f32[24,512]{1,0:T(8,128)S(1)} collective-permute-done((f32[24,512]{1,0:T(8,128)S(1)}, f32[24,512]{1,0:T(8,128)S(1)}, u32[]{:S(2)}, u32[]{:S(2)}) %collective-permute-start.6) | collective-permute-done | bytes 49184 | tf_op jit(solution)/shard_map/ppermute | solution.py:387
  28.0 0.1 collective-permute-start.7
  28.1 0.3 %quadrant.1 = (f32[512,512]{1,0:T(8,128)S(1)}, bf16[512,256]{1,0:T(8,128)(2,1)S(1)}, bf16[256,512]{1,0:T(8,128)(2,1)S(1)}) custom-call(f32[24,512]{1,0:T(8,128)S(1)} %get-tuple-element.17.refs_0_, f32[24,512]{1,0:T(8,128)S(1)} %collective-permute-done.4.refs_1_, f32[24,512]{1,0:T(8,128)S(1)} %collective-permute-done.5.refs_2_, ...), custom_call_target="tpu_custom_call" | custom-call | flops 268435456 | bytes 1048576 | tf_op jit(solution)/shard_map/quadrant/pallas_call | solution.py:314
  28.4 1.0 %collective-permute-done.7.bundle = f32[64,512]{1,0:T(8,128)S(1)} collective-permute-done((f32[64,512]{1,0:T(8,128)S(1)}, f32[64,512]{1,0:T(8,128)S(1)}, u32[]{:S(2)}, u32[]{:S(2)}) %collective-permute-start.7) | collective-permute-done | bytes 131104 | tf_op jit(solution)/shard_map/ppermute | solution.py:388
  29.4 2.3 %fisher.1 = (f32[8,1024]{1,0:T(8,128)}, f32[1024,1024]{1,0:T(8,128)}) custom-call(f32[512,512]{1,0:T(8,128)S(1)} %get-tuple-element.21.quadrant, bf16[512,256]{1,0:T(8,128)(2,1)S(1)} %get-tuple-element.22.left, bf16[256,512]{1,0:T(8,128)(2,1)S(1)} %get-tuple-element.23.right, f32[64,512]{1,0:T(8,128)S(1)} %collective-permute-done.7.bundle, ...), custom_call_target="tpu_custom_call" | custom-call | tf_op jit(solution)/shard_map/fisher/pallas_call | solution.py:335
  (2 shorter events, 0.0 us)
Async XLA Ops:
  3.6 9.5 %collective-permute-start = (f32[4,128,128]{2,1,0:T(8,128)S(1)}, f32[4,128,128]{2,1,0:T(8,128)S(1)}, u32[]{:S(2)}, u32[]{:S(2)}) collective-permute-start(f32[4,128,128]{2,1,0:T(8,128)S(1)} %project_acts.1.own), channel_id=1, source_target_pairs={{0,2},{2,0},{1,3},{3,1},{4,6},{6,4},{5,7},{7,5},{8,10},{10,8},{9,1... | collective-permute-start | bytes 786440 | tf_op jit(solution)/shard_map/ppermute | solution.py:361
  13.6 4.3 %collective-permute-start.1 = (f32[8,2048]{1,0:T(8,128)S(1)}, f32[8,2048]{1,0:T(8,128)S(1)}, u32[]{:S(2)}, u32[]{:S(2)}) collective-permute-start(f32[8,2048]{1,0:T(8,128)S(1)} %get-tuple-element.13), channel_id=1, source_target_pairs={{0,3},{1,2},{2,1},{3,0},{4,7},{5,6},{6,5},{7,4},{8,11},{9,10},{10,... | collective-permute-start | bytes 196616 | tf_op jit(solution)/shard_map/ppermute | solution.py:382
  13.8 5.7 %collective-permute-start.2 = (f32[8,2048]{1,0:T(8,128)S(1)}, f32[8,2048]{1,0:T(8,128)S(1)}, u32[]{:S(2)}, u32[]{:S(2)}) collective-permute-start(f32[8,2048]{1,0:T(8,128)S(1)} %get-tuple-element.14), channel_id=1, source_target_pairs={{0,2},{2,0},{1,3},{3,1},{4,6},{6,4},{5,7},{7,5},{8,10},{10,8},{9,1... | collective-permute-start | bytes 196616 | tf_op jit(solution)/shard_map/ppermute | solution.py:383
  15.3 4.1 %collective-permute-start.3 = (f32[8,2048]{1,0:T(8,128)S(1)}, f32[8,2048]{1,0:T(8,128)S(1)}, u32[]{:S(2)}, u32[]{:S(2)}) collective-permute-start(f32[8,2048]{1,0:T(8,128)S(1)} %get-tuple-element.15), channel_id=1, source_target_pairs={{0,1},{1,0},{2,3},{3,2},{4,5},{5,4},{6,7},{7,6},{8,9},{9,8},{10,11... | collective-permute-start | bytes 196616 | tf_op jit(solution)/shard_map/ppermute | solution.py:384
  19.5 5.9 %collective-permute-start.4 = (f32[24,512]{1,0:T(8,128)S(1)}, f32[24,512]{1,0:T(8,128)S(1)}, u32[]{:S(2)}, u32[]{:S(2)}) collective-permute-start(f32[24,512]{1,0:T(8,128)S(1)} %get-tuple-element.18), channel_id=1, source_target_pairs={{0,4},{4,8},{8,12},{12,0},{1,5},{5,9},{9,13},{13,1},{2,6},{6,10},{... | collective-permute-start | bytes 147464 | tf_op jit(solution)/shard_map/ppermute | solution.py:387
  21.2 6.4 %collective-permute-start.5 = (f32[24,512]{1,0:T(8,128)S(1)}, f32[24,512]{1,0:T(8,128)S(1)}, u32[]{:S(2)}, u32[]{:S(2)}) collective-permute-start(f32[24,512]{1,0:T(8,128)S(1)} %get-tuple-element.19), channel_id=1, source_target_pairs={{0,8},{4,12},{8,0},{12,4},{1,9},{5,13},{9,1},{13,5},{2,10},{6,14},... | collective-permute-start | bytes 147464 | tf_op jit(solution)/shard_map/ppermute | solution.py:387
  23.8 4.2 %collective-permute-start.6 = (f32[24,512]{1,0:T(8,128)S(1)}, f32[24,512]{1,0:T(8,128)S(1)}, u32[]{:S(2)}, u32[]{:S(2)}) collective-permute-start(f32[24,512]{1,0:T(8,128)S(1)} %get-tuple-element.20), channel_id=1, source_target_pairs={{0,12},{4,0},{8,4},{12,8},{1,13},{5,1},{9,5},{13,9},{2,14},{6,2},{... | collective-permute-start | bytes 147464 | tf_op jit(solution)/shard_map/ppermute | solution.py:387
  28.0 1.4 %collective-permute-start.7 = (f32[64,512]{1,0:T(8,128)S(1)}, f32[64,512]{1,0:T(8,128)S(1)}, u32[]{:S(2)}, u32[]{:S(2)}) collective-permute-start(f32[64,512]{1,0:T(8,128)S(1)} %bundle.1), channel_id=1, source_target_pairs={{0,1},{1,0},{2,3},{3,2},{4,5},{5,4},{6,7},{7,6},{8,9},{9,8},{10,11... | collective-permute-start | bytes 393224 | tf_op jit(solution)/shard_map/ppermute | solution.py:388

commit v20 on v15

--- a/solution.py
+++ b/solution.py
@@ -76,7 +76,7 @@
 
 
 def project_kernel(widths, ids, signs, table, rows_ref, out, *refs):
-    spread, matrix, held, total, own_table, own_ids, own_signs, sems, *signed = refs
+    spread, matrix, across, held, total, own_table, own_ids, own_signs, sems, *signed = refs
     signed = signed[0] if signed else None
     copies, starts, start = [], [], 0
     for c, width in enumerate(widths):
@@ -96,18 +96,22 @@
         sign_table(spread, signed)
     small[1].wait()
     small[2].wait()
-    lay = functools.partial(lay_blocks, own_ids, own_signs, spread, signed, matrix)
-    lay(0, widths[0] // BLOCK)
+
+    def lay(c):
+        lay_blocks(
+            own_ids, own_signs, spread, signed, matrix, starts[c] // BLOCK, (starts[c] + widths[c]) // BLOCK
+        )
+        rows = pl.ds(starts[c], widths[c])
+        across[:, rows] = matrix[rows, :].T[:PROJ, :]
+
+    lay(0)
     for c, copy in enumerate(copies):
         columns = pl.ds(starts[c], widths[c])
         copy.wait()
         if c + 1 < len(widths):
-            lay(starts[c + 1] // BLOCK, (starts[c + 1] + widths[c + 1]) // BLOCK)
+            lay(c + 1)
         part = lax.dot_general(
-            matrix[columns, :PROJ],
-            held[:, columns],
-            (((0,), (1,)), ((), ())),
-            preferred_element_type=jnp.float32,
+            across[:, columns], held[:, columns], (((1,), (1,)), ((), ())), preferred_element_type=jnp.float32
         )
         if c == 0:
             total[...] = part
@@ -140,6 +144,7 @@
         scratch_shapes=[
             pltpu.VMEM((entries * STRIDE, LANES), jnp.float32),
             pltpu.VMEM((width, LANES), jnp.bfloat16),
+            pltpu.VMEM((PROJ, width), jnp.bfloat16),
             pltpu.VMEM((rows, width), jnp.bfloat16),
             pltpu.VMEM((PROJ, rows), jnp.float32),
             pltpu.VMEM(table.shape, table.dtype),

time: 31.5 us -> 31.5 us (level)
  no operation moved by 1% of the time
where the time goes in v20:
time: 31.5 us; the launch traced here: 31.4 us
  Pallas kernels  13.2 us (42%)
  starting transfers between devices  10.6 us (34%)
  waiting for transfers between devices  6.89 us (22%)
  between operations  0.69 us (2%)
    pallas_call x2, Pallas kernels, project(): pl.pallas_call(functools.partial(project_kernel, widths), out_shape=jax.S...  9.48 us
    ppermute x3, starting transfers between devices, local(): lax.ppermute(parcels[k], 'dp', [(d, (d + k) % dp) for d in range(dp)])  5.57 us
    ppermute x1, starting transfers between devices, local(): other = lax.ppermute(act, 'tensor', swap)  3 us
    ppermute x3, waiting for transfers between devices, local(): lax.ppermute(parcels[k], 'dp', [(d, (d + k) % dp) for d in range(dp)])  2.87 us
    ppermute x1, waiting for transfers between devices, local(): lax.ppermute(krons[1], ('tensor', 'seq'), [(p, 3 - p) for p in range(shar...  2.5 us
    pallas_call x1, Pallas kernels, fisher_block(): pl.pallas_call(functools.partial(fisher_kernel, 1.0 / (rows * len(parcels...  1.94 us
    ppermute x1, starting transfers between devices, local(): beside = lax.ppermute(krons[2], 'tensor', swap)  1.51 us
    ppermute x1, waiting for transfers between devices, local(): beside = lax.ppermute(krons[2], 'tensor', swap)  1.43 us
  transfers between devices with their start and end apart: 8, of which 6 were waited for; matrix products, arithmetic and copies ran while one was open for 0% of the time, Pallas kernels for 25%

profile of v20, /device:TPU:0, one launch (start us, length us, event | category | flops | bytes accessed | tf_op | source)
XLA Modules:
  0.0 31.4 jit_solution(17812519831694930208)
XLA Ops:
  0.6 2.9 %project_acts.1.own = f32[4,128,128]{2,1,0:T(8,128)S(1)} custom-call(s32[32]{0:T(128)} %ids.3, s32[32]{0:T(128)} %signs.3, bf16[32,4096]{1,0:T(8,128)(2,1)} %table.3, bf16[1024,2048]{1,0:T(8,128)(2,1)} %bitcast.3), custom_call_target="tpu_custom_call" | custom-call | flops 536870912 | bytes 4194304 | tf_op jit(solution)/shard_map/project_acts/pallas_call | solution.py:139
  3.6 3.0 %collective-permute-start = (f32[4,128,128]{2,1,0:T(8,128)S(1)}, f32[4,128,128]{2,1,0:T(8,128)S(1)}, u32[]{:S(2)}, u32[]{:S(2)}) collective-permute-start(f32[4,128,128]{2,1,0:T(8,128)S(1)} %project_acts.1.own), channel_id=1, source_target_pairs={{0,2},{2,0},{1,3},{3,1},{4,6},{6,4},{5,7},{7,5},{8,10},{10,8},{9,1... | collective-permute-start | bytes 786440 | tf_op jit(solution)/shard_map/ppermute | solution.py:382
  6.6 6.5 %project_grads.1.grads = f32[4,128,128]{2,1,0:T(8,128)S(1)} custom-call(s32[112]{0:T(128)} %ids.2, s32[112]{0:T(128)} %signs.2, bf16[32,4096]{1,0:T(8,128)(2,1)} %table.2, bf16[1024,7168]{1,0:T(8,128)(2,1)} %bitcast.2), custom_call_target="tpu_custom_call" | custom-call | flops 1879048192 | bytes 14680064 | tf_op jit(solution)/shard_map/project_grads/pallas_call | solution.py:139
  13.1 0.0 collective-permute-done.act
  13.1 0.5 %kron.1 = (f32[8,2048]{1,0:T(8,128)S(1)}, f32[8,2048]{1,0:T(8,128)S(1)}, f32[8,2048]{1,0:T(8,128)S(1)}, f32[8,2048]{1,0:T(8,128)S(1)}) custom-call(f32[4,128,128]{2,1,0:T(8,128)S(1)} %project_grads.1.grads, f32[4,128,128]{2,1,0:T(8,128)S(1)} %project_acts.1.own, f32[4,128,128]{2,1,0:T(8,128)S(1)} %collective-permute-done.act), custom_call_target="tpu_custom_call" | custom-call | tf_op jit(solution)/shard_map/kron/pallas_call | solution.py:195
  13.7 0.1 collective-permute-start.1
  13.8 1.5 %collective-permute-start.2 = (f32[8,2048]{1,0:T(8,128)S(1)}, f32[8,2048]{1,0:T(8,128)S(1)}, u32[]{:S(2)}, u32[]{:S(2)}) collective-permute-start(f32[8,2048]{1,0:T(8,128)S(1)} %get-tuple-element.14), channel_id=1, source_target_pairs={{0,2},{2,0},{1,3},{3,1},{4,6},{6,4},{5,7},{7,5},{8,10},{10,8},{9,1... | collective-permute-start | bytes 196616 | tf_op jit(solution)/shard_map/ppermute | solution.py:404
  15.3 0.3 collective-permute-start.3
  15.6 2.5 %collective-permute-done.1.refs_0_ = f32[8,2048]{1,0:T(8,128)S(1)} collective-permute-done((f32[8,2048]{1,0:T(8,128)S(1)}, f32[8,2048]{1,0:T(8,128)S(1)}, u32[]{:S(2)}, u32[]{:S(2)}) %collective-permute-start.1) | collective-permute-done | bytes 65568 | tf_op jit(solution)/shard_map/ppermute | solution.py:403
  18.1 1.4 %collective-permute-done.2.refs_1_ = f32[8,2048]{1,0:T(8,128)S(1)} collective-permute-done((f32[8,2048]{1,0:T(8,128)S(1)}, f32[8,2048]{1,0:T(8,128)S(1)}, u32[]{:S(2)}, u32[]{:S(2)}) %collective-permute-start.2) | collective-permute-done | bytes 65568 | tf_op jit(solution)/shard_map/ppermute | solution.py:404
  19.5 0.0 collective-permute-done.3.refs_2_
  19.6 1.6 %collective-permute-start.4 = (f32[24,512]{1,0:T(8,128)S(1)}, f32[24,512]{1,0:T(8,128)S(1)}, u32[]{:S(2)}, u32[]{:S(2)}) collective-permute-start(f32[24,512]{1,0:T(8,128)S(1)} %get-tuple-element.18), channel_id=1, source_target_pairs={{0,4},{4,8},{8,12},{12,0},{1,5},{5,9},{9,13},{13,1},{2,6},{6,10},{... | collective-permute-start | bytes 147464 | tf_op jit(solution)/shard_map/ppermute | solution.py:408
  21.2 2.6 %collective-permute-start.5 = (f32[24,512]{1,0:T(8,128)S(1)}, f32[24,512]{1,0:T(8,128)S(1)}, u32[]{:S(2)}, u32[]{:S(2)}) collective-permute-start(f32[24,512]{1,0:T(8,128)S(1)} %get-tuple-element.19), channel_id=1, source_target_pairs={{0,8},{4,12},{8,0},{12,4},{1,9},{5,13},{9,1},{13,5},{2,10},{6,14},... | collective-permute-start | bytes 147464 | tf_op jit(solution)/shard_map/ppermute | solution.py:408
  23.8 1.3 %collective-permute-start.6 = (f32[24,512]{1,0:T(8,128)S(1)}, f32[24,512]{1,0:T(8,128)S(1)}, u32[]{:S(2)}, u32[]{:S(2)}) collective-permute-start(f32[24,512]{1,0:T(8,128)S(1)} %get-tuple-element.20), channel_id=1, source_target_pairs={{0,12},{4,0},{8,4},{12,8},{1,13},{5,1},{9,5},{13,9},{2,14},{6,2},{... | collective-permute-start | bytes 147464 | tf_op jit(solution)/shard_map/ppermute | solution.py:408
  25.1 0.4 %collective-permute-done.4.refs_1_ = f32[24,512]{1,0:T(8,128)S(1)} collective-permute-done((f32[24,512]{1,0:T(8,128)S(1)}, f32[24,512]{1,0:T(8,128)S(1)}, u32[]{:S(2)}, u32[]{:S(2)}) %collective-permute-start.4) | collective-permute-done | bytes 49184 | tf_op jit(solution)/shard_map/ppermute | solution.py:408
  25.5 2.1 %collective-permute-done.5.refs_2_ = f32[24,512]{1,0:T(8,128)S(1)} collective-permute-done((f32[24,512]{1,0:T(8,128)S(1)}, f32[24,512]{1,0:T(8,128)S(1)}, u32[]{:S(2)}, u32[]{:S(2)}) %collective-permute-start.5) | collective-permute-done | bytes 49184 | tf_op jit(solution)/shard_map/ppermute | solution.py:408
  27.6 0.4 %collective-permute-done.6.refs_3_ = f32[24,512]{1,0:T(8,128)S(1)} collective-permute-done((f32[24,512]{1,0:T(8,128)S(1)}, f32[24,512]{1,0:T(8,128)S(1)}, u32[]{:S(2)}, u32[]{:S(2)}) %collective-permute-start.6) | collective-permute-done | bytes 49184 | tf_op jit(solution)/shard_map/ppermute | solution.py:408
  28.0 0.1 collective-permute-start.7
  28.1 1.3 %quadrant.1 = (f32[1024,1024]{1,0:T(8,128)}, bf16[512,256]{1,0:T(8,128)(2,1)S(1)}, bf16[256,512]{1,0:T(8,128)(2,1)S(1)}) custom-call(f32[24,512]{1,0:T(8,128)S(1)} %get-tuple-element.17.refs_0_, f32[24,512]{1,0:T(8,128)S(1)} %collective-permute-done.4.refs_1_, f32[24,512]{1,0:T(8,128)S(1)} %collective-permute-done.5.refs_2_, ...), custom_call_target="tpu_custom_call" | custom-call | flops 268435456 | bytes 1048576 | tf_op jit(solution)/shard_map/quadrant/pallas_call | solution.py:333
  29.4 0.1 collective-permute-done.7.bundle
  29.4 1.9 %fisher.1 = (f32[8,1024]{1,0:T(8,128)}, f32[1024,1024]{1,0:T(8,128)}) custom-call(f32[1024,1024]{1,0:T(8,128)} %get-tuple-element.21.begun, bf16[512,256]{1,0:T(8,128)(2,1)S(1)} %get-tuple-element.22.left, bf16[256,512]{1,0:T(8,128)(2,1)S(1)} %get-tuple-element.23.right, ...), custom_call_target="tpu_custom_call", output_to_operand_aliasing={{1}: (0, {})} | custom-call | tf_op jit(solution)/shard_map/fisher/pallas_call | solution.py:355
  (2 shorter events, 0.0 us)
Async XLA Ops:
  3.6 9.6 %collective-permute-start = (f32[4,128,128]{2,1,0:T(8,128)S(1)}, f32[4,128,128]{2,1,0:T(8,128)S(1)}, u32[]{:S(2)}, u32[]{:S(2)}) collective-permute-start(f32[4,128,128]{2,1,0:T(8,128)S(1)} %project_acts.1.own), channel_id=1, source_target_pairs={{0,2},{2,0},{1,3},{3,1},{4,6},{6,4},{5,7},{7,5},{8,10},{10,8},{9,1... | collective-permute-start | bytes 786440 | tf_op jit(solution)/shard_map/ppermute | solution.py:382
  13.7 4.4 %collective-permute-start.1 = (f32[8,2048]{1,0:T(8,128)S(1)}, f32[8,2048]{1,0:T(8,128)S(1)}, u32[]{:S(2)}, u32[]{:S(2)}) collective-permute-start(f32[8,2048]{1,0:T(8,128)S(1)} %get-tuple-element.13), channel_id=1, source_target_pairs={{0,3},{1,2},{2,1},{3,0},{4,7},{5,6},{6,5},{7,4},{8,11},{9,10},{10,... | collective-permute-start | bytes 196616 | tf_op jit(solution)/shard_map/ppermute | solution.py:403
  13.8 5.8 %collective-permute-start.2 = (f32[8,2048]{1,0:T(8,128)S(1)}, f32[8,2048]{1,0:T(8,128)S(1)}, u32[]{:S(2)}, u32[]{:S(2)}) collective-permute-start(f32[8,2048]{1,0:T(8,128)S(1)} %get-tuple-element.14), channel_id=1, source_target_pairs={{0,2},{2,0},{1,3},{3,1},{4,6},{6,4},{5,7},{7,5},{8,10},{10,8},{9,1... | collective-permute-start | bytes 196616 | tf_op jit(solution)/shard_map/ppermute | solution.py:404
  15.3 4.2 %collective-permute-start.3 = (f32[8,2048]{1,0:T(8,128)S(1)}, f32[8,2048]{1,0:T(8,128)S(1)}, u32[]{:S(2)}, u32[]{:S(2)}) collective-permute-start(f32[8,2048]{1,0:T(8,128)S(1)} %get-tuple-element.15), channel_id=1, source_target_pairs={{0,1},{1,0},{2,3},{3,2},{4,5},{5,4},{6,7},{7,6},{8,9},{9,8},{10,11... | collective-permute-start | bytes 196616 | tf_op jit(solution)/shard_map/ppermute | solution.py:405
  19.6 5.9 %collective-permute-start.4 = (f32[24,512]{1,0:T(8,128)S(1)}, f32[24,512]{1,0:T(8,128)S(1)}, u32[]{:S(2)}, u32[]{:S(2)}) collective-permute-start(f32[24,512]{1,0:T(8,128)S(1)} %get-tuple-element.18), channel_id=1, source_target_pairs={{0,4},{4,8},{8,12},{12,0},{1,5},{5,9},{9,13},{13,1},{2,6},{6,10},{... | collective-permute-start | bytes 147464 | tf_op jit(solution)/shard_map/ppermute | solution.py:408
  21.2 6.4 %collective-permute-start.5 = (f32[24,512]{1,0:T(8,128)S(1)}, f32[24,512]{1,0:T(8,128)S(1)}, u32[]{:S(2)}, u32[]{:S(2)}) collective-permute-start(f32[24,512]{1,0:T(8,128)S(1)} %get-tuple-element.19), channel_id=1, source_target_pairs={{0,8},{4,12},{8,0},{12,4},{1,9},{5,13},{9,1},{13,5},{2,10},{6,14},... | collective-permute-start | bytes 147464 | tf_op jit(solution)/shard_map/ppermute | solution.py:408
  23.8 4.2 %collective-permute-start.6 = (f32[24,512]{1,0:T(8,128)S(1)}, f32[24,512]{1,0:T(8,128)S(1)}, u32[]{:S(2)}, u32[]{:S(2)}) collective-permute-start(f32[24,512]{1,0:T(8,128)S(1)} %get-tuple-element.20), channel_id=1, source_target_pairs={{0,12},{4,0},{8,4},{12,8},{1,13},{5,1},{9,5},{13,9},{2,14},{6,2},{... | collective-permute-start | bytes 147464 | tf_op jit(solution)/shard_map/ppermute | solution.py:408
  28.0 1.4 %collective-permute-start.7 = (f32[64,512]{1,0:T(8,128)S(1)}, f32[64,512]{1,0:T(8,128)S(1)}, u32[]{:S(2)}, u32[]{:S(2)}) collective-permute-start(f32[64,512]{1,0:T(8,128)S(1)} %bundle.1), channel_id=1, source_target_pairs={{0,1},{1,0},{2,3},{3,2},{4,5},{5,4},{6,7},{7,6},{8,9},{9,8},{10,11... | collective-permute-start | bytes 393224 | tf_op jit(solution)/shard_map/ppermute | solution.py:409

commit v21 on v20

--- a/solution.py
+++ b/solution.py
@@ -14,17 +14,14 @@
 VMEM_BYTES = 48 * 1024 * 1024
 
 
-def chunks_of(width, most):
-    if width < 4 * most or most % (4 * LANES):
-        chunk = most
-        while width % chunk:
-            chunk -= LANES
-        return [chunk] * (width // chunk)
-    inner = width - most
-    chunk = most
-    while inner % chunk:
+def chunks_of(width, shares):
+    unit = width // sum(shares)
+    if unit * sum(shares) == width and unit % LANES == 0:
+        return [share * unit for share in shares]
+    chunk = 8 * LANES
+    while width % chunk:
         chunk -= LANES
-    return [most // 2] + [chunk] * (inner // chunk) + [most // 4] * 2
+    return [chunk] * (width // chunk)
 
 
 def split3(x):
@@ -125,9 +122,9 @@
             out[pair, pl.ds(side * PROJ, PROJ), :] = part[:, example * tokens : (example + 1) * tokens]
 
 
-def project(values, ids, signs, table, most, name):
+def project(values, ids, signs, table, shares, name):
     count, tokens, width = values.shape
-    widths = chunks_of(width, most)
+    widths = chunks_of(width, shares)
     rows = count * tokens
     entries = table.shape[0]
     blocks = ids.shape[0]
@@ -163,7 +160,7 @@
 
 def kron_kernel(cuts, grads, own, act, *refs):
     parts = cuts[1]
-    outs, rows, products = refs[:-2], refs[-2], refs[-1]
+    outs, products = refs[:-1], refs[-1]
     pairs = act.shape[0]
     for pair in range(pairs):
         both = products_with(operand(grads[pair]), own[pair] + act[pair])
@@ -173,17 +170,27 @@
     lower = lax.broadcasted_iota(jnp.int32, (count, LANES), 1) < PROJ
     even = lax.broadcasted_iota(jnp.int32, (count, LANES), 0) % 2 == 0
     here = even == lower
-    tiles = rows.shape[2] // LANES // cuts[0]
+    tiles = outs[0].shape[1] // LANES // cuts[0]
+    made = []
     for tile in range(PROJ * PROJ // LANES):
         both = []
         for p in (2 * tile, 2 * tile + 1):
             v = products[pl.ds(p, count, stride=STRIDE), :]
             both.append(jnp.where(here, v, pltpu.roll(v, PROJ, 1)))
-        block, part, within = tile // tiles // parts, tile // tiles % parts, tile % tiles
-        rows[part, :, pl.ds((block * tiles + within) * LANES, LANES)] = jnp.where(lower, both[0], both[1])
-    for k, out in enumerate(outs):
-        part = lax.rem(lax.axis_index("seq") + k % 2, parts) if parts > 1 else 0
-        out[...] = rows[part]
+        made.append(jnp.where(lower, both[0], both[1]))
+
+    def store(shift):
+        for tile, value in enumerate(made):
+            block, part, within = tile // tiles // parts, tile // tiles % parts, tile % tiles
+            into = pl.ds((block * tiles + within) * LANES, LANES)
+            for out in outs[(part - shift) % parts :: parts]:
+                out[:, into] = value
+
+    if parts == 1:
+        store(0)
+    else:
+        for core in range(parts):
+            pl.when(lax.axis_index("seq") == core)(functools.partial(store, core))
 
 
 def kron_of(grads, own, act, cuts):
@@ -198,7 +205,6 @@
         in_specs=[vmem] * 3,
         out_specs=[vmem] * outs,
         scratch_shapes=[
-            pltpu.VMEM((parts, 2 * pairs, width), jnp.float32),
             pltpu.VMEM((2 * pairs * STRIDE, LANES), jnp.float32),
         ],
         compiler_params=pltpu.CompilerParams(vmem_limit_bytes=VMEM_BYTES),
@@ -377,13 +383,13 @@
     small = tensor == 2 and seq == 2 and dp == 4
     swap = [(0, 1), (1, 0)]
 
-    act = project(acts, in_ids, in_signs, in_table, 512, "project_acts")
+    act = project(acts, in_ids, in_signs, in_table, (2, 3, 2, 1), "project_acts")
     if tensor == 2:
         other = lax.ppermute(act, "tensor", swap)
     else:
         act = lax.psum(act, "tensor")
         other = jnp.zeros_like(act)
-    grad = project(grads, out_ids, out_signs, out_table, 1024, "project_grads")
+    grad = project(grads, out_ids, out_signs, out_table, (2, 4, 4, 4, 4, 4, 4, 1, 1), "project_grads")
     krons = kron_of(grad, act, other, (shards, seq) if small else (1, 1))
 
     if not small:

time: 31.5 us -> 31.6 us (level)
  no operation moved by 1% of the time
where the time goes in v21:
time: 31.6 us; the launch traced here: 31.5 us
  Pallas kernels  13.3 us (42%)
  starting transfers between devices  10.6 us (34%)
  waiting for transfers between devices  6.89 us (22%)
  between operations  0.69 us (2%)
    pallas_call x2, Pallas kernels, project(): pl.pallas_call(functools.partial(project_kernel, widths), out_shape=jax.S...  9.57 us
    ppermute x3, starting transfers between devices, local(): lax.ppermute(parcels[k], 'dp', [(d, (d + k) % dp) for d in range(dp)])  5.57 us
    ppermute x1, starting transfers between devices, local(): other = lax.ppermute(act, 'tensor', swap)  3 us
    ppermute x3, waiting for transfers between devices, local(): lax.ppermute(parcels[k], 'dp', [(d, (d + k) % dp) for d in range(dp)])  2.87 us
    ppermute x1, waiting for transfers between devices, local(): lax.ppermute(krons[1], ('tensor', 'seq'), [(p, 3 - p) for p in range(shar...  2.5 us
    pallas_call x1, Pallas kernels, fisher_block(): pl.pallas_call(functools.partial(fisher_kernel, 1.0 / (rows * len(parcels...  1.94 us
    ppermute x1, starting transfers between devices, local(): beside = lax.ppermute(krons[2], 'tensor', swap)  1.49 us
    ppermute x1, waiting for transfers between devices, local(): beside = lax.ppermute(krons[2], 'tensor', swap)  1.44 us
  transfers between devices with their start and end apart: 8, of which 6 were waited for; matrix products, arithmetic and copies ran while one was open for 0% of the time, Pallas kernels for 25%

profile of v21, /device:TPU:0, one launch (start us, length us, event | category | flops | bytes accessed | tf_op | source)
XLA Modules:
  0.0 31.5 jit_solution(10431704480734274491)
XLA Ops:
  0.6 3.0 %project_acts.1.own = f32[4,128,128]{2,1,0:T(8,128)S(1)} custom-call(s32[32]{0:T(128)} %ids.3, s32[32]{0:T(128)} %signs.3, bf16[32,4096]{1,0:T(8,128)(2,1)} %table.3, bf16[1024,2048]{1,0:T(8,128)(2,1)} %bitcast.3), custom_call_target="tpu_custom_call" | custom-call | flops 536870912 | bytes 4194304 | tf_op jit(solution)/shard_map/project_acts/pallas_call | solution.py:136
  3.7 3.0 %collective-permute-start = (f32[4,128,128]{2,1,0:T(8,128)S(1)}, f32[4,128,128]{2,1,0:T(8,128)S(1)}, u32[]{:S(2)}, u32[]{:S(2)}) collective-permute-start(f32[4,128,128]{2,1,0:T(8,128)S(1)} %project_acts.1.own), channel_id=1, source_target_pairs={{0,2},{2,0},{1,3},{3,1},{4,6},{6,4},{5,7},{7,5},{8,10},{10,8},{9,1... | collective-permute-start | bytes 786440 | tf_op jit(solution)/shard_map/ppermute | solution.py:388
  6.7 6.5 %project_grads.1.grads = f32[4,128,128]{2,1,0:T(8,128)S(1)} custom-call(s32[112]{0:T(128)} %ids.2, s32[112]{0:T(128)} %signs.2, bf16[32,4096]{1,0:T(8,128)(2,1)} %table.2, bf16[1024,7168]{1,0:T(8,128)(2,1)} %bitcast.2), custom_call_target="tpu_custom_call" | custom-call | flops 1879048192 | bytes 14680064 | tf_op jit(solution)/shard_map/project_grads/pallas_call | solution.py:136
  13.2 0.0 collective-permute-done.act
  13.2 0.5 %kron.1 = (f32[8,2048]{1,0:T(8,128)S(1)}, f32[8,2048]{1,0:T(8,128)S(1)}, f32[8,2048]{1,0:T(8,128)S(1)}, f32[8,2048]{1,0:T(8,128)S(1)}) custom-call(f32[4,128,128]{2,1,0:T(8,128)S(1)} %project_grads.1.grads, f32[4,128,128]{2,1,0:T(8,128)S(1)} %project_acts.1.own, f32[4,128,128]{2,1,0:T(8,128)S(1)} %collective-permute-done.act), custom_call_target="tpu_custom_call" | custom-call | tf_op jit(solution)/shard_map/kron/pallas_call | solution.py:202
  13.7 0.1 collective-permute-start.1
  13.9 1.5 %collective-permute-start.2 = (f32[8,2048]{1,0:T(8,128)S(1)}, f32[8,2048]{1,0:T(8,128)S(1)}, u32[]{:S(2)}, u32[]{:S(2)}) collective-permute-start(f32[8,2048]{1,0:T(8,128)S(1)} %get-tuple-element.14), channel_id=1, source_target_pairs={{0,2},{2,0},{1,3},{3,1},{4,6},{6,4},{5,7},{7,5},{8,10},{10,8},{9,1... | collective-permute-start | bytes 196616 | tf_op jit(solution)/shard_map/ppermute | solution.py:410
  15.4 0.3 collective-permute-start.3
  15.7 2.5 %collective-permute-done.1.refs_0_ = f32[8,2048]{1,0:T(8,128)S(1)} collective-permute-done((f32[8,2048]{1,0:T(8,128)S(1)}, f32[8,2048]{1,0:T(8,128)S(1)}, u32[]{:S(2)}, u32[]{:S(2)}) %collective-permute-start.1) | collective-permute-done | bytes 65568 | tf_op jit(solution)/shard_map/ppermute | solution.py:409
  18.2 1.4 %collective-permute-done.2.refs_1_ = f32[8,2048]{1,0:T(8,128)S(1)} collective-permute-done((f32[8,2048]{1,0:T(8,128)S(1)}, f32[8,2048]{1,0:T(8,128)S(1)}, u32[]{:S(2)}, u32[]{:S(2)}) %collective-permute-start.2) | collective-permute-done | bytes 65568 | tf_op jit(solution)/shard_map/ppermute | solution.py:410
  19.6 0.0 collective-permute-done.3.refs_2_
  19.6 1.6 %collective-permute-start.4 = (f32[24,512]{1,0:T(8,128)S(1)}, f32[24,512]{1,0:T(8,128)S(1)}, u32[]{:S(2)}, u32[]{:S(2)}) collective-permute-start(f32[24,512]{1,0:T(8,128)S(1)} %get-tuple-element.18), channel_id=1, source_target_pairs={{0,4},{4,8},{8,12},{12,0},{1,5},{5,9},{9,13},{13,1},{2,6},{6,10},{... | collective-permute-start | bytes 147464 | tf_op jit(solution)/shard_map/ppermute | solution.py:414
  21.3 2.6 %collective-permute-start.5 = (f32[24,512]{1,0:T(8,128)S(1)}, f32[24,512]{1,0:T(8,128)S(1)}, u32[]{:S(2)}, u32[]{:S(2)}) collective-permute-start(f32[24,512]{1,0:T(8,128)S(1)} %get-tuple-element.19), channel_id=1, source_target_pairs={{0,8},{4,12},{8,0},{12,4},{1,9},{5,13},{9,1},{13,5},{2,10},{6,14},... | collective-permute-start | bytes 147464 | tf_op jit(solution)/shard_map/ppermute | solution.py:414
  23.9 1.3 %collective-permute-start.6 = (f32[24,512]{1,0:T(8,128)S(1)}, f32[24,512]{1,0:T(8,128)S(1)}, u32[]{:S(2)}, u32[]{:S(2)}) collective-permute-start(f32[24,512]{1,0:T(8,128)S(1)} %get-tuple-element.20), channel_id=1, source_target_pairs={{0,12},{4,0},{8,4},{12,8},{1,13},{5,1},{9,5},{13,9},{2,14},{6,2},{... | collective-permute-start | bytes 147464 | tf_op jit(solution)/shard_map/ppermute | solution.py:414
  25.2 0.4 %collective-permute-done.4.refs_1_ = f32[24,512]{1,0:T(8,128)S(1)} collective-permute-done((f32[24,512]{1,0:T(8,128)S(1)}, f32[24,512]{1,0:T(8,128)S(1)}, u32[]{:S(2)}, u32[]{:S(2)}) %collective-permute-start.4) | collective-permute-done | bytes 49184 | tf_op jit(solution)/shard_map/ppermute | solution.py:414
  25.6 2.1 %collective-permute-done.5.refs_2_ = f32[24,512]{1,0:T(8,128)S(1)} collective-permute-done((f32[24,512]{1,0:T(8,128)S(1)}, f32[24,512]{1,0:T(8,128)S(1)}, u32[]{:S(2)}, u32[]{:S(2)}) %collective-permute-start.5) | collective-permute-done | bytes 49184 | tf_op jit(solution)/shard_map/ppermute | solution.py:414
  27.7 0.4 %collective-permute-done.6.refs_3_ = f32[24,512]{1,0:T(8,128)S(1)} collective-permute-done((f32[24,512]{1,0:T(8,128)S(1)}, f32[24,512]{1,0:T(8,128)S(1)}, u32[]{:S(2)}, u32[]{:S(2)}) %collective-permute-start.6) | collective-permute-done | bytes 49184 | tf_op jit(solution)/shard_map/ppermute | solution.py:414
  28.1 0.1 collective-permute-start.7
  28.2 1.3 %quadrant.1 = (f32[1024,1024]{1,0:T(8,128)}, bf16[512,256]{1,0:T(8,128)(2,1)S(1)}, bf16[256,512]{1,0:T(8,128)(2,1)S(1)}) custom-call(f32[24,512]{1,0:T(8,128)S(1)} %get-tuple-element.17.refs_0_, f32[24,512]{1,0:T(8,128)S(1)} %collective-permute-done.4.refs_1_, f32[24,512]{1,0:T(8,128)S(1)} %collective-permute-done.5.refs_2_, ...), custom_call_target="tpu_custom_call" | custom-call | flops 268435456 | bytes 1048576 | tf_op jit(solution)/shard_map/quadrant/pallas_call | solution.py:339
  29.4 0.1 collective-permute-done.7.bundle
  29.5 1.9 %fisher.1 = (f32[8,1024]{1,0:T(8,128)}, f32[1024,1024]{1,0:T(8,128)}) custom-call(f32[1024,1024]{1,0:T(8,128)} %get-tuple-element.21.begun, bf16[512,256]{1,0:T(8,128)(2,1)S(1)} %get-tuple-element.22.left, bf16[256,512]{1,0:T(8,128)(2,1)S(1)} %get-tuple-element.23.right, ...), custom_call_target="tpu_custom_call", output_to_operand_aliasing={{1}: (0, {})} | custom-call | tf_op jit(solution)/shard_map/fisher/pallas_call | solution.py:361
  (2 shorter events, 0.0 us)
Async XLA Ops:
  3.7 9.6 %collective-permute-start = (f32[4,128,128]{2,1,0:T(8,128)S(1)}, f32[4,128,128]{2,1,0:T(8,128)S(1)}, u32[]{:S(2)}, u32[]{:S(2)}) collective-permute-start(f32[4,128,128]{2,1,0:T(8,128)S(1)} %project_acts.1.own), channel_id=1, source_target_pairs={{0,2},{2,0},{1,3},{3,1},{4,6},{6,4},{5,7},{7,5},{8,10},{10,8},{9,1... | collective-permute-start | bytes 786440 | tf_op jit(solution)/shard_map/ppermute | solution.py:388
  13.7 4.4 %collective-permute-start.1 = (f32[8,2048]{1,0:T(8,128)S(1)}, f32[8,2048]{1,0:T(8,128)S(1)}, u32[]{:S(2)}, u32[]{:S(2)}) collective-permute-start(f32[8,2048]{1,0:T(8,128)S(1)} %get-tuple-element.13), channel_id=1, source_target_pairs={{0,3},{1,2},{2,1},{3,0},{4,7},{5,6},{6,5},{7,4},{8,11},{9,10},{10,... | collective-permute-start | bytes 196616 | tf_op jit(solution)/shard_map/ppermute | solution.py:409
  13.9 5.7 %collective-permute-start.2 = (f32[8,2048]{1,0:T(8,128)S(1)}, f32[8,2048]{1,0:T(8,128)S(1)}, u32[]{:S(2)}, u32[]{:S(2)}) collective-permute-start(f32[8,2048]{1,0:T(8,128)S(1)} %get-tuple-element.14), channel_id=1, source_target_pairs={{0,2},{2,0},{1,3},{3,1},{4,6},{6,4},{5,7},{7,5},{8,10},{10,8},{9,1... | collective-permute-start | bytes 196616 | tf_op jit(solution)/shard_map/ppermute | solution.py:410
  15.4 4.2 %collective-permute-start.3 = (f32[8,2048]{1,0:T(8,128)S(1)}, f32[8,2048]{1,0:T(8,128)S(1)}, u32[]{:S(2)}, u32[]{:S(2)}) collective-permute-start(f32[8,2048]{1,0:T(8,128)S(1)} %get-tuple-element.15), channel_id=1, source_target_pairs={{0,1},{1,0},{2,3},{3,2},{4,5},{5,4},{6,7},{7,6},{8,9},{9,8},{10,11... | collective-permute-start | bytes 196616 | tf_op jit(solution)/shard_map/ppermute | solution.py:411
  19.6 5.9 %collective-permute-start.4 = (f32[24,512]{1,0:T(8,128)S(1)}, f32[24,512]{1,0:T(8,128)S(1)}, u32[]{:S(2)}, u32[]{:S(2)}) collective-permute-start(f32[24,512]{1,0:T(8,128)S(1)} %get-tuple-element.18), channel_id=1, source_target_pairs={{0,4},{4,8},{8,12},{12,0},{1,5},{5,9},{9,13},{13,1},{2,6},{6,10},{... | collective-permute-start | bytes 147464 | tf_op jit(solution)/shard_map/ppermute | solution.py:414
  21.3 6.4 %collective-permute-start.5 = (f32[24,512]{1,0:T(8,128)S(1)}, f32[24,512]{1,0:T(8,128)S(1)}, u32[]{:S(2)}, u32[]{:S(2)}) collective-permute-start(f32[24,512]{1,0:T(8,128)S(1)} %get-tuple-element.19), channel_id=1, source_target_pairs={{0,8},{4,12},{8,0},{12,4},{1,9},{5,13},{9,1},{13,5},{2,10},{6,14},... | collective-permute-start | bytes 147464 | tf_op jit(solution)/shard_map/ppermute | solution.py:414
  23.9 4.2 %collective-permute-start.6 = (f32[24,512]{1,0:T(8,128)S(1)}, f32[24,512]{1,0:T(8,128)S(1)}, u32[]{:S(2)}, u32[]{:S(2)}) collective-permute-start(f32[24,512]{1,0:T(8,128)S(1)} %get-tuple-element.20), channel_id=1, source_target_pairs={{0,12},{4,0},{8,4},{12,8},{1,13},{5,1},{9,5},{13,9},{2,14},{6,2},{... | collective-permute-start | bytes 147464 | tf_op jit(solution)/shard_map/ppermute | solution.py:414
  28.1 1.4 %collective-permute-start.7 = (f32[64,512]{1,0:T(8,128)S(1)}, f32[64,512]{1,0:T(8,128)S(1)}, u32[]{:S(2)}, u32[]{:S(2)}) collective-permute-start(f32[64,512]{1,0:T(8,128)S(1)} %bundle.1), channel_id=1, source_target_pairs={{0,1},{1,0},{2,3},{3,2},{4,5},{5,4},{6,7},{7,6},{8,9},{9,8},{10,11... | collective-permute-start | bytes 393224 | tf_op jit(solution)/shard_map/ppermute | solution.py:415

commit v22 on v15

--- a/solution.py
+++ b/solution.py
@@ -398,7 +398,7 @@
     across = lax.ppermute(krons[1], ("tensor", "seq"), [(p, 3 - p) for p in range(shards)])
     beside = lax.ppermute(krons[2], "tensor", swap)
     mate = lax.ppermute(krons[3], "seq", swap)
-    parcels = list(parcels_of([across, beside, mate, krons[0]], dp))
+    parcels = list(parcels_of([beside, across, mate, krons[0]], dp))
     for k in range(1, dp):
         parcels[k] = lax.ppermute(parcels[k], "dp", [(d, (d + k) % dp) for d in range(dp)])
     bundle = lax.ppermute(bundle_of(parcels), "seq", swap)

time: 31.5 us -> 31.4 us (level)
  waiting for transfers between devices: 6.88 us -> 6.45 us
    ppermute x1, waiting for transfers between devices: 2.4 us -> 1.4 us  [local(): lax.ppermute(krons[1], ('tensor', 'seq'), [(p, 3 - p) for p in range(shar...]
    ppermute x1, waiting for transfers between devices: 1.54 us -> 2.12 us  [local(): beside = lax.ppermute(krons[2], 'tensor', swap)]
    ppermute x1, starting transfers between devices: 0.21 us -> 0.57 us  [local(): mate = lax.ppermute(krons[3], 'seq', swap)]
where the time goes in v22:
time: 31.4 us; the launch traced here: 31.2 us
  Pallas kernels  13.1 us (42%)
  starting transfers between devices  10.9 us (35%)
  waiting for transfers between devices  6.45 us (21%)
  between operations  0.69 us (2%)
    pallas_call x2, Pallas kernels, project(): pl.pallas_call(functools.partial(project_kernel, widths), out_shape=jax.S...  9.37 us
    ppermute x3, starting transfers between devices, local(): lax.ppermute(parcels[k], 'dp', [(d, (d + k) % dp) for d in range(dp)])  5.65 us
    ppermute x1, starting transfers between devices, local(): other = lax.ppermute(act, 'tensor', swap)  3.01 us
    ppermute x3, waiting for transfers between devices, local(): lax.ppermute(parcels[k], 'dp', [(d, (d + k) % dp) for d in range(dp)])  2.85 us
    ppermute x1, waiting for transfers between devices, local(): beside = lax.ppermute(krons[2], 'tensor', swap)  2.12 us
    pallas_call x1, Pallas kernels, fisher_block(): pl.pallas_call(functools.partial(fisher_kernel, 1.0 / (rows * len(parcels...  1.94 us
    ppermute x1, starting transfers between devices, local(): beside = lax.ppermute(krons[2], 'tensor', swap)  1.64 us
    ppermute x1, waiting for transfers between devices, local(): lax.ppermute(krons[1], ('tensor', 'seq'), [(p, 3 - p) for p in range(shar...  1.4 us
  transfers between devices with their start and end apart: 8, of which 6 were waited for; matrix products, arithmetic and copies ran while one was open for 0% of the time, Pallas kernels for 25%

profile of v22, /device:TPU:0, one launch (start us, length us, event | category | flops | bytes accessed | tf_op | source)
XLA Modules:
  0.0 31.2 jit_solution(14250658355947159384)
XLA Ops:
  0.6 2.9 %project_acts.1.own = f32[4,128,128]{2,1,0:T(8,128)S(1)} custom-call(s32[32]{0:T(128)} %ids.3, s32[32]{0:T(128)} %signs.3, bf16[32,4096]{1,0:T(8,128)(2,1)} %table.3, bf16[1024,2048]{1,0:T(8,128)(2,1)} %bitcast.3), custom_call_target="tpu_custom_call" | custom-call | flops 536870912 | bytes 4194304 | tf_op jit(solution)/shard_map/project_acts/pallas_call | solution.py:135
  3.6 3.0 %collective-permute-start = (f32[4,128,128]{2,1,0:T(8,128)S(1)}, f32[4,128,128]{2,1,0:T(8,128)S(1)}, u32[]{:S(2)}, u32[]{:S(2)}) collective-permute-start(f32[4,128,128]{2,1,0:T(8,128)S(1)} %project_acts.1.own), channel_id=1, source_target_pairs={{0,2},{2,0},{1,3},{3,1},{4,6},{6,4},{5,7},{7,5},{8,10},{10,8},{9,1... | collective-permute-start | bytes 786440 | tf_op jit(solution)/shard_map/ppermute | solution.py:377
  6.6 6.4 %project_grads.1.grads = f32[4,128,128]{2,1,0:T(8,128)S(1)} custom-call(s32[112]{0:T(128)} %ids.2, s32[112]{0:T(128)} %signs.2, bf16[32,4096]{1,0:T(8,128)(2,1)} %table.2, bf16[1024,7168]{1,0:T(8,128)(2,1)} %bitcast.2), custom_call_target="tpu_custom_call" | custom-call | flops 1879048192 | bytes 14680064 | tf_op jit(solution)/shard_map/project_grads/pallas_call | solution.py:135
  13.0 0.0 collective-permute-done.act
  13.0 0.5 %kron.1 = (f32[8,2048]{1,0:T(8,128)S(1)}, f32[8,2048]{1,0:T(8,128)S(1)}, f32[8,2048]{1,0:T(8,128)S(1)}, f32[8,2048]{1,0:T(8,128)S(1)}) custom-call(f32[4,128,128]{2,1,0:T(8,128)S(1)} %project_grads.1.grads, f32[4,128,128]{2,1,0:T(8,128)S(1)} %project_acts.1.own, f32[4,128,128]{2,1,0:T(8,128)S(1)} %collective-permute-done.act), custom_call_target="tpu_custom_call" | custom-call | tf_op jit(solution)/shard_map/kron/pallas_call | solution.py:190
  13.6 1.6 %collective-permute-start.1 = (f32[8,2048]{1,0:T(8,128)S(1)}, f32[8,2048]{1,0:T(8,128)S(1)}, u32[]{:S(2)}, u32[]{:S(2)}) collective-permute-start(f32[8,2048]{1,0:T(8,128)S(1)} %get-tuple-element.13), channel_id=1, source_target_pairs={{0,2},{2,0},{1,3},{3,1},{4,6},{6,4},{5,7},{7,5},{8,10},{10,8},{9,1... | collective-permute-start | bytes 196616 | tf_op jit(solution)/shard_map/ppermute | solution.py:399
  15.2 0.0 collective-permute-start.2
  15.2 0.6 %collective-permute-start.3 = (f32[8,2048]{1,0:T(8,128)S(1)}, f32[8,2048]{1,0:T(8,128)S(1)}, u32[]{:S(2)}, u32[]{:S(2)}) collective-permute-start(f32[8,2048]{1,0:T(8,128)S(1)} %get-tuple-element.15), channel_id=1, source_target_pairs={{0,1},{1,0},{2,3},{3,2},{4,5},{5,4},{6,7},{7,6},{8,9},{9,8},{10,11... | collective-permute-start | bytes 196616 | tf_op jit(solution)/shard_map/ppermute | solution.py:400
  15.8 2.1 %collective-permute-done.1.refs_0_ = f32[8,2048]{1,0:T(8,128)S(1)} collective-permute-done((f32[8,2048]{1,0:T(8,128)S(1)}, f32[8,2048]{1,0:T(8,128)S(1)}, u32[]{:S(2)}, u32[]{:S(2)}) %collective-permute-start.1) | collective-permute-done | bytes 65568 | tf_op jit(solution)/shard_map/ppermute | solution.py:399
  17.9 1.4 %collective-permute-done.2.refs_1_ = f32[8,2048]{1,0:T(8,128)S(1)} collective-permute-done((f32[8,2048]{1,0:T(8,128)S(1)}, f32[8,2048]{1,0:T(8,128)S(1)}, u32[]{:S(2)}, u32[]{:S(2)}) %collective-permute-start.2) | collective-permute-done | bytes 65568 | tf_op jit(solution)/shard_map/ppermute | solution.py:398
  19.3 0.0 collective-permute-done.3.refs_2_
  19.3 1.7 %collective-permute-start.4 = (f32[24,512]{1,0:T(8,128)S(1)}, f32[24,512]{1,0:T(8,128)S(1)}, u32[]{:S(2)}, u32[]{:S(2)}) collective-permute-start(f32[24,512]{1,0:T(8,128)S(1)} %get-tuple-element.18), channel_id=1, source_target_pairs={{0,4},{4,8},{8,12},{12,0},{1,5},{5,9},{9,13},{13,1},{2,6},{6,10},{... | collective-permute-start | bytes 147464 | tf_op jit(solution)/shard_map/ppermute | solution.py:403
  21.0 2.6 %collective-permute-start.5 = (f32[24,512]{1,0:T(8,128)S(1)}, f32[24,512]{1,0:T(8,128)S(1)}, u32[]{:S(2)}, u32[]{:S(2)}) collective-permute-start(f32[24,512]{1,0:T(8,128)S(1)} %get-tuple-element.19), channel_id=1, source_target_pairs={{0,8},{4,12},{8,0},{12,4},{1,9},{5,13},{9,1},{13,5},{2,10},{6,14},... | collective-permute-start | bytes 147464 | tf_op jit(solution)/shard_map/ppermute | solution.py:403
  23.6 1.4 %collective-permute-start.6 = (f32[24,512]{1,0:T(8,128)S(1)}, f32[24,512]{1,0:T(8,128)S(1)}, u32[]{:S(2)}, u32[]{:S(2)}) collective-permute-start(f32[24,512]{1,0:T(8,128)S(1)} %get-tuple-element.20), channel_id=1, source_target_pairs={{0,12},{4,0},{8,4},{12,8},{1,13},{5,1},{9,5},{13,9},{2,14},{6,2},{... | collective-permute-start | bytes 147464 | tf_op jit(solution)/shard_map/ppermute | solution.py:403
  25.0 0.4 %collective-permute-done.4.refs_1_ = f32[24,512]{1,0:T(8,128)S(1)} collective-permute-done((f32[24,512]{1,0:T(8,128)S(1)}, f32[24,512]{1,0:T(8,128)S(1)}, u32[]{:S(2)}, u32[]{:S(2)}) %collective-permute-start.4) | collective-permute-done | bytes 49184 | tf_op jit(solution)/shard_map/ppermute | solution.py:403
  25.4 2.0 %collective-permute-done.5.refs_2_ = f32[24,512]{1,0:T(8,128)S(1)} collective-permute-done((f32[24,512]{1,0:T(8,128)S(1)}, f32[24,512]{1,0:T(8,128)S(1)}, u32[]{:S(2)}, u32[]{:S(2)}) %collective-permute-start.5) | collective-permute-done | bytes 49184 | tf_op jit(solution)/shard_map/ppermute | solution.py:403
  27.4 0.4 %collective-permute-done.6.refs_3_ = f32[24,512]{1,0:T(8,128)S(1)} collective-permute-done((f32[24,512]{1,0:T(8,128)S(1)}, f32[24,512]{1,0:T(8,128)S(1)}, u32[]{:S(2)}, u32[]{:S(2)}) %collective-permute-start.6) | collective-permute-done | bytes 49184 | tf_op jit(solution)/shard_map/ppermute | solution.py:403
  27.9 0.1 collective-permute-start.7
  27.9 1.3 %quadrant.1 = (f32[1024,1024]{1,0:T(8,128)}, bf16[512,256]{1,0:T(8,128)(2,1)S(1)}, bf16[256,512]{1,0:T(8,128)(2,1)S(1)}) custom-call(f32[24,512]{1,0:T(8,128)S(1)} %get-tuple-element.17.refs_0_, f32[24,512]{1,0:T(8,128)S(1)} %collective-permute-done.4.refs_1_, f32[24,512]{1,0:T(8,128)S(1)} %collective-permute-done.5.refs_2_, ...), custom_call_target="tpu_custom_call" | custom-call | flops 268435456 | bytes 1048576 | tf_op jit(solution)/shard_map/quadrant/pallas_call | solution.py:328
  29.2 0.1 collective-permute-done.7.bundle
  29.3 1.9 %fisher.1 = (f32[8,1024]{1,0:T(8,128)}, f32[1024,1024]{1,0:T(8,128)}) custom-call(f32[1024,1024]{1,0:T(8,128)} %get-tuple-element.21.begun, bf16[512,256]{1,0:T(8,128)(2,1)S(1)} %get-tuple-element.22.left, bf16[256,512]{1,0:T(8,128)(2,1)S(1)} %get-tuple-element.23.right, ...), custom_call_target="tpu_custom_call", output_to_operand_aliasing={{1}: (0, {})} | custom-call | tf_op jit(solution)/shard_map/fisher/pallas_call | solution.py:350
  (2 shorter events, 0.0 us)
Async XLA Ops:
  3.6 9.5 %collective-permute-start = (f32[4,128,128]{2,1,0:T(8,128)S(1)}, f32[4,128,128]{2,1,0:T(8,128)S(1)}, u32[]{:S(2)}, u32[]{:S(2)}) collective-permute-start(f32[4,128,128]{2,1,0:T(8,128)S(1)} %project_acts.1.own), channel_id=1, source_target_pairs={{0,2},{2,0},{1,3},{3,1},{4,6},{6,4},{5,7},{7,5},{8,10},{10,8},{9,1... | collective-permute-start | bytes 786440 | tf_op jit(solution)/shard_map/ppermute | solution.py:377
  13.6 4.3 %collective-permute-start.1 = (f32[8,2048]{1,0:T(8,128)S(1)}, f32[8,2048]{1,0:T(8,128)S(1)}, u32[]{:S(2)}, u32[]{:S(2)}) collective-permute-start(f32[8,2048]{1,0:T(8,128)S(1)} %get-tuple-element.13), channel_id=1, source_target_pairs={{0,2},{2,0},{1,3},{3,1},{4,6},{6,4},{5,7},{7,5},{8,10},{10,8},{9,1... | collective-permute-start | bytes 196616 | tf_op jit(solution)/shard_map/ppermute | solution.py:399
  15.2 4.1 %collective-permute-start.2 = (f32[8,2048]{1,0:T(8,128)S(1)}, f32[8,2048]{1,0:T(8,128)S(1)}, u32[]{:S(2)}, u32[]{:S(2)}) collective-permute-start(f32[8,2048]{1,0:T(8,128)S(1)} %get-tuple-element.14), channel_id=1, source_target_pairs={{0,3},{1,2},{2,1},{3,0},{4,7},{5,6},{6,5},{7,4},{8,11},{9,10},{10,... | collective-permute-start | bytes 196616 | tf_op jit(solution)/shard_map/ppermute | solution.py:398
  15.2 4.1 %collective-permute-start.3 = (f32[8,2048]{1,0:T(8,128)S(1)}, f32[8,2048]{1,0:T(8,128)S(1)}, u32[]{:S(2)}, u32[]{:S(2)}) collective-permute-start(f32[8,2048]{1,0:T(8,128)S(1)} %get-tuple-element.15), channel_id=1, source_target_pairs={{0,1},{1,0},{2,3},{3,2},{4,5},{5,4},{6,7},{7,6},{8,9},{9,8},{10,11... | collective-permute-start | bytes 196616 | tf_op jit(solution)/shard_map/ppermute | solution.py:400
  19.3 6.1 %collective-permute-start.4 = (f32[24,512]{1,0:T(8,128)S(1)}, f32[24,512]{1,0:T(8,128)S(1)}, u32[]{:S(2)}, u32[]{:S(2)}) collective-permute-start(f32[24,512]{1,0:T(8,128)S(1)} %get-tuple-element.18), channel_id=1, source_target_pairs={{0,4},{4,8},{8,12},{12,0},{1,5},{5,9},{9,13},{13,1},{2,6},{6,10},{... | collective-permute-start | bytes 147464 | tf_op jit(solution)/shard_map/ppermute | solution.py:403
  21.0 6.4 %collective-permute-start.5 = (f32[24,512]{1,0:T(8,128)S(1)}, f32[24,512]{1,0:T(8,128)S(1)}, u32[]{:S(2)}, u32[]{:S(2)}) collective-permute-start(f32[24,512]{1,0:T(8,128)S(1)} %get-tuple-element.19), channel_id=1, source_target_pairs={{0,8},{4,12},{8,0},{12,4},{1,9},{5,13},{9,1},{13,5},{2,10},{6,14},... | collective-permute-start | bytes 147464 | tf_op jit(solution)/shard_map/ppermute | solution.py:403
  23.6 4.2 %collective-permute-start.6 = (f32[24,512]{1,0:T(8,128)S(1)}, f32[24,512]{1,0:T(8,128)S(1)}, u32[]{:S(2)}, u32[]{:S(2)}) collective-permute-start(f32[24,512]{1,0:T(8,128)S(1)} %get-tuple-element.20), channel_id=1, source_target_pairs={{0,12},{4,0},{8,4},{12,8},{1,13},{5,1},{9,5},{13,9},{2,14},{6,2},{... | collective-permute-start | bytes 147464 | tf_op jit(solution)/shard_map/ppermute | solution.py:403
  27.9 1.4 %collective-permute-start.7 = (f32[64,512]{1,0:T(8,128)S(1)}, f32[64,512]{1,0:T(8,128)S(1)}, u32[]{:S(2)}, u32[]{:S(2)}) collective-permute-start(f32[64,512]{1,0:T(8,128)S(1)} %bundle.1), channel_id=1, source_target_pairs={{0,1},{1,0},{2,3},{3,2},{4,5},{5,4},{6,7},{7,6},{8,9},{9,8},{10,11... | collective-permute-start | bytes 393224 | tf_op jit(solution)/shard_map/ppermute | solution.py:404

commit v23 on v15

--- a/solution.py
+++ b/solution.py
@@ -272,7 +272,7 @@
     return [pl.ds(pl.multiple_of(place * part, part), part) for place in (core, 1 - core)]
 
 
-TILE = 256
+TILE = 128
 
 
 def quadrant_kernel(scale, *refs):

time: 31.5 us -> 31.5 us (level)
  no operation moved by 1% of the time
where the time goes in v23:
time: 31.5 us; the launch traced here: 31.3 us
  Pallas kernels  13.1 us (42%)
  starting transfers between devices  10.7 us (34%)
  waiting for transfers between devices  6.88 us (22%)
  between operations  0.69 us (2%)
    pallas_call x2, Pallas kernels, project(): pl.pallas_call(functools.partial(project_kernel, widths), out_shape=jax.S...  9.37 us
    ppermute x3, starting transfers between devices, local(): lax.ppermute(parcels[k], 'dp', [(d, (d + k) % dp) for d in range(dp)])  5.65 us
    ppermute x1, starting transfers between devices, local(): other = lax.ppermute(act, 'tensor', swap)  3.01 us
    ppermute x3, waiting for transfers between devices, local(): lax.ppermute(parcels[k], 'dp', [(d, (d + k) % dp) for d in range(dp)])  2.86 us
    ppermute x1, waiting for transfers between devices, local(): lax.ppermute(krons[1], ('tensor', 'seq'), [(p, 3 - p) for p in range(shar...  2.4 us
    pallas_call x1, Pallas kernels, fisher_block(): pl.pallas_call(functools.partial(fisher_kernel, 1.0 / (rows * len(parcels...  1.93 us
    ppermute x1, waiting for transfers between devices, local(): beside = lax.ppermute(krons[2], 'tensor', swap)  1.54 us
    ppermute x1, starting transfers between devices, local(): beside = lax.ppermute(krons[2], 'tensor', swap)  1.51 us
  transfers between devices with their start and end apart: 8, of which 6 were waited for; matrix products, arithmetic and copies ran while one was open for 0% of the time, Pallas kernels for 25%

profile of v23, /device:TPU:0, one launch (start us, length us, event | category | flops | bytes accessed | tf_op | source)
XLA Modules:
  0.0 31.3 jit_solution(17100778414027127846)
XLA Ops:
  0.6 2.9 %project_acts.1.own = f32[4,128,128]{2,1,0:T(8,128)S(1)} custom-call(s32[32]{0:T(128)} %ids.3, s32[32]{0:T(128)} %signs.3, bf16[32,4096]{1,0:T(8,128)(2,1)} %table.3, bf16[1024,2048]{1,0:T(8,128)(2,1)} %bitcast.3), custom_call_target="tpu_custom_call" | custom-call | flops 536870912 | bytes 4194304 | tf_op jit(solution)/shard_map/project_acts/pallas_call | solution.py:135
  3.6 3.0 %collective-permute-start = (f32[4,128,128]{2,1,0:T(8,128)S(1)}, f32[4,128,128]{2,1,0:T(8,128)S(1)}, u32[]{:S(2)}, u32[]{:S(2)}) collective-permute-start(f32[4,128,128]{2,1,0:T(8,128)S(1)} %project_acts.1.own), channel_id=1, source_target_pairs={{0,2},{2,0},{1,3},{3,1},{4,6},{6,4},{5,7},{7,5},{8,10},{10,8},{9,1... | collective-permute-start | bytes 786440 | tf_op jit(solution)/shard_map/ppermute | solution.py:377
  6.6 6.4 %project_grads.1.grads = f32[4,128,128]{2,1,0:T(8,128)S(1)} custom-call(s32[112]{0:T(128)} %ids.2, s32[112]{0:T(128)} %signs.2, bf16[32,4096]{1,0:T(8,128)(2,1)} %table.2, bf16[1024,7168]{1,0:T(8,128)(2,1)} %bitcast.2), custom_call_target="tpu_custom_call" | custom-call | flops 1879048192 | bytes 14680064 | tf_op jit(solution)/shard_map/project_grads/pallas_call | solution.py:135
  13.0 0.0 collective-permute-done.act
  13.0 0.5 %kron.1 = (f32[8,2048]{1,0:T(8,128)S(1)}, f32[8,2048]{1,0:T(8,128)S(1)}, f32[8,2048]{1,0:T(8,128)S(1)}, f32[8,2048]{1,0:T(8,128)S(1)}) custom-call(f32[4,128,128]{2,1,0:T(8,128)S(1)} %project_grads.1.grads, f32[4,128,128]{2,1,0:T(8,128)S(1)} %project_acts.1.own, f32[4,128,128]{2,1,0:T(8,128)S(1)} %collective-permute-done.act), custom_call_target="tpu_custom_call" | custom-call | tf_op jit(solution)/shard_map/kron/pallas_call | solution.py:190
  13.6 0.2 collective-permute-start.1
  13.8 1.5 %collective-permute-start.2 = (f32[8,2048]{1,0:T(8,128)S(1)}, f32[8,2048]{1,0:T(8,128)S(1)}, u32[]{:S(2)}, u32[]{:S(2)}) collective-permute-start(f32[8,2048]{1,0:T(8,128)S(1)} %get-tuple-element.14), channel_id=1, source_target_pairs={{0,2},{2,0},{1,3},{3,1},{4,6},{6,4},{5,7},{7,5},{8,10},{10,8},{9,1... | collective-permute-start | bytes 196616 | tf_op jit(solution)/shard_map/ppermute | solution.py:399
  15.3 0.2 collective-permute-start.3
  15.5 2.4 %collective-permute-done.1.refs_0_ = f32[8,2048]{1,0:T(8,128)S(1)} collective-permute-done((f32[8,2048]{1,0:T(8,128)S(1)}, f32[8,2048]{1,0:T(8,128)S(1)}, u32[]{:S(2)}, u32[]{:S(2)}) %collective-permute-start.1) | collective-permute-done | bytes 65568 | tf_op jit(solution)/shard_map/ppermute | solution.py:398
  17.9 1.5 %collective-permute-done.2.refs_1_ = f32[8,2048]{1,0:T(8,128)S(1)} collective-permute-done((f32[8,2048]{1,0:T(8,128)S(1)}, f32[8,2048]{1,0:T(8,128)S(1)}, u32[]{:S(2)}, u32[]{:S(2)}) %collective-permute-start.2) | collective-permute-done | bytes 65568 | tf_op jit(solution)/shard_map/ppermute | solution.py:399
  19.4 0.0 collective-permute-done.3.refs_2_
  19.5 1.7 %collective-permute-start.4 = (f32[24,512]{1,0:T(8,128)S(1)}, f32[24,512]{1,0:T(8,128)S(1)}, u32[]{:S(2)}, u32[]{:S(2)}) collective-permute-start(f32[24,512]{1,0:T(8,128)S(1)} %get-tuple-element.18), channel_id=1, source_target_pairs={{0,4},{4,8},{8,12},{12,0},{1,5},{5,9},{9,13},{13,1},{2,6},{6,10},{... | collective-permute-start | bytes 147464 | tf_op jit(solution)/shard_map/ppermute | solution.py:403
  21.2 2.6 %collective-permute-start.5 = (f32[24,512]{1,0:T(8,128)S(1)}, f32[24,512]{1,0:T(8,128)S(1)}, u32[]{:S(2)}, u32[]{:S(2)}) collective-permute-start(f32[24,512]{1,0:T(8,128)S(1)} %get-tuple-element.19), channel_id=1, source_target_pairs={{0,8},{4,12},{8,0},{12,4},{1,9},{5,13},{9,1},{13,5},{2,10},{6,14},... | collective-permute-start | bytes 147464 | tf_op jit(solution)/shard_map/ppermute | solution.py:403
  23.8 1.3 %collective-permute-start.6 = (f32[24,512]{1,0:T(8,128)S(1)}, f32[24,512]{1,0:T(8,128)S(1)}, u32[]{:S(2)}, u32[]{:S(2)}) collective-permute-start(f32[24,512]{1,0:T(8,128)S(1)} %get-tuple-element.20), channel_id=1, source_target_pairs={{0,12},{4,0},{8,4},{12,8},{1,13},{5,1},{9,5},{13,9},{2,14},{6,2},{... | collective-permute-start | bytes 147464 | tf_op jit(solution)/shard_map/ppermute | solution.py:403
  25.1 0.3 collective-permute-done.4.refs_1_
  25.4 2.2 %collective-permute-done.5.refs_2_ = f32[24,512]{1,0:T(8,128)S(1)} collective-permute-done((f32[24,512]{1,0:T(8,128)S(1)}, f32[24,512]{1,0:T(8,128)S(1)}, u32[]{:S(2)}, u32[]{:S(2)}) %collective-permute-start.5) | collective-permute-done | bytes 49184 | tf_op jit(solution)/shard_map/ppermute | solution.py:403
  27.6 0.4 %collective-permute-done.6.refs_3_ = f32[24,512]{1,0:T(8,128)S(1)} collective-permute-done((f32[24,512]{1,0:T(8,128)S(1)}, f32[24,512]{1,0:T(8,128)S(1)}, u32[]{:S(2)}, u32[]{:S(2)}) %collective-permute-start.6) | collective-permute-done | bytes 49184 | tf_op jit(solution)/shard_map/ppermute | solution.py:403
  28.0 0.1 collective-permute-start.7
  28.1 1.2 %quadrant.1 = (f32[1024,1024]{1,0:T(8,128)}, bf16[512,256]{1,0:T(8,128)(2,1)S(1)}, bf16[256,512]{1,0:T(8,128)(2,1)S(1)}) custom-call(f32[24,512]{1,0:T(8,128)S(1)} %get-tuple-element.17.refs_0_, f32[24,512]{1,0:T(8,128)S(1)} %collective-permute-done.4.refs_1_, f32[24,512]{1,0:T(8,128)S(1)} %collective-permute-done.5.refs_2_, ...), custom_call_target="tpu_custom_call" | custom-call | flops 268435456 | bytes 1048576 | tf_op jit(solution)/shard_map/quadrant/pallas_call | solution.py:328
  29.3 0.1 collective-permute-done.7.bundle
  29.4 1.9 %fisher.1 = (f32[8,1024]{1,0:T(8,128)}, f32[1024,1024]{1,0:T(8,128)}) custom-call(f32[1024,1024]{1,0:T(8,128)} %get-tuple-element.21.begun, bf16[512,256]{1,0:T(8,128)(2,1)S(1)} %get-tuple-element.22.left, bf16[256,512]{1,0:T(8,128)(2,1)S(1)} %get-tuple-element.23.right, ...), custom_call_target="tpu_custom_call", output_to_operand_aliasing={{1}: (0, {})} | custom-call | tf_op jit(solution)/shard_map/fisher/pallas_call | solution.py:350
  (2 shorter events, 0.0 us)
Async XLA Ops:
  3.6 9.5 %collective-permute-start = (f32[4,128,128]{2,1,0:T(8,128)S(1)}, f32[4,128,128]{2,1,0:T(8,128)S(1)}, u32[]{:S(2)}, u32[]{:S(2)}) collective-permute-start(f32[4,128,128]{2,1,0:T(8,128)S(1)} %project_acts.1.own), channel_id=1, source_target_pairs={{0,2},{2,0},{1,3},{3,1},{4,6},{6,4},{5,7},{7,5},{8,10},{10,8},{9,1... | collective-permute-start | bytes 786440 | tf_op jit(solution)/shard_map/ppermute | solution.py:377
  13.6 4.3 %collective-permute-start.1 = (f32[8,2048]{1,0:T(8,128)S(1)}, f32[8,2048]{1,0:T(8,128)S(1)}, u32[]{:S(2)}, u32[]{:S(2)}) collective-permute-start(f32[8,2048]{1,0:T(8,128)S(1)} %get-tuple-element.13), channel_id=1, source_target_pairs={{0,3},{1,2},{2,1},{3,0},{4,7},{5,6},{6,5},{7,4},{8,11},{9,10},{10,... | collective-permute-start | bytes 196616 | tf_op jit(solution)/shard_map/ppermute | solution.py:398
  13.8 5.7 %collective-permute-start.2 = (f32[8,2048]{1,0:T(8,128)S(1)}, f32[8,2048]{1,0:T(8,128)S(1)}, u32[]{:S(2)}, u32[]{:S(2)}) collective-permute-start(f32[8,2048]{1,0:T(8,128)S(1)} %get-tuple-element.14), channel_id=1, source_target_pairs={{0,2},{2,0},{1,3},{3,1},{4,6},{6,4},{5,7},{7,5},{8,10},{10,8},{9,1... | collective-permute-start | bytes 196616 | tf_op jit(solution)/shard_map/ppermute | solution.py:399
  15.3 4.1 %collective-permute-start.3 = (f32[8,2048]{1,0:T(8,128)S(1)}, f32[8,2048]{1,0:T(8,128)S(1)}, u32[]{:S(2)}, u32[]{:S(2)}) collective-permute-start(f32[8,2048]{1,0:T(8,128)S(1)} %get-tuple-element.15), channel_id=1, source_target_pairs={{0,1},{1,0},{2,3},{3,2},{4,5},{5,4},{6,7},{7,6},{8,9},{9,8},{10,11... | collective-permute-start | bytes 196616 | tf_op jit(solution)/shard_map/ppermute | solution.py:400
  19.5 5.9 %collective-permute-start.4 = (f32[24,512]{1,0:T(8,128)S(1)}, f32[24,512]{1,0:T(8,128)S(1)}, u32[]{:S(2)}, u32[]{:S(2)}) collective-permute-start(f32[24,512]{1,0:T(8,128)S(1)} %get-tuple-element.18), channel_id=1, source_target_pairs={{0,4},{4,8},{8,12},{12,0},{1,5},{5,9},{9,13},{13,1},{2,6},{6,10},{... | collective-permute-start | bytes 147464 | tf_op jit(solution)/shard_map/ppermute | solution.py:403
  21.2 6.4 %collective-permute-start.5 = (f32[24,512]{1,0:T(8,128)S(1)}, f32[24,512]{1,0:T(8,128)S(1)}, u32[]{:S(2)}, u32[]{:S(2)}) collective-permute-start(f32[24,512]{1,0:T(8,128)S(1)} %get-tuple-element.19), channel_id=1, source_target_pairs={{0,8},{4,12},{8,0},{12,4},{1,9},{5,13},{9,1},{13,5},{2,10},{6,14},... | collective-permute-start | bytes 147464 | tf_op jit(solution)/shard_map/ppermute | solution.py:403
  23.8 4.2 %collective-permute-start.6 = (f32[24,512]{1,0:T(8,128)S(1)}, f32[24,512]{1,0:T(8,128)S(1)}, u32[]{:S(2)}, u32[]{:S(2)}) collective-permute-start(f32[24,512]{1,0:T(8,128)S(1)} %get-tuple-element.20), channel_id=1, source_target_pairs={{0,12},{4,0},{8,4},{12,8},{1,13},{5,1},{9,5},{13,9},{2,14},{6,2},{... | collective-permute-start | bytes 147464 | tf_op jit(solution)/shard_map/ppermute | solution.py:403
  28.0 1.4 %collective-permute-start.7 = (f32[64,512]{1,0:T(8,128)S(1)}, f32[64,512]{1,0:T(8,128)S(1)}, u32[]{:S(2)}, u32[]{:S(2)}) collective-permute-start(f32[64,512]{1,0:T(8,128)S(1)} %bundle.1), channel_id=1, source_target_pairs={{0,1},{1,0},{2,3},{3,2},{4,5},{5,4},{6,7},{7,6},{8,9},{9,8},{10,11... | collective-permute-start | bytes 393224 | tf_op jit(solution)/shard_map/ppermute | solution.py:404

commit v24 on v22

--- a/solution.py
+++ b/solution.py
@@ -11,6 +11,7 @@
 BLOCK = 64
 LANES = 128
 STRIDE = 72
+ROUTES = ((0, 1, 2, 3), (1, 3, 0, 2), (3, 2, 1, 0), (2, 0, 3, 1))
 VMEM_BYTES = 48 * 1024 * 1024
 
 
@@ -209,7 +210,10 @@
     core, chip = lax.axis_index("seq"), lax.axis_index("tensor") * 2
     blocks = [chip + core, chip + 1 - core]
     for k, parcel in enumerate(parcels):
-        for step, block in enumerate(blocks + [lax.rem(lax.axis_index("dp") + k, dp)]):
+        need = ROUTES[k][0]
+        for d in range(1, dp):
+            need = jnp.where(lax.axis_index("dp") == d, ROUTES[k][d], need)
+        for step, block in enumerate(blocks + [need]):
             lanes = pl.ds(pl.multiple_of(block * width, LANES), width)
             row = summands[0][:, lanes]
             for other in summands[1:]:
@@ -400,7 +404,7 @@
     mate = lax.ppermute(krons[3], "seq", swap)
     parcels = list(parcels_of([beside, across, mate, krons[0]], dp))
     for k in range(1, dp):
-        parcels[k] = lax.ppermute(parcels[k], "dp", [(d, (d + k) % dp) for d in range(dp)])
+        parcels[k] = lax.ppermute(parcels[k], "dp", list(enumerate(ROUTES[k])))
     bundle = lax.ppermute(bundle_of(parcels), "seq", swap)
     mine, fisher = fisher_block(quadrant_of(parcels), parcels, bundle)
     return mine, fisher

time: 31.4 us -> 31.4 us (level)
  transfers between devices with their start and end apart: 8 -> 8, of which waited for: 6 -> 5; matrix products, arithmetic and copies ran while one was open for 0% -> 0% of each run, Pallas kernels for 25% -> 25%
where the time goes in v24:
time: 31.4 us; the launch traced here: 31.2 us
  Pallas kernels  13.1 us (42%)
  starting transfers between devices  11 us (35%)
  waiting for transfers between devices  6.33 us (20%)
  between operations  0.69 us (2%)
    pallas_call x2, Pallas kernels, project(): pl.pallas_call(functools.partial(project_kernel, widths), out_shape=jax.S...  9.38 us
    ppermute x3, starting transfers between devices, local(): parcels[k] = lax.ppermute(parcels[k], 'dp', list(enumerate(ROUTES[k])))  5.77 us
    ppermute x1, starting transfers between devices, local(): other = lax.ppermute(act, 'tensor', swap)  3 us
    ppermute x3, waiting for transfers between devices, local(): parcels[k] = lax.ppermute(parcels[k], 'dp', list(enumerate(ROUTES[k])))  2.73 us
    ppermute x1, waiting for transfers between devices, local(): beside = lax.ppermute(krons[2], 'tensor', swap)  2.12 us
    pallas_call x1, Pallas kernels, fisher_block(): pl.pallas_call(functools.partial(fisher_kernel, 1.0 / (rows * len(parcels...  1.94 us
    ppermute x1, starting transfers between devices, local(): beside = lax.ppermute(krons[2], 'tensor', swap)  1.64 us
    ppermute x1, waiting for transfers between devices, local(): lax.ppermute(krons[1], ('tensor', 'seq'), [(p, 3 - p) for p in range(shar...  1.4 us
  transfers between devices with their start and end apart: 8, of which 5 were waited for; matrix products, arithmetic and copies ran while one was open for 0% of the time, Pallas kernels for 25%

profile of v24, /device:TPU:0, one launch (start us, length us, event | category | flops | bytes accessed | tf_op | source)
XLA Modules:
  0.0 31.2 jit_solution(15024064670288190831)
XLA Ops:
  0.6 2.9 %project_acts.1.own = f32[4,128,128]{2,1,0:T(8,128)S(1)} custom-call(s32[32]{0:T(128)} %ids.3, s32[32]{0:T(128)} %signs.3, bf16[32,4096]{1,0:T(8,128)(2,1)} %table.3, bf16[1024,2048]{1,0:T(8,128)(2,1)} %bitcast.3), custom_call_target="tpu_custom_call" | custom-call | flops 536870912 | bytes 4194304 | tf_op jit(solution)/shard_map/project_acts/pallas_call | solution.py:136
  3.6 3.0 %collective-permute-start = (f32[4,128,128]{2,1,0:T(8,128)S(1)}, f32[4,128,128]{2,1,0:T(8,128)S(1)}, u32[]{:S(2)}, u32[]{:S(2)}) collective-permute-start(f32[4,128,128]{2,1,0:T(8,128)S(1)} %project_acts.1.own), channel_id=1, source_target_pairs={{0,2},{2,0},{1,3},{3,1},{4,6},{6,4},{5,7},{7,5},{8,10},{10,8},{9,1... | collective-permute-start | bytes 786440 | tf_op jit(solution)/shard_map/ppermute | solution.py:381
  6.6 6.4 %project_grads.1.grads = f32[4,128,128]{2,1,0:T(8,128)S(1)} custom-call(s32[112]{0:T(128)} %ids.2, s32[112]{0:T(128)} %signs.2, bf16[32,4096]{1,0:T(8,128)(2,1)} %table.2, bf16[1024,7168]{1,0:T(8,128)(2,1)} %bitcast.2), custom_call_target="tpu_custom_call" | custom-call | flops 1879048192 | bytes 14680064 | tf_op jit(solution)/shard_map/project_grads/pallas_call | solution.py:136
  13.0 0.0 collective-permute-done.act
  13.0 0.5 %kron.1 = (f32[8,2048]{1,0:T(8,128)S(1)}, f32[8,2048]{1,0:T(8,128)S(1)}, f32[8,2048]{1,0:T(8,128)S(1)}, f32[8,2048]{1,0:T(8,128)S(1)}) custom-call(f32[4,128,128]{2,1,0:T(8,128)S(1)} %project_grads.1.grads, f32[4,128,128]{2,1,0:T(8,128)S(1)} %project_acts.1.own, f32[4,128,128]{2,1,0:T(8,128)S(1)} %collective-permute-done.act), custom_call_target="tpu_custom_call" | custom-call | tf_op jit(solution)/shard_map/kron/pallas_call | solution.py:191
  13.6 1.6 %collective-permute-start.1 = (f32[8,2048]{1,0:T(8,128)S(1)}, f32[8,2048]{1,0:T(8,128)S(1)}, u32[]{:S(2)}, u32[]{:S(2)}) collective-permute-start(f32[8,2048]{1,0:T(8,128)S(1)} %get-tuple-element.13), channel_id=1, source_target_pairs={{0,2},{2,0},{1,3},{3,1},{4,6},{6,4},{5,7},{7,5},{8,10},{10,8},{9,1... | collective-permute-start | bytes 196616 | tf_op jit(solution)/shard_map/ppermute | solution.py:403
  15.2 0.0 collective-permute-start.2
  15.2 0.6 %collective-permute-start.3 = (f32[8,2048]{1,0:T(8,128)S(1)}, f32[8,2048]{1,0:T(8,128)S(1)}, u32[]{:S(2)}, u32[]{:S(2)}) collective-permute-start(f32[8,2048]{1,0:T(8,128)S(1)} %get-tuple-element.15), channel_id=1, source_target_pairs={{0,1},{1,0},{2,3},{3,2},{4,5},{5,4},{6,7},{7,6},{8,9},{9,8},{10,11... | collective-permute-start | bytes 196616 | tf_op jit(solution)/shard_map/ppermute | solution.py:404
  15.8 2.1 %collective-permute-done.1.refs_0_ = f32[8,2048]{1,0:T(8,128)S(1)} collective-permute-done((f32[8,2048]{1,0:T(8,128)S(1)}, f32[8,2048]{1,0:T(8,128)S(1)}, u32[]{:S(2)}, u32[]{:S(2)}) %collective-permute-start.1) | collective-permute-done | bytes 65568 | tf_op jit(solution)/shard_map/ppermute | solution.py:403
  17.9 1.4 %collective-permute-done.2.refs_1_ = f32[8,2048]{1,0:T(8,128)S(1)} collective-permute-done((f32[8,2048]{1,0:T(8,128)S(1)}, f32[8,2048]{1,0:T(8,128)S(1)}, u32[]{:S(2)}, u32[]{:S(2)}) %collective-permute-start.2) | collective-permute-done | bytes 65568 | tf_op jit(solution)/shard_map/ppermute | solution.py:402
  19.3 0.0 collective-permute-done.3.refs_2_
  19.3 1.7 %collective-permute-start.4 = (f32[24,512]{1,0:T(8,128)S(1)}, f32[24,512]{1,0:T(8,128)S(1)}, u32[]{:S(2)}, u32[]{:S(2)}) collective-permute-start(f32[24,512]{1,0:T(8,128)S(1)} %get-tuple-element.18), channel_id=1, source_target_pairs={{0,4},{4,12},{8,0},{12,8},{1,5},{5,13},{9,1},{13,9},{2,6},{6,14},{... | collective-permute-start | bytes 147464 | tf_op jit(solution)/shard_map/ppermute | solution.py:407
  21.0 2.5 %collective-permute-start.5 = (f32[24,512]{1,0:T(8,128)S(1)}, f32[24,512]{1,0:T(8,128)S(1)}, u32[]{:S(2)}, u32[]{:S(2)}) collective-permute-start(f32[24,512]{1,0:T(8,128)S(1)} %get-tuple-element.19), channel_id=1, source_target_pairs={{0,12},{4,8},{8,4},{12,0},{1,13},{5,9},{9,5},{13,1},{2,14},{6,10},... | collective-permute-start | bytes 147464 | tf_op jit(solution)/shard_map/ppermute | solution.py:407
  23.5 1.6 %collective-permute-start.6 = (f32[24,512]{1,0:T(8,128)S(1)}, f32[24,512]{1,0:T(8,128)S(1)}, u32[]{:S(2)}, u32[]{:S(2)}) collective-permute-start(f32[24,512]{1,0:T(8,128)S(1)} %get-tuple-element.20), channel_id=1, source_target_pairs={{0,8},{4,0},{8,12},{12,4},{1,9},{5,1},{9,13},{13,5},{2,10},{6,2},{... | collective-permute-start | bytes 147464 | tf_op jit(solution)/shard_map/ppermute | solution.py:407
  25.1 0.0 collective-permute-done.4.refs_1_
  25.1 2.2 %collective-permute-done.5.refs_2_ = f32[24,512]{1,0:T(8,128)S(1)} collective-permute-done((f32[24,512]{1,0:T(8,128)S(1)}, f32[24,512]{1,0:T(8,128)S(1)}, u32[]{:S(2)}, u32[]{:S(2)}) %collective-permute-start.5) | collective-permute-done | bytes 49184 | tf_op jit(solution)/shard_map/ppermute | solution.py:407
  27.3 0.5 %collective-permute-done.6.refs_3_ = f32[24,512]{1,0:T(8,128)S(1)} collective-permute-done((f32[24,512]{1,0:T(8,128)S(1)}, f32[24,512]{1,0:T(8,128)S(1)}, u32[]{:S(2)}, u32[]{:S(2)}) %collective-permute-start.6) | collective-permute-done | bytes 49184 | tf_op jit(solution)/shard_map/ppermute | solution.py:407
  27.8 0.1 collective-permute-start.7
  27.9 1.3 %quadrant.1 = (f32[1024,1024]{1,0:T(8,128)}, bf16[512,256]{1,0:T(8,128)(2,1)S(1)}, bf16[256,512]{1,0:T(8,128)(2,1)S(1)}) custom-call(f32[24,512]{1,0:T(8,128)S(1)} %get-tuple-element.17.refs_0_, f32[24,512]{1,0:T(8,128)S(1)} %collective-permute-done.4.refs_1_, f32[24,512]{1,0:T(8,128)S(1)} %collective-permute-done.5.refs_2_, ...), custom_call_target="tpu_custom_call" | custom-call | flops 268435456 | bytes 1048576 | tf_op jit(solution)/shard_map/quadrant/pallas_call | solution.py:332
  29.2 0.1 collective-permute-done.7.bundle
  29.3 1.9 %fisher.1 = (f32[8,1024]{1,0:T(8,128)}, f32[1024,1024]{1,0:T(8,128)}) custom-call(f32[1024,1024]{1,0:T(8,128)} %get-tuple-element.21.begun, bf16[512,256]{1,0:T(8,128)(2,1)S(1)} %get-tuple-element.22.left, bf16[256,512]{1,0:T(8,128)(2,1)S(1)} %get-tuple-element.23.right, ...), custom_call_target="tpu_custom_call", output_to_operand_aliasing={{1}: (0, {})} | custom-call | tf_op jit(solution)/shard_map/fisher/pallas_call | solution.py:354
  (2 shorter events, 0.0 us)
Async XLA Ops:
  3.6 9.5 %collective-permute-start = (f32[4,128,128]{2,1,0:T(8,128)S(1)}, f32[4,128,128]{2,1,0:T(8,128)S(1)}, u32[]{:S(2)}, u32[]{:S(2)}) collective-permute-start(f32[4,128,128]{2,1,0:T(8,128)S(1)} %project_acts.1.own), channel_id=1, source_target_pairs={{0,2},{2,0},{1,3},{3,1},{4,6},{6,4},{5,7},{7,5},{8,10},{10,8},{9,1... | collective-permute-start | bytes 786440 | tf_op jit(solution)/shard_map/ppermute | solution.py:381
  13.6 4.3 %collective-permute-start.1 = (f32[8,2048]{1,0:T(8,128)S(1)}, f32[8,2048]{1,0:T(8,128)S(1)}, u32[]{:S(2)}, u32[]{:S(2)}) collective-permute-start(f32[8,2048]{1,0:T(8,128)S(1)} %get-tuple-element.13), channel_id=1, source_target_pairs={{0,2},{2,0},{1,3},{3,1},{4,6},{6,4},{5,7},{7,5},{8,10},{10,8},{9,1... | collective-permute-start | bytes 196616 | tf_op jit(solution)/shard_map/ppermute | solution.py:403
  15.2 4.1 %collective-permute-start.2 = (f32[8,2048]{1,0:T(8,128)S(1)}, f32[8,2048]{1,0:T(8,128)S(1)}, u32[]{:S(2)}, u32[]{:S(2)}) collective-permute-start(f32[8,2048]{1,0:T(8,128)S(1)} %get-tuple-element.14), channel_id=1, source_target_pairs={{0,3},{1,2},{2,1},{3,0},{4,7},{5,6},{6,5},{7,4},{8,11},{9,10},{10,... | collective-permute-start | bytes 196616 | tf_op jit(solution)/shard_map/ppermute | solution.py:402
  15.2 4.1 %collective-permute-start.3 = (f32[8,2048]{1,0:T(8,128)S(1)}, f32[8,2048]{1,0:T(8,128)S(1)}, u32[]{:S(2)}, u32[]{:S(2)}) collective-permute-start(f32[8,2048]{1,0:T(8,128)S(1)} %get-tuple-element.15), channel_id=1, source_target_pairs={{0,1},{1,0},{2,3},{3,2},{4,5},{5,4},{6,7},{7,6},{8,9},{9,8},{10,11... | collective-permute-start | bytes 196616 | tf_op jit(solution)/shard_map/ppermute | solution.py:404
  19.3 5.8 %collective-permute-start.4 = (f32[24,512]{1,0:T(8,128)S(1)}, f32[24,512]{1,0:T(8,128)S(1)}, u32[]{:S(2)}, u32[]{:S(2)}) collective-permute-start(f32[24,512]{1,0:T(8,128)S(1)} %get-tuple-element.18), channel_id=1, source_target_pairs={{0,4},{4,12},{8,0},{12,8},{1,5},{5,13},{9,1},{13,9},{2,6},{6,14},{... | collective-permute-start | bytes 147464 | tf_op jit(solution)/shard_map/ppermute | solution.py:407
  21.0 6.3 %collective-permute-start.5 = (f32[24,512]{1,0:T(8,128)S(1)}, f32[24,512]{1,0:T(8,128)S(1)}, u32[]{:S(2)}, u32[]{:S(2)}) collective-permute-start(f32[24,512]{1,0:T(8,128)S(1)} %get-tuple-element.19), channel_id=1, source_target_pairs={{0,12},{4,8},{8,4},{12,0},{1,13},{5,9},{9,5},{13,1},{2,14},{6,10},... | collective-permute-start | bytes 147464 | tf_op jit(solution)/shard_map/ppermute | solution.py:407
  23.5 4.3 %collective-permute-start.6 = (f32[24,512]{1,0:T(8,128)S(1)}, f32[24,512]{1,0:T(8,128)S(1)}, u32[]{:S(2)}, u32[]{:S(2)}) collective-permute-start(f32[24,512]{1,0:T(8,128)S(1)} %get-tuple-element.20), channel_id=1, source_target_pairs={{0,8},{4,0},{8,12},{12,4},{1,9},{5,1},{9,13},{13,5},{2,10},{6,2},{... | collective-permute-start | bytes 147464 | tf_op jit(solution)/shard_map/ppermute | solution.py:407
  27.8 1.4 %collective-permute-start.7 = (f32[64,512]{1,0:T(8,128)S(1)}, f32[64,512]{1,0:T(8,128)S(1)}, u32[]{:S(2)}, u32[]{:S(2)}) collective-permute-start(f32[64,512]{1,0:T(8,128)S(1)} %bundle.1), channel_id=1, source_target_pairs={{0,1},{1,0},{2,3},{3,2},{4,5},{5,4},{6,7},{7,6},{8,9},{9,8},{10,11... | collective-permute-start | bytes 393224 | tf_op jit(solution)/shard_map/ppermute | solution.py:408

commit v25 on v24

--- a/solution.py
+++ b/solution.py
@@ -402,7 +402,7 @@
     across = lax.ppermute(krons[1], ("tensor", "seq"), [(p, 3 - p) for p in range(shards)])
     beside = lax.ppermute(krons[2], "tensor", swap)
     mate = lax.ppermute(krons[3], "seq", swap)
-    parcels = list(parcels_of([beside, across, mate, krons[0]], dp))
+    parcels = list(parcels_of([across, beside, mate, krons[0]], dp))
     for k in range(1, dp):
         parcels[k] = lax.ppermute(parcels[k], "dp", list(enumerate(ROUTES[k])))
     bundle = lax.ppermute(bundle_of(parcels), "seq", swap)

time: 31.4 us -> 31.5 us (level)
  waiting for transfers between devices: 6.33 us -> 6.74 us
    ppermute x1, waiting for transfers between devices: 1.4 us -> 2.4 us  [local(): lax.ppermute(krons[1], ('tensor', 'seq'), [(p, 3 - p) for p in range(shar...]
    ppermute x1, waiting for transfers between devices: 2.12 us -> 1.54 us  [local(): beside = lax.ppermute(krons[2], 'tensor', swap)]
    ppermute x1, starting transfers between devices: 0.57 us -> 0.21 us  [local(): mate = lax.ppermute(krons[3], 'seq', swap)]
where the time goes in v25:
time: 31.5 us; the launch traced here: 31.3 us
  Pallas kernels  13.1 us (42%)
  starting transfers between devices  10.8 us (34%)
  waiting for transfers between devices  6.74 us (21%)
  between operations  0.69 us (2%)
    pallas_call x2, Pallas kernels, project(): pl.pallas_call(functools.partial(project_kernel, widths), out_shape=jax.S...  9.37 us
    ppermute x3, starting transfers between devices, local(): parcels[k] = lax.ppermute(parcels[k], 'dp', list(enumerate(ROUTES[k])))  5.76 us
    ppermute x1, starting transfers between devices, local(): other = lax.ppermute(act, 'tensor', swap)  3.01 us
    ppermute x3, waiting for transfers between devices, local(): parcels[k] = lax.ppermute(parcels[k], 'dp', list(enumerate(ROUTES[k])))  2.73 us
    ppermute x1, waiting for transfers between devices, local(): lax.ppermute(krons[1], ('tensor', 'seq'), [(p, 3 - p) for p in range(shar...  2.4 us
    pallas_call x1, Pallas kernels, fisher_block(): pl.pallas_call(functools.partial(fisher_kernel, 1.0 / (rows * len(parcels...  1.94 us
    ppermute x1, waiting for transfers between devices, local(): beside = lax.ppermute(krons[2], 'tensor', swap)  1.54 us
    ppermute x1, starting transfers between devices, local(): beside = lax.ppermute(krons[2], 'tensor', swap)  1.52 us
  transfers between devices with their start and end apart: 8, of which 5 were waited for; matrix products, arithmetic and copies ran while one was open for 0% of the time, Pallas kernels for 25%

profile of v25, /device:TPU:0, one launch (start us, length us, event | category | flops | bytes accessed | tf_op | source)
XLA Modules:
  0.0 31.3 jit_solution(13873273749989525395)
XLA Ops:
  0.6 2.9 %project_acts.1.own = f32[4,128,128]{2,1,0:T(8,128)S(1)} custom-call(s32[32]{0:T(128)} %ids.3, s32[32]{0:T(128)} %signs.3, bf16[32,4096]{1,0:T(8,128)(2,1)} %table.3, bf16[1024,2048]{1,0:T(8,128)(2,1)} %bitcast.3), custom_call_target="tpu_custom_call" | custom-call | flops 536870912 | bytes 4194304 | tf_op jit(solution)/shard_map/project_acts/pallas_call | solution.py:136
  3.6 3.0 %collective-permute-start = (f32[4,128,128]{2,1,0:T(8,128)S(1)}, f32[4,128,128]{2,1,0:T(8,128)S(1)}, u32[]{:S(2)}, u32[]{:S(2)}) collective-permute-start(f32[4,128,128]{2,1,0:T(8,128)S(1)} %project_acts.1.own), channel_id=1, source_target_pairs={{0,2},{2,0},{1,3},{3,1},{4,6},{6,4},{5,7},{7,5},{8,10},{10,8},{9,1... | collective-permute-start | bytes 786440 | tf_op jit(solution)/shard_map/ppermute | solution.py:381
  6.6 6.4 %project_grads.1.grads = f32[4,128,128]{2,1,0:T(8,128)S(1)} custom-call(s32[112]{0:T(128)} %ids.2, s32[112]{0:T(128)} %signs.2, bf16[32,4096]{1,0:T(8,128)(2,1)} %table.2, bf16[1024,7168]{1,0:T(8,128)(2,1)} %bitcast.2), custom_call_target="tpu_custom_call" | custom-call | flops 1879048192 | bytes 14680064 | tf_op jit(solution)/shard_map/project_grads/pallas_call | solution.py:136
  13.0 0.0 collective-permute-done.act
  13.0 0.5 %kron.1 = (f32[8,2048]{1,0:T(8,128)S(1)}, f32[8,2048]{1,0:T(8,128)S(1)}, f32[8,2048]{1,0:T(8,128)S(1)}, f32[8,2048]{1,0:T(8,128)S(1)}) custom-call(f32[4,128,128]{2,1,0:T(8,128)S(1)} %project_grads.1.grads, f32[4,128,128]{2,1,0:T(8,128)S(1)} %project_acts.1.own, f32[4,128,128]{2,1,0:T(8,128)S(1)} %collective-permute-done.act), custom_call_target="tpu_custom_call" | custom-call | tf_op jit(solution)/shard_map/kron/pallas_call | solution.py:191
  13.6 0.2 collective-permute-start.1
  13.8 1.5 %collective-permute-start.2 = (f32[8,2048]{1,0:T(8,128)S(1)}, f32[8,2048]{1,0:T(8,128)S(1)}, u32[]{:S(2)}, u32[]{:S(2)}) collective-permute-start(f32[8,2048]{1,0:T(8,128)S(1)} %get-tuple-element.14), channel_id=1, source_target_pairs={{0,2},{2,0},{1,3},{3,1},{4,6},{6,4},{5,7},{7,5},{8,10},{10,8},{9,1... | collective-permute-start | bytes 196616 | tf_op jit(solution)/shard_map/ppermute | solution.py:403
  15.3 0.2 collective-permute-start.3
  15.5 2.4 %collective-permute-done.1.refs_0_ = f32[8,2048]{1,0:T(8,128)S(1)} collective-permute-done((f32[8,2048]{1,0:T(8,128)S(1)}, f32[8,2048]{1,0:T(8,128)S(1)}, u32[]{:S(2)}, u32[]{:S(2)}) %collective-permute-start.1) | collective-permute-done | bytes 65568 | tf_op jit(solution)/shard_map/ppermute | solution.py:402
  17.9 1.5 %collective-permute-done.2.refs_1_ = f32[8,2048]{1,0:T(8,128)S(1)} collective-permute-done((f32[8,2048]{1,0:T(8,128)S(1)}, f32[8,2048]{1,0:T(8,128)S(1)}, u32[]{:S(2)}, u32[]{:S(2)}) %collective-permute-start.2) | collective-permute-done | bytes 65568 | tf_op jit(solution)/shard_map/ppermute | solution.py:403
  19.4 0.0 collective-permute-done.3.refs_2_
  19.5 1.7 %collective-permute-start.4 = (f32[24,512]{1,0:T(8,128)S(1)}, f32[24,512]{1,0:T(8,128)S(1)}, u32[]{:S(2)}, u32[]{:S(2)}) collective-permute-start(f32[24,512]{1,0:T(8,128)S(1)} %get-tuple-element.18), channel_id=1, source_target_pairs={{0,4},{4,12},{8,0},{12,8},{1,5},{5,13},{9,1},{13,9},{2,6},{6,14},{... | collective-permute-start | bytes 147464 | tf_op jit(solution)/shard_map/ppermute | solution.py:407
  21.2 2.5 %collective-permute-start.5 = (f32[24,512]{1,0:T(8,128)S(1)}, f32[24,512]{1,0:T(8,128)S(1)}, u32[]{:S(2)}, u32[]{:S(2)}) collective-permute-start(f32[24,512]{1,0:T(8,128)S(1)} %get-tuple-element.19), channel_id=1, source_target_pairs={{0,12},{4,8},{8,4},{12,0},{1,13},{5,9},{9,5},{13,1},{2,14},{6,10},... | collective-permute-start | bytes 147464 | tf_op jit(solution)/shard_map/ppermute | solution.py:407
  23.6 1.6 %collective-permute-start.6 = (f32[24,512]{1,0:T(8,128)S(1)}, f32[24,512]{1,0:T(8,128)S(1)}, u32[]{:S(2)}, u32[]{:S(2)}) collective-permute-start(f32[24,512]{1,0:T(8,128)S(1)} %get-tuple-element.20), channel_id=1, source_target_pairs={{0,8},{4,0},{8,12},{12,4},{1,9},{5,1},{9,13},{13,5},{2,10},{6,2},{... | collective-permute-start | bytes 147464 | tf_op jit(solution)/shard_map/ppermute | solution.py:407
  25.2 0.0 collective-permute-done.4.refs_1_
  25.2 2.4 %collective-permute-done.5.refs_2_ = f32[24,512]{1,0:T(8,128)S(1)} collective-permute-done((f32[24,512]{1,0:T(8,128)S(1)}, f32[24,512]{1,0:T(8,128)S(1)}, u32[]{:S(2)}, u32[]{:S(2)}) %collective-permute-start.5) | collective-permute-done | bytes 49184 | tf_op jit(solution)/shard_map/ppermute | solution.py:407
  27.6 0.4 %collective-permute-done.6.refs_3_ = f32[24,512]{1,0:T(8,128)S(1)} collective-permute-done((f32[24,512]{1,0:T(8,128)S(1)}, f32[24,512]{1,0:T(8,128)S(1)}, u32[]{:S(2)}, u32[]{:S(2)}) %collective-permute-start.6) | collective-permute-done | bytes 49184 | tf_op jit(solution)/shard_map/ppermute | solution.py:407
  28.0 0.1 collective-permute-start.7
  28.0 1.3 %quadrant.1 = (f32[1024,1024]{1,0:T(8,128)}, bf16[512,256]{1,0:T(8,128)(2,1)S(1)}, bf16[256,512]{1,0:T(8,128)(2,1)S(1)}) custom-call(f32[24,512]{1,0:T(8,128)S(1)} %get-tuple-element.17.refs_0_, f32[24,512]{1,0:T(8,128)S(1)} %collective-permute-done.4.refs_1_, f32[24,512]{1,0:T(8,128)S(1)} %collective-permute-done.5.refs_2_, ...), custom_call_target="tpu_custom_call" | custom-call | flops 268435456 | bytes 1048576 | tf_op jit(solution)/shard_map/quadrant/pallas_call | solution.py:332
  29.3 0.1 collective-permute-done.7.bundle
  29.4 1.9 %fisher.1 = (f32[8,1024]{1,0:T(8,128)}, f32[1024,1024]{1,0:T(8,128)}) custom-call(f32[1024,1024]{1,0:T(8,128)} %get-tuple-element.21.begun, bf16[512,256]{1,0:T(8,128)(2,1)S(1)} %get-tuple-element.22.left, bf16[256,512]{1,0:T(8,128)(2,1)S(1)} %get-tuple-element.23.right, ...), custom_call_target="tpu_custom_call", output_to_operand_aliasing={{1}: (0, {})} | custom-call | tf_op jit(solution)/shard_map/fisher/pallas_call | solution.py:354
  (2 shorter events, 0.0 us)
Async XLA Ops:
  3.6 9.5 %collective-permute-start = (f32[4,128,128]{2,1,0:T(8,128)S(1)}, f32[4,128,128]{2,1,0:T(8,128)S(1)}, u32[]{:S(2)}, u32[]{:S(2)}) collective-permute-start(f32[4,128,128]{2,1,0:T(8,128)S(1)} %project_acts.1.own), channel_id=1, source_target_pairs={{0,2},{2,0},{1,3},{3,1},{4,6},{6,4},{5,7},{7,5},{8,10},{10,8},{9,1... | collective-permute-start | bytes 786440 | tf_op jit(solution)/shard_map/ppermute | solution.py:381
  13.6 4.3 %collective-permute-start.1 = (f32[8,2048]{1,0:T(8,128)S(1)}, f32[8,2048]{1,0:T(8,128)S(1)}, u32[]{:S(2)}, u32[]{:S(2)}) collective-permute-start(f32[8,2048]{1,0:T(8,128)S(1)} %get-tuple-element.13), channel_id=1, source_target_pairs={{0,3},{1,2},{2,1},{3,0},{4,7},{5,6},{6,5},{7,4},{8,11},{9,10},{10,... | collective-permute-start | bytes 196616 | tf_op jit(solution)/shard_map/ppermute | solution.py:402
  13.8 5.7 %collective-permute-start.2 = (f32[8,2048]{1,0:T(8,128)S(1)}, f32[8,2048]{1,0:T(8,128)S(1)}, u32[]{:S(2)}, u32[]{:S(2)}) collective-permute-start(f32[8,2048]{1,0:T(8,128)S(1)} %get-tuple-element.14), channel_id=1, source_target_pairs={{0,2},{2,0},{1,3},{3,1},{4,6},{6,4},{5,7},{7,5},{8,10},{10,8},{9,1... | collective-permute-start | bytes 196616 | tf_op jit(solution)/shard_map/ppermute | solution.py:403
  15.3 4.1 %collective-permute-start.3 = (f32[8,2048]{1,0:T(8,128)S(1)}, f32[8,2048]{1,0:T(8,128)S(1)}, u32[]{:S(2)}, u32[]{:S(2)}) collective-permute-start(f32[8,2048]{1,0:T(8,128)S(1)} %get-tuple-element.15), channel_id=1, source_target_pairs={{0,1},{1,0},{2,3},{3,2},{4,5},{5,4},{6,7},{7,6},{8,9},{9,8},{10,11... | collective-permute-start | bytes 196616 | tf_op jit(solution)/shard_map/ppermute | solution.py:404
  19.5 5.8 %collective-permute-start.4 = (f32[24,512]{1,0:T(8,128)S(1)}, f32[24,512]{1,0:T(8,128)S(1)}, u32[]{:S(2)}, u32[]{:S(2)}) collective-permute-start(f32[24,512]{1,0:T(8,128)S(1)} %get-tuple-element.18), channel_id=1, source_target_pairs={{0,4},{4,12},{8,0},{12,8},{1,5},{5,13},{9,1},{13,9},{2,6},{6,14},{... | collective-permute-start | bytes 147464 | tf_op jit(solution)/shard_map/ppermute | solution.py:407
  21.2 6.4 %collective-permute-start.5 = (f32[24,512]{1,0:T(8,128)S(1)}, f32[24,512]{1,0:T(8,128)S(1)}, u32[]{:S(2)}, u32[]{:S(2)}) collective-permute-start(f32[24,512]{1,0:T(8,128)S(1)} %get-tuple-element.19), channel_id=1, source_target_pairs={{0,12},{4,8},{8,4},{12,0},{1,13},{5,9},{9,5},{13,1},{2,14},{6,10},... | collective-permute-start | bytes 147464 | tf_op jit(solution)/shard_map/ppermute | solution.py:407
  23.6 4.3 %collective-permute-start.6 = (f32[24,512]{1,0:T(8,128)S(1)}, f32[24,512]{1,0:T(8,128)S(1)}, u32[]{:S(2)}, u32[]{:S(2)}) collective-permute-start(f32[24,512]{1,0:T(8,128)S(1)} %get-tuple-element.20), channel_id=1, source_target_pairs={{0,8},{4,0},{8,12},{12,4},{1,9},{5,1},{9,13},{13,5},{2,10},{6,2},{... | collective-permute-start | bytes 147464 | tf_op jit(solution)/shard_map/ppermute | solution.py:407
  28.0 1.4 %collective-permute-start.7 = (f32[64,512]{1,0:T(8,128)S(1)}, f32[64,512]{1,0:T(8,128)S(1)}, u32[]{:S(2)}, u32[]{:S(2)}) collective-permute-start(f32[64,512]{1,0:T(8,128)S(1)} %bundle.1), channel_id=1, source_target_pairs={{0,1},{1,0},{2,3},{3,2},{4,5},{5,4},{6,7},{7,6},{8,9},{9,8},{10,11... | collective-permute-start | bytes 393224 | tf_op jit(solution)/shard_map/ppermute | solution.py:408

commit v26 on v24

--- a/solution.py
+++ b/solution.py
@@ -25,7 +25,7 @@
     chunk = most
     while inner % chunk:
         chunk -= LANES
-    return [most // 2] + [chunk] * (inner // chunk) + [most // 4] * 2
+    return [most // 2] + [chunk] * (inner // chunk) + [most // 2]
 
 
 def split3(x):

time: 31.4 us -> 31.3 us (level)
  no operation moved by 1% of the time
where the time goes in v26:
time: 31.3 us; the launch traced here: 31.1 us
  Pallas kernels  13 us (42%)
  starting transfers between devices  11.1 us (35%)
  waiting for transfers between devices  6.33 us (20%)
  between operations  0.69 us (2%)
    pallas_call x2, Pallas kernels, project(): pl.pallas_call(functools.partial(project_kernel, widths), out_shape=jax.S...  9.28 us
    ppermute x3, starting transfers between devices, local(): parcels[k] = lax.ppermute(parcels[k], 'dp', list(enumerate(ROUTES[k])))  5.78 us
    ppermute x1, starting transfers between devices, local(): other = lax.ppermute(act, 'tensor', swap)  3 us
    ppermute x3, waiting for transfers between devices, local(): parcels[k] = lax.ppermute(parcels[k], 'dp', list(enumerate(ROUTES[k])))  2.73 us
    ppermute x1, waiting for transfers between devices, local(): beside = lax.ppermute(krons[2], 'tensor', swap)  2.12 us
    pallas_call x1, Pallas kernels, fisher_block(): pl.pallas_call(functools.partial(fisher_kernel, 1.0 / (rows * len(parcels...  1.94 us
    ppermute x1, starting transfers between devices, local(): beside = lax.ppermute(krons[2], 'tensor', swap)  1.65 us
    ppermute x1, waiting for transfers between devices, local(): lax.ppermute(krons[1], ('tensor', 'seq'), [(p, 3 - p) for p in range(shar...  1.4 us
  transfers between devices with their start and end apart: 8, of which 5 were waited for; matrix products, arithmetic and copies ran while one was open for 0% of the time, Pallas kernels for 25%

profile of v26, /device:TPU:0, one launch (start us, length us, event | category | flops | bytes accessed | tf_op | source)
XLA Modules:
  0.0 31.1 jit_solution(1923141927656068222)
XLA Ops:
  0.6 2.9 %project_acts.1.own = f32[4,128,128]{2,1,0:T(8,128)S(1)} custom-call(s32[32]{0:T(128)} %ids.3, s32[32]{0:T(128)} %signs.3, bf16[32,4096]{1,0:T(8,128)(2,1)} %table.3, bf16[1024,2048]{1,0:T(8,128)(2,1)} %bitcast.3), custom_call_target="tpu_custom_call" | custom-call | flops 536870912 | bytes 4194304 | tf_op jit(solution)/shard_map/project_acts/pallas_call | solution.py:136
  3.5 3.0 %collective-permute-start = (f32[4,128,128]{2,1,0:T(8,128)S(1)}, f32[4,128,128]{2,1,0:T(8,128)S(1)}, u32[]{:S(2)}, u32[]{:S(2)}) collective-permute-start(f32[4,128,128]{2,1,0:T(8,128)S(1)} %project_acts.1.own), channel_id=1, source_target_pairs={{0,2},{2,0},{1,3},{3,1},{4,6},{6,4},{5,7},{7,5},{8,10},{10,8},{9,1... | collective-permute-start | bytes 786440 | tf_op jit(solution)/shard_map/ppermute | solution.py:381
  6.5 6.4 %project_grads.1.grads = f32[4,128,128]{2,1,0:T(8,128)S(1)} custom-call(s32[112]{0:T(128)} %ids.2, s32[112]{0:T(128)} %signs.2, bf16[32,4096]{1,0:T(8,128)(2,1)} %table.2, bf16[1024,7168]{1,0:T(8,128)(2,1)} %bitcast.2), custom_call_target="tpu_custom_call" | custom-call | flops 1879048192 | bytes 14680064 | tf_op jit(solution)/shard_map/project_grads/pallas_call | solution.py:136
  12.9 0.0 collective-permute-done.act
  12.9 0.5 %kron.1 = (f32[8,2048]{1,0:T(8,128)S(1)}, f32[8,2048]{1,0:T(8,128)S(1)}, f32[8,2048]{1,0:T(8,128)S(1)}, f32[8,2048]{1,0:T(8,128)S(1)}) custom-call(f32[4,128,128]{2,1,0:T(8,128)S(1)} %project_grads.1.grads, f32[4,128,128]{2,1,0:T(8,128)S(1)} %project_acts.1.own, f32[4,128,128]{2,1,0:T(8,128)S(1)} %collective-permute-done.act), custom_call_target="tpu_custom_call" | custom-call | tf_op jit(solution)/shard_map/kron/pallas_call | solution.py:191
  13.5 1.7 %collective-permute-start.1 = (f32[8,2048]{1,0:T(8,128)S(1)}, f32[8,2048]{1,0:T(8,128)S(1)}, u32[]{:S(2)}, u32[]{:S(2)}) collective-permute-start(f32[8,2048]{1,0:T(8,128)S(1)} %get-tuple-element.13), channel_id=1, source_target_pairs={{0,2},{2,0},{1,3},{3,1},{4,6},{6,4},{5,7},{7,5},{8,10},{10,8},{9,1... | collective-permute-start | bytes 196616 | tf_op jit(solution)/shard_map/ppermute | solution.py:403
  15.1 0.0 collective-permute-start.2
  15.1 0.5 %collective-permute-start.3 = (f32[8,2048]{1,0:T(8,128)S(1)}, f32[8,2048]{1,0:T(8,128)S(1)}, u32[]{:S(2)}, u32[]{:S(2)}) collective-permute-start(f32[8,2048]{1,0:T(8,128)S(1)} %get-tuple-element.15), channel_id=1, source_target_pairs={{0,1},{1,0},{2,3},{3,2},{4,5},{5,4},{6,7},{7,6},{8,9},{9,8},{10,11... | collective-permute-start | bytes 196616 | tf_op jit(solution)/shard_map/ppermute | solution.py:404
  15.7 2.1 %collective-permute-done.1.refs_0_ = f32[8,2048]{1,0:T(8,128)S(1)} collective-permute-done((f32[8,2048]{1,0:T(8,128)S(1)}, f32[8,2048]{1,0:T(8,128)S(1)}, u32[]{:S(2)}, u32[]{:S(2)}) %collective-permute-start.1) | collective-permute-done | bytes 65568 | tf_op jit(solution)/shard_map/ppermute | solution.py:403
  17.8 1.4 %collective-permute-done.2.refs_1_ = f32[8,2048]{1,0:T(8,128)S(1)} collective-permute-done((f32[8,2048]{1,0:T(8,128)S(1)}, f32[8,2048]{1,0:T(8,128)S(1)}, u32[]{:S(2)}, u32[]{:S(2)}) %collective-permute-start.2) | collective-permute-done | bytes 65568 | tf_op jit(solution)/shard_map/ppermute | solution.py:402
  19.2 0.0 collective-permute-done.3.refs_2_
  19.2 1.7 %collective-permute-start.4 = (f32[24,512]{1,0:T(8,128)S(1)}, f32[24,512]{1,0:T(8,128)S(1)}, u32[]{:S(2)}, u32[]{:S(2)}) collective-permute-start(f32[24,512]{1,0:T(8,128)S(1)} %get-tuple-element.18), channel_id=1, source_target_pairs={{0,4},{4,12},{8,0},{12,8},{1,5},{5,13},{9,1},{13,9},{2,6},{6,14},{... | collective-permute-start | bytes 147464 | tf_op jit(solution)/shard_map/ppermute | solution.py:407
  21.0 2.5 %collective-permute-start.5 = (f32[24,512]{1,0:T(8,128)S(1)}, f32[24,512]{1,0:T(8,128)S(1)}, u32[]{:S(2)}, u32[]{:S(2)}) collective-permute-start(f32[24,512]{1,0:T(8,128)S(1)} %get-tuple-element.19), channel_id=1, source_target_pairs={{0,12},{4,8},{8,4},{12,0},{1,13},{5,9},{9,5},{13,1},{2,14},{6,10},... | collective-permute-start | bytes 147464 | tf_op jit(solution)/shard_map/ppermute | solution.py:407
  23.4 1.6 %collective-permute-start.6 = (f32[24,512]{1,0:T(8,128)S(1)}, f32[24,512]{1,0:T(8,128)S(1)}, u32[]{:S(2)}, u32[]{:S(2)}) collective-permute-start(f32[24,512]{1,0:T(8,128)S(1)} %get-tuple-element.20), channel_id=1, source_target_pairs={{0,8},{4,0},{8,12},{12,4},{1,9},{5,1},{9,13},{13,5},{2,10},{6,2},{... | collective-permute-start | bytes 147464 | tf_op jit(solution)/shard_map/ppermute | solution.py:407
  25.0 0.0 collective-permute-done.4.refs_1_
  25.0 2.2 %collective-permute-done.5.refs_2_ = f32[24,512]{1,0:T(8,128)S(1)} collective-permute-done((f32[24,512]{1,0:T(8,128)S(1)}, f32[24,512]{1,0:T(8,128)S(1)}, u32[]{:S(2)}, u32[]{:S(2)}) %collective-permute-start.5) | collective-permute-done | bytes 49184 | tf_op jit(solution)/shard_map/ppermute | solution.py:407
  27.3 0.5 %collective-permute-done.6.refs_3_ = f32[24,512]{1,0:T(8,128)S(1)} collective-permute-done((f32[24,512]{1,0:T(8,128)S(1)}, f32[24,512]{1,0:T(8,128)S(1)}, u32[]{:S(2)}, u32[]{:S(2)}) %collective-permute-start.6) | collective-permute-done | bytes 49184 | tf_op jit(solution)/shard_map/ppermute | solution.py:407
  27.8 0.1 collective-permute-start.7
  27.8 1.3 %quadrant.1 = (f32[1024,1024]{1,0:T(8,128)}, bf16[512,256]{1,0:T(8,128)(2,1)S(1)}, bf16[256,512]{1,0:T(8,128)(2,1)S(1)}) custom-call(f32[24,512]{1,0:T(8,128)S(1)} %get-tuple-element.17.refs_0_, f32[24,512]{1,0:T(8,128)S(1)} %collective-permute-done.4.refs_1_, f32[24,512]{1,0:T(8,128)S(1)} %collective-permute-done.5.refs_2_, ...), custom_call_target="tpu_custom_call" | custom-call | flops 268435456 | bytes 1048576 | tf_op jit(solution)/shard_map/quadrant/pallas_call | solution.py:332
  29.1 0.1 collective-permute-done.7.bundle
  29.2 1.9 %fisher.1 = (f32[8,1024]{1,0:T(8,128)}, f32[1024,1024]{1,0:T(8,128)}) custom-call(f32[1024,1024]{1,0:T(8,128)} %get-tuple-element.21.begun, bf16[512,256]{1,0:T(8,128)(2,1)S(1)} %get-tuple-element.22.left, bf16[256,512]{1,0:T(8,128)(2,1)S(1)} %get-tuple-element.23.right, ...), custom_call_target="tpu_custom_call", output_to_operand_aliasing={{1}: (0, {})} | custom-call | tf_op jit(solution)/shard_map/fisher/pallas_call | solution.py:354
  (2 shorter events, 0.0 us)
Async XLA Ops:
  3.5 9.4 %collective-permute-start = (f32[4,128,128]{2,1,0:T(8,128)S(1)}, f32[4,128,128]{2,1,0:T(8,128)S(1)}, u32[]{:S(2)}, u32[]{:S(2)}) collective-permute-start(f32[4,128,128]{2,1,0:T(8,128)S(1)} %project_acts.1.own), channel_id=1, source_target_pairs={{0,2},{2,0},{1,3},{3,1},{4,6},{6,4},{5,7},{7,5},{8,10},{10,8},{9,1... | collective-permute-start | bytes 786440 | tf_op jit(solution)/shard_map/ppermute | solution.py:381
  13.5 4.3 %collective-permute-start.1 = (f32[8,2048]{1,0:T(8,128)S(1)}, f32[8,2048]{1,0:T(8,128)S(1)}, u32[]{:S(2)}, u32[]{:S(2)}) collective-permute-start(f32[8,2048]{1,0:T(8,128)S(1)} %get-tuple-element.13), channel_id=1, source_target_pairs={{0,2},{2,0},{1,3},{3,1},{4,6},{6,4},{5,7},{7,5},{8,10},{10,8},{9,1... | collective-permute-start | bytes 196616 | tf_op jit(solution)/shard_map/ppermute | solution.py:403
  15.1 4.1 %collective-permute-start.2 = (f32[8,2048]{1,0:T(8,128)S(1)}, f32[8,2048]{1,0:T(8,128)S(1)}, u32[]{:S(2)}, u32[]{:S(2)}) collective-permute-start(f32[8,2048]{1,0:T(8,128)S(1)} %get-tuple-element.14), channel_id=1, source_target_pairs={{0,3},{1,2},{2,1},{3,0},{4,7},{5,6},{6,5},{7,4},{8,11},{9,10},{10,... | collective-permute-start | bytes 196616 | tf_op jit(solution)/shard_map/ppermute | solution.py:402
  15.1 4.1 %collective-permute-start.3 = (f32[8,2048]{1,0:T(8,128)S(1)}, f32[8,2048]{1,0:T(8,128)S(1)}, u32[]{:S(2)}, u32[]{:S(2)}) collective-permute-start(f32[8,2048]{1,0:T(8,128)S(1)} %get-tuple-element.15), channel_id=1, source_target_pairs={{0,1},{1,0},{2,3},{3,2},{4,5},{5,4},{6,7},{7,6},{8,9},{9,8},{10,11... | collective-permute-start | bytes 196616 | tf_op jit(solution)/shard_map/ppermute | solution.py:404
  19.2 5.8 %collective-permute-start.4 = (f32[24,512]{1,0:T(8,128)S(1)}, f32[24,512]{1,0:T(8,128)S(1)}, u32[]{:S(2)}, u32[]{:S(2)}) collective-permute-start(f32[24,512]{1,0:T(8,128)S(1)} %get-tuple-element.18), channel_id=1, source_target_pairs={{0,4},{4,12},{8,0},{12,8},{1,5},{5,13},{9,1},{13,9},{2,6},{6,14},{... | collective-permute-start | bytes 147464 | tf_op jit(solution)/shard_map/ppermute | solution.py:407
  21.0 6.3 %collective-permute-start.5 = (f32[24,512]{1,0:T(8,128)S(1)}, f32[24,512]{1,0:T(8,128)S(1)}, u32[]{:S(2)}, u32[]{:S(2)}) collective-permute-start(f32[24,512]{1,0:T(8,128)S(1)} %get-tuple-element.19), channel_id=1, source_target_pairs={{0,12},{4,8},{8,4},{12,0},{1,13},{5,9},{9,5},{13,1},{2,14},{6,10},... | collective-permute-start | bytes 147464 | tf_op jit(solution)/shard_map/ppermute | solution.py:407
  23.4 4.3 %collective-permute-start.6 = (f32[24,512]{1,0:T(8,128)S(1)}, f32[24,512]{1,0:T(8,128)S(1)}, u32[]{:S(2)}, u32[]{:S(2)}) collective-permute-start(f32[24,512]{1,0:T(8,128)S(1)} %get-tuple-element.20), channel_id=1, source_target_pairs={{0,8},{4,0},{8,12},{12,4},{1,9},{5,1},{9,13},{13,5},{2,10},{6,2},{... | collective-permute-start | bytes 147464 | tf_op jit(solution)/shard_map/ppermute | solution.py:407
  27.8 1.4 %collective-permute-start.7 = (f32[64,512]{1,0:T(8,128)S(1)}, f32[64,512]{1,0:T(8,128)S(1)}, u32[]{:S(2)}, u32[]{:S(2)}) collective-permute-start(f32[64,512]{1,0:T(8,128)S(1)} %bundle.1), channel_id=1, source_target_pairs={{0,1},{1,0},{2,3},{3,2},{4,5},{5,4},{6,7},{7,6},{8,9},{9,8},{10,11... | collective-permute-start | bytes 393224 | tf_op jit(solution)/shard_map/ppermute | solution.py:408
